TPU v7x, 32 devices: a whole 2x2x4 slice. The times are simulated.
32 devices in a mesh: img: 8 (over y, x, core), txt: 4 (over z).
Axes of the slice: x: 2, y: 2, z: 4, core: 2. Of those that a mesh axis runs over, the one named last changes fastest.
Arguments:
- image_emb: float32 [1024, 768], P(('img', 'txt')), may hold values from -0.6 to 0.6
- text_emb: float32 [1024, 768], P(('txt', 'img')), may hold values from -0.6 to 0.6
- pairs: int32 [1024], P('img'), may hold values from 0 to 1023, each once
- log_scale: float32 [1], replicated, may hold values from 2 to 2.6
- bias: float32 [1], replicated, may hold values from -12 to -8
Outputs:
- image_loss: float32 [1024], P('img')
- image_grad: float32 [1024, 768], P(('img', 'txt'))
- text_grad: float32 [1024, 768], P(('txt', 'img'))
Inputs may be any that keep to these rules, and one draw needn't show every extreme that they name: `pairs`: each text is matched to exactly one image.
All inputs are finite; a program needn't handle non-finite values.
Results may differ from a plain program's by a relative error of at most 0.0003.
Values sent between devices are 32-bit elements; how exact they have to be, the bound alone decides.
No kernel may reach another device: no remote copies, remote signals or barrier semaphores. Data moves between devices by JAX's collectives and lax.ppermute only.
A program may use at most 64 MiB of HBM per device.

v0:
```python
import jax
import jax.numpy as jnp
from jax import lax
from jax.sharding import PartitionSpec as P


def per_device(image_emb, text_emb, pairs, log_scale, bias):
    images = lax.all_gather(image_emb, "txt", axis=0, tiled=True)
    texts = lax.all_gather(text_emb, "img", axis=0, tiled=True)
    scale = jnp.exp(log_scale[0])
    shift = bias[0]
    text_count = texts.shape[0]
    dots = lax.dot_general(
        images,
        texts,
        (((1,), (1,)), ((), ())),
        precision=lax.Precision.HIGHEST,
        preferred_element_type=jnp.float32,
    )
    logits = scale * dots + shift
    columns = lax.axis_index("txt") * text_count + jnp.arange(text_count, dtype=jnp.int32)
    sign = jnp.where(pairs[:, None] == columns[None, :], 1.0, -1.0).astype(jnp.float32)
    loss_part = jnp.sum(jax.nn.softplus(-sign * logits), axis=1)
    image_loss = lax.psum(loss_part, "txt")
    dlogits = -sign * jax.nn.sigmoid(-sign * logits)
    image_term = scale * jnp.dot(
        dlogits, texts, precision=lax.Precision.HIGHEST, preferred_element_type=jnp.float32
    )
    image_grad = lax.psum_scatter(image_term, "txt", scatter_dimension=0, tiled=True)
    text_term = scale * lax.dot_general(
        dlogits,
        images,
        (((0,), (0,)), ((), ())),
        precision=lax.Precision.HIGHEST,
        preferred_element_type=jnp.float32,
    )
    text_grad = lax.psum_scatter(text_term, "img", scatter_dimension=0, tiled=True)
    return (image_loss, image_grad, text_grad)


def solution(mesh):
    return jax.shard_map(
        per_device,
        mesh=mesh,
        in_specs=(P(("img", "txt"), None), P(("txt", "img"), None), P("img"), P(), P()),
        out_specs=(P("img"), P(("img", "txt"), None), P(("txt", "img"), None)),
        check_vma=False,
    )
```

profile of v0, /device:TPU:0, one launch (start us, length us, event | category | flops | bytes accessed | tf_op | source)
XLA Modules:
  0.0 104.5 jit_solution(4938364873603050519)
XLA Ops:
  7.2 0.0 reduce-scatter.3.cloned.1.call-start
  7.9 0.0 copy-start
  7.9 16.6 %all_gather.6 = f32[128,768]{1,0:T(8,128)S(1)} all-gather(f32[32,768]{1,0:T(8,128)} %param.5), channel_id=1, replica_groups=mesh['img'=8,'txt'=4] {'txt'}, dimensions={0}, use_global_device_ids=true | all-gather | bytes 491520 | tf_op jit(solution)/shard_map/all_gather | solution.py:8
  24.4 0.0 copy-done
  24.4 10.4 %all_gather.7 = f32[256,768]{1,0:T(8,128)S(1)} all-gather(f32[32,768]{1,0:T(8,128)S(1)} %copy-done), channel_id=1, replica_groups=mesh['img'=8,'txt'=4] {'img'}, dimensions={0}, use_global_device_ids=true | all-gather | bytes 884736 | tf_op jit(solution)/shard_map/all_gather | solution.py:9
  35.6 0.0 copy-start.1
  35.6 0.6 copy-done.1
  36.2 1.1 %fusion.2 = (f32[128]{0:T(128)S(1)}, f32[128,256]{1,0:T(8,128)S(1)}) fusion(f32[]{:T(128)} %bitcast.6, f32[128,768]{1,0:T(8,128)S(1)} %all_gather.6, f32[256,768]{1,0:T(8,128)S(1)} %all_gather.7, f32[]{:T(128)} %bitcast, s32[256]{0:T(256)S(1)} %iota_add_fusion, s32[128]{0:T(128)S(1)} %copy-done.1), kind=kOutput, calls=%fused_computation.6 | convolution fusion | flops 302415744 | bytes 1312776 | tf_op jit(solution)/shard_map/dot_general | solution.py:13
  37.3 1.4 %convolution_multiply_fusion.1 = f32[128,768]{1,0:T(8,128)} fusion(f32[256,768]{1,0:T(8,128)S(1)} %all_gather.7, f32[]{:T(128)} %bitcast, f32[128,256]{1,0:T(8,128)S(1)} %get-tuple-element.4, s32[256]{0:T(256)S(1)} %iota_add_fusion, s32[128]{0:T(128)S(1)} %copy-done.1), kind=kOutput, calls=%fused_computation.1 | convolution fusion | flops 302317568 | bytes 1312260 | tf_op jit(solution)/shard_map/dot_general | solution.py:26
  38.6 0.0 reduce-scatter.3.cloned.1.call-update
  38.7 0.0 reduce-scatter.5.cloned.1.call-start
  38.7 1.8 %convolution_multiply_fusion = f32[256,768]{1,0:T(8,128)} fusion(f32[128,768]{1,0:T(8,128)S(1)} %all_gather.6, f32[]{:T(128)} %bitcast, f32[128,256]{1,0:T(8,128)S(1)} %get-tuple-element.4, s32[256]{0:T(256)S(1)} %iota_add_fusion, s32[128]{0:T(128)S(1)} %copy-done.1), kind=kOutput, calls=%fused_computation | convolution fusion | flops 302415872 | bytes 1312260 | tf_op jit(solution)/shard_map/dot_general | solution.py:30
  40.5 0.0 reduce-scatter.5.cloned.1.call-update
  40.5 13.0 %psum.7 = f32[128]{0:T(128)} all-reduce(f32[128]{0:T(128)S(1)} %get-tuple-element.3), channel_id=1, replica_groups=mesh['img'=8,'txt'=4] {'txt'}, use_global_device_ids=true, to_apply=%region_1.2 | all-reduce | flops 128 | bytes 1024 | tf_op jit(solution)/shard_map/psum | solution.py:24
  53.6 6.7 %reduce-scatter.3.cloned.1.call-done = f32[32,768]{1,0:T(8,128)} async-done(((f32[128,768]{1,0:T(8,128)}), f32[32,768]{1,0:T(8,128)}) %reduce-scatter.3.cloned.1.call-update) | async-done | bytes 98320 | tf_op jit(solution)/shard_map/reduce_scatter | solution.py:29
  60.3 37.3 %reduce-scatter.5.cloned.1.call-done = f32[32,768]{1,0:T(8,128)} async-done(((f32[256,768]{1,0:T(8,128)}), f32[32,768]{1,0:T(8,128)}) %reduce-scatter.5.cloned.1.call-update) | async-done | bytes 98320 | tf_op jit(solution)/shard_map/reduce_scatter | solution.py:37
  (1 shorter events, 0.0 us)
Async XLA Ops:
  7.2 53.1 %reduce-scatter.3.cloned.1.call-start = ((), (), s32[]{:S(2)}) async-start(), calls=%async_computation.2 | async-start | bytes 491520 | tf_op jit(solution)/shard_map/reduce_scatter | solution.py:29
  7.9 16.6 %copy-start = (f32[32,768]{1,0:T(8,128)S(1)}, f32[32,768]{1,0:T(8,128)}, u32[]{:S(2)}) copy-start(f32[32,768]{1,0:T(8,128)} %param.6) | copy-start | bytes 294916
  35.6 0.7 copy-start.1
  38.7 58.9 %reduce-scatter.5.cloned.1.call-start = ((), (), s32[]{:S(2)}) async-start(), calls=%async_computation.3 | async-start | bytes 884736 | tf_op jit(solution)/shard_map/reduce_scatter | solution.py:37
Sparse Core Ops, SparseCore 0:
  38.8 21.4 reduce-scatter.2
  64.3 33.2 reduce-scatter.4
where the time goes:
time: 105 us; the launch traced here: 104 us
  waiting for transfers between devices  44.1 us (42%)
  blocking collectives  40 us (38%)
  between operations  15.4 us (15%)
  matrix products  4.21 us (4%)
    reduce_scatter x1, waiting for transfers between devices, per_device(): lax.psum_scatter(text_term, 'img', scatter_dimension=0, tiled=True)  37.3 us
    all_gather x1, blocking collectives, per_device(): images = lax.all_gather(image_emb, 'txt', axis=0, tiled=True)  16.6 us
    psum x1, blocking collectives, per_device(): image_loss = lax.psum(loss_part, 'txt')  13 us
    all_gather x1, blocking collectives, per_device(): texts = lax.all_gather(text_emb, 'img', axis=0, tiled=True)  10.4 us
    reduce_scatter x1, waiting for transfers between devices, per_device(): lax.psum_scatter(image_term, 'txt', scatter_dimension=0, tiled=True)  6.72 us
  transfers between devices with their start and end apart: 2, of which 2 were waited for; matrix products, arithmetic and copies ran while one was open for 2% of the time, Pallas kernels for 0%

commit v1 on v0

--- a/solution.py
+++ b/solution.py
@@ -4,7 +4,75 @@
 from jax.sharding import PartitionSpec as P
 
 
-def per_device(image_emb, text_emb, pairs, log_scale, bias):
+def partner(n, me, k):
+    if n & (n - 1) == 0:
+        return me ^ k
+    return (k - me) % n
+
+
+def rounds(n):
+    if n & (n - 1) == 0:
+        return range(1, n)
+    return range(n)
+
+
+def swap(x, axis, n, k):
+    return lax.ppermute(x, axis, [(i, partner(n, i, k)) for i in range(n)])
+
+
+def per_device(sizes, image_emb, text_emb, pairs, log_scale, bias):
+    n_img, n_txt = sizes
+    me_img, me_txt = lax.axis_index("img"), lax.axis_index("txt")
+    rows, cols = image_emb.shape[0], text_emb.shape[0]
+
+    images = jnp.concatenate(
+        [image_emb] + [swap(image_emb, "txt", n_txt, k) for k in range(1, n_txt)]
+    )
+    texts = jnp.concatenate(
+        [text_emb] + [swap(text_emb, "img", n_img, k) for k in range(1, n_img)]
+    )
+    image_order = jnp.stack([partner(n_txt, me_txt, k) for k in range(n_txt)])
+    text_order = jnp.stack([partner(n_img, me_img, k) for k in range(n_img)])
+    scale = jnp.exp(log_scale[0])
+    shift = bias[0]
+    dots = lax.dot_general(
+        images,
+        texts,
+        (((1,), (1,)), ((), ())),
+        precision=lax.Precision.HIGHEST,
+        preferred_element_type=jnp.float32,
+    )
+    logits = scale * dots + shift
+    matched = pairs.reshape(n_txt, rows)[image_order].reshape(-1)
+    columns = (
+        (me_txt * n_img + text_order)[:, None] * cols + jnp.arange(cols, dtype=jnp.int32)
+    ).reshape(-1)
+    sign = jnp.where(matched[:, None] == columns[None, :], 1.0, -1.0).astype(jnp.float32)
+    loss_part = jnp.sum(jax.nn.softplus(-sign * logits), axis=1)
+    loss_part = loss_part.reshape(n_txt, rows)[image_order].reshape(-1)
+    dlogits = -sign * jax.nn.sigmoid(-sign * logits)
+    image_term = scale * jnp.dot(
+        dlogits, texts, precision=lax.Precision.HIGHEST, preferred_element_type=jnp.float32
+    )
+    text_term = scale * lax.dot_general(
+        dlogits,
+        images,
+        (((0,), (0,)), ((), ())),
+        precision=lax.Precision.HIGHEST,
+        preferred_element_type=jnp.float32,
+    )
+    loss_row = jnp.pad(loss_part, (0, image_emb.shape[1] - loss_part.shape[0]))[None]
+    image_msgs = [
+        jnp.concatenate([image_term[k * rows:(k + 1) * rows], loss_row]) for k in range(n_txt)
+    ]
+    image_sum = image_msgs[0] + sum(swap(image_msgs[k], "txt", n_txt, k) for k in range(1, n_txt))
+    text_grad = text_term[:cols] + sum(
+        swap(text_term[k * cols:(k + 1) * cols], "img", n_img, k) for k in range(1, n_img)
+    )
+    return (image_sum[rows, :loss_part.shape[0]], image_sum[:rows], text_grad)
+
+
+def per_device_large(image_emb, text_emb, pairs, log_scale, bias):
     images = lax.all_gather(image_emb, "txt", axis=0, tiled=True)
     texts = lax.all_gather(text_emb, "img", axis=0, tiled=True)
     scale = jnp.exp(log_scale[0])
@@ -39,8 +107,13 @@
 
 
 def solution(mesh):
+    sizes = (mesh.shape["img"], mesh.shape["txt"])
+    if max(sizes) <= 8:
+        body = lambda *arrays: per_device(sizes, *arrays)
+    else:
+        body = per_device_large
     return jax.shard_map(
-        per_device,
+        body,
         mesh=mesh,
         in_specs=(P(("img", "txt"), None), P(("txt", "img"), None), P("img"), P(), P()),
         out_specs=(P("img"), P(("img", "txt"), None), P(("txt", "img"), None)),

time: 105 us -> 52.3 us (0.50)
  blocking collectives: 40 us -> 0 us
  waiting for transfers between devices: 44.1 us -> 17.6 us
  starting transfers between devices: 0.08 us -> 24.9 us
  between operations: 15.4 us -> 2.19 us
  local copies, waits for them, and re-layouts: 0.65 us -> 3.88 us
  matrix products: 4.21 us -> 2.6 us
    reduce_scatter x2 -> x0, waiting for transfers between devices: 44 us -> none  [the longest x1 37.3 us: per_device(): lax.psum_scatter(text_term, 'img', scatter_dimension=0, tiled=True)]
    all_gather x2 -> x0, blocking collectives: 27 us -> none  [the longest x1 16.6 us: per_device(): images = lax.all_gather(image_emb, 'txt', axis=0, tiled=True)]
    ppermute x0 -> x20, starting transfers between devices: none -> 24.9 us  [swap(): return lax.ppermute(x, axis, [(i, partner(n, i, k)) for i in range(n)])]
    ppermute x0 -> x20, waiting for transfers between devices: none -> 17.6 us  [swap(): return lax.ppermute(x, axis, [(i, partner(n, i, k)) for i in range(n)])]
    psum x1 -> x0, blocking collectives: 13 us -> none  [per_device(): image_loss = lax.psum(loss_part, 'txt')]
    gather x0 -> x2, local copies, waits for them, and re-layouts: none -> 1.12 us  [the longest x1 0.56 us: per_device(): matched = pairs.reshape(n_txt, rows)[image_order].reshape(-1)]
  transfers between devices with their start and end apart: 2 -> 20, of which waited for: 2 -> 8; matrix products, arithmetic and copies ran while one was open for 2% -> 7% of each run, Pallas kernels for 0% -> 0%
where the time goes in v1:
time: 52.3 us; the launch traced here: 52.1 us
  starting transfers between devices  24.9 us (48%)
  waiting for transfers between devices  17.6 us (34%)
  local copies, waits for them, and re-layouts  3.88 us (7%)
  matrix products  2.6 us (5%)
  between operations  2.19 us (4%)
  other arithmetic  0.92 us (2%)
    ppermute x20, starting transfers between devices, swap(): return lax.ppermute(x, axis, [(i, partner(n, i, k)) for i in range(n)])  24.9 us
    ppermute x20, waiting for transfers between devices, swap(): return lax.ppermute(x, axis, [(i, partner(n, i, k)) for i in range(n)])  17.6 us
    dot_general x1, matrix products, per_device(): lax.dot_general(images, texts, (((1,), (1,)), ((), ())), precision=lax.Pr...  1.08 us
  transfers between devices with their start and end apart: 20, of which 8 were waited for; matrix products, arithmetic and copies ran while one was open for 7% of the time, Pallas kernels for 0%

profile of v1, /device:TPU:0, one launch (start us, length us, event | category | flops | bytes accessed | tf_op | source)
XLA Modules:
  0.0 52.1 jit_solution(12842700084091818267)
XLA Ops:
  0.6 3.1 %collective-permute-start = (f32[32,768]{1,0:T(8,128)}, f32[32,768]{1,0:T(8,128)S(1)}, u32[]{:S(2)}, u32[]{:S(2)}) collective-permute-start(f32[32,768]{1,0:T(8,128)} %param.5), channel_id=1, source_target_pairs={{0,1},{1,0},{2,3},{3,2},{4,5},{5,4},{6,7},{7,6},{8,9},{9,8},{10,11... | collective-permute-start | bytes 294920 | tf_op jit(solution)/shard_map/ppermute | solution.py:20
  3.7 2.6 %collective-permute-start.1 = (f32[32,768]{1,0:T(8,128)}, f32[32,768]{1,0:T(8,128)S(1)}, u32[]{:S(2)}, u32[]{:S(2)}) collective-permute-start(f32[32,768]{1,0:T(8,128)} %param.5), channel_id=1, source_target_pairs={{0,2},{1,3},{2,0},{3,1},{4,6},{5,7},{6,4},{7,5},{8,10},{9,11},{10,... | collective-permute-start | bytes 294920 | tf_op jit(solution)/shard_map/ppermute | solution.py:20
  6.3 0.0 collective-permute-start.2
  6.3 0.0 collective-permute-start.3
  6.3 1.7 %collective-permute-start.4 = (f32[32,768]{1,0:T(8,128)}, f32[32,768]{1,0:T(8,128)S(1)}, u32[]{:S(2)}, u32[]{:S(2)}) collective-permute-start(f32[32,768]{1,0:T(8,128)} %param.6), channel_id=1, source_target_pairs={{0,8},{4,12},{8,0},{12,4},{16,24},{20,28},{24,16},{28,20},{1,9},{5... | collective-permute-start | bytes 294920 | tf_op jit(solution)/shard_map/ppermute | solution.py:20
  8.0 0.9 %constant_dynamic-update-slice_fusion.3 = f32[128,768]{1,0:T(8,128)S(1)} fusion(f32[32,768]{1,0:T(8,128)} %param.5), kind=kLoop, calls=%fused_computation.20 | loop fusion | bytes 196608
  10.3 0.1 stack.55
  10.4 0.1 iota_add_fusion
  10.5 0.1 add.92
  10.6 0.1 reshape.259
  10.7 0.1 fusion.4
  10.7 0.6 %gather_fusion = s32[4,32]{1,0:T(4,128)S(1)} fusion(s32[4,32]{1,0:T(4,128)S(1)} %reshape.259, s32[1024]{0:T(1024)S(1)} %pad_clamp_fusion), kind=kCustom, calls=%fused_computation | custom fusion | bytes 1040 | tf_op jit(solution)/shard_map/gather | solution.py:46
  11.3 0.1 eq.15
  11.4 0.0 collective-permute-done
  11.4 0.2 collective-permute-start.5
  11.6 2.7 %collective-permute-done.1 = f32[32,768]{1,0:T(8,128)S(1)} collective-permute-done((f32[32,768]{1,0:T(8,128)}, f32[32,768]{1,0:T(8,128)S(1)}, u32[]{:S(2)}, u32[]{:S(2)}) %collective-permute-start.1) | collective-permute-done | bytes 98336 | tf_op jit(solution)/shard_map/ppermute | solution.py:20
  14.4 1.5 %collective-permute-start.6 = (f32[32,768]{1,0:T(8,128)S(1)}, f32[32,768]{1,0:T(8,128)S(1)}, u32[]{:S(2)}, u32[]{:S(2)}) collective-permute-start(f32[32,768]{1,0:T(8,128)S(1)} %copy-done), channel_id=1, source_target_pairs={{0,16},{4,20},{8,24},{12,28},{16,0},{20,4},{24,8},{28,12},{1,17},{... | collective-permute-start | bytes 294920 | tf_op jit(solution)/shard_map/ppermute | solution.py:20
  15.9 0.1 collective-permute-start.7
  16.0 1.5 %collective-permute-start.8 = (f32[32,768]{1,0:T(8,128)S(1)}, f32[32,768]{1,0:T(8,128)S(1)}, u32[]{:S(2)}, u32[]{:S(2)}) collective-permute-start(f32[32,768]{1,0:T(8,128)S(1)} %copy-done), channel_id=1, source_target_pairs={{0,24},{4,28},{8,16},{12,20},{16,8},{20,12},{24,0},{28,4},{1,25},{... | collective-permute-start | bytes 294920 | tf_op jit(solution)/shard_map/ppermute | solution.py:20
  17.5 1.5 %collective-permute-start.9 = (f32[32,768]{1,0:T(8,128)S(1)}, f32[32,768]{1,0:T(8,128)S(1)}, u32[]{:S(2)}, u32[]{:S(2)}) collective-permute-start(f32[32,768]{1,0:T(8,128)S(1)} %copy-done), channel_id=1, source_target_pairs={{0,28},{4,24},{8,20},{12,16},{16,12},{20,8},{24,4},{28,0},{1,29},{... | collective-permute-start | bytes 294920 | tf_op jit(solution)/shard_map/ppermute | solution.py:20
  19.1 4.1 %collective-permute-done.6 = f32[32,768]{1,0:T(8,128)S(1)} collective-permute-done((f32[32,768]{1,0:T(8,128)S(1)}, f32[32,768]{1,0:T(8,128)S(1)}, u32[]{:S(2)}, u32[]{:S(2)}) %collective-permute-start.6) | collective-permute-done | bytes 98336 | tf_op jit(solution)/shard_map/ppermute | solution.py:20
  23.1 2.1 %collective-permute-done.7 = f32[32,768]{1,0:T(8,128)S(1)} collective-permute-done((f32[32,768]{1,0:T(8,128)S(1)}, f32[32,768]{1,0:T(8,128)S(1)}, u32[]{:S(2)}, u32[]{:S(2)}) %collective-permute-start.7) | collective-permute-done | bytes 98336 | tf_op jit(solution)/shard_map/ppermute | solution.py:20
  25.3 0.0 collective-permute-done.8
  25.4 1.1 %fusion.2 = (f32[128]{0:T(128)S(1)}, f32[128,256]{1,0:T(8,128)S(1)}) fusion(f32[]{:T(128)} %bitcast.22, f32[128,768]{1,0:T(8,128)S(1)} %constant_dynamic-update-slice_fusion, f32[256,768]{1,0:T(8,128)S(1)} %constant_dynamic-update-slice_fusion.4, f32[]{:T(128)} %bitcast, s32[256]{0:T(256)S(1)} %add.92, s32[128]{0:T(128)S(1)} %eq.15), kind=kOutput, calls=%fused_computation.12 | convolution fusion | flops 302415744 | bytes 1312776 | tf_op jit(solution)/shard_map/dot_general | solution.py:38
  26.4 0.6 %convolution_multiply_fusion.1 = f32[128,768]{1,0:T(8,128)S(1)} fusion(f32[256,768]{1,0:T(8,128)S(1)} %constant_dynamic-update-slice_fusion.4, f32[]{:T(128)} %bitcast, f32[128,256]{1,0:T(8,128)S(1)} %get-tuple-element.18, s32[256]{0:T(256)S(1)} %add.92, s32[128]{0:T(128)S(1)} %eq.15), kind=kOutput, calls=%fused_computation.3 | convolution fusion | flops 302317568 | bytes 1312260 | tf_op jit(solution)/shard_map/dot_general | solution.py:54
  27.1 0.9 %convolution_multiply_fusion = f32[256,768]{1,0:T(8,128)S(1)} fusion(f32[128,768]{1,0:T(8,128)S(1)} %constant_dynamic-update-slice_fusion, f32[]{:T(128)} %bitcast, f32[128,256]{1,0:T(8,128)S(1)} %get-tuple-element.18, s32[256]{0:T(256)S(1)} %add.92, s32[128]{0:T(128)S(1)} %eq.15), kind=kOutput, calls=%fused_computation.2 | convolution fusion | flops 302415872 | bytes 1312260 | tf_op jit(solution)/shard_map/dot_general | solution.py:57
  28.0 2.0 %collective-permute-start.19 = (f32[32,768]{1,0:T(8,128)S(1)}, f32[32,768]{1,0:T(8,128)S(1)}, u32[]{:S(2)}, u32[]{:S(2)}) collective-permute-start(f32[32,768]{1,0:T(8,128)S(1)} %get-tuple-element.4), channel_id=1, source_target_pairs={{0,28},{4,24},{8,20},{12,16},{16,12},{20,8},{24,4},{28,0},{1,29},{... | collective-permute-start | bytes 294920 | tf_op jit(solution)/shard_map/ppermute | solution.py:20
  30.0 0.8 %collective-permute-start.18 = (f32[32,768]{1,0:T(8,128)S(1)}, f32[32,768]{1,0:T(8,128)S(1)}, u32[]{:S(2)}, u32[]{:S(2)}) collective-permute-start(f32[32,768]{1,0:T(8,128)S(1)} %get-tuple-element.5), channel_id=1, source_target_pairs={{0,24},{4,28},{8,16},{12,20},{16,8},{20,12},{24,0},{28,4},{1,25},{... | collective-permute-start | bytes 294920 | tf_op jit(solution)/shard_map/ppermute | solution.py:20
  30.8 0.1 reshape.260
  30.8 0.6 %gather_fusion.1 = f32[4,32]{1,0:T(4,128)S(1)} fusion(f32[4,32]{1,0:T(4,128)S(1)} %reshape.260, s32[1024]{0:T(1024)S(1)} %pad_clamp_fusion), kind=kCustom, calls=%fused_computation.1 | custom fusion | bytes 1040 | tf_op jit(solution)/shard_map/gather | solution.py:52
  31.4 0.1 reshape.261
  31.5 0.3 collective-permute-start.17
  31.8 1.6 %collective-permute-start.16 = (f32[32,768]{1,0:T(8,128)S(1)}, f32[32,768]{1,0:T(8,128)S(1)}, u32[]{:S(2)}, u32[]{:S(2)}) collective-permute-start(f32[32,768]{1,0:T(8,128)S(1)} %get-tuple-element.7), channel_id=1, source_target_pairs={{0,16},{4,20},{8,24},{12,28},{16,0},{20,4},{24,8},{28,12},{1,17},{... | collective-permute-start | bytes 294920 | tf_op jit(solution)/shard_map/ppermute | solution.py:20
  33.4 1.2 %collective-permute-start.15 = (f32[32,768]{1,0:T(8,128)S(1)}, f32[32,768]{1,0:T(8,128)S(1)}, u32[]{:S(2)}, u32[]{:S(2)}) collective-permute-start(f32[32,768]{1,0:T(8,128)S(1)} %get-tuple-element.8), channel_id=1, source_target_pairs={{0,12},{4,8},{8,4},{12,0},{16,28},{20,24},{24,20},{28,16},{1,13},{... | collective-permute-start | bytes 294920 | tf_op jit(solution)/shard_map/ppermute | solution.py:20
  34.6 0.3 collective-permute-start.13
  34.9 1.4 %collective-permute-done.18 = f32[32,768]{1,0:T(8,128)S(1)} collective-permute-done((f32[32,768]{1,0:T(8,128)S(1)}, f32[32,768]{1,0:T(8,128)S(1)}, u32[]{:S(2)}, u32[]{:S(2)}) %collective-permute-start.18) | collective-permute-done | bytes 98336 | tf_op jit(solution)/shard_map/ppermute | solution.py:20
  36.3 1.5 %collective-permute-start.14 = (f32[32,768]{1,0:T(8,128)S(1)}, f32[32,768]{1,0:T(8,128)S(1)}, u32[]{:S(2)}, u32[]{:S(2)}) collective-permute-start(f32[32,768]{1,0:T(8,128)S(1)} %get-tuple-element.3), channel_id=1, source_target_pairs={{0,8},{4,12},{8,0},{12,4},{16,24},{20,28},{24,16},{28,20},{1,9},{5... | collective-permute-start | bytes 294920 | tf_op jit(solution)/shard_map/ppermute | solution.py:20
  37.8 0.5 collective-permute-done.17
  38.3 2.5 %collective-permute-start.12 = (f32[33,768]{1,0:T(8,128)S(1)}, f32[33,768]{1,0:T(8,128)S(1)}, u32[]{:S(2)}, u32[]{:S(2)}) collective-permute-start(f32[33,768]{1,0:T(8,128)S(1)} %get-tuple-element.16), channel_id=1, source_target_pairs={{0,3},{1,2},{2,1},{3,0},{4,7},{5,6},{6,5},{7,4},{8,11},{9,10},{10,... | collective-permute-start | bytes 304136 | tf_op jit(solution)/shard_map/ppermute | solution.py:20
  40.7 2.7 %collective-permute-start.11 = (f32[33,768]{1,0:T(8,128)S(1)}, f32[33,768]{1,0:T(8,128)S(1)}, u32[]{:S(2)}, u32[]{:S(2)}) collective-permute-start(f32[33,768]{1,0:T(8,128)S(1)} %get-tuple-element.14), channel_id=1, source_target_pairs={{0,2},{1,3},{2,0},{3,1},{4,6},{5,7},{6,4},{7,5},{8,10},{9,11},{10,... | collective-permute-start | bytes 304136 | tf_op jit(solution)/shard_map/ppermute | solution.py:20
  43.4 0.0 collective-permute-done.13
  43.4 0.0 collective-permute-done.14
  43.4 0.7 %slice_add_fusion = f32[32,768]{1,0:T(8,128)} fusion(f32[256,768]{1,0:T(8,128)S(1)} %convolution_multiply_fusion, f32[32,768]{1,0:T(8,128)S(1)} %collective-permute-done.19, f32[32,768]{1,0:T(8,128)S(1)} %collective-permute-done.18, f32[32,768]{1,0:T(8,128)S(1)} %collective-permute-done.17, f32[32,768]{1,0:T(8,128)S(1)} %collective-permute-done.16, ...), kind=kLoop, calls=%fused_computation.16 | loop fusion | flops 172032 | bytes 884736 | tf_op jit(solution)/shard_map/add | solution.py:69
  44.1 2.2 %collective-permute-done.12 = f32[33,768]{1,0:T(8,128)S(1)} collective-permute-done((f32[33,768]{1,0:T(8,128)S(1)}, f32[33,768]{1,0:T(8,128)S(1)}, u32[]{:S(2)}, u32[]{:S(2)}) %collective-permute-start.12) | collective-permute-done | bytes 101408 | tf_op jit(solution)/shard_map/ppermute | solution.py:20
  46.3 4.4 %collective-permute-done.10 = f32[33,768]{1,0:T(8,128)S(1)} collective-permute-done((f32[33,768]{1,0:T(8,128)S(1)}, f32[33,768]{1,0:T(8,128)S(1)}, u32[]{:S(2)}, u32[]{:S(2)}) %collective-permute-start.10) | collective-permute-done | bytes 101408 | tf_op jit(solution)/shard_map/ppermute | solution.py:20
  50.7 0.2 collective-permute-done.11
  50.9 0.5 slice_bitcast_fusion
  51.4 0.6 %slice.65 = f32[32,768]{1,0:T(8,128)} slice(f32[33,768]{1,0:T(8,128)S(1)} %fusion.3), slice={[0:32], [0:768]} | slice | bytes 196608 | tf_op jit(solution)/shard_map/slice | solution.py:72
  (32 shorter events, 0.3 us)
Async XLA Ops:
  0.6 10.8 %collective-permute-start = (f32[32,768]{1,0:T(8,128)}, f32[32,768]{1,0:T(8,128)S(1)}, u32[]{:S(2)}, u32[]{:S(2)}) collective-permute-start(f32[32,768]{1,0:T(8,128)} %param.5), channel_id=1, source_target_pairs={{0,1},{1,0},{2,3},{3,2},{4,5},{5,4},{6,7},{7,6},{8,9},{9,8},{10,11... | collective-permute-start | bytes 294920 | tf_op jit(solution)/shard_map/ppermute | solution.py:20
  3.7 10.6 %collective-permute-start.1 = (f32[32,768]{1,0:T(8,128)}, f32[32,768]{1,0:T(8,128)S(1)}, u32[]{:S(2)}, u32[]{:S(2)}) collective-permute-start(f32[32,768]{1,0:T(8,128)} %param.5), channel_id=1, source_target_pairs={{0,2},{1,3},{2,0},{3,1},{4,6},{5,7},{6,4},{7,5},{8,10},{9,11},{10,... | collective-permute-start | bytes 294920 | tf_op jit(solution)/shard_map/ppermute | solution.py:20
  6.3 9.6 %collective-permute-start.2 = (f32[32,768]{1,0:T(8,128)}, f32[32,768]{1,0:T(8,128)S(1)}, u32[]{:S(2)}, u32[]{:S(2)}) collective-permute-start(f32[32,768]{1,0:T(8,128)} %param.5), channel_id=1, source_target_pairs={{0,3},{1,2},{2,1},{3,0},{4,7},{5,6},{6,5},{7,4},{8,11},{9,10},{10,... | collective-permute-start | bytes 294920 | tf_op jit(solution)/shard_map/ppermute | solution.py:20
  6.3 9.7 %collective-permute-start.3 = (f32[32,768]{1,0:T(8,128)}, f32[32,768]{1,0:T(8,128)S(1)}, u32[]{:S(2)}, u32[]{:S(2)}) collective-permute-start(f32[32,768]{1,0:T(8,128)} %param.6), channel_id=1, source_target_pairs={{0,4},{4,0},{8,12},{12,8},{16,20},{20,16},{24,28},{28,24},{1,5},{5... | collective-permute-start | bytes 294920 | tf_op jit(solution)/shard_map/ppermute | solution.py:20
  6.3 11.2 %collective-permute-start.4 = (f32[32,768]{1,0:T(8,128)}, f32[32,768]{1,0:T(8,128)S(1)}, u32[]{:S(2)}, u32[]{:S(2)}) collective-permute-start(f32[32,768]{1,0:T(8,128)} %param.6), channel_id=1, source_target_pairs={{0,8},{4,12},{8,0},{12,4},{16,24},{20,28},{24,16},{28,20},{1,9},{5... | collective-permute-start | bytes 294920 | tf_op jit(solution)/shard_map/ppermute | solution.py:20
  8.0 2.5 %copy-start.1 = (s32[128]{0:T(128)S(1)}, s32[128]{0:T(128)}, u32[]{:S(2)}) copy-start(s32[128]{0:T(128)} %param.7) | copy-start | bytes 1540
  8.9 2.5 %copy-start = (f32[32,768]{1,0:T(8,128)S(1)}, f32[32,768]{1,0:T(8,128)}, u32[]{:S(2)}) copy-start(f32[32,768]{1,0:T(8,128)} %param.6) | copy-start | bytes 294916
  11.4 7.6 %collective-permute-start.5 = (f32[32,768]{1,0:T(8,128)S(1)}, f32[32,768]{1,0:T(8,128)S(1)}, u32[]{:S(2)}, u32[]{:S(2)}) collective-permute-start(f32[32,768]{1,0:T(8,128)S(1)} %copy-done), channel_id=1, source_target_pairs={{0,12},{4,8},{8,4},{12,0},{16,28},{20,24},{24,20},{28,16},{1,13},{... | collective-permute-start | bytes 294920 | tf_op jit(solution)/shard_map/ppermute | solution.py:20
  14.4 8.8 %collective-permute-start.6 = (f32[32,768]{1,0:T(8,128)S(1)}, f32[32,768]{1,0:T(8,128)S(1)}, u32[]{:S(2)}, u32[]{:S(2)}) collective-permute-start(f32[32,768]{1,0:T(8,128)S(1)} %copy-done), channel_id=1, source_target_pairs={{0,16},{4,20},{8,24},{12,28},{16,0},{20,4},{24,8},{28,12},{1,17},{... | collective-permute-start | bytes 294920 | tf_op jit(solution)/shard_map/ppermute | solution.py:20
  15.9 9.4 %collective-permute-start.7 = (f32[32,768]{1,0:T(8,128)S(1)}, f32[32,768]{1,0:T(8,128)S(1)}, u32[]{:S(2)}, u32[]{:S(2)}) collective-permute-start(f32[32,768]{1,0:T(8,128)S(1)} %copy-done), channel_id=1, source_target_pairs={{0,20},{4,16},{8,28},{12,24},{16,4},{20,0},{24,12},{28,8},{1,21},{... | collective-permute-start | bytes 294920 | tf_op jit(solution)/shard_map/ppermute | solution.py:20
  16.0 9.3 %collective-permute-start.8 = (f32[32,768]{1,0:T(8,128)S(1)}, f32[32,768]{1,0:T(8,128)S(1)}, u32[]{:S(2)}, u32[]{:S(2)}) collective-permute-start(f32[32,768]{1,0:T(8,128)S(1)} %copy-done), channel_id=1, source_target_pairs={{0,24},{4,28},{8,16},{12,20},{16,8},{20,12},{24,0},{28,4},{1,25},{... | collective-permute-start | bytes 294920 | tf_op jit(solution)/shard_map/ppermute | solution.py:20
  17.5 7.8 %collective-permute-start.9 = (f32[32,768]{1,0:T(8,128)S(1)}, f32[32,768]{1,0:T(8,128)S(1)}, u32[]{:S(2)}, u32[]{:S(2)}) collective-permute-start(f32[32,768]{1,0:T(8,128)S(1)} %copy-done), channel_id=1, source_target_pairs={{0,28},{4,24},{8,20},{12,16},{16,12},{20,8},{24,4},{28,0},{1,29},{... | collective-permute-start | bytes 294920 | tf_op jit(solution)/shard_map/ppermute | solution.py:20
  28.0 6.5 %collective-permute-start.19 = (f32[32,768]{1,0:T(8,128)S(1)}, f32[32,768]{1,0:T(8,128)S(1)}, u32[]{:S(2)}, u32[]{:S(2)}) collective-permute-start(f32[32,768]{1,0:T(8,128)S(1)} %get-tuple-element.4), channel_id=1, source_target_pairs={{0,28},{4,24},{8,20},{12,16},{16,12},{20,8},{24,4},{28,0},{1,29},{... | collective-permute-start | bytes 294920 | tf_op jit(solution)/shard_map/ppermute | solution.py:20
  30.0 6.3 %collective-permute-start.18 = (f32[32,768]{1,0:T(8,128)S(1)}, f32[32,768]{1,0:T(8,128)S(1)}, u32[]{:S(2)}, u32[]{:S(2)}) collective-permute-start(f32[32,768]{1,0:T(8,128)S(1)} %get-tuple-element.5), channel_id=1, source_target_pairs={{0,24},{4,28},{8,16},{12,20},{16,8},{20,12},{24,0},{28,4},{1,25},{... | collective-permute-start | bytes 294920 | tf_op jit(solution)/shard_map/ppermute | solution.py:20
  31.5 6.8 %collective-permute-start.17 = (f32[32,768]{1,0:T(8,128)S(1)}, f32[32,768]{1,0:T(8,128)S(1)}, u32[]{:S(2)}, u32[]{:S(2)}) collective-permute-start(f32[32,768]{1,0:T(8,128)S(1)} %get-tuple-element.6), channel_id=1, source_target_pairs={{0,20},{4,16},{8,28},{12,24},{16,4},{20,0},{24,12},{28,8},{1,21},{... | collective-permute-start | bytes 294920 | tf_op jit(solution)/shard_map/ppermute | solution.py:20
  31.8 8.9 %collective-permute-start.16 = (f32[32,768]{1,0:T(8,128)S(1)}, f32[32,768]{1,0:T(8,128)S(1)}, u32[]{:S(2)}, u32[]{:S(2)}) collective-permute-start(f32[32,768]{1,0:T(8,128)S(1)} %get-tuple-element.7), channel_id=1, source_target_pairs={{0,16},{4,20},{8,24},{12,28},{16,0},{20,4},{24,8},{28,12},{1,17},{... | collective-permute-start | bytes 294920 | tf_op jit(solution)/shard_map/ppermute | solution.py:20
  33.4 7.4 %collective-permute-start.15 = (f32[32,768]{1,0:T(8,128)S(1)}, f32[32,768]{1,0:T(8,128)S(1)}, u32[]{:S(2)}, u32[]{:S(2)}) collective-permute-start(f32[32,768]{1,0:T(8,128)S(1)} %get-tuple-element.8), channel_id=1, source_target_pairs={{0,12},{4,8},{8,4},{12,0},{16,28},{20,24},{24,20},{28,16},{1,13},{... | collective-permute-start | bytes 294920 | tf_op jit(solution)/shard_map/ppermute | solution.py:20
  34.6 8.9 %collective-permute-start.13 = (f32[32,768]{1,0:T(8,128)S(1)}, f32[32,768]{1,0:T(8,128)S(1)}, u32[]{:S(2)}, u32[]{:S(2)}) collective-permute-start(f32[32,768]{1,0:T(8,128)S(1)} %get-tuple-element.9), channel_id=1, source_target_pairs={{0,4},{4,0},{8,12},{12,8},{16,20},{20,16},{24,28},{28,24},{1,5},{5... | collective-permute-start | bytes 294920 | tf_op jit(solution)/shard_map/ppermute | solution.py:20
  36.3 7.1 %collective-permute-start.14 = (f32[32,768]{1,0:T(8,128)S(1)}, f32[32,768]{1,0:T(8,128)S(1)}, u32[]{:S(2)}, u32[]{:S(2)}) collective-permute-start(f32[32,768]{1,0:T(8,128)S(1)} %get-tuple-element.3), channel_id=1, source_target_pairs={{0,8},{4,12},{8,0},{12,4},{16,24},{20,28},{24,16},{28,20},{1,9},{5... | collective-permute-start | bytes 294920 | tf_op jit(solution)/shard_map/ppermute | solution.py:20
  38.3 8.1 %collective-permute-start.12 = (f32[33,768]{1,0:T(8,128)S(1)}, f32[33,768]{1,0:T(8,128)S(1)}, u32[]{:S(2)}, u32[]{:S(2)}) collective-permute-start(f32[33,768]{1,0:T(8,128)S(1)} %get-tuple-element.16), channel_id=1, source_target_pairs={{0,3},{1,2},{2,1},{3,0},{4,7},{5,6},{6,5},{7,4},{8,11},{9,10},{10,... | collective-permute-start | bytes 304136 | tf_op jit(solution)/shard_map/ppermute | solution.py:20
  40.7 10.0 %collective-permute-start.10 = (f32[33,768]{1,0:T(8,128)S(1)}, f32[33,768]{1,0:T(8,128)S(1)}, u32[]{:S(2)}, u32[]{:S(2)}) collective-permute-start(f32[33,768]{1,0:T(8,128)S(1)} %get-tuple-element.15), channel_id=1, source_target_pairs={{0,1},{1,0},{2,3},{3,2},{4,5},{5,4},{6,7},{7,6},{8,9},{9,8},{10,11... | collective-permute-start | bytes 304136 | tf_op jit(solution)/shard_map/ppermute | solution.py:20
  40.7 10.1 %collective-permute-start.11 = (f32[33,768]{1,0:T(8,128)S(1)}, f32[33,768]{1,0:T(8,128)S(1)}, u32[]{:S(2)}, u32[]{:S(2)}) collective-permute-start(f32[33,768]{1,0:T(8,128)S(1)} %get-tuple-element.14), channel_id=1, source_target_pairs={{0,2},{1,3},{2,0},{3,1},{4,6},{5,7},{6,4},{7,5},{8,10},{9,11},{10,... | collective-permute-start | bytes 304136 | tf_op jit(solution)/shard_map/ppermute | solution.py:20

commit v2 on v1

--- a/solution.py
+++ b/solution.py
@@ -4,35 +4,18 @@
 from jax.sharding import PartitionSpec as P
 
 
-def partner(n, me, k):
-    if n & (n - 1) == 0:
-        return me ^ k
-    return (k - me) % n
-
-
-def rounds(n):
-    if n & (n - 1) == 0:
-        return range(1, n)
-    return range(n)
-
-
-def swap(x, axis, n, k):
-    return lax.ppermute(x, axis, [(i, partner(n, i, k)) for i in range(n)])
+def spread(x, axis, n):
+    return lax.all_to_all(jnp.broadcast_to(x[None], (n,) + x.shape), axis, 0, 0)
 
 
 def per_device(sizes, image_emb, text_emb, pairs, log_scale, bias):
     n_img, n_txt = sizes
-    me_img, me_txt = lax.axis_index("img"), lax.axis_index("txt")
+    me_txt = lax.axis_index("txt")
     rows, cols = image_emb.shape[0], text_emb.shape[0]
 
-    images = jnp.concatenate(
-        [image_emb] + [swap(image_emb, "txt", n_txt, k) for k in range(1, n_txt)]
-    )
-    texts = jnp.concatenate(
-        [text_emb] + [swap(text_emb, "img", n_img, k) for k in range(1, n_img)]
-    )
-    image_order = jnp.stack([partner(n_txt, me_txt, k) for k in range(n_txt)])
-    text_order = jnp.stack([partner(n_img, me_img, k) for k in range(n_img)])
+    width = image_emb.shape[1]
+    images = spread(image_emb, "txt", n_txt).reshape(-1, width)
+    texts = spread(text_emb, "img", n_img).reshape(-1, width)
     scale = jnp.exp(log_scale[0])
     shift = bias[0]
     dots = lax.dot_general(
@@ -43,13 +26,9 @@
         preferred_element_type=jnp.float32,
     )
     logits = scale * dots + shift
-    matched = pairs.reshape(n_txt, rows)[image_order].reshape(-1)
-    columns = (
-        (me_txt * n_img + text_order)[:, None] * cols + jnp.arange(cols, dtype=jnp.int32)
-    ).reshape(-1)
-    sign = jnp.where(matched[:, None] == columns[None, :], 1.0, -1.0).astype(jnp.float32)
+    columns = me_txt * texts.shape[0] + jnp.arange(texts.shape[0], dtype=jnp.int32)
+    sign = jnp.where(pairs[:, None] == columns[None, :], 1.0, -1.0).astype(jnp.float32)
     loss_part = jnp.sum(jax.nn.softplus(-sign * logits), axis=1)
-    loss_part = loss_part.reshape(n_txt, rows)[image_order].reshape(-1)
     dlogits = -sign * jax.nn.sigmoid(-sign * logits)
     image_term = scale * jnp.dot(
         dlogits, texts, precision=lax.Precision.HIGHEST, preferred_element_type=jnp.float32
@@ -61,14 +40,15 @@
         precision=lax.Precision.HIGHEST,
         preferred_element_type=jnp.float32,
     )
-    loss_row = jnp.pad(loss_part, (0, image_emb.shape[1] - loss_part.shape[0]))[None]
-    image_msgs = [
-        jnp.concatenate([image_term[k * rows:(k + 1) * rows], loss_row]) for k in range(n_txt)
-    ]
-    image_sum = image_msgs[0] + sum(swap(image_msgs[k], "txt", n_txt, k) for k in range(1, n_txt))
-    text_grad = text_term[:cols] + sum(
-        swap(text_term[k * cols:(k + 1) * cols], "img", n_img, k) for k in range(1, n_img)
+    text_grad = jnp.sum(
+        lax.all_to_all(text_term.reshape(n_img, cols, width), "img", 0, 0), axis=0
     )
+    loss_row = jnp.pad(loss_part, (0, width - loss_part.shape[0]))
+    image_msgs = jnp.concatenate(
+        [image_term.reshape(n_txt, rows, width), jnp.broadcast_to(loss_row, (n_txt, 1, width))],
+        axis=1,
+    )
+    image_sum = jnp.sum(lax.all_to_all(image_msgs, "txt", 0, 0), axis=0)
     return (image_sum[rows, :loss_part.shape[0]], image_sum[:rows], text_grad)
 
 

time: 52.3 us -> 73.2 us (1.40)
  blocking collectives: 0 us -> 17.9 us
  waiting for transfers between devices: 17.6 us -> 32.1 us
  starting transfers between devices: 24.9 us -> 12 us
  matrix products: 2.6 us -> 3.48 us
    all_to_all x0 -> x3, waiting for transfers between devices: none -> 32.1 us  [the longest x1 11.4 us: per_device(): lax.all_to_all(text_term.reshape(n_img, cols, width), 'img', 0, 0)]
    ppermute x20 -> x0, starting transfers between devices: 24.9 us -> none  [swap(): return lax.ppermute(x, axis, [(i, partner(n, i, k)) for i in range(n)])]
    all_to_all x0 -> x1, blocking collectives: none -> 17.9 us  [spread(): return lax.all_to_all(jnp.broadcast_to(x[None], (n,) + x.shape), axis, 0, 0)]
    ppermute x20 -> x0, waiting for transfers between devices: 17.6 us -> none  [swap(): return lax.ppermute(x, axis, [(i, partner(n, i, k)) for i in range(n)])]
    all_to_all x0 -> x3, starting transfers between devices: none -> 12 us  [the longest x1 4.82 us: per_device(): lax.all_to_all(text_term.reshape(n_img, cols, width), 'img', 0, 0)]
    broadcast_in_dim x1 -> x3, local copies, waits for them, and re-layouts: 0.01 us -> 1.88 us  [the longest x2 1.87 us: spread(): return lax.all_to_all(jnp.broadcast_to(x[None], (n,) + x.shape), axis, 0, 0)]
    gather x2 -> x0, local copies, waits for them, and re-layouts: 1.12 us -> none  [the longest x1 0.56 us: per_device(): matched = pairs.reshape(n_txt, rows)[image_order].reshape(-1)]
    dot_general x1, matrix products: 0.9 us -> 1.79 us  [per_device(): lax.dot_general(dlogits, images, (((0,), (0,)), ((), ())), precision=lax....]
  transfers between devices with their start and end apart: 20 -> 3, of which waited for: 8 -> 3; matrix products, arithmetic and copies ran while one was open for 7% -> 4% of each run, Pallas kernels for 0% -> 0%
where the time goes in v2:
time: 73.2 us; the launch traced here: 72.8 us
  waiting for transfers between devices  32.1 us (44%)
  blocking collectives  17.9 us (24%)
  starting transfers between devices  12 us (16%)
  local copies, waits for them, and re-layouts  3.7 us (5%)
  matrix products  3.48 us (5%)
  between operations  2.03 us (3%)
  other arithmetic  1.54 us (2%)
    all_to_all x1, blocking collectives, spread(): return lax.all_to_all(jnp.broadcast_to(x[None], (n,) + x.shape), axis, 0, 0)  17.9 us
    all_to_all x1, waiting for transfers between devices, per_device(): lax.all_to_all(text_term.reshape(n_img, cols, width), 'img', 0, 0)  11.4 us
    all_to_all x1, waiting for transfers between devices, spread(): return lax.all_to_all(jnp.broadcast_to(x[None], (n,) + x.shape), axis, 0, 0)  11.3 us
    all_to_all x1, waiting for transfers between devices, per_device(): image_sum = jnp.sum(lax.all_to_all(image_msgs, 'txt', 0, 0), axis=0)  9.44 us
    all_to_all x1, starting transfers between devices, per_device(): lax.all_to_all(text_term.reshape(n_img, cols, width), 'img', 0, 0)  4.82 us
    all_to_all x1, starting transfers between devices, spread(): return lax.all_to_all(jnp.broadcast_to(x[None], (n,) + x.shape), axis, 0, 0)  3.72 us
    all_to_all x1, starting transfers between devices, per_device(): image_sum = jnp.sum(lax.all_to_all(image_msgs, 'txt', 0, 0), axis=0)  3.47 us
    broadcast_in_dim x2, local copies, waits for them, and re-layouts, spread(): return lax.all_to_all(jnp.broadcast_to(x[None], (n,) + x.shape), axis, 0, 0)  1.87 us
  transfers between devices with their start and end apart: 3, of which 3 were waited for; matrix products, arithmetic and copies ran while one was open for 4% of the time, Pallas kernels for 0%

profile of v2, /device:TPU:0, one launch (start us, length us, event | category | flops | bytes accessed | tf_op | source)
XLA Modules:
  0.0 72.8 jit_solution(1895588990308991319)
XLA Ops:
  0.6 0.9 %broadcast_in_dim.27 = f32[4,32,768]{2,1,0:T(8,128)S(1)} broadcast(f32[32,768]{1,0:T(8,128)} %param.5), dimensions={1,2} | broadcast | bytes 491520 | tf_op jit(solution)/shard_map/broadcast_in_dim | solution.py:8
  1.6 0.0 copy-start
  1.6 17.9 %all_to_all.20 = f32[4,32,768]{2,1,0:T(8,128)S(1)} all-to-all(f32[4,32,768]{2,1,0:T(8,128)S(1)} %broadcast_in_dim.27), channel_id=1, replica_groups=mesh['img'=8,'txt'=4] {'txt'}, dimensions={0} | all-to-all | bytes 786432 | tf_op jit(solution)/shard_map/all_to_all | solution.py:8
  19.5 0.0 copy-done
  19.5 0.9 %broadcast_in_dim.28 = f32[8,32,768]{2,1,0:T(8,128)} broadcast(f32[32,768]{1,0:T(8,128)S(1)} %copy-done), dimensions={1,2} | broadcast | bytes 884736 | tf_op jit(solution)/shard_map/broadcast_in_dim | solution.py:8
  20.4 3.7 %all-to-all-start.1 = ((f32[8,32,768]{2,1,0:T(8,128)}), f32[8,32,768]{2,1,0:T(8,128)S(1)}, u32[]{:S(2)}, u32[]{:S(2)}) async-start(f32[8,32,768]{2,1,0:T(8,128)} %broadcast_in_dim.28), calls=%async_computation.1 | async-start | bytes 1572864 | tf_op jit(solution)/shard_map/all_to_all | solution.py:8
  25.5 11.3 %all-to-all-done.1 = f32[8,32,768]{2,1,0:T(8,128)S(1)} async-done(((f32[8,32,768]{2,1,0:T(8,128)}), f32[8,32,768]{2,1,0:T(8,128)S(1)}, u32[]{:S(2)}, u32[]{:S(2)}) %all-to-all-start.1) | async-done | bytes 786464 | tf_op jit(solution)/shard_map/all_to_all | solution.py:8
  36.8 0.0 copy-start.1
  36.8 0.7 copy-done.1
  37.4 1.1 %fusion.2 = (f32[128]{0:T(128)S(1)}, f32[128,256]{1,0:T(8,128)S(1)}) fusion(f32[]{:T(128)} %bitcast.12, f32[128,768]{1,0:T(8,128)S(1)} %bitcast.15, f32[256,768]{1,0:T(8,128)S(1)} %bitcast.13, f32[]{:T(128)} %bitcast, s32[256]{0:T(256)S(1)} %iota_add_fusion, s32[128]{0:T(128)S(1)} %copy-done.1), kind=kOutput, calls=%fused_computation.7 | convolution fusion | flops 302415744 | bytes 1312776 | tf_op jit(solution)/shard_map/dot_general | solution.py:21
  38.5 0.6 convolution_multiply_fusion.1
  39.2 0.8 %pad_maximum_fusion = f32[4,33,768]{2,1,0:T(8,128)} fusion(f32[4,1,768]{2,1,0:T(1,128)S(1)} %broadcast_in_dim.29, f32[4,32,768]{2,1,0:T(8,128)S(1)} %bitcast.17), kind=kLoop, calls=%fused_computation.5 | loop fusion | flops 101376 | bytes 811008 | tf_op jit(solution)/shard_map/concatenate | solution.py:47
  40.0 3.5 %all-to-all-start.2 = ((f32[4,33,768]{2,1,0:T(8,128)}), f32[4,33,768]{2,1,0:T(8,128)S(1)}, u32[]{:S(2)}, u32[]{:S(2)}) async-start(f32[4,33,768]{2,1,0:T(8,128)} %pad_maximum_fusion), calls=%async_computation.2 | async-start | bytes 983040 | tf_op jit(solution)/shard_map/all_to_all | solution.py:51
  43.5 1.8 %convolution_multiply_fusion = f32[256,768]{1,0:T(8,128)} fusion(f32[128,768]{1,0:T(8,128)S(1)} %bitcast.16, f32[]{:T(128)} %bitcast, f32[128,256]{1,0:T(8,128)S(1)} %get-tuple-element.4, s32[256]{0:T(256)S(1)} %iota_add_fusion, s32[128]{0:T(128)S(1)} %copy-done.1), kind=kOutput, calls=%fused_computation | convolution fusion | flops 302415872 | bytes 1312260 | tf_op jit(solution)/shard_map/dot_general | solution.py:36
  45.3 9.4 %all-to-all-done.2 = f32[4,33,768]{2,1,0:T(8,128)S(1)} async-done(((f32[4,33,768]{2,1,0:T(8,128)}), f32[4,33,768]{2,1,0:T(8,128)S(1)}, u32[]{:S(2)}, u32[]{:S(2)}) %all-to-all-start.2) | async-done | bytes 405536 | tf_op jit(solution)/shard_map/all_to_all | solution.py:51
  54.7 4.8 %all-to-all-start.3 = ((f32[8,32,768]{2,1,0:T(8,128)}), f32[8,32,768]{2,1,0:T(8,128)S(1)}, u32[]{:S(2)}, u32[]{:S(2)}) async-start(f32[8,32,768]{2,1,0:T(8,128)} %bitcast.6), calls=%async_computation.3 | async-start | bytes 1572864 | tf_op jit(solution)/shard_map/all_to_all | solution.py:44
  59.5 0.6 slice.9
  60.2 0.5 slice_bitcast_fusion
  60.7 11.4 %all-to-all-done.3 = f32[8,32,768]{2,1,0:T(8,128)S(1)} async-done(((f32[8,32,768]{2,1,0:T(8,128)}), f32[8,32,768]{2,1,0:T(8,128)S(1)}, u32[]{:S(2)}, u32[]{:S(2)}) %all-to-all-start.3) | async-done | bytes 786464 | tf_op jit(solution)/shard_map/all_to_all | solution.py:44
  72.1 0.7 reduce_sum.29
  (4 shorter events, 0.0 us)
Async XLA Ops:
  1.6 17.9 %copy-start = (f32[32,768]{1,0:T(8,128)S(1)}, f32[32,768]{1,0:T(8,128)}, u32[]{:S(2)}) copy-start(f32[32,768]{1,0:T(8,128)} %param.6) | copy-start | bytes 294916
  20.4 16.3 %all-to-all-start.1 = ((f32[8,32,768]{2,1,0:T(8,128)}), f32[8,32,768]{2,1,0:T(8,128)S(1)}, u32[]{:S(2)}, u32[]{:S(2)}) async-start(f32[8,32,768]{2,1,0:T(8,128)} %broadcast_in_dim.28), calls=%async_computation.1 | async-start | bytes 1572864 | tf_op jit(solution)/shard_map/all_to_all | solution.py:8
  36.8 0.7 copy-start.1
  40.0 14.7 %all-to-all-start.2 = ((f32[4,33,768]{2,1,0:T(8,128)}), f32[4,33,768]{2,1,0:T(8,128)S(1)}, u32[]{:S(2)}, u32[]{:S(2)}) async-start(f32[4,33,768]{2,1,0:T(8,128)} %pad_maximum_fusion), calls=%async_computation.2 | async-start | bytes 983040 | tf_op jit(solution)/shard_map/all_to_all | solution.py:51
  54.7 17.4 %all-to-all-start.3 = ((f32[8,32,768]{2,1,0:T(8,128)}), f32[8,32,768]{2,1,0:T(8,128)S(1)}, u32[]{:S(2)}, u32[]{:S(2)}) async-start(f32[8,32,768]{2,1,0:T(8,128)} %bitcast.6), calls=%async_computation.3 | async-start | bytes 1572864 | tf_op jit(solution)/shard_map/all_to_all | solution.py:44

commit v3 on v0

--- a/solution.py
+++ b/solution.py
@@ -4,7 +4,89 @@
 from jax.sharding import PartitionSpec as P
 
 
-def per_device(image_emb, text_emb, pairs, log_scale, bias):
+def exchange(x, axis, n, k):
+    return lax.ppermute(x, axis, [(i, i ^ k) for i in range(n)])
+
+
+def untwist(blocks, me):
+    n = blocks.shape[0]
+    bit = 1
+    while bit < n:
+        paired = blocks.reshape((n // (2 * bit), 2, bit) + blocks.shape[1:])
+        flipped = paired[:, ::-1]
+        blocks = jnp.where(me & bit, flipped, paired).reshape(blocks.shape)
+        bit *= 2
+    return blocks
+
+
+def dot(a, b, contract):
+    return lax.dot_general(
+        a,
+        b,
+        ((contract[:1], contract[1:]), ((), ())),
+        precision=lax.Precision.HIGH,
+        preferred_element_type=jnp.float32,
+    )
+
+
+def losses(images, texts, matched, columns, scale, shift):
+    logits = scale * dot(images, texts, (1, 1)) + shift
+    match = matched[:, None] == columns[None, :]
+    v = jnp.where(match, -logits, logits)
+    e = jnp.exp(-jnp.abs(v))
+    loss = jnp.maximum(v, 0.0) + jnp.log1p(e)
+    s = scale * jnp.where(v >= 0, 1.0, e) / (1.0 + e)
+    return jnp.sum(loss, axis=1), jnp.where(match, -s, s)
+
+
+def per_device(sizes, image_emb, text_emb, pairs, log_scale, bias):
+    n_img, n_txt = sizes
+    chips = n_img // 2
+    me_img, me_txt = lax.axis_index("img"), lax.axis_index("txt")
+    rows, cols, width = image_emb.shape[0], text_emb.shape[0], image_emb.shape[1]
+    scale = jnp.exp(log_scale[0])
+    shift = bias[0]
+
+    image_blocks, text_blocks = [image_emb], [text_emb]
+    for k in range(1, max(n_txt, chips)):
+        if k < n_txt:
+            image_blocks.append(exchange(image_emb, "txt", n_txt, k))
+        if k < chips:
+            text_blocks.append(exchange(text_emb, "img", n_img, 2 * k))
+    near = jnp.concatenate(text_blocks)
+    far = exchange(near, "img", n_img, 1)
+    images = jnp.concatenate(image_blocks)
+
+    matched = untwist(pairs.reshape(n_txt, rows), me_txt).reshape(-1)
+    place = jnp.arange(chips * cols, dtype=jnp.int32)
+    chip = (me_img // 2) ^ (place // cols)
+    column = (me_txt * n_img + 2 * chip) * cols + place % cols
+    core = me_img % 2
+    loss_near, d_near = losses(images, near, matched, column + core * cols, scale, shift)
+    loss_far, d_far = losses(images, far, matched, column + (1 - core) * cols, scale, shift)
+
+    text_far = dot(d_far, images, (0, 0))
+    text_back = exchange(text_far, "img", n_img, 1)
+    image_term = dot(d_near, near, (1, 0)) + dot(d_far, far, (1, 0))
+    loss_part = (loss_near + loss_far).reshape(n_txt, rows)
+    image_back, loss_sum = [image_term[:rows]], loss_part
+    for k in range(1, n_txt):
+        loss_row = jnp.stack([loss_part[k ^ m] for m in range(n_txt)]).reshape(1, -1)
+        loss_row = jnp.pad(loss_row, ((0, 7), (0, width - loss_row.shape[1])))
+        sent = jnp.concatenate([image_term[k * rows:(k + 1) * rows], loss_row])
+        got = exchange(sent, "txt", n_txt, k)
+        image_back.append(got[:rows])
+        loss_sum = loss_sum + got[rows, :n_txt * rows].reshape(n_txt, rows)
+    text_term = dot(d_near, images, (0, 0)) + text_back
+    text_grad = text_term[:cols]
+    for k in range(1, chips):
+        text_grad = text_grad + exchange(text_term[k * cols:(k + 1) * cols], "img", n_img, 2 * k)
+    image_grad = sum(image_back)
+    image_loss = untwist(loss_sum, me_txt).reshape(-1)
+    return (image_loss, image_grad, text_grad)
+
+
+def per_device_large(image_emb, text_emb, pairs, log_scale, bias):
     images = lax.all_gather(image_emb, "txt", axis=0, tiled=True)
     texts = lax.all_gather(text_emb, "img", axis=0, tiled=True)
     scale = jnp.exp(log_scale[0])
@@ -39,8 +121,13 @@
 
 
 def solution(mesh):
+    sizes = (mesh.shape["img"], mesh.shape["txt"])
+    if all(n in (2, 4, 8) for n in sizes):
+        body = lambda *arrays: per_device(sizes, *arrays)
+    else:
+        body = per_device_large
     return jax.shard_map(
-        per_device,
+        body,
         mesh=mesh,
         in_specs=(P(("img", "txt"), None), P(("txt", "img"), None), P("img"), P(), P()),
         out_specs=(P("img"), P(("img", "txt"), None), P(("txt", "img"), None)),

time: 105 us -> 45.1 us (0.43)
  blocking collectives: 40 us -> 0 us
  waiting for transfers between devices: 44.1 us -> 17.5 us
  starting transfers between devices: 0.08 us -> 18.2 us
  between operations: 15.4 us -> 2.19 us
  local copies, waits for them, and re-layouts: 0.65 us -> 3.19 us
  matrix products: 4.21 us -> 2.39 us
  other arithmetic: 0.01 us -> 1.43 us
    reduce_scatter x2 -> x0, waiting for transfers between devices: 44 us -> none  [the longest x1 37.3 us: per_device(): lax.psum_scatter(text_term, 'img', scatter_dimension=0, tiled=True)]
    all_gather x2 -> x0, blocking collectives: 27 us -> none  [the longest x1 16.6 us: per_device(): images = lax.all_gather(image_emb, 'txt', axis=0, tiled=True)]
    ppermute x0 -> x14, starting transfers between devices: none -> 18.2 us  [exchange(): return lax.ppermute(x, axis, [(i, i ^ k) for i in range(n)])]
    ppermute x0 -> x14, waiting for transfers between devices: none -> 17.5 us  [exchange(): return lax.ppermute(x, axis, [(i, i ^ k) for i in range(n)])]
    psum x1 -> x0, blocking collectives: 13 us -> none  [per_device(): image_loss = lax.psum(loss_part, 'txt')]
    dot_general x3 -> x6, matrix products: 4.21 us -> 2.39 us  [dot(): lax.dot_general(a, b, ((contract[:1], contract[1:]), ((), ())), precision...]
    add x1 -> x6, other arithmetic: 0.01 us -> 1.37 us  [the longest x1 0.67 us: per_device(): image_grad = sum(image_back)]
  transfers between devices with their start and end apart: 2 -> 14, of which waited for: 2 -> 8; matrix products, arithmetic and copies ran while one was open for 2% -> 8% of each run, Pallas kernels for 0% -> 0%
where the time goes in v3:
time: 45.1 us; the launch traced here: 44.9 us
  starting transfers between devices  18.2 us (40%)
  waiting for transfers between devices  17.5 us (39%)
  local copies, waits for them, and re-layouts  3.19 us (7%)
  matrix products  2.39 us (5%)
  between operations  2.19 us (5%)
  other arithmetic  1.43 us (3%)
    ppermute x14, starting transfers between devices, exchange(): return lax.ppermute(x, axis, [(i, i ^ k) for i in range(n)])  18.2 us
    ppermute x14, waiting for transfers between devices, exchange(): return lax.ppermute(x, axis, [(i, i ^ k) for i in range(n)])  17.5 us
    dot_general x6, matrix products, dot(): lax.dot_general(a, b, ((contract[:1], contract[1:]), ((), ())), precision...  2.39 us
    unnamed x10, local copies, waits for them, and re-layouts  1.59 us
  transfers between devices with their start and end apart: 14, of which 8 were waited for; matrix products, arithmetic and copies ran while one was open for 8% of the time, Pallas kernels for 0%

profile of v3, /device:TPU:0, one launch (start us, length us, event | category | flops | bytes accessed | tf_op | source)
XLA Modules:
  0.0 44.9 jit_solution(3825617200127151934)
XLA Ops:
  0.6 4.1 %collective-permute-start.1 = (f32[32,768]{1,0:T(8,128)}, f32[32,768]{1,0:T(8,128)S(1)}, u32[]{:S(2)}, u32[]{:S(2)}) collective-permute-start(f32[32,768]{1,0:T(8,128)} %param.5), channel_id=1, source_target_pairs={{0,2},{1,3},{2,0},{3,1},{4,6},{5,7},{6,4},{7,5},{8,10},{9,11},{10,... | collective-permute-start | bytes 294920 | tf_op jit(solution)/shard_map/ppermute | solution.py:8
  4.7 1.6 %collective-permute-start = (f32[32,768]{1,0:T(8,128)}, f32[32,768]{1,0:T(8,128)S(1)}, u32[]{:S(2)}, u32[]{:S(2)}) collective-permute-start(f32[32,768]{1,0:T(8,128)} %param.5), channel_id=1, source_target_pairs={{0,1},{1,0},{2,3},{3,2},{4,5},{5,4},{6,7},{7,6},{8,9},{9,8},{10,11... | collective-permute-start | bytes 294920 | tf_op jit(solution)/shard_map/ppermute | solution.py:8
  6.3 0.0 collective-permute-start.2
  6.3 1.7 %collective-permute-start.4 = (f32[32,768]{1,0:T(8,128)}, f32[32,768]{1,0:T(8,128)S(1)}, u32[]{:S(2)}, u32[]{:S(2)}) collective-permute-start(f32[32,768]{1,0:T(8,128)} %param.6), channel_id=1, source_target_pairs={{0,16},{4,20},{8,24},{12,28},{16,0},{20,4},{24,8},{28,12},{1,17},{... | collective-permute-start | bytes 294920 | tf_op jit(solution)/shard_map/ppermute | solution.py:8
  8.1 1.5 %collective-permute-start.3 = (f32[32,768]{1,0:T(8,128)}, f32[32,768]{1,0:T(8,128)S(1)}, u32[]{:S(2)}, u32[]{:S(2)}) collective-permute-start(f32[32,768]{1,0:T(8,128)} %param.6), channel_id=1, source_target_pairs={{0,8},{4,12},{8,0},{12,4},{16,24},{20,28},{24,16},{28,20},{1,9},{5... | collective-permute-start | bytes 294920 | tf_op jit(solution)/shard_map/ppermute | solution.py:8
  9.5 0.9 %constant_dynamic-update-slice_fusion.3 = f32[128,768]{1,0:T(8,128)S(1)} fusion(f32[32,768]{1,0:T(8,128)} %param.5), kind=kLoop, calls=%fused_computation.27 | loop fusion | bytes 196608
  10.5 0.0 copy-done
  11.8 0.0 copy-start.1
  11.9 0.6 %copy-done.1 = s32[128]{0:T(128)S(1)} copy-done((s32[128]{0:T(128)S(1)}, s32[128]{0:T(128)}, u32[]{:S(2)}) %copy-start.1) | copy-done | bytes 536
  12.5 0.1 reshape_reshape.12
  12.6 0.1 eq.16
  12.7 0.2 collective-permute-done.3
  12.9 1.4 %collective-permute-start.5 = (f32[32,768]{1,0:T(8,128)S(1)}, f32[32,768]{1,0:T(8,128)S(1)}, u32[]{:S(2)}, u32[]{:S(2)}) collective-permute-start(f32[32,768]{1,0:T(8,128)S(1)} %copy-done), channel_id=1, source_target_pairs={{0,24},{4,28},{8,16},{12,20},{16,8},{20,12},{24,0},{28,4},{1,25},{... | collective-permute-start | bytes 294920 | tf_op jit(solution)/shard_map/ppermute | solution.py:8
  14.3 0.0 collective-permute-done.4
  14.4 4.0 %collective-permute-done.5 = f32[32,768]{1,0:T(8,128)S(1)} collective-permute-done((f32[32,768]{1,0:T(8,128)S(1)}, f32[32,768]{1,0:T(8,128)S(1)}, u32[]{:S(2)}, u32[]{:S(2)}) %collective-permute-start.5) | collective-permute-done | bytes 98336 | tf_op jit(solution)/shard_map/ppermute | solution.py:8
  18.4 0.1 collective-permute-start.6
  18.5 0.0 collective-permute-done
  18.5 0.0 collective-permute-done.1
  18.6 0.4 add_reduce_fusion.1
  19.0 1.2 %collective-permute-done.6 = f32[128,768]{1,0:T(8,128)S(1)} collective-permute-done((f32[128,768]{1,0:T(8,128)S(1)}, f32[128,768]{1,0:T(8,128)S(1)}, u32[]{:S(2)}, u32[]{:S(2)}) %collective-permute-start.6) | collective-permute-done | bytes 393248 | tf_op jit(solution)/shard_map/ppermute | solution.py:8
  20.2 0.4 add_reduce_fusion
  20.6 0.1 slice_bitcast_fusion.1
  20.7 0.1 reshape.104
  20.8 0.1 reshape.103
  20.9 0.4 fusion.9
  21.2 0.4 fusion.10
  21.7 0.4 convolution_add_fusion.1
  22.2 1.8 %collective-permute-start.8 = (f32[40,768]{1,0:T(8,128)S(1)}, f32[40,768]{1,0:T(8,128)S(1)}, u32[]{:S(2)}, u32[]{:S(2)}) collective-permute-start(f32[40,768]{1,0:T(8,128)S(1)} %select_maximum_fusion.1), channel_id=1, source_target_pairs={{0,2},{1,3},{2,0},{3,1},{4,6},{5,7},{6,4},{7,5},{8,10},{9,11},{10,... | collective-permute-start | bytes 368648 | tf_op jit(solution)/shard_map/ppermute | solution.py:8
  23.9 0.1 reshape.102
  24.0 1.9 %collective-permute-start.9 = (f32[40,768]{1,0:T(8,128)S(1)}, f32[40,768]{1,0:T(8,128)S(1)}, u32[]{:S(2)}, u32[]{:S(2)}) collective-permute-start(f32[40,768]{1,0:T(8,128)S(1)} %select_maximum_fusion), channel_id=1, source_target_pairs={{0,3},{1,2},{2,1},{3,0},{4,7},{5,6},{6,5},{7,4},{8,11},{9,10},{10,... | collective-permute-start | bytes 368648 | tf_op jit(solution)/shard_map/ppermute | solution.py:8
  26.0 0.1 add.180
  26.0 0.6 %collective-permute-start.7 = (f32[40,768]{1,0:T(8,128)S(1)}, f32[40,768]{1,0:T(8,128)S(1)}, u32[]{:S(2)}, u32[]{:S(2)}) collective-permute-start(f32[40,768]{1,0:T(8,128)S(1)} %select_maximum_fusion.2), channel_id=1, source_target_pairs={{0,1},{1,0},{2,3},{3,2},{4,5},{5,4},{6,7},{7,6},{8,9},{9,8},{10,11... | collective-permute-start | bytes 368648 | tf_op jit(solution)/shard_map/ppermute | solution.py:8
  26.6 0.0 collective-permute-start.10
  26.6 8.0 %collective-permute-done.8 = f32[40,768]{1,0:T(8,128)S(1)} collective-permute-done((f32[40,768]{1,0:T(8,128)S(1)}, f32[40,768]{1,0:T(8,128)S(1)}, u32[]{:S(2)}, u32[]{:S(2)}) %collective-permute-start.8) | collective-permute-done | bytes 122912 | tf_op jit(solution)/shard_map/ppermute | solution.py:8
  34.6 0.1 reshape_squeeze.10
  34.7 0.1 reshape_squeeze.11
  34.8 0.5 %collective-permute-done.7 = f32[40,768]{1,0:T(8,128)S(1)} collective-permute-done((f32[40,768]{1,0:T(8,128)S(1)}, f32[40,768]{1,0:T(8,128)S(1)}, u32[]{:S(2)}, u32[]{:S(2)}) %collective-permute-start.7) | collective-permute-done | bytes 122912 | tf_op jit(solution)/shard_map/ppermute | solution.py:8
  35.3 0.1 reshape_squeeze.9
  35.5 0.7 %slice_add_fusion.1 = f32[32,768]{1,0:T(8,128)} fusion(f32[40,768]{1,0:T(8,128)S(1)} %collective-permute-done.9, f32[40,768]{1,0:T(8,128)S(1)} %collective-permute-done.8, f32[40,768]{1,0:T(8,128)S(1)} %collective-permute-done.7, f32[128,768]{1,0:T(8,128)S(1)} %convolution_add_fusion.1), kind=kLoop, calls=%fused_computation.13 | loop fusion | flops 73728 | bytes 491520 | tf_op jit(solution)/shard_map/add | solution.py:84
  36.1 0.4 convolution_add_fusion
  36.5 1.6 %collective-permute-start.11 = (f32[32,768]{1,0:T(8,128)S(1)}, f32[32,768]{1,0:T(8,128)S(1)}, u32[]{:S(2)}, u32[]{:S(2)}) collective-permute-start(f32[32,768]{1,0:T(8,128)S(1)} %get-tuple-element.3), channel_id=1, source_target_pairs={{0,8},{4,12},{8,0},{12,4},{16,24},{20,28},{24,16},{28,20},{1,9},{5... | collective-permute-start | bytes 294920 | tf_op jit(solution)/shard_map/ppermute | solution.py:8
  38.1 0.4 collective-permute-start.13
  38.5 1.6 %collective-permute-start.12 = (f32[32,768]{1,0:T(8,128)S(1)}, f32[32,768]{1,0:T(8,128)S(1)}, u32[]{:S(2)}, u32[]{:S(2)}) collective-permute-start(f32[32,768]{1,0:T(8,128)S(1)} %get-tuple-element.5), channel_id=1, source_target_pairs={{0,16},{4,20},{8,24},{12,28},{16,0},{20,4},{24,8},{28,12},{1,17},{... | collective-permute-start | bytes 294920 | tf_op jit(solution)/shard_map/ppermute | solution.py:8
  40.1 0.6 %reshape_reshape.15 = f32[128]{0:T(128)} reshape(f32[1,2,2,32]{3,2,1,0:T(2,128)S(1)} %reverse_select_fusion) | data formatting | bytes 1024 | tf_op jit(solution)/shard_map/reshape;reshape | solution.py:85
  40.7 0.9 %collective-permute-done.11 = f32[32,768]{1,0:T(8,128)S(1)} collective-permute-done((f32[32,768]{1,0:T(8,128)S(1)}, f32[32,768]{1,0:T(8,128)S(1)}, u32[]{:S(2)}, u32[]{:S(2)}) %collective-permute-start.11) | collective-permute-done | bytes 98336 | tf_op jit(solution)/shard_map/ppermute | solution.py:8
  41.6 2.1 %collective-permute-done.13 = f32[32,768]{1,0:T(8,128)S(1)} collective-permute-done((f32[32,768]{1,0:T(8,128)S(1)}, f32[32,768]{1,0:T(8,128)S(1)}, u32[]{:S(2)}, u32[]{:S(2)}) %collective-permute-start.13) | collective-permute-done | bytes 98336 | tf_op jit(solution)/shard_map/ppermute | solution.py:8
  43.7 0.6 %collective-permute-done.12 = f32[32,768]{1,0:T(8,128)S(1)} collective-permute-done((f32[32,768]{1,0:T(8,128)S(1)}, f32[32,768]{1,0:T(8,128)S(1)}, u32[]{:S(2)}, u32[]{:S(2)}) %collective-permute-start.12) | collective-permute-done | bytes 98336 | tf_op jit(solution)/shard_map/ppermute | solution.py:8
  44.2 0.7 %fusion.3 = f32[32,768]{1,0:T(8,128)} fusion(f32[32,768]{1,0:T(8,128)S(1)} %collective-permute-done.13, f32[32,768]{1,0:T(8,128)S(1)} %collective-permute-done.12, f32[32,768]{1,0:T(8,128)S(1)} %collective-permute-done.11, f32[128,768]{1,0:T(8,128)S(1)} %convolution_add_fusion), kind=kLoop, calls=%fused_computation.12 | loop fusion | flops 73728 | bytes 491520 | tf_op jit(solution)/shard_map/add | solution.py:83
  (30 shorter events, 0.3 us)
Async XLA Ops:
  0.6 17.9 %collective-permute-start.1 = (f32[32,768]{1,0:T(8,128)}, f32[32,768]{1,0:T(8,128)S(1)}, u32[]{:S(2)}, u32[]{:S(2)}) collective-permute-start(f32[32,768]{1,0:T(8,128)} %param.5), channel_id=1, source_target_pairs={{0,2},{1,3},{2,0},{3,1},{4,6},{5,7},{6,4},{7,5},{8,10},{9,11},{10,... | collective-permute-start | bytes 294920 | tf_op jit(solution)/shard_map/ppermute | solution.py:8
  4.7 13.8 %collective-permute-start = (f32[32,768]{1,0:T(8,128)}, f32[32,768]{1,0:T(8,128)S(1)}, u32[]{:S(2)}, u32[]{:S(2)}) collective-permute-start(f32[32,768]{1,0:T(8,128)} %param.5), channel_id=1, source_target_pairs={{0,1},{1,0},{2,3},{3,2},{4,5},{5,4},{6,7},{7,6},{8,9},{9,8},{10,11... | collective-permute-start | bytes 294920 | tf_op jit(solution)/shard_map/ppermute | solution.py:8
  6.3 12.2 %collective-permute-start.2 = (f32[32,768]{1,0:T(8,128)}, f32[32,768]{1,0:T(8,128)S(1)}, u32[]{:S(2)}, u32[]{:S(2)}) collective-permute-start(f32[32,768]{1,0:T(8,128)} %param.5), channel_id=1, source_target_pairs={{0,3},{1,2},{2,1},{3,0},{4,7},{5,6},{6,5},{7,4},{8,11},{9,10},{10,... | collective-permute-start | bytes 294920 | tf_op jit(solution)/shard_map/ppermute | solution.py:8
  6.3 8.0 %collective-permute-start.4 = (f32[32,768]{1,0:T(8,128)}, f32[32,768]{1,0:T(8,128)S(1)}, u32[]{:S(2)}, u32[]{:S(2)}) collective-permute-start(f32[32,768]{1,0:T(8,128)} %param.6), channel_id=1, source_target_pairs={{0,16},{4,20},{8,24},{12,28},{16,0},{20,4},{24,8},{28,12},{1,17},{... | collective-permute-start | bytes 294920 | tf_op jit(solution)/shard_map/ppermute | solution.py:8
  8.1 4.8 %collective-permute-start.3 = (f32[32,768]{1,0:T(8,128)}, f32[32,768]{1,0:T(8,128)S(1)}, u32[]{:S(2)}, u32[]{:S(2)}) collective-permute-start(f32[32,768]{1,0:T(8,128)} %param.6), channel_id=1, source_target_pairs={{0,8},{4,12},{8,0},{12,4},{16,24},{20,28},{24,16},{28,20},{1,9},{5... | collective-permute-start | bytes 294920 | tf_op jit(solution)/shard_map/ppermute | solution.py:8
  9.5 0.9 %copy-start = (f32[32,768]{1,0:T(8,128)S(1)}, f32[32,768]{1,0:T(8,128)}, u32[]{:S(2)}) copy-start(f32[32,768]{1,0:T(8,128)} %param.6) | copy-start | bytes 294916
  11.8 0.7 %copy-start.1 = (s32[128]{0:T(128)S(1)}, s32[128]{0:T(128)}, u32[]{:S(2)}) copy-start(s32[128]{0:T(128)} %param.7) | copy-start | bytes 1540
  12.9 5.5 %collective-permute-start.5 = (f32[32,768]{1,0:T(8,128)S(1)}, f32[32,768]{1,0:T(8,128)S(1)}, u32[]{:S(2)}, u32[]{:S(2)}) collective-permute-start(f32[32,768]{1,0:T(8,128)S(1)} %copy-done), channel_id=1, source_target_pairs={{0,24},{4,28},{8,16},{12,20},{16,8},{20,12},{24,0},{28,4},{1,25},{... | collective-permute-start | bytes 294920 | tf_op jit(solution)/shard_map/ppermute | solution.py:8
  18.4 1.8 %collective-permute-start.6 = (f32[128,768]{1,0:T(8,128)S(1)}, f32[128,768]{1,0:T(8,128)S(1)}, u32[]{:S(2)}, u32[]{:S(2)}) collective-permute-start(f32[128,768]{1,0:T(8,128)S(1)} %constant_dynamic-update-slice_fusion.4), channel_id=1, source_target_pairs={{0,4},{4,0},{8,12},{12,8},{16,20},{20,16},{24,28},{28,24},{1,5},{5... | collective-permute-start | bytes 1179656 | tf_op jit(solution)/shard_map/ppermute | solution.py:8
  22.2 12.5 %collective-permute-start.8 = (f32[40,768]{1,0:T(8,128)S(1)}, f32[40,768]{1,0:T(8,128)S(1)}, u32[]{:S(2)}, u32[]{:S(2)}) collective-permute-start(f32[40,768]{1,0:T(8,128)S(1)} %select_maximum_fusion.1), channel_id=1, source_target_pairs={{0,2},{1,3},{2,0},{3,1},{4,6},{5,7},{6,4},{7,5},{8,10},{9,11},{10,... | collective-permute-start | bytes 368648 | tf_op jit(solution)/shard_map/ppermute | solution.py:8
  24.0 10.7 %collective-permute-start.9 = (f32[40,768]{1,0:T(8,128)S(1)}, f32[40,768]{1,0:T(8,128)S(1)}, u32[]{:S(2)}, u32[]{:S(2)}) collective-permute-start(f32[40,768]{1,0:T(8,128)S(1)} %select_maximum_fusion), channel_id=1, source_target_pairs={{0,3},{1,2},{2,1},{3,0},{4,7},{5,6},{6,5},{7,4},{8,11},{9,10},{10,... | collective-permute-start | bytes 368648 | tf_op jit(solution)/shard_map/ppermute | solution.py:8
  26.0 9.3 %collective-permute-start.7 = (f32[40,768]{1,0:T(8,128)S(1)}, f32[40,768]{1,0:T(8,128)S(1)}, u32[]{:S(2)}, u32[]{:S(2)}) collective-permute-start(f32[40,768]{1,0:T(8,128)S(1)} %select_maximum_fusion.2), channel_id=1, source_target_pairs={{0,1},{1,0},{2,3},{3,2},{4,5},{5,4},{6,7},{7,6},{8,9},{9,8},{10,11... | collective-permute-start | bytes 368648 | tf_op jit(solution)/shard_map/ppermute | solution.py:8
  26.6 9.5 %collective-permute-start.10 = (f32[128,768]{1,0:T(8,128)S(1)}, f32[128,768]{1,0:T(8,128)S(1)}, u32[]{:S(2)}, u32[]{:S(2)}) collective-permute-start(f32[128,768]{1,0:T(8,128)S(1)} %fusion.9), channel_id=1, source_target_pairs={{0,4},{4,0},{8,12},{12,8},{16,20},{20,16},{24,28},{28,24},{1,5},{5... | collective-permute-start | bytes 1179656 | tf_op jit(solution)/shard_map/ppermute | solution.py:8
  36.5 5.0 %collective-permute-start.11 = (f32[32,768]{1,0:T(8,128)S(1)}, f32[32,768]{1,0:T(8,128)S(1)}, u32[]{:S(2)}, u32[]{:S(2)}) collective-permute-start(f32[32,768]{1,0:T(8,128)S(1)} %get-tuple-element.3), channel_id=1, source_target_pairs={{0,8},{4,12},{8,0},{12,4},{16,24},{20,28},{24,16},{28,20},{1,9},{5... | collective-permute-start | bytes 294920 | tf_op jit(solution)/shard_map/ppermute | solution.py:8
  38.1 5.6 %collective-permute-start.13 = (f32[32,768]{1,0:T(8,128)S(1)}, f32[32,768]{1,0:T(8,128)S(1)}, u32[]{:S(2)}, u32[]{:S(2)}) collective-permute-start(f32[32,768]{1,0:T(8,128)S(1)} %get-tuple-element.4), channel_id=1, source_target_pairs={{0,24},{4,28},{8,16},{12,20},{16,8},{20,12},{24,0},{28,4},{1,25},{... | collective-permute-start | bytes 294920 | tf_op jit(solution)/shard_map/ppermute | solution.py:8
  38.5 5.8 %collective-permute-start.12 = (f32[32,768]{1,0:T(8,128)S(1)}, f32[32,768]{1,0:T(8,128)S(1)}, u32[]{:S(2)}, u32[]{:S(2)}) collective-permute-start(f32[32,768]{1,0:T(8,128)S(1)} %get-tuple-element.5), channel_id=1, source_target_pairs={{0,16},{4,20},{8,24},{12,28},{16,0},{20,4},{24,8},{28,12},{1,17},{... | collective-permute-start | bytes 294920 | tf_op jit(solution)/shard_map/ppermute | solution.py:8

commit v4 on v3

--- a/solution.py
+++ b/solution.py
@@ -29,7 +29,11 @@
     )
 
 
-def losses(images, texts, matched, columns, scale, shift):
+def after(x, *others):
+    return lax.optimization_barrier((x,) + others)[0]
+
+
+def quadrant(images, texts, matched, columns, scale, shift):
     logits = scale * dot(images, texts, (1, 1)) + shift
     match = matched[:, None] == columns[None, :]
     v = jnp.where(match, -logits, logits)
@@ -47,26 +51,31 @@
     scale = jnp.exp(log_scale[0])
     shift = bias[0]
 
-    image_blocks, text_blocks = [image_emb], [text_emb]
+    matched = untwist(pairs.reshape(n_txt, rows), me_txt).reshape(-1)
+    text_blocks = {0: text_emb}
+    image_blocks = {0: image_emb}
     for k in range(1, max(n_txt, chips)):
-        if k < n_txt:
-            image_blocks.append(exchange(image_emb, "txt", n_txt, k))
         if k < chips:
-            text_blocks.append(exchange(text_emb, "img", n_img, 2 * k))
-    near = jnp.concatenate(text_blocks)
+            text_blocks[k] = exchange(text_emb, "img", n_img, 2 * k)
+        if 1 < k < n_txt:
+            image_blocks[k] = exchange(image_emb, "txt", n_txt, k)
+    image_blocks[1] = exchange(after(image_emb, text_blocks[1]), "txt", n_txt, 1)
+    near = jnp.concatenate([text_blocks[k] for k in range(chips)])
     far = exchange(near, "img", n_img, 1)
-    images = jnp.concatenate(image_blocks)
+    images = jnp.concatenate([image_blocks[k] for k in range(n_txt)])
+    count = n_txt * rows
+    pair_row = jnp.pad(matched.astype(jnp.float32)[None], ((0, 7), (0, width - count)))
+    pair = exchange(jnp.concatenate([images, pair_row]), "img", n_img, 1)
+    pair_images, matched_pair = pair[:count], pair[count, :count].astype(jnp.int32)
 
-    matched = untwist(pairs.reshape(n_txt, rows), me_txt).reshape(-1)
     place = jnp.arange(chips * cols, dtype=jnp.int32)
     chip = (me_img // 2) ^ (place // cols)
-    column = (me_txt * n_img + 2 * chip) * cols + place % cols
     core = me_img % 2
-    loss_near, d_near = losses(images, near, matched, column + core * cols, scale, shift)
-    loss_far, d_far = losses(images, far, matched, column + (1 - core) * cols, scale, shift)
+    column = (me_txt * n_img + 2 * chip + core) * cols + place % cols
+    far_column = column + (1 - 2 * core) * cols
+    loss_near, d_near = quadrant(images, near, matched, column, scale, shift)
+    loss_far, d_far = quadrant(images, far, matched, far_column, scale, shift)
 
-    text_far = dot(d_far, images, (0, 0))
-    text_back = exchange(text_far, "img", n_img, 1)
     image_term = dot(d_near, near, (1, 0)) + dot(d_far, far, (1, 0))
     loss_part = (loss_near + loss_far).reshape(n_txt, rows)
     image_back, loss_sum = [image_term[:rows]], loss_part
@@ -76,8 +85,10 @@
         sent = jnp.concatenate([image_term[k * rows:(k + 1) * rows], loss_row])
         got = exchange(sent, "txt", n_txt, k)
         image_back.append(got[:rows])
-        loss_sum = loss_sum + got[rows, :n_txt * rows].reshape(n_txt, rows)
-    text_term = dot(d_near, images, (0, 0)) + text_back
+        loss_sum = loss_sum + got[rows, :count].reshape(n_txt, rows)
+
+    _, d_pair = quadrant(pair_images, near, matched_pair, column, scale, shift)
+    text_term = dot(d_near, images, (0, 0)) + dot(d_pair, pair_images, (0, 0))
     text_grad = text_term[:cols]
     for k in range(1, chips):
         text_grad = text_grad + exchange(text_term[k * cols:(k + 1) * cols], "img", n_img, 2 * k)

time: 45.1 us -> 35.2 us (0.78)
  waiting for transfers between devices: 17.5 us -> 6.56 us
    ppermute x14, waiting for transfers between devices: 17.5 us -> 6.56 us  [exchange(): return lax.ppermute(x, axis, [(i, i ^ k) for i in range(n)])]
    dot_general x6 -> x7, matrix products: 2.39 us -> 2.74 us  [dot(): lax.dot_general(a, b, ((contract[:1], contract[1:]), ((), ())), precision...]
    unnamed x10 -> x13, local copies, waits for them, and re-layouts: 1.59 us -> 1.7 us
  transfers between devices with their start and end apart: 14 -> 14, of which waited for: 8 -> 5; matrix products, arithmetic and copies ran while one was open for 8% -> 18% of each run, Pallas kernels for 0% -> 0%
where the time goes in v4:
time: 35.2 us; the launch traced here: 35 us
  starting transfers between devices  18.6 us (53%)
  waiting for transfers between devices  6.56 us (19%)
  local copies, waits for them, and re-layouts  3.37 us (10%)
  matrix products  2.74 us (8%)
  between operations  2.21 us (6%)
  other arithmetic  1.44 us (4%)
    ppermute x14, starting transfers between devices, exchange(): return lax.ppermute(x, axis, [(i, i ^ k) for i in range(n)])  18.6 us
    ppermute x14, waiting for transfers between devices, exchange(): return lax.ppermute(x, axis, [(i, i ^ k) for i in range(n)])  6.56 us
    dot_general x7, matrix products, dot(): lax.dot_general(a, b, ((contract[:1], contract[1:]), ((), ())), precision...  2.74 us
    unnamed x13, local copies, waits for them, and re-layouts  1.7 us
  transfers between devices with their start and end apart: 14, of which 5 were waited for; matrix products, arithmetic and copies ran while one was open for 18% of the time, Pallas kernels for 0%

profile of v4, /device:TPU:0, one launch (start us, length us, event | category | flops | bytes accessed | tf_op | source)
XLA Modules:
  0.0 35.0 jit_solution(17826239135741971774)
XLA Ops:
  0.6 4.1 %collective-permute-start.2 = (f32[32,768]{1,0:T(8,128)}, f32[32,768]{1,0:T(8,128)S(1)}, u32[]{:S(2)}, u32[]{:S(2)}) collective-permute-start(f32[32,768]{1,0:T(8,128)} %param.5), channel_id=1, source_target_pairs={{0,2},{1,3},{2,0},{3,1},{4,6},{5,7},{6,4},{7,5},{8,10},{9,11},{10,... | collective-permute-start | bytes 294920 | tf_op jit(solution)/shard_map/ppermute | solution.py:8
  4.7 1.3 %collective-permute-start.3 = (f32[32,768]{1,0:T(8,128)}, f32[32,768]{1,0:T(8,128)S(1)}, u32[]{:S(2)}, u32[]{:S(2)}) collective-permute-start(f32[32,768]{1,0:T(8,128)} %param.5), channel_id=1, source_target_pairs={{0,3},{1,2},{2,1},{3,0},{4,7},{5,6},{6,5},{7,4},{8,11},{9,10},{10,... | collective-permute-start | bytes 294920 | tf_op jit(solution)/shard_map/ppermute | solution.py:8
  6.1 1.5 %collective-permute-start = (f32[32,768]{1,0:T(8,128)}, f32[32,768]{1,0:T(8,128)S(1)}, u32[]{:S(2)}, u32[]{:S(2)}) collective-permute-start(f32[32,768]{1,0:T(8,128)} %param.6), channel_id=1, source_target_pairs={{0,8},{4,12},{8,0},{12,4},{16,24},{20,28},{24,16},{28,20},{1,9},{5... | collective-permute-start | bytes 294920 | tf_op jit(solution)/shard_map/ppermute | solution.py:8
  7.6 1.5 %collective-permute-start.4 = (f32[32,768]{1,0:T(8,128)}, f32[32,768]{1,0:T(8,128)S(1)}, u32[]{:S(2)}, u32[]{:S(2)}) collective-permute-start(f32[32,768]{1,0:T(8,128)} %param.6), channel_id=1, source_target_pairs={{0,16},{4,20},{8,24},{12,28},{16,0},{20,4},{24,8},{28,12},{1,17},{... | collective-permute-start | bytes 294920 | tf_op jit(solution)/shard_map/ppermute | solution.py:8
  9.1 0.5 %collective-permute-start.5 = (f32[32,768]{1,0:T(8,128)}, f32[32,768]{1,0:T(8,128)S(1)}, u32[]{:S(2)}, u32[]{:S(2)}) collective-permute-start(f32[32,768]{1,0:T(8,128)} %param.6), channel_id=1, source_target_pairs={{0,24},{4,28},{8,16},{12,20},{16,8},{20,12},{24,0},{28,4},{1,25},{... | collective-permute-start | bytes 294920 | tf_op jit(solution)/shard_map/ppermute | solution.py:8
  9.6 0.9 %constant_dynamic-update-slice_fusion.12 = (f32[136,768]{1,0:T(8,128)S(1)}, f32[128,768]{1,0:T(8,128)S(1)}) fusion(f32[32,768]{1,0:T(8,128)} %param.5), kind=kLoop, calls=%fused_computation.67 | loop fusion | bytes 294912
  10.5 0.0 copy-start.1
  10.6 0.0 copy-start.2
  10.6 0.7 %copy-done.2 = s32[128]{0:T(128)S(1)} copy-done((s32[128]{0:T(128)S(1)}, s32[128]{0:T(128)}, u32[]{:S(2)}) %copy-start.2) | copy-done | bytes 536
  11.3 0.1 reshape_reshape.13
  11.4 0.1 convert_element_type.29
  12.8 0.1 eq.20
  12.9 0.0 collective-permute-done
  12.9 0.3 collective-permute-start.1
  13.2 0.2 collective-permute-done.4
  13.5 1.4 %collective-permute-done.5 = f32[32,768]{1,0:T(8,128)S(1)} collective-permute-done((f32[32,768]{1,0:T(8,128)}, f32[32,768]{1,0:T(8,128)S(1)}, u32[]{:S(2)}, u32[]{:S(2)}) %collective-permute-start.5) | collective-permute-done | bytes 98336 | tf_op jit(solution)/shard_map/ppermute | solution.py:8
  14.8 0.1 collective-permute-start.6
  14.9 2.7 %collective-permute-done.1 = f32[32,768]{1,0:T(8,128)S(1)} collective-permute-done((f32[32,768]{1,0:T(8,128)S(1)}, f32[32,768]{1,0:T(8,128)S(1)}, u32[]{:S(2)}, u32[]{:S(2)}) %collective-permute-start.1) | collective-permute-done | bytes 98336 | tf_op jit(solution)/shard_map/ppermute | solution.py:8
  17.7 0.1 collective-permute-start.10
  17.8 0.4 %add_reduce_fusion.1 = (f32[128]{0:T(128)S(1)}, f32[128,128]{0,1:T(8,128)S(1)}) fusion(f32[]{:T(128)} %bitcast.24, f32[128,768]{1,0:T(8,128)S(1)} %get-tuple-element.16, f32[128,768]{1,0:T(8,128)S(1)} %constant_dynamic-update-slice_fusion.4, f32[]{:T(128)} %bitcast.1, s32[128]{0:T(128)S(1)} %get-tuple-element.8, s32[128]{0:T(128)S(1)} %eq.20), kind=kOutput, calls=%fused_computation.41 | convolution fusion | flops 75661184 | bytes 853512 | tf_op jit(solution)/shard_map/dot_general | solution.py:23
  18.2 0.0 collective-permute-done.6
  18.2 0.4 %add_reduce_fusion = (f32[128]{0:T(128)S(1)}, f32[128,128]{0,1:T(8,128)S(1)}) fusion(f32[]{:T(128)} %bitcast.26, f32[128,768]{1,0:T(8,128)S(1)} %get-tuple-element.16, f32[128,768]{1,0:T(8,128)S(1)} %collective-permute-done.6, f32[]{:T(128)} %bitcast.1, s32[128]{0:T(128)S(1)} %get-tuple-element.7, s32[128]{0:T(128)S(1)} %eq.20), kind=kOutput, calls=%fused_computation.39 | convolution fusion | flops 75661184 | bytes 853512 | tf_op jit(solution)/shard_map/dot_general | solution.py:23
  18.6 0.1 slice_bitcast_fusion.1
  18.7 0.1 add.192
  18.8 0.4 %fusion.10 = f32[128,768]{1,0:T(8,128)S(1)} fusion(f32[128,768]{1,0:T(8,128)S(1)} %collective-permute-done.6, f32[128,128]{0,1:T(8,128)S(1)} %get-tuple-element.33, f32[]{:T(128)} %bitcast.1, s32[128]{0:T(128)S(1)} %eq.20, s32[128]{0:T(128)S(1)} %get-tuple-element.7), kind=kOutput, calls=%fused_computation.27 | convolution fusion | flops 75661312 | bytes 852996 | tf_op jit(solution)/shard_map/dot_general | solution.py:23
  19.2 0.4 %convolution_add_fusion.1 = f32[128,768]{1,0:T(8,128)S(1)} fusion(f32[128,768]{1,0:T(8,128)S(1)} %fusion.10, f32[128,768]{1,0:T(8,128)S(1)} %constant_dynamic-update-slice_fusion.4, f32[128,128]{0,1:T(8,128)S(1)} %get-tuple-element.31, f32[]{:T(128)} %bitcast.1, s32[128]{0:T(128)S(1)} %eq.20, s32[128]{0:T(128)S(1)} %get-tuple-element.8), kind=kOutput, calls=%fused_computation.1 | convolution fusion | flops 75759616 | bytes 1246212 | tf_op jit(solution)/shard_map/dot_general | solution.py:23
  19.7 0.1 reshape.119
  19.8 0.3 collective-permute-start.7
  20.1 0.1 reshape.120
  20.2 2.9 %collective-permute-start.8 = (f32[40,768]{1,0:T(8,128)S(1)}, f32[40,768]{1,0:T(8,128)S(1)}, u32[]{:S(2)}, u32[]{:S(2)}) collective-permute-start(f32[40,768]{1,0:T(8,128)S(1)} %select_maximum_fusion.1), channel_id=1, source_target_pairs={{0,2},{1,3},{2,0},{3,1},{4,6},{5,7},{6,4},{7,5},{8,10},{9,11},{10,... | collective-permute-start | bytes 368648 | tf_op jit(solution)/shard_map/ppermute | solution.py:8
  23.1 0.1 reshape.121
  23.1 1.4 %collective-permute-start.9 = (f32[40,768]{1,0:T(8,128)S(1)}, f32[40,768]{1,0:T(8,128)S(1)}, u32[]{:S(2)}, u32[]{:S(2)}) collective-permute-start(f32[40,768]{1,0:T(8,128)S(1)} %select_maximum_fusion), channel_id=1, source_target_pairs={{0,3},{1,2},{2,1},{3,0},{4,7},{5,6},{6,5},{7,4},{8,11},{9,10},{10,... | collective-permute-start | bytes 368648 | tf_op jit(solution)/shard_map/ppermute | solution.py:8
  24.6 0.0 collective-permute-done.10
  24.6 0.4 %negate_select_fusion.1 = f32[128,128]{0,1:T(8,128)S(1)} fusion(f32[128,768]{1,0:T(8,128)S(1)} %constant_dynamic-update-slice_fusion.4, f32[136,768]{1,0:T(8,128)S(1)} %collective-permute-done.10, s32[128]{0:T(128)S(1)} %fusion.40, f32[]{:T(128)} %bitcast.25, f32[]{:T(128)} %bitcast.1, s32[128]{0:T(128)S(1)} %get-tuple-element.8), kind=kOutput, calls=%fused_computation.22 | convolution fusion | flops 75579392 | bytes 853000 | tf_op jit(solution)/shard_map/dot_general | solution.py:23
  24.9 0.4 %fusion.3 = f32[128,768]{1,0:T(8,128)S(1)} fusion(f32[136,768]{1,0:T(8,128)S(1)} %collective-permute-done.10, f32[128,128]{0,1:T(8,128)S(1)} %negate_select_fusion.1, s32[128]{0:T(128)S(1)} %fusion.40, f32[]{:T(128)} %bitcast.1, s32[128]{0:T(128)S(1)} %get-tuple-element.8), kind=kOutput, calls=%fused_computation.8 | convolution fusion | flops 75661312 | bytes 852996 | tf_op jit(solution)/shard_map/dot_general | solution.py:23
  25.3 0.4 %convolution_add_fusion = f32[128,768]{1,0:T(8,128)S(1)} fusion(f32[128,768]{1,0:T(8,128)S(1)} %fusion.3, f32[128,768]{1,0:T(8,128)S(1)} %get-tuple-element.16, f32[128,128]{0,1:T(8,128)S(1)} %get-tuple-element.31, f32[]{:T(128)} %bitcast.1, s32[128]{0:T(128)S(1)} %eq.20, s32[128]{0:T(128)S(1)} %get-tuple-element.8), kind=kOutput, calls=%fused_computation | convolution fusion | flops 75759616 | bytes 1246212 | tf_op jit(solution)/shard_map/dot_general | solution.py:23
  25.7 1.6 %collective-permute-start.11 = (f32[32,768]{1,0:T(8,128)S(1)}, f32[32,768]{1,0:T(8,128)S(1)}, u32[]{:S(2)}, u32[]{:S(2)}) collective-permute-start(f32[32,768]{1,0:T(8,128)S(1)} %get-tuple-element.9), channel_id=1, source_target_pairs={{0,8},{4,12},{8,0},{12,4},{16,24},{20,28},{24,16},{28,20},{1,9},{5... | collective-permute-start | bytes 294920 | tf_op jit(solution)/shard_map/ppermute | solution.py:8
  27.3 1.5 %collective-permute-start.12 = (f32[32,768]{1,0:T(8,128)S(1)}, f32[32,768]{1,0:T(8,128)S(1)}, u32[]{:S(2)}, u32[]{:S(2)}) collective-permute-start(f32[32,768]{1,0:T(8,128)S(1)} %get-tuple-element.11), channel_id=1, source_target_pairs={{0,16},{4,20},{8,24},{12,28},{16,0},{20,4},{24,8},{28,12},{1,17},{... | collective-permute-start | bytes 294920 | tf_op jit(solution)/shard_map/ppermute | solution.py:8
  28.8 1.6 %collective-permute-start.13 = (f32[32,768]{1,0:T(8,128)S(1)}, f32[32,768]{1,0:T(8,128)S(1)}, u32[]{:S(2)}, u32[]{:S(2)}) collective-permute-start(f32[32,768]{1,0:T(8,128)S(1)} %get-tuple-element.10), channel_id=1, source_target_pairs={{0,24},{4,28},{8,16},{12,20},{16,8},{20,12},{24,0},{28,4},{1,25},{... | collective-permute-start | bytes 294920 | tf_op jit(solution)/shard_map/ppermute | solution.py:8
  30.4 0.1 reshape_squeeze.9
  30.5 2.1 %collective-permute-done.8 = f32[40,768]{1,0:T(8,128)S(1)} collective-permute-done((f32[40,768]{1,0:T(8,128)S(1)}, f32[40,768]{1,0:T(8,128)S(1)}, u32[]{:S(2)}, u32[]{:S(2)}) %collective-permute-start.8) | collective-permute-done | bytes 122912 | tf_op jit(solution)/shard_map/ppermute | solution.py:8
  32.6 0.1 reshape_squeeze.10
  32.7 0.0 collective-permute-done.9
  32.7 0.1 reshape_squeeze.11
  32.9 0.7 %slice_add_fusion.1 = f32[32,768]{1,0:T(8,128)} fusion(f32[40,768]{1,0:T(8,128)S(1)} %collective-permute-done.9, f32[40,768]{1,0:T(8,128)S(1)} %collective-permute-done.8, f32[40,768]{1,0:T(8,128)S(1)} %collective-permute-done.7, f32[128,768]{1,0:T(8,128)S(1)} %convolution_add_fusion.1), kind=kLoop, calls=%fused_computation.18 | loop fusion | flops 73728 | bytes 491520 | tf_op jit(solution)/shard_map/add | solution.py:95
  33.5 0.6 %reshape_reshape.16 = f32[128]{0:T(128)} reshape(f32[1,2,2,32]{3,2,1,0:T(2,128)S(1)} %reverse_select_fusion) | data formatting | bytes 1024 | tf_op jit(solution)/shard_map/reshape;reshape | solution.py:96
  34.1 0.2 collective-permute-done.13
  34.3 0.7 %fusion.7 = f32[32,768]{1,0:T(8,128)} fusion(f32[32,768]{1,0:T(8,128)S(1)} %collective-permute-done.13, f32[32,768]{1,0:T(8,128)S(1)} %collective-permute-done.12, f32[32,768]{1,0:T(8,128)S(1)} %collective-permute-done.11, f32[128,768]{1,0:T(8,128)S(1)} %convolution_add_fusion), kind=kLoop, calls=%fused_computation.17 | loop fusion | flops 73728 | bytes 491520 | tf_op jit(solution)/shard_map/add | solution.py:94
  (35 shorter events, 0.4 us)
Async XLA Ops:
  0.6 17.0 %collective-permute-start.2 = (f32[32,768]{1,0:T(8,128)}, f32[32,768]{1,0:T(8,128)S(1)}, u32[]{:S(2)}, u32[]{:S(2)}) collective-permute-start(f32[32,768]{1,0:T(8,128)} %param.5), channel_id=1, source_target_pairs={{0,2},{1,3},{2,0},{3,1},{4,6},{5,7},{6,4},{7,5},{8,10},{9,11},{10,... | collective-permute-start | bytes 294920 | tf_op jit(solution)/shard_map/ppermute | solution.py:8
  4.7 12.9 %collective-permute-start.3 = (f32[32,768]{1,0:T(8,128)}, f32[32,768]{1,0:T(8,128)S(1)}, u32[]{:S(2)}, u32[]{:S(2)}) collective-permute-start(f32[32,768]{1,0:T(8,128)} %param.5), channel_id=1, source_target_pairs={{0,3},{1,2},{2,1},{3,0},{4,7},{5,6},{6,5},{7,4},{8,11},{9,10},{10,... | collective-permute-start | bytes 294920 | tf_op jit(solution)/shard_map/ppermute | solution.py:8
  6.1 6.8 %collective-permute-start = (f32[32,768]{1,0:T(8,128)}, f32[32,768]{1,0:T(8,128)S(1)}, u32[]{:S(2)}, u32[]{:S(2)}) collective-permute-start(f32[32,768]{1,0:T(8,128)} %param.6), channel_id=1, source_target_pairs={{0,8},{4,12},{8,0},{12,4},{16,24},{20,28},{24,16},{28,20},{1,9},{5... | collective-permute-start | bytes 294920 | tf_op jit(solution)/shard_map/ppermute | solution.py:8
  7.6 5.9 %collective-permute-start.4 = (f32[32,768]{1,0:T(8,128)}, f32[32,768]{1,0:T(8,128)S(1)}, u32[]{:S(2)}, u32[]{:S(2)}) collective-permute-start(f32[32,768]{1,0:T(8,128)} %param.6), channel_id=1, source_target_pairs={{0,16},{4,20},{8,24},{12,28},{16,0},{20,4},{24,8},{28,12},{1,17},{... | collective-permute-start | bytes 294920 | tf_op jit(solution)/shard_map/ppermute | solution.py:8
  9.1 5.7 %collective-permute-start.5 = (f32[32,768]{1,0:T(8,128)}, f32[32,768]{1,0:T(8,128)S(1)}, u32[]{:S(2)}, u32[]{:S(2)}) collective-permute-start(f32[32,768]{1,0:T(8,128)} %param.6), channel_id=1, source_target_pairs={{0,24},{4,28},{8,16},{12,20},{16,8},{20,12},{24,0},{28,4},{1,25},{... | collective-permute-start | bytes 294920 | tf_op jit(solution)/shard_map/ppermute | solution.py:8
  9.6 1.0 %copy-start = (f32[32,768]{1,0:T(8,128)S(1)}, f32[32,768]{1,0:T(8,128)}, u32[]{:S(2)}) copy-start(f32[32,768]{1,0:T(8,128)} %param.6) | copy-start | bytes 294916
  10.5 2.4 %copy-start.1 = (f32[32,768]{1,0:T(8,128)S(1)}, f32[32,768]{1,0:T(8,128)}, u32[]{:S(2)}) copy-start(f32[32,768]{1,0:T(8,128)} %param.5) | copy-start | bytes 294916
  10.6 0.7 %copy-start.2 = (s32[128]{0:T(128)S(1)}, s32[128]{0:T(128)}, u32[]{:S(2)}) copy-start(s32[128]{0:T(128)} %param.7) | copy-start | bytes 1540
  12.9 4.7 %collective-permute-start.1 = (f32[32,768]{1,0:T(8,128)S(1)}, f32[32,768]{1,0:T(8,128)S(1)}, u32[]{:S(2)}, u32[]{:S(2)}) collective-permute-start(f32[32,768]{1,0:T(8,128)S(1)} %copy-done.1), channel_id=1, source_target_pairs={{0,1},{1,0},{2,3},{3,2},{4,5},{5,4},{6,7},{7,6},{8,9},{9,8},{10,11... | collective-permute-start | bytes 294920 | tf_op jit(solution)/shard_map/ppermute | solution.py:8
  14.8 3.4 %collective-permute-start.6 = (f32[128,768]{1,0:T(8,128)S(1)}, f32[128,768]{1,0:T(8,128)S(1)}, u32[]{:S(2)}, u32[]{:S(2)}) collective-permute-start(f32[128,768]{1,0:T(8,128)S(1)} %constant_dynamic-update-slice_fusion.4), channel_id=1, source_target_pairs={{0,4},{4,0},{8,12},{12,8},{16,20},{20,16},{24,28},{28,24},{1,5},{5... | collective-permute-start | bytes 1179656 | tf_op jit(solution)/shard_map/ppermute | solution.py:8
  17.7 6.9 %collective-permute-start.10 = (f32[136,768]{1,0:T(8,128)S(1)}, f32[136,768]{1,0:T(8,128)S(1)}, u32[]{:S(2)}, u32[]{:S(2)}) collective-permute-start(f32[136,768]{1,0:T(8,128)S(1)} %constant_dynamic-update-slice_fusion.8), channel_id=1, source_target_pairs={{0,4},{4,0},{8,12},{12,8},{16,20},{20,16},{24,28},{28,24},{1,5},{5... | collective-permute-start | bytes 1253384 | tf_op jit(solution)/shard_map/ppermute | solution.py:8
  19.8 9.0 %collective-permute-start.7 = (f32[40,768]{1,0:T(8,128)S(1)}, f32[40,768]{1,0:T(8,128)S(1)}, u32[]{:S(2)}, u32[]{:S(2)}) collective-permute-start(f32[40,768]{1,0:T(8,128)S(1)} %select_maximum_fusion.2), channel_id=1, source_target_pairs={{0,1},{1,0},{2,3},{3,2},{4,5},{5,4},{6,7},{7,6},{8,9},{9,8},{10,11... | collective-permute-start | bytes 368648 | tf_op jit(solution)/shard_map/ppermute | solution.py:8
  20.2 12.4 %collective-permute-start.8 = (f32[40,768]{1,0:T(8,128)S(1)}, f32[40,768]{1,0:T(8,128)S(1)}, u32[]{:S(2)}, u32[]{:S(2)}) collective-permute-start(f32[40,768]{1,0:T(8,128)S(1)} %select_maximum_fusion.1), channel_id=1, source_target_pairs={{0,2},{1,3},{2,0},{3,1},{4,6},{5,7},{6,4},{7,5},{8,10},{9,11},{10,... | collective-permute-start | bytes 368648 | tf_op jit(solution)/shard_map/ppermute | solution.py:8
  23.1 9.6 %collective-permute-start.9 = (f32[40,768]{1,0:T(8,128)S(1)}, f32[40,768]{1,0:T(8,128)S(1)}, u32[]{:S(2)}, u32[]{:S(2)}) collective-permute-start(f32[40,768]{1,0:T(8,128)S(1)} %select_maximum_fusion), channel_id=1, source_target_pairs={{0,3},{1,2},{2,1},{3,0},{4,7},{5,6},{6,5},{7,4},{8,11},{9,10},{10,... | collective-permute-start | bytes 368648 | tf_op jit(solution)/shard_map/ppermute | solution.py:8
  25.7 8.4 %collective-permute-start.11 = (f32[32,768]{1,0:T(8,128)S(1)}, f32[32,768]{1,0:T(8,128)S(1)}, u32[]{:S(2)}, u32[]{:S(2)}) collective-permute-start(f32[32,768]{1,0:T(8,128)S(1)} %get-tuple-element.9), channel_id=1, source_target_pairs={{0,8},{4,12},{8,0},{12,4},{16,24},{20,28},{24,16},{28,20},{1,9},{5... | collective-permute-start | bytes 294920 | tf_op jit(solution)/shard_map/ppermute | solution.py:8
  27.3 6.9 %collective-permute-start.12 = (f32[32,768]{1,0:T(8,128)S(1)}, f32[32,768]{1,0:T(8,128)S(1)}, u32[]{:S(2)}, u32[]{:S(2)}) collective-permute-start(f32[32,768]{1,0:T(8,128)S(1)} %get-tuple-element.11), channel_id=1, source_target_pairs={{0,16},{4,20},{8,24},{12,28},{16,0},{20,4},{24,8},{28,12},{1,17},{... | collective-permute-start | bytes 294920 | tf_op jit(solution)/shard_map/ppermute | solution.py:8
  28.8 5.5 %collective-permute-start.13 = (f32[32,768]{1,0:T(8,128)S(1)}, f32[32,768]{1,0:T(8,128)S(1)}, u32[]{:S(2)}, u32[]{:S(2)}) collective-permute-start(f32[32,768]{1,0:T(8,128)S(1)} %get-tuple-element.10), channel_id=1, source_target_pairs={{0,24},{4,28},{8,16},{12,20},{16,8},{20,12},{24,0},{28,4},{1,25},{... | collective-permute-start | bytes 294920 | tf_op jit(solution)/shard_map/ppermute | solution.py:8

commit v5 on v4

--- a/solution.py
+++ b/solution.py
@@ -29,10 +29,6 @@
     )
 
 
-def after(x, *others):
-    return lax.optimization_barrier((x,) + others)[0]
-
-
 def quadrant(images, texts, matched, columns, scale, shift):
     logits = scale * dot(images, texts, (1, 1)) + shift
     match = matched[:, None] == columns[None, :]
@@ -52,15 +48,18 @@
     shift = bias[0]
 
     matched = untwist(pairs.reshape(n_txt, rows), me_txt).reshape(-1)
-    text_blocks = {0: text_emb}
+    near = text_emb
     image_blocks = {0: image_emb}
-    for k in range(1, max(n_txt, chips)):
-        if k < chips:
-            text_blocks[k] = exchange(text_emb, "img", n_img, 2 * k)
-        if 1 < k < n_txt:
+    order = [k for k in range(2, n_txt)] + [1]
+    step = 1
+    while step < chips:
+        near = jnp.concatenate([near, exchange(near, "img", n_img, 2 * step)])
+        for k in order[:2]:
             image_blocks[k] = exchange(image_emb, "txt", n_txt, k)
-    image_blocks[1] = exchange(after(image_emb, text_blocks[1]), "txt", n_txt, 1)
-    near = jnp.concatenate([text_blocks[k] for k in range(chips)])
+        order = order[2:]
+        step *= 2
+    for k in order:
+        image_blocks[k] = exchange(image_emb, "txt", n_txt, k)
     far = exchange(near, "img", n_img, 1)
     images = jnp.concatenate([image_blocks[k] for k in range(n_txt)])
     count = n_txt * rows
@@ -78,21 +77,22 @@
 
     image_term = dot(d_near, near, (1, 0)) + dot(d_far, far, (1, 0))
     loss_part = (loss_near + loss_far).reshape(n_txt, rows)
-    image_back, loss_sum = [image_term[:rows]], loss_part
+    image_grad, loss_sum = image_term[:rows], loss_part
     for k in range(1, n_txt):
-        loss_row = jnp.stack([loss_part[k ^ m] for m in range(n_txt)]).reshape(1, -1)
-        loss_row = jnp.pad(loss_row, ((0, 7), (0, width - loss_row.shape[1])))
-        sent = jnp.concatenate([image_term[k * rows:(k + 1) * rows], loss_row])
-        got = exchange(sent, "txt", n_txt, k)
-        image_back.append(got[:rows])
-        loss_sum = loss_sum + got[rows, :count].reshape(n_txt, rows)
+        loss_tile = jnp.stack([loss_part[k ^ m] for m in range(n_txt)]).reshape(-1, 128)
+        loss_tile = jnp.pad(loss_tile, ((0, -loss_tile.shape[0] % 8), (0, 0))).reshape(-1, 8, 128)
+        term_tiles = image_term[k * rows:(k + 1) * rows].reshape(rows // 8, 8, width // 128, 128)
+        term_tiles = jnp.swapaxes(term_tiles, 1, 2).reshape(-1, 8, 128)
+        got = exchange(jnp.concatenate([term_tiles, loss_tile]), "txt", n_txt, k)
+        got_tiles = got[:term_tiles.shape[0]].reshape(rows // 8, width // 128, 8, 128)
+        image_grad = image_grad + jnp.swapaxes(got_tiles, 1, 2).reshape(rows, width)
+        loss_sum = loss_sum + got[term_tiles.shape[0]:].reshape(-1)[:count].reshape(n_txt, rows)
 
     _, d_pair = quadrant(pair_images, near, matched_pair, column, scale, shift)
     text_term = dot(d_near, images, (0, 0)) + dot(d_pair, pair_images, (0, 0))
     text_grad = text_term[:cols]
     for k in range(1, chips):
         text_grad = text_grad + exchange(text_term[k * cols:(k + 1) * cols], "img", n_img, 2 * k)
-    image_grad = sum(image_back)
     image_loss = untwist(loss_sum, me_txt).reshape(-1)
     return (image_loss, image_grad, text_grad)
 

time: 35.2 us -> 44 us (1.25)
  waiting for transfers between devices: 6.56 us -> 15.8 us
  starting transfers between devices: 18.6 us -> 17.3 us
  local copies, waits for them, and re-layouts: 3.37 us -> 4.29 us
    ppermute x14 -> x13, waiting for transfers between devices: 6.56 us -> 15.8 us  [exchange(): return lax.ppermute(x, axis, [(i, i ^ k) for i in range(n)])]
    ppermute x14 -> x13, starting transfers between devices: 18.6 us -> 17.3 us  [exchange(): return lax.ppermute(x, axis, [(i, i ^ k) for i in range(n)])]
    slice x4 -> x9, local copies, waits for them, and re-layouts: 0.08 us -> 1.01 us  [the longest x5 0.93 us: per_device(): got[:term_tiles.shape[0]].reshape(rows // 8, width // 128, 8, 128)]
    unnamed x13 -> x14, local copies, waits for them, and re-layouts: 1.7 us -> 1.66 us
  transfers between devices with their start and end apart: 14 -> 13, of which waited for: 5 -> 7; matrix products, arithmetic and copies ran while one was open for 18% -> 9% of each run, Pallas kernels for 0% -> 0%
where the time goes in v5:
time: 44 us; the launch traced here: 43.8 us
  starting transfers between devices  17.3 us (39%)
  waiting for transfers between devices  15.8 us (36%)
  local copies, waits for them, and re-layouts  4.29 us (10%)
  matrix products  2.74 us (6%)
  between operations  2.21 us (5%)
  other arithmetic  1.45 us (3%)
    ppermute x13, starting transfers between devices, exchange(): return lax.ppermute(x, axis, [(i, i ^ k) for i in range(n)])  17.3 us
    ppermute x13, waiting for transfers between devices, exchange(): return lax.ppermute(x, axis, [(i, i ^ k) for i in range(n)])  15.8 us
    dot_general x7, matrix products, dot(): lax.dot_general(a, b, ((contract[:1], contract[1:]), ((), ())), precision...  2.74 us
    unnamed x14, local copies, waits for them, and re-layouts  1.66 us
    slice x5, local copies, waits for them, and re-layouts, per_device(): got[:term_tiles.shape[0]].reshape(rows // 8, width // 128, 8, 128)  0.93 us
  transfers between devices with their start and end apart: 13, of which 7 were waited for; matrix products, arithmetic and copies ran while one was open for 9% of the time, Pallas kernels for 0%

profile of v5, /device:TPU:0, one launch (start us, length us, event | category | flops | bytes accessed | tf_op | source)
XLA Modules:
  0.0 43.8 jit_solution(13821443050048353934)
XLA Ops:
  0.6 3.1 %collective-permute-start = (f32[32,768]{1,0:T(8,128)}, f32[32,768]{1,0:T(8,128)S(1)}, u32[]{:S(2)}, u32[]{:S(2)}) collective-permute-start(f32[32,768]{1,0:T(8,128)} %param.5), channel_id=1, source_target_pairs={{0,1},{1,0},{2,3},{3,2},{4,5},{5,4},{6,7},{7,6},{8,9},{9,8},{10,11... | collective-permute-start | bytes 294920 | tf_op jit(solution)/shard_map/ppermute | solution.py:8
  3.7 2.6 %collective-permute-start.1 = (f32[32,768]{1,0:T(8,128)}, f32[32,768]{1,0:T(8,128)S(1)}, u32[]{:S(2)}, u32[]{:S(2)}) collective-permute-start(f32[32,768]{1,0:T(8,128)} %param.5), channel_id=1, source_target_pairs={{0,2},{1,3},{2,0},{3,1},{4,6},{5,7},{6,4},{7,5},{8,10},{9,11},{10,... | collective-permute-start | bytes 294920 | tf_op jit(solution)/shard_map/ppermute | solution.py:8
  6.3 0.0 collective-permute-start.2
  6.3 1.7 %collective-permute-start.3 = (f32[32,768]{1,0:T(8,128)}, f32[32,768]{1,0:T(8,128)S(1)}, u32[]{:S(2)}, u32[]{:S(2)}) collective-permute-start(f32[32,768]{1,0:T(8,128)} %param.6), channel_id=1, source_target_pairs={{0,8},{4,12},{8,0},{12,4},{16,24},{20,28},{24,16},{28,20},{1,9},{5... | collective-permute-start | bytes 294920 | tf_op jit(solution)/shard_map/ppermute | solution.py:8
  8.0 0.9 %constant_dynamic-update-slice_fusion.11 = (f32[136,768]{1,0:T(8,128)S(1)}, f32[128,768]{1,0:T(8,128)S(1)}) fusion(f32[32,768]{1,0:T(8,128)} %param.5), kind=kLoop, calls=%fused_computation.66 | loop fusion | bytes 294912
  9.0 0.0 copy-start.3
  9.0 0.6 %copy-done.3 = s32[128]{0:T(128)S(1)} copy-done((s32[128]{0:T(128)S(1)}, s32[128]{0:T(128)}, u32[]{:S(2)}) %copy-start.3) | copy-done | bytes 536
  9.7 0.1 reshape_reshape.13
  9.8 0.1 convert_element_type.30
  11.2 0.1 eq.20
  11.4 1.6 %collective-permute-start.4 = (f32[64,768]{1,0:T(8,128)S(1)}, f32[64,768]{1,0:T(8,128)S(1)}, u32[]{:S(2)}, u32[]{:S(2)}) collective-permute-start(f32[64,768]{1,0:T(8,128)S(1)} %pad_maximum_fusion), channel_id=1, source_target_pairs={{0,16},{4,20},{8,24},{12,28},{16,0},{20,4},{24,8},{28,12},{1,17},{... | collective-permute-start | bytes 589832 | tf_op jit(solution)/shard_map/ppermute | solution.py:8
  13.0 0.0 collective-permute-done
  13.0 1.4 %collective-permute-done.1 = f32[32,768]{1,0:T(8,128)S(1)} collective-permute-done((f32[32,768]{1,0:T(8,128)}, f32[32,768]{1,0:T(8,128)S(1)}, u32[]{:S(2)}, u32[]{:S(2)}) %collective-permute-start.1) | collective-permute-done | bytes 98336 | tf_op jit(solution)/shard_map/ppermute | solution.py:8
  14.4 0.0 collective-permute-done.2
  14.4 0.1 collective-permute-start.9
  14.5 2.6 %collective-permute-done.4 = f32[64,768]{1,0:T(8,128)S(1)} collective-permute-done((f32[64,768]{1,0:T(8,128)S(1)}, f32[64,768]{1,0:T(8,128)S(1)}, u32[]{:S(2)}, u32[]{:S(2)}) %collective-permute-start.4) | collective-permute-done | bytes 196640 | tf_op jit(solution)/shard_map/ppermute | solution.py:8
  17.1 0.1 collective-permute-start.5
  17.2 0.4 add_reduce_fusion.1
  17.6 0.4 negate_select_fusion.1
  18.0 0.4 fusion.3
  18.3 0.4 convolution_add_fusion
  18.7 1.6 %collective-permute-start.10 = (f32[32,768]{1,0:T(8,128)S(1)}, f32[32,768]{1,0:T(8,128)S(1)}, u32[]{:S(2)}, u32[]{:S(2)}) collective-permute-start(f32[32,768]{1,0:T(8,128)S(1)} %get-tuple-element.7), channel_id=1, source_target_pairs={{0,8},{4,12},{8,0},{12,4},{16,24},{20,28},{24,16},{28,20},{1,9},{5... | collective-permute-start | bytes 294920 | tf_op jit(solution)/shard_map/ppermute | solution.py:8
  20.3 1.5 %collective-permute-start.11 = (f32[32,768]{1,0:T(8,128)S(1)}, f32[32,768]{1,0:T(8,128)S(1)}, u32[]{:S(2)}, u32[]{:S(2)}) collective-permute-start(f32[32,768]{1,0:T(8,128)S(1)} %get-tuple-element.9), channel_id=1, source_target_pairs={{0,16},{4,20},{8,24},{12,28},{16,0},{20,4},{24,8},{28,12},{1,17},{... | collective-permute-start | bytes 294920 | tf_op jit(solution)/shard_map/ppermute | solution.py:8
  21.8 0.5 %collective-permute-start.12 = (f32[32,768]{1,0:T(8,128)S(1)}, f32[32,768]{1,0:T(8,128)S(1)}, u32[]{:S(2)}, u32[]{:S(2)}) collective-permute-start(f32[32,768]{1,0:T(8,128)S(1)} %get-tuple-element.8), channel_id=1, source_target_pairs={{0,24},{4,28},{8,16},{12,20},{16,8},{20,12},{24,0},{28,4},{1,25},{... | collective-permute-start | bytes 294920 | tf_op jit(solution)/shard_map/ppermute | solution.py:8
  22.3 1.7 %collective-permute-done.10 = f32[32,768]{1,0:T(8,128)S(1)} collective-permute-done((f32[32,768]{1,0:T(8,128)S(1)}, f32[32,768]{1,0:T(8,128)S(1)}, u32[]{:S(2)}, u32[]{:S(2)}) %collective-permute-start.10) | collective-permute-done | bytes 98336 | tf_op jit(solution)/shard_map/ppermute | solution.py:8
  24.0 2.4 %collective-permute-done.11 = f32[32,768]{1,0:T(8,128)S(1)} collective-permute-done((f32[32,768]{1,0:T(8,128)S(1)}, f32[32,768]{1,0:T(8,128)S(1)}, u32[]{:S(2)}, u32[]{:S(2)}) %collective-permute-start.11) | collective-permute-done | bytes 98336 | tf_op jit(solution)/shard_map/ppermute | solution.py:8
  26.4 1.0 %collective-permute-done.12 = f32[32,768]{1,0:T(8,128)S(1)} collective-permute-done((f32[32,768]{1,0:T(8,128)S(1)}, f32[32,768]{1,0:T(8,128)S(1)}, u32[]{:S(2)}, u32[]{:S(2)}) %collective-permute-start.12) | collective-permute-done | bytes 98336 | tf_op jit(solution)/shard_map/ppermute | solution.py:8
  27.4 0.7 %fusion.7 = f32[32,768]{1,0:T(8,128)} fusion(f32[32,768]{1,0:T(8,128)S(1)} %collective-permute-done.12, f32[32,768]{1,0:T(8,128)S(1)} %collective-permute-done.11, f32[32,768]{1,0:T(8,128)S(1)} %collective-permute-done.10, f32[128,768]{1,0:T(8,128)S(1)} %convolution_add_fusion), kind=kLoop, calls=%fused_computation.17 | loop fusion | flops 73728 | bytes 491520 | tf_op jit(solution)/shard_map/add | solution.py:95
  28.0 0.4 add_reduce_fusion
  28.4 0.1 slice_bitcast_fusion.1
  28.5 0.1 add.192
  28.6 0.4 fusion.12
  29.0 0.4 convolution_add_fusion.1
  29.5 0.1 reshape.184
  29.6 0.7 %collective-permute-start.6 = (f32[25,8,128]{2,1,0:T(8,128)S(1)}, f32[25,8,128]{2,1,0:T(8,128)S(1)}, u32[]{:S(2)}, u32[]{:S(2)}) collective-permute-start(f32[25,8,128]{2,1,0:T(8,128)S(1)} %pad_maximum_fusion.1), channel_id=1, source_target_pairs={{0,1},{1,0},{2,3},{3,2},{4,5},{5,4},{6,7},{7,6},{8,9},{9,8},{10,11... | collective-permute-start | bytes 307208 | tf_op jit(solution)/shard_map/ppermute | solution.py:8
  30.4 0.1 reshape.189
  30.5 3.5 %collective-permute-start.7 = (f32[25,8,128]{2,1,0:T(8,128)S(1)}, f32[25,8,128]{2,1,0:T(8,128)S(1)}, u32[]{:S(2)}, u32[]{:S(2)}) collective-permute-start(f32[25,8,128]{2,1,0:T(8,128)S(1)} %pad_maximum_fusion.2), channel_id=1, source_target_pairs={{0,2},{1,3},{2,0},{3,1},{4,6},{5,7},{6,4},{7,5},{8,10},{9,11},{10,... | collective-permute-start | bytes 307208 | tf_op jit(solution)/shard_map/ppermute | solution.py:8
  34.0 0.1 reshape.194
  34.1 0.3 collective-permute-start.8
  34.4 0.7 %collective-permute-done.6 = f32[25,8,128]{2,1,0:T(8,128)S(1)} collective-permute-done((f32[25,8,128]{2,1,0:T(8,128)S(1)}, f32[25,8,128]{2,1,0:T(8,128)S(1)}, u32[]{:S(2)}, u32[]{:S(2)}) %collective-permute-start.6) | collective-permute-done | bytes 102432 | tf_op jit(solution)/shard_map/ppermute | solution.py:8
  35.1 0.1 reshape.186
  35.2 6.1 %collective-permute-done.7 = f32[25,8,128]{2,1,0:T(8,128)S(1)} collective-permute-done((f32[25,8,128]{2,1,0:T(8,128)S(1)}, f32[25,8,128]{2,1,0:T(8,128)S(1)}, u32[]{:S(2)}, u32[]{:S(2)}) %collective-permute-start.7) | collective-permute-done | bytes 102432 | tf_op jit(solution)/shard_map/ppermute | solution.py:8
  41.3 0.1 reshape.191
  41.4 0.1 reshape.196
  41.6 0.6 %reshape_reshape.16 = f32[128]{0:T(128)} reshape(f32[1,2,2,32]{3,2,1,0:T(2,128)S(1)} %reverse_select_fusion) | data formatting | bytes 1024 | tf_op jit(solution)/shard_map/reshape;reshape | solution.py:96
  42.2 0.9 %slice-done = f32[24,8,128]{2,1,0:T(8,128)S(1)} async-done(((f32[25,8,128]{2,1,0:T(8,128)}), f32[24,8,128]{2,1,0:T(8,128)S(1)}, s32[]{:S(2)}) %slice-start) | async-done | bytes 98328 | tf_op jit(solution)/shard_map/slice | solution.py:87
  43.1 0.0 slice-done.1
  43.1 0.7 %fusion.9 = f32[32,768]{1,0:T(8,128)} fusion(f32[32,768]{1,0:T(8,128)S(1)} %bitcast.68, f32[32,768]{1,0:T(8,128)S(1)} %bitcast.67, f32[32,768]{1,0:T(8,128)S(1)} %bitcast.66, f32[128,768]{1,0:T(8,128)S(1)} %convolution_add_fusion.1), kind=kLoop, calls=%fused_computation.20 | loop fusion | flops 73728 | bytes 491520 | tf_op jit(solution)/shard_map/add | solution.py:88
  (43 shorter events, 0.4 us)
Async XLA Ops:
  0.6 12.3 %collective-permute-start = (f32[32,768]{1,0:T(8,128)}, f32[32,768]{1,0:T(8,128)S(1)}, u32[]{:S(2)}, u32[]{:S(2)}) collective-permute-start(f32[32,768]{1,0:T(8,128)} %param.5), channel_id=1, source_target_pairs={{0,1},{1,0},{2,3},{3,2},{4,5},{5,4},{6,7},{7,6},{8,9},{9,8},{10,11... | collective-permute-start | bytes 294920 | tf_op jit(solution)/shard_map/ppermute | solution.py:8
  3.7 10.6 %collective-permute-start.1 = (f32[32,768]{1,0:T(8,128)}, f32[32,768]{1,0:T(8,128)S(1)}, u32[]{:S(2)}, u32[]{:S(2)}) collective-permute-start(f32[32,768]{1,0:T(8,128)} %param.5), channel_id=1, source_target_pairs={{0,2},{1,3},{2,0},{3,1},{4,6},{5,7},{6,4},{7,5},{8,10},{9,11},{10,... | collective-permute-start | bytes 294920 | tf_op jit(solution)/shard_map/ppermute | solution.py:8
  6.3 8.1 %collective-permute-start.2 = (f32[32,768]{1,0:T(8,128)}, f32[32,768]{1,0:T(8,128)S(1)}, u32[]{:S(2)}, u32[]{:S(2)}) collective-permute-start(f32[32,768]{1,0:T(8,128)} %param.5), channel_id=1, source_target_pairs={{0,3},{1,2},{2,1},{3,0},{4,7},{5,6},{6,5},{7,4},{8,11},{9,10},{10,... | collective-permute-start | bytes 294920 | tf_op jit(solution)/shard_map/ppermute | solution.py:8
  6.3 5.0 %collective-permute-start.3 = (f32[32,768]{1,0:T(8,128)}, f32[32,768]{1,0:T(8,128)S(1)}, u32[]{:S(2)}, u32[]{:S(2)}) collective-permute-start(f32[32,768]{1,0:T(8,128)} %param.6), channel_id=1, source_target_pairs={{0,8},{4,12},{8,0},{12,4},{16,24},{20,28},{24,16},{28,20},{1,9},{5... | collective-permute-start | bytes 294920 | tf_op jit(solution)/shard_map/ppermute | solution.py:8
  8.0 1.0 %copy-start = (f32[32,768]{1,0:T(8,128)S(1)}, f32[32,768]{1,0:T(8,128)}, u32[]{:S(2)}) copy-start(f32[32,768]{1,0:T(8,128)} %param.6) | copy-start | bytes 294916
  9.0 0.7 %copy-start.3 = (s32[128]{0:T(128)S(1)}, s32[128]{0:T(128)}, u32[]{:S(2)}) copy-start(s32[128]{0:T(128)} %param.7) | copy-start | bytes 1540
  11.4 5.7 %collective-permute-start.4 = (f32[64,768]{1,0:T(8,128)S(1)}, f32[64,768]{1,0:T(8,128)S(1)}, u32[]{:S(2)}, u32[]{:S(2)}) collective-permute-start(f32[64,768]{1,0:T(8,128)S(1)} %pad_maximum_fusion), channel_id=1, source_target_pairs={{0,16},{4,20},{8,24},{12,28},{16,0},{20,4},{24,8},{28,12},{1,17},{... | collective-permute-start | bytes 589832 | tf_op jit(solution)/shard_map/ppermute | solution.py:8
  14.4 3.2 %collective-permute-start.9 = (f32[136,768]{1,0:T(8,128)S(1)}, f32[136,768]{1,0:T(8,128)S(1)}, u32[]{:S(2)}, u32[]{:S(2)}) collective-permute-start(f32[136,768]{1,0:T(8,128)S(1)} %constant_dynamic-update-slice_fusion.7), channel_id=1, source_target_pairs={{0,4},{4,0},{8,12},{12,8},{16,20},{20,16},{24,28},{28,24},{1,5},{5... | collective-permute-start | bytes 1253384 | tf_op jit(solution)/shard_map/ppermute | solution.py:8
  17.1 10.9 %collective-permute-start.5 = (f32[128,768]{1,0:T(8,128)S(1)}, f32[128,768]{1,0:T(8,128)S(1)}, u32[]{:S(2)}, u32[]{:S(2)}) collective-permute-start(f32[128,768]{1,0:T(8,128)S(1)} %constant_dynamic-update-slice_fusion.4), channel_id=1, source_target_pairs={{0,4},{4,0},{8,12},{12,8},{16,20},{20,16},{24,28},{28,24},{1,5},{5... | collective-permute-start | bytes 1179656 | tf_op jit(solution)/shard_map/ppermute | solution.py:8
  18.7 5.3 %collective-permute-start.10 = (f32[32,768]{1,0:T(8,128)S(1)}, f32[32,768]{1,0:T(8,128)S(1)}, u32[]{:S(2)}, u32[]{:S(2)}) collective-permute-start(f32[32,768]{1,0:T(8,128)S(1)} %get-tuple-element.7), channel_id=1, source_target_pairs={{0,8},{4,12},{8,0},{12,4},{16,24},{20,28},{24,16},{28,20},{1,9},{5... | collective-permute-start | bytes 294920 | tf_op jit(solution)/shard_map/ppermute | solution.py:8
  20.3 6.1 %collective-permute-start.11 = (f32[32,768]{1,0:T(8,128)S(1)}, f32[32,768]{1,0:T(8,128)S(1)}, u32[]{:S(2)}, u32[]{:S(2)}) collective-permute-start(f32[32,768]{1,0:T(8,128)S(1)} %get-tuple-element.9), channel_id=1, source_target_pairs={{0,16},{4,20},{8,24},{12,28},{16,0},{20,4},{24,8},{28,12},{1,17},{... | collective-permute-start | bytes 294920 | tf_op jit(solution)/shard_map/ppermute | solution.py:8
  21.8 5.5 %collective-permute-start.12 = (f32[32,768]{1,0:T(8,128)S(1)}, f32[32,768]{1,0:T(8,128)S(1)}, u32[]{:S(2)}, u32[]{:S(2)}) collective-permute-start(f32[32,768]{1,0:T(8,128)S(1)} %get-tuple-element.8), channel_id=1, source_target_pairs={{0,24},{4,28},{8,16},{12,20},{16,8},{20,12},{24,0},{28,4},{1,25},{... | collective-permute-start | bytes 294920 | tf_op jit(solution)/shard_map/ppermute | solution.py:8
  29.6 5.5 %collective-permute-start.6 = (f32[25,8,128]{2,1,0:T(8,128)S(1)}, f32[25,8,128]{2,1,0:T(8,128)S(1)}, u32[]{:S(2)}, u32[]{:S(2)}) collective-permute-start(f32[25,8,128]{2,1,0:T(8,128)S(1)} %pad_maximum_fusion.1), channel_id=1, source_target_pairs={{0,1},{1,0},{2,3},{3,2},{4,5},{5,4},{6,7},{7,6},{8,9},{9,8},{10,11... | collective-permute-start | bytes 307208 | tf_op jit(solution)/shard_map/ppermute | solution.py:8
  30.5 10.8 %collective-permute-start.7 = (f32[25,8,128]{2,1,0:T(8,128)S(1)}, f32[25,8,128]{2,1,0:T(8,128)S(1)}, u32[]{:S(2)}, u32[]{:S(2)}) collective-permute-start(f32[25,8,128]{2,1,0:T(8,128)S(1)} %pad_maximum_fusion.2), channel_id=1, source_target_pairs={{0,2},{1,3},{2,0},{3,1},{4,6},{5,7},{6,4},{7,5},{8,10},{9,11},{10,... | collective-permute-start | bytes 307208 | tf_op jit(solution)/shard_map/ppermute | solution.py:8
  34.1 7.3 %collective-permute-start.8 = (f32[25,8,128]{2,1,0:T(8,128)S(1)}, f32[25,8,128]{2,1,0:T(8,128)S(1)}, u32[]{:S(2)}, u32[]{:S(2)}) collective-permute-start(f32[25,8,128]{2,1,0:T(8,128)S(1)} %pad_maximum_fusion.3), channel_id=1, source_target_pairs={{0,3},{1,2},{2,1},{3,0},{4,7},{5,6},{6,5},{7,4},{8,11},{9,10},{10,... | collective-permute-start | bytes 307208 | tf_op jit(solution)/shard_map/ppermute | solution.py:8
  35.1 7.0 %copy-start.1 = (f32[25,8,128]{2,1,0:T(8,128)}, f32[25,8,128]{2,1,0:T(8,128)S(1)}, u32[]{:S(2)}) copy-start(f32[25,8,128]{2,1,0:T(8,128)S(1)} %collective-permute-done.6) | copy-start | bytes 307204
  41.3 0.9 %copy-start.2 = (f32[25,8,128]{2,1,0:T(8,128)}, f32[25,8,128]{2,1,0:T(8,128)S(1)}, u32[]{:S(2)}) copy-start(f32[25,8,128]{2,1,0:T(8,128)S(1)} %collective-permute-done.7) | copy-start | bytes 307204
  42.2 0.9 %slice-start = ((f32[25,8,128]{2,1,0:T(8,128)}), f32[24,8,128]{2,1,0:T(8,128)S(1)}, s32[]{:S(2)}) async-start(f32[25,8,128]{2,1,0:T(8,128)} %copy-done.1), calls=%async_computation | async-start | bytes 196608 | tf_op jit(solution)/shard_map/slice | solution.py:87
  42.2 0.9 %slice-start.1 = ((f32[25,8,128]{2,1,0:T(8,128)}), f32[24,8,128]{2,1,0:T(8,128)S(1)}, s32[]{:S(2)}) async-start(f32[25,8,128]{2,1,0:T(8,128)} %copy-done.2), calls=%async_computation.1 | async-start | bytes 196608 | tf_op jit(solution)/shard_map/slice | solution.py:87

commit v6 on v5

--- a/solution.py
+++ b/solution.py
@@ -77,13 +77,17 @@
 
     image_term = dot(d_near, near, (1, 0)) + dot(d_far, far, (1, 0))
     loss_part = (loss_near + loss_far).reshape(n_txt, rows)
-    image_grad, loss_sum = image_term[:rows], loss_part
+    messages = {}
     for k in range(1, n_txt):
         loss_tile = jnp.stack([loss_part[k ^ m] for m in range(n_txt)]).reshape(-1, 128)
         loss_tile = jnp.pad(loss_tile, ((0, -loss_tile.shape[0] % 8), (0, 0))).reshape(-1, 8, 128)
         term_tiles = image_term[k * rows:(k + 1) * rows].reshape(rows // 8, 8, width // 128, 128)
         term_tiles = jnp.swapaxes(term_tiles, 1, 2).reshape(-1, 8, 128)
-        got = exchange(jnp.concatenate([term_tiles, loss_tile]), "txt", n_txt, k)
+        messages[k] = jnp.concatenate([term_tiles, loss_tile])
+    pair_images, messages = lax.optimization_barrier((pair_images, messages))
+    image_grad, loss_sum = image_term[:rows], loss_part
+    for k in range(1, n_txt):
+        got = exchange(messages[k], "txt", n_txt, k)
         got_tiles = got[:term_tiles.shape[0]].reshape(rows // 8, width // 128, 8, 128)
         image_grad = image_grad + jnp.swapaxes(got_tiles, 1, 2).reshape(rows, width)
         loss_sum = loss_sum + got[term_tiles.shape[0]:].reshape(-1)[:count].reshape(n_txt, rows)

time: 44 us -> 39.8 us (0.905)
  waiting for transfers between devices: 15.8 us -> 11.3 us
    ppermute x13, waiting for transfers between devices: 15.8 us -> 11.3 us  [exchange(): return lax.ppermute(x, axis, [(i, i ^ k) for i in range(n)])]
    unnamed x14 -> x13, local copies, waits for them, and re-layouts: 1.66 us -> 1.65 us
  transfers between devices with their start and end apart: 13 -> 13, of which waited for: 7 -> 6; matrix products, arithmetic and copies ran while one was open for 9% -> 7% of each run, Pallas kernels for 0% -> 0%
where the time goes in v6:
time: 39.8 us; the launch traced here: 39.6 us
  starting transfers between devices  17.6 us (44%)
  waiting for transfers between devices  11.3 us (28%)
  local copies, waits for them, and re-layouts  4.32 us (11%)
  matrix products  2.73 us (7%)
  between operations  2.23 us (6%)
  other arithmetic  1.45 us (4%)
    ppermute x13, starting transfers between devices, exchange(): return lax.ppermute(x, axis, [(i, i ^ k) for i in range(n)])  17.6 us
    ppermute x13, waiting for transfers between devices, exchange(): return lax.ppermute(x, axis, [(i, i ^ k) for i in range(n)])  11.3 us
    dot_general x7, matrix products, dot(): lax.dot_general(a, b, ((contract[:1], contract[1:]), ((), ())), precision...  2.73 us
    unnamed x13, local copies, waits for them, and re-layouts  1.65 us
    slice x5, local copies, waits for them, and re-layouts, per_device(): got[:term_tiles.shape[0]].reshape(rows // 8, width // 128, 8, 128)  0.93 us
  transfers between devices with their start and end apart: 13, of which 6 were waited for; matrix products, arithmetic and copies ran while one was open for 7% of the time, Pallas kernels for 0%

profile of v6, /device:TPU:0, one launch (start us, length us, event | category | flops | bytes accessed | tf_op | source)
XLA Modules:
  0.0 39.6 jit_solution(18267945741781451389)
XLA Ops:
  0.6 3.1 %collective-permute-start = (f32[32,768]{1,0:T(8,128)}, f32[32,768]{1,0:T(8,128)S(1)}, u32[]{:S(2)}, u32[]{:S(2)}) collective-permute-start(f32[32,768]{1,0:T(8,128)} %param.5), channel_id=1, source_target_pairs={{0,1},{1,0},{2,3},{3,2},{4,5},{5,4},{6,7},{7,6},{8,9},{9,8},{10,11... | collective-permute-start | bytes 294920 | tf_op jit(solution)/shard_map/ppermute | solution.py:8
  3.7 2.6 %collective-permute-start.1 = (f32[32,768]{1,0:T(8,128)}, f32[32,768]{1,0:T(8,128)S(1)}, u32[]{:S(2)}, u32[]{:S(2)}) collective-permute-start(f32[32,768]{1,0:T(8,128)} %param.5), channel_id=1, source_target_pairs={{0,2},{1,3},{2,0},{3,1},{4,6},{5,7},{6,4},{7,5},{8,10},{9,11},{10,... | collective-permute-start | bytes 294920 | tf_op jit(solution)/shard_map/ppermute | solution.py:8
  6.3 1.7 %collective-permute-start.3 = (f32[32,768]{1,0:T(8,128)}, f32[32,768]{1,0:T(8,128)S(1)}, u32[]{:S(2)}, u32[]{:S(2)}) collective-permute-start(f32[32,768]{1,0:T(8,128)} %param.6), channel_id=1, source_target_pairs={{0,8},{4,12},{8,0},{12,4},{16,24},{20,28},{24,16},{28,20},{1,9},{5... | collective-permute-start | bytes 294920 | tf_op jit(solution)/shard_map/ppermute | solution.py:8
  8.0 0.9 %constant_dynamic-update-slice_fusion.3 = (f32[128,768]{1,0:T(8,128)S(1)}, f32[136,768]{1,0:T(8,128)S(1)}) fusion(f32[32,768]{1,0:T(8,128)} %param.5), kind=kLoop, calls=%fused_computation.56 | loop fusion | bytes 294912
  9.0 0.0 copy-start.3
  9.0 0.6 %copy-done.3 = s32[128]{0:T(128)S(1)} copy-done((s32[128]{0:T(128)S(1)}, s32[128]{0:T(128)}, u32[]{:S(2)}) %copy-start.3) | copy-done | bytes 536
  9.7 0.1 reshape_reshape.13
  9.8 0.1 eq.20
  11.2 0.1 convert_element_type.30
  11.3 0.0 collective-permute-done.3
  11.4 1.6 %collective-permute-start.4 = (f32[64,768]{1,0:T(8,128)S(1)}, f32[64,768]{1,0:T(8,128)S(1)}, u32[]{:S(2)}, u32[]{:S(2)}) collective-permute-start(f32[64,768]{1,0:T(8,128)S(1)} %pad_maximum_fusion), channel_id=1, source_target_pairs={{0,16},{4,20},{8,24},{12,28},{16,0},{20,4},{24,8},{28,12},{1,17},{... | collective-permute-start | bytes 589832 | tf_op jit(solution)/shard_map/ppermute | solution.py:8
  13.0 0.0 collective-permute-done
  13.0 1.4 %collective-permute-done.1 = f32[32,768]{1,0:T(8,128)S(1)} collective-permute-done((f32[32,768]{1,0:T(8,128)}, f32[32,768]{1,0:T(8,128)S(1)}, u32[]{:S(2)}, u32[]{:S(2)}) %collective-permute-start.1) | collective-permute-done | bytes 98336 | tf_op jit(solution)/shard_map/ppermute | solution.py:8
  14.4 0.0 collective-permute-done.2
  14.4 0.1 collective-permute-start.6
  14.5 2.6 %collective-permute-done.4 = f32[64,768]{1,0:T(8,128)S(1)} collective-permute-done((f32[64,768]{1,0:T(8,128)S(1)}, f32[64,768]{1,0:T(8,128)S(1)}, u32[]{:S(2)}, u32[]{:S(2)}) %collective-permute-start.4) | collective-permute-done | bytes 196640 | tf_op jit(solution)/shard_map/ppermute | solution.py:8
  17.1 0.1 collective-permute-start.5
  17.2 0.4 add_reduce_fusion.1
  17.6 1.3 %collective-permute-done.5 = f32[128,768]{1,0:T(8,128)S(1)} collective-permute-done((f32[128,768]{1,0:T(8,128)S(1)}, f32[128,768]{1,0:T(8,128)S(1)}, u32[]{:S(2)}, u32[]{:S(2)}) %collective-permute-start.5) | collective-permute-done | bytes 393248 | tf_op jit(solution)/shard_map/ppermute | solution.py:8
  18.9 0.4 add_reduce_fusion
  19.3 0.4 %fusion.7 = f32[128,768]{1,0:T(8,128)S(1)} fusion(f32[128,768]{1,0:T(8,128)S(1)} %collective-permute-done.5, f32[128,128]{0,1:T(8,128)S(1)} %get-tuple-element.39, f32[]{:T(128)} %bitcast.1, s32[128]{0:T(128)S(1)} %eq.20, s32[128]{0:T(128)S(1)} %get-tuple-element.11), kind=kOutput, calls=%fused_computation.24 | convolution fusion | flops 75661312 | bytes 852996 | tf_op jit(solution)/shard_map/dot_general | solution.py:23
  19.7 0.4 %convolution_add_fusion.1 = f32[128,768]{1,0:T(8,128)S(1)} fusion(f32[128,768]{1,0:T(8,128)S(1)} %fusion.7, f32[128,768]{1,0:T(8,128)S(1)} %constant_dynamic-update-slice_fusion.4, f32[128,128]{0,1:T(8,128)S(1)} %get-tuple-element.37, f32[]{:T(128)} %bitcast.1, s32[128]{0:T(128)S(1)} %eq.20, s32[128]{0:T(128)S(1)} %get-tuple-element.12), kind=kOutput, calls=%fused_computation.1 | convolution fusion | flops 75759616 | bytes 1246212 | tf_op jit(solution)/shard_map/dot_general | solution.py:23
  20.2 0.1 slice_bitcast_fusion.3
  20.3 0.1 reshape.192
  20.4 0.1 reshape.188
  20.5 0.1 reshape.184
  20.6 0.4 negate_select_fusion.1
  21.0 0.4 fusion.8
  21.3 0.4 convolution_add_fusion
  21.7 1.6 %collective-permute-start.10 = (f32[32,768]{1,0:T(8,128)S(1)}, f32[32,768]{1,0:T(8,128)S(1)}, u32[]{:S(2)}, u32[]{:S(2)}) collective-permute-start(f32[32,768]{1,0:T(8,128)S(1)} %get-tuple-element.15), channel_id=1, source_target_pairs={{0,8},{4,12},{8,0},{12,4},{16,24},{20,28},{24,16},{28,20},{1,9},{5... | collective-permute-start | bytes 294920 | tf_op jit(solution)/shard_map/ppermute | solution.py:8
  23.3 1.5 %collective-permute-start.11 = (f32[32,768]{1,0:T(8,128)S(1)}, f32[32,768]{1,0:T(8,128)S(1)}, u32[]{:S(2)}, u32[]{:S(2)}) collective-permute-start(f32[32,768]{1,0:T(8,128)S(1)} %get-tuple-element.17), channel_id=1, source_target_pairs={{0,16},{4,20},{8,24},{12,28},{16,0},{20,4},{24,8},{28,12},{1,17},{... | collective-permute-start | bytes 294920 | tf_op jit(solution)/shard_map/ppermute | solution.py:8
  24.8 0.5 %collective-permute-start.12 = (f32[32,768]{1,0:T(8,128)S(1)}, f32[32,768]{1,0:T(8,128)S(1)}, u32[]{:S(2)}, u32[]{:S(2)}) collective-permute-start(f32[32,768]{1,0:T(8,128)S(1)} %get-tuple-element.16), channel_id=1, source_target_pairs={{0,24},{4,28},{8,16},{12,20},{16,8},{20,12},{24,0},{28,4},{1,25},{... | collective-permute-start | bytes 294920 | tf_op jit(solution)/shard_map/ppermute | solution.py:8
  25.3 0.1 add.192
  25.4 0.7 %collective-permute-start.7 = (f32[25,8,128]{2,1,0:T(8,128)S(1)}, f32[25,8,128]{2,1,0:T(8,128)S(1)}, u32[]{:S(2)}, u32[]{:S(2)}) collective-permute-start(f32[25,8,128]{2,1,0:T(8,128)S(1)} %get-tuple-element.7), channel_id=1, source_target_pairs={{0,1},{1,0},{2,3},{3,2},{4,5},{5,4},{6,7},{7,6},{8,9},{9,8},{10,11... | collective-permute-start | bytes 307208 | tf_op jit(solution)/shard_map/ppermute | solution.py:8
  26.1 3.5 %collective-permute-start.8 = (f32[25,8,128]{2,1,0:T(8,128)S(1)}, f32[25,8,128]{2,1,0:T(8,128)S(1)}, u32[]{:S(2)}, u32[]{:S(2)}) collective-permute-start(f32[25,8,128]{2,1,0:T(8,128)S(1)} %get-tuple-element.8), channel_id=1, source_target_pairs={{0,2},{1,3},{2,0},{3,1},{4,6},{5,7},{6,4},{7,5},{8,10},{9,11},{10,... | collective-permute-start | bytes 307208 | tf_op jit(solution)/shard_map/ppermute | solution.py:8
  29.6 0.0 collective-permute-done.10
  29.6 0.7 %collective-permute-start.9 = (f32[25,8,128]{2,1,0:T(8,128)S(1)}, f32[25,8,128]{2,1,0:T(8,128)S(1)}, u32[]{:S(2)}, u32[]{:S(2)}) collective-permute-start(f32[25,8,128]{2,1,0:T(8,128)S(1)} %pad_maximum_fusion.3), channel_id=1, source_target_pairs={{0,3},{1,2},{2,1},{3,0},{4,7},{5,6},{6,5},{7,4},{8,11},{9,10},{10,... | collective-permute-start | bytes 307208 | tf_op jit(solution)/shard_map/ppermute | solution.py:8
  30.3 0.1 collective-permute-done.12
  30.3 0.7 %fusion.4 = f32[32,768]{1,0:T(8,128)} fusion(f32[32,768]{1,0:T(8,128)S(1)} %collective-permute-done.12, f32[32,768]{1,0:T(8,128)S(1)} %collective-permute-done.11, f32[32,768]{1,0:T(8,128)S(1)} %collective-permute-done.10, f32[128,768]{1,0:T(8,128)S(1)} %convolution_add_fusion), kind=kLoop, calls=%fused_computation.14 | loop fusion | flops 73728 | bytes 491520 | tf_op jit(solution)/shard_map/add | solution.py:99
  31.0 0.1 collective-permute-done.7
  31.1 0.1 reshape.194
  31.2 5.9 %collective-permute-done.8 = f32[25,8,128]{2,1,0:T(8,128)S(1)} collective-permute-done((f32[25,8,128]{2,1,0:T(8,128)S(1)}, f32[25,8,128]{2,1,0:T(8,128)S(1)}, u32[]{:S(2)}, u32[]{:S(2)}) %collective-permute-start.8) | collective-permute-done | bytes 102432 | tf_op jit(solution)/shard_map/ppermute | solution.py:8
  37.1 0.1 reshape.195
  37.2 0.1 reshape.196
  37.4 0.6 %reshape_reshape.16 = f32[128]{0:T(128)} reshape(f32[1,2,2,32]{3,2,1,0:T(2,128)S(1)} %reverse_select_fusion) | data formatting | bytes 1024 | tf_op jit(solution)/shard_map/reshape;reshape | solution.py:100
  38.0 0.9 %slice-done = f32[24,8,128]{2,1,0:T(8,128)S(1)} async-done(((f32[25,8,128]{2,1,0:T(8,128)}), f32[24,8,128]{2,1,0:T(8,128)S(1)}, s32[]{:S(2)}) %slice-start) | async-done | bytes 98328 | tf_op jit(solution)/shard_map/slice | solution.py:91
  38.9 0.0 slice-done.1
  38.9 0.7 %fusion.6 = f32[32,768]{1,0:T(8,128)} fusion(f32[32,768]{1,0:T(8,128)S(1)} %bitcast.70, f32[32,768]{1,0:T(8,128)S(1)} %bitcast.69, f32[32,768]{1,0:T(8,128)S(1)} %bitcast.68, f32[128,768]{1,0:T(8,128)S(1)} %convolution_add_fusion.1), kind=kLoop, calls=%fused_computation.17 | loop fusion | flops 73728 | bytes 491520 | tf_op jit(solution)/shard_map/add | solution.py:92
  (43 shorter events, 0.4 us)
Async XLA Ops:
  0.6 12.3 %collective-permute-start = (f32[32,768]{1,0:T(8,128)}, f32[32,768]{1,0:T(8,128)S(1)}, u32[]{:S(2)}, u32[]{:S(2)}) collective-permute-start(f32[32,768]{1,0:T(8,128)} %param.5), channel_id=1, source_target_pairs={{0,1},{1,0},{2,3},{3,2},{4,5},{5,4},{6,7},{7,6},{8,9},{9,8},{10,11... | collective-permute-start | bytes 294920 | tf_op jit(solution)/shard_map/ppermute | solution.py:8
  3.7 10.6 %collective-permute-start.1 = (f32[32,768]{1,0:T(8,128)}, f32[32,768]{1,0:T(8,128)S(1)}, u32[]{:S(2)}, u32[]{:S(2)}) collective-permute-start(f32[32,768]{1,0:T(8,128)} %param.5), channel_id=1, source_target_pairs={{0,2},{1,3},{2,0},{3,1},{4,6},{5,7},{6,4},{7,5},{8,10},{9,11},{10,... | collective-permute-start | bytes 294920 | tf_op jit(solution)/shard_map/ppermute | solution.py:8
  6.3 8.1 %collective-permute-start.2 = (f32[32,768]{1,0:T(8,128)}, f32[32,768]{1,0:T(8,128)S(1)}, u32[]{:S(2)}, u32[]{:S(2)}) collective-permute-start(f32[32,768]{1,0:T(8,128)} %param.5), channel_id=1, source_target_pairs={{0,3},{1,2},{2,1},{3,0},{4,7},{5,6},{6,5},{7,4},{8,11},{9,10},{10,... | collective-permute-start | bytes 294920 | tf_op jit(solution)/shard_map/ppermute | solution.py:8
  6.3 5.0 %collective-permute-start.3 = (f32[32,768]{1,0:T(8,128)}, f32[32,768]{1,0:T(8,128)S(1)}, u32[]{:S(2)}, u32[]{:S(2)}) collective-permute-start(f32[32,768]{1,0:T(8,128)} %param.6), channel_id=1, source_target_pairs={{0,8},{4,12},{8,0},{12,4},{16,24},{20,28},{24,16},{28,20},{1,9},{5... | collective-permute-start | bytes 294920 | tf_op jit(solution)/shard_map/ppermute | solution.py:8
  8.0 1.0 %copy-start = (f32[32,768]{1,0:T(8,128)S(1)}, f32[32,768]{1,0:T(8,128)}, u32[]{:S(2)}) copy-start(f32[32,768]{1,0:T(8,128)} %param.6) | copy-start | bytes 294916
  9.0 0.7 %copy-start.3 = (s32[128]{0:T(128)S(1)}, s32[128]{0:T(128)}, u32[]{:S(2)}) copy-start(s32[128]{0:T(128)} %param.7) | copy-start | bytes 1540
  11.4 5.7 %collective-permute-start.4 = (f32[64,768]{1,0:T(8,128)S(1)}, f32[64,768]{1,0:T(8,128)S(1)}, u32[]{:S(2)}, u32[]{:S(2)}) collective-permute-start(f32[64,768]{1,0:T(8,128)S(1)} %pad_maximum_fusion), channel_id=1, source_target_pairs={{0,16},{4,20},{8,24},{12,28},{16,0},{20,4},{24,8},{28,12},{1,17},{... | collective-permute-start | bytes 589832 | tf_op jit(solution)/shard_map/ppermute | solution.py:8
  14.4 3.1 %collective-permute-start.6 = (f32[136,768]{1,0:T(8,128)S(1)}, f32[136,768]{1,0:T(8,128)S(1)}, u32[]{:S(2)}, u32[]{:S(2)}) collective-permute-start(f32[136,768]{1,0:T(8,128)S(1)} %constant_dynamic-update-slice_fusion.7), channel_id=1, source_target_pairs={{0,4},{4,0},{8,12},{12,8},{16,20},{20,16},{24,28},{28,24},{1,5},{5... | collective-permute-start | bytes 1253384 | tf_op jit(solution)/shard_map/ppermute | solution.py:8
  17.1 1.8 %collective-permute-start.5 = (f32[128,768]{1,0:T(8,128)S(1)}, f32[128,768]{1,0:T(8,128)S(1)}, u32[]{:S(2)}, u32[]{:S(2)}) collective-permute-start(f32[128,768]{1,0:T(8,128)S(1)} %constant_dynamic-update-slice_fusion.4), channel_id=1, source_target_pairs={{0,4},{4,0},{8,12},{12,8},{16,20},{20,16},{24,28},{28,24},{1,5},{5... | collective-permute-start | bytes 1179656 | tf_op jit(solution)/shard_map/ppermute | solution.py:8
  21.7 7.8 %collective-permute-start.10 = (f32[32,768]{1,0:T(8,128)S(1)}, f32[32,768]{1,0:T(8,128)S(1)}, u32[]{:S(2)}, u32[]{:S(2)}) collective-permute-start(f32[32,768]{1,0:T(8,128)S(1)} %get-tuple-element.15), channel_id=1, source_target_pairs={{0,8},{4,12},{8,0},{12,4},{16,24},{20,28},{24,16},{28,20},{1,9},{5... | collective-permute-start | bytes 294920 | tf_op jit(solution)/shard_map/ppermute | solution.py:8
  23.3 7.0 %collective-permute-start.11 = (f32[32,768]{1,0:T(8,128)S(1)}, f32[32,768]{1,0:T(8,128)S(1)}, u32[]{:S(2)}, u32[]{:S(2)}) collective-permute-start(f32[32,768]{1,0:T(8,128)S(1)} %get-tuple-element.17), channel_id=1, source_target_pairs={{0,16},{4,20},{8,24},{12,28},{16,0},{20,4},{24,8},{28,12},{1,17},{... | collective-permute-start | bytes 294920 | tf_op jit(solution)/shard_map/ppermute | solution.py:8
  24.8 5.5 %collective-permute-start.12 = (f32[32,768]{1,0:T(8,128)S(1)}, f32[32,768]{1,0:T(8,128)S(1)}, u32[]{:S(2)}, u32[]{:S(2)}) collective-permute-start(f32[32,768]{1,0:T(8,128)S(1)} %get-tuple-element.16), channel_id=1, source_target_pairs={{0,24},{4,28},{8,16},{12,20},{16,8},{20,12},{24,0},{28,4},{1,25},{... | collective-permute-start | bytes 294920 | tf_op jit(solution)/shard_map/ppermute | solution.py:8
  25.4 5.7 %collective-permute-start.7 = (f32[25,8,128]{2,1,0:T(8,128)S(1)}, f32[25,8,128]{2,1,0:T(8,128)S(1)}, u32[]{:S(2)}, u32[]{:S(2)}) collective-permute-start(f32[25,8,128]{2,1,0:T(8,128)S(1)} %get-tuple-element.7), channel_id=1, source_target_pairs={{0,1},{1,0},{2,3},{3,2},{4,5},{5,4},{6,7},{7,6},{8,9},{9,8},{10,11... | collective-permute-start | bytes 307208 | tf_op jit(solution)/shard_map/ppermute | solution.py:8
  26.1 11.0 %collective-permute-start.8 = (f32[25,8,128]{2,1,0:T(8,128)S(1)}, f32[25,8,128]{2,1,0:T(8,128)S(1)}, u32[]{:S(2)}, u32[]{:S(2)}) collective-permute-start(f32[25,8,128]{2,1,0:T(8,128)S(1)} %get-tuple-element.8), channel_id=1, source_target_pairs={{0,2},{1,3},{2,0},{3,1},{4,6},{5,7},{6,4},{7,5},{8,10},{9,11},{10,... | collective-permute-start | bytes 307208 | tf_op jit(solution)/shard_map/ppermute | solution.py:8
  29.6 7.7 %collective-permute-start.9 = (f32[25,8,128]{2,1,0:T(8,128)S(1)}, f32[25,8,128]{2,1,0:T(8,128)S(1)}, u32[]{:S(2)}, u32[]{:S(2)}) collective-permute-start(f32[25,8,128]{2,1,0:T(8,128)S(1)} %pad_maximum_fusion.3), channel_id=1, source_target_pairs={{0,3},{1,2},{2,1},{3,0},{4,7},{5,6},{6,5},{7,4},{8,11},{9,10},{10,... | collective-permute-start | bytes 307208 | tf_op jit(solution)/shard_map/ppermute | solution.py:8
  31.1 6.9 %copy-start.1 = (f32[25,8,128]{2,1,0:T(8,128)}, f32[25,8,128]{2,1,0:T(8,128)S(1)}, u32[]{:S(2)}) copy-start(f32[25,8,128]{2,1,0:T(8,128)S(1)} %collective-permute-done.7) | copy-start | bytes 307204
  37.1 0.9 %copy-start.2 = (f32[25,8,128]{2,1,0:T(8,128)}, f32[25,8,128]{2,1,0:T(8,128)S(1)}, u32[]{:S(2)}) copy-start(f32[25,8,128]{2,1,0:T(8,128)S(1)} %collective-permute-done.8) | copy-start | bytes 307204
  38.0 0.9 %slice-start = ((f32[25,8,128]{2,1,0:T(8,128)}), f32[24,8,128]{2,1,0:T(8,128)S(1)}, s32[]{:S(2)}) async-start(f32[25,8,128]{2,1,0:T(8,128)} %copy-done.1), calls=%async_computation | async-start | bytes 196608 | tf_op jit(solution)/shard_map/slice | solution.py:91
  38.0 0.9 %slice-start.1 = ((f32[25,8,128]{2,1,0:T(8,128)}), f32[24,8,128]{2,1,0:T(8,128)S(1)}, s32[]{:S(2)}) async-start(f32[25,8,128]{2,1,0:T(8,128)} %copy-done.2), calls=%async_computation.1 | async-start | bytes 196608 | tf_op jit(solution)/shard_map/slice | solution.py:91

commit v7 on v0

--- a/solution.py
+++ b/solution.py
@@ -1,10 +1,196 @@
+import functools
+
 import jax
 import jax.numpy as jnp
 from jax import lax
+from jax.experimental import pallas as pl
+from jax.experimental.pallas import tpu as pltpu
 from jax.sharding import PartitionSpec as P
 
-
-def per_device(image_emb, text_emb, pairs, log_scale, bias):
+LANES = 128
+
+
+def exchange(x, axis, n, k):
+    return lax.ppermute(x, axis, [(i, i ^ k) for i in range(n)])
+
+
+def halves(x):
+    high = x.astype(jnp.bfloat16)
+    return high, (x - high.astype(jnp.float32)).astype(jnp.bfloat16)
+
+
+def dot(a, b, contract):
+    def part(x, y):
+        dims = ((contract[:1], contract[1:]), ((), ()))
+        return lax.dot_general(x, y, dims, preferred_element_type=jnp.float32)
+
+    return part(a[0], b[0]) + (part(a[0], b[1]) + part(a[1], b[0]))
+
+
+def untwist(row, block, me):
+    lane = lax.broadcasted_iota(jnp.int32, row.shape, 1)
+    step = block
+    while step < LANES:
+        up, down = pltpu.roll(row, LANES - step, 1), pltpu.roll(row, step, 1)
+        flipped = jnp.where((lane // step) % 2 == 0, up, down)
+        row = jnp.where((me // (step // block)) % 2 == 1, flipped, row)
+        step *= 2
+    return row
+
+
+def text_ids(shape, n_img, cols, far):
+    me_img, me_txt = lax.axis_index("img"), lax.axis_index("txt")
+    place = lax.broadcasted_iota(jnp.int32, shape, 0)
+    half = n_img // 2 * cols
+    core = me_img % 2
+    if far:
+        core = core ^ (place // half)
+        place = place % half
+    chip = (me_img // 2) ^ (place // cols)
+    return (me_txt * n_img + 2 * chip + core) * cols + place % cols
+
+
+def derivative(texts, images, ids, matched, scale, shift):
+    logits = scale * dot(texts, images, (1, 1)) + shift
+    match = ids == matched
+    v = jnp.where(match, -logits, logits)
+    e = jnp.exp(-jnp.abs(v))
+    loss = jnp.maximum(v, 0.0) + jnp.log1p(e)
+    s = scale * jnp.where(v >= 0, 1.0, e) / (1.0 + e)
+    return loss, jnp.where(match, -s, s)
+
+
+def image_kernel(n_img, n_txt, rows, cols, *refs):
+    log_scale, bias, bundle, near, far, own_ref, loss_ref, d_ref = refs[:8]
+    message_refs = refs[8:]
+    count = n_txt * rows
+    me_txt = lax.axis_index("txt")
+    scale = jnp.exp(jnp.full((1, LANES), log_scale[0], jnp.float32))
+    images = halves(bundle[:count])
+    texts = halves(jnp.concatenate([near[...], far[...]]))
+    matched = untwist(bundle[count:count + 1, :LANES], rows, me_txt).astype(jnp.int32)
+    ids = text_ids((texts[0].shape[0], count), n_img, cols, True)
+    loss, d = derivative(texts, images, ids, matched, scale, bias[0])
+    d_ref[...] = d[:near.shape[0]]
+    term = dot(halves(d), texts, (0, 0))
+    own_ref[...] = term[:rows]
+    loss_row = untwist(jnp.sum(loss, axis=0, keepdims=True), rows, me_txt)
+    loss_tile = jnp.broadcast_to(loss_row, (8, LANES))
+    loss_ref[...] = loss_tile
+    across = term.shape[1] // LANES
+    for k, ref in enumerate(message_refs, 1):
+        for r in range(rows // 8):
+            for c in range(across):
+                ref[r * across + c] = term[
+                    k * rows + r * 8:k * rows + r * 8 + 8, c * LANES:(c + 1) * LANES
+                ]
+        ref[rows // 8 * across] = loss_tile
+
+
+def text_kernel(n_img, n_txt, rows, cols, *refs):
+    log_scale, bias, bundle, pair, near, d_ref = refs[:6]
+    block_refs = refs[6:]
+    count = n_txt * rows
+    scale = jnp.exp(jnp.full((1, LANES), log_scale[0], jnp.float32))
+    others = halves(pair[:count])
+    texts = halves(near[...])
+    matched = untwist(pair[count:count + 1, :LANES], rows, lax.axis_index("txt")).astype(jnp.int32)
+    ids = text_ids((texts[0].shape[0], count), n_img, cols, False)
+    _, d = derivative(texts, others, ids, matched, scale, bias[0])
+    term = dot(halves(d_ref[...]), halves(bundle[:count]), (1, 0)) + dot(halves(d), others, (1, 0))
+    for k, ref in enumerate(block_refs):
+        ref[...] = term[k * cols:(k + 1) * cols]
+
+
+def image_sum_kernel(n_txt, own_ref, loss_ref, *refs):
+    messages, (image_loss, image_grad) = refs[:n_txt - 1], refs[n_txt - 1:]
+    rows, width = own_ref.shape
+    across = width // LANES
+    for r in range(rows // 8):
+        for c in range(across):
+            at = (slice(r * 8, r * 8 + 8), slice(c * LANES, (c + 1) * LANES))
+            image_grad[at] = own_ref[at] + sum(m[r * across + c] for m in messages)
+    image_loss[...] = (loss_ref[...] + sum(m[rows // 8 * across] for m in messages))[:1]
+
+
+def text_sum_kernel(_, *refs):
+    blocks, text_grad = refs[:-1], refs[-1]
+    text_grad[...] = sum(b[...] for b in blocks)
+
+
+def in_vmem(*arrays):
+    return [pltpu.with_memory_space_constraint(x, pltpu.VMEM) for x in arrays]
+
+
+def vmem(shape):
+    return pltpu.VMEM(shape, jnp.float32)
+
+
+def per_device(sizes, image_emb, text_emb, pairs, log_scale, bias):
+    n_img, n_txt = sizes
+    chips = n_img // 2
+    rows, cols, width = image_emb.shape[0], text_emb.shape[0], image_emb.shape[1]
+    count = n_txt * rows
+    tiles = rows * width // (8 * LANES)
+    smem, whole = pl.BlockSpec(memory_space=pltpu.SMEM), pl.BlockSpec(memory_space=pltpu.VMEM)
+
+    near = text_emb
+    image_blocks = {0: image_emb}
+    order = [k for k in range(2, n_txt)] + [1]
+    step = 1
+    while step < chips:
+        near = jnp.concatenate([near, exchange(near, "img", n_img, 2 * step)])
+        for k in order[:2]:
+            image_blocks[k] = exchange(image_emb, "txt", n_txt, k)
+        order = order[2:]
+        step *= 2
+    for k in order:
+        image_blocks[k] = exchange(image_emb, "txt", n_txt, k)
+    far = exchange(near, "img", n_img, 1)
+    pair_row = jnp.pad(pairs.astype(jnp.float32)[None], ((0, 7), (0, width - count)))
+    bundle = jnp.concatenate([image_blocks[k] for k in range(n_txt)] + [pair_row])
+    pair = exchange(bundle, "img", n_img, 1)
+
+    own, loss_tile, d_near, *messages = pl.pallas_call(
+        functools.partial(image_kernel, n_img, n_txt, rows, cols),
+        out_shape=[vmem((rows, width)), vmem((8, LANES)), vmem((chips * cols, count))]
+        + [vmem((tiles + 1, 8, LANES))] * (n_txt - 1),
+        in_specs=[smem] * 2 + [whole] * 3,
+        out_specs=[whole] * (2 + n_txt),
+        name="image_terms",
+    )(log_scale, bias, *in_vmem(bundle, near, far))
+    messages = [exchange(m, "txt", n_txt, k) for k, m in enumerate(messages, 1)]
+
+    blocks = pl.pallas_call(
+        functools.partial(text_kernel, n_img, n_txt, rows, cols),
+        out_shape=[vmem((cols, width))] * chips,
+        in_specs=[smem] * 2 + [whole] * 4,
+        out_specs=[whole] * chips,
+        name="text_terms",
+    )(log_scale, bias, *in_vmem(bundle, pair, near, d_near))
+    blocks = [blocks[0]] + [exchange(blocks[k], "img", n_img, 2 * k) for k in range(1, chips)]
+
+    image_loss, image_grad = pl.pallas_call(
+        functools.partial(image_sum_kernel, n_txt),
+        out_shape=[
+            jax.ShapeDtypeStruct((1, LANES), jnp.float32),
+            jax.ShapeDtypeStruct(image_emb.shape, jnp.float32),
+        ],
+        in_specs=[whole] * (1 + n_txt),
+        out_specs=[whole] * 2,
+        name="image_sums",
+    )(*in_vmem(own, loss_tile, *messages))
+    text_grad = pl.pallas_call(
+        text_sum_kernel,
+        out_shape=jax.ShapeDtypeStruct(text_emb.shape, jnp.float32),
+        in_specs=[pl.BlockSpec(memory_space=pl.ANY)] + [whole] * chips,
+        out_specs=whole,
+        name="text_sums",
+    )(image_loss, *in_vmem(*blocks))
+    return (image_loss.reshape(count), image_grad, text_grad)
+
+
+def per_device_large(image_emb, text_emb, pairs, log_scale, bias):
     images = lax.all_gather(image_emb, "txt", axis=0, tiled=True)
     texts = lax.all_gather(text_emb, "img", axis=0, tiled=True)
     scale = jnp.exp(log_scale[0])
@@ -39,8 +225,16 @@
 
 
 def solution(mesh):
+    sizes = (mesh.shape["img"], mesh.shape["txt"])
+
+    def body(image_emb, *others):
+        small = all(n in (2, 4, 8) for n in sizes)
+        if small and sizes[1] * image_emb.shape[0] == LANES and image_emb.shape[0] % 8 == 0:
+            return per_device(sizes, image_emb, *others)
+        return per_device_large(image_emb, *others)
+
     return jax.shard_map(
-        per_device,
+        body,
         mesh=mesh,
         in_specs=(P(("img", "txt"), None), P(("txt", "img"), None), P("img"), P(), P()),
         out_specs=(P("img"), P(("img", "txt"), None), P(("txt", "img"), None)),

time: 105 us -> 35 us (0.33)
  blocking collectives: 40 us -> 0 us
  waiting for transfers between devices: 44.1 us -> 10.6 us
  starting transfers between devices: 0.08 us -> 17.8 us
  between operations: 15.4 us -> 2.07 us
  matrix products: 4.21 us -> 0 us
  Pallas kernels: 0 us -> 3.41 us
    reduce_scatter x2 -> x0, waiting for transfers between devices: 44 us -> none  [the longest x1 37.3 us: per_device(): lax.psum_scatter(text_term, 'img', scatter_dimension=0, tiled=True)]
    all_gather x2 -> x0, blocking collectives: 27 us -> none  [the longest x1 16.6 us: per_device(): images = lax.all_gather(image_emb, 'txt', axis=0, tiled=True)]
    ppermute x0 -> x13, starting transfers between devices: none -> 17.8 us  [exchange(): return lax.ppermute(x, axis, [(i, i ^ k) for i in range(n)])]
    psum x1 -> x0, blocking collectives: 13 us -> none  [per_device(): image_loss = lax.psum(loss_part, 'txt')]
    ppermute x0 -> x13, waiting for transfers between devices: none -> 10.6 us  [exchange(): return lax.ppermute(x, axis, [(i, i ^ k) for i in range(n)])]
    dot_general x3 -> x0, matrix products: 4.21 us -> none  [the longest x1 1.78 us: per_device(): lax.dot_general(dlogits, images, (((0,), (0,)), ((), ())), precision=lax....]
    pallas_call x0 -> x4, Pallas kernels: none -> 3.41 us  [the longest x1 1.16 us: per_device(): pl.pallas_call(functools.partial(image_kernel, n_img, n_txt, rows, cols),...]
  transfers between devices with their start and end apart: 2 -> 13, of which waited for: 2 -> 5; matrix products, arithmetic and copies ran while one was open for 2% -> 3% of each run, Pallas kernels for 0% -> 8%
where the time goes in v7:
time: 35 us; the launch traced here: 34.8 us
  starting transfers between devices  17.8 us (51%)
  waiting for transfers between devices  10.6 us (30%)
  Pallas kernels  3.41 us (10%)
  between operations  2.07 us (6%)
  local copies, waits for them, and re-layouts  0.97 us (3%)
    ppermute x13, starting transfers between devices, exchange(): return lax.ppermute(x, axis, [(i, i ^ k) for i in range(n)])  17.8 us
    ppermute x13, waiting for transfers between devices, exchange(): return lax.ppermute(x, axis, [(i, i ^ k) for i in range(n)])  10.6 us
    pallas_call x1, Pallas kernels, per_device(): pl.pallas_call(functools.partial(image_kernel, n_img, n_txt, rows, cols),...  1.16 us
    unnamed x10, local copies, waits for them, and re-layouts  0.95 us
    pallas_call x1, Pallas kernels, per_device(): pl.pallas_call(functools.partial(text_kernel, n_img, n_txt, rows, cols),...  0.89 us
  transfers between devices with their start and end apart: 13, of which 5 were waited for; matrix products, arithmetic and copies ran while one was open for 3% of the time, Pallas kernels for 8%

profile of v7, /device:TPU:0, one launch (start us, length us, event | category | flops | bytes accessed | tf_op | source)
XLA Modules:
  0.0 34.8 jit_solution(11223263196328601611)
XLA Ops:
  0.6 0.0 copy-start
  0.6 0.0 copy-start.1
  0.7 3.1 %collective-permute-start = (f32[32,768]{1,0:T(8,128)}, f32[32,768]{1,0:T(8,128)S(1)}, u32[]{:S(2)}, u32[]{:S(2)}) collective-permute-start(f32[32,768]{1,0:T(8,128)} %param.5), channel_id=1, source_target_pairs={{0,1},{1,0},{2,3},{3,2},{4,5},{5,4},{6,7},{7,6},{8,9},{9,8},{10,11... | collective-permute-start | bytes 294920 | tf_op jit(solution)/shard_map/ppermute | solution.py:14
  3.7 2.6 %collective-permute-start.1 = (f32[32,768]{1,0:T(8,128)}, f32[32,768]{1,0:T(8,128)S(1)}, u32[]{:S(2)}, u32[]{:S(2)}) collective-permute-start(f32[32,768]{1,0:T(8,128)} %param.5), channel_id=1, source_target_pairs={{0,2},{1,3},{2,0},{3,1},{4,6},{5,7},{6,4},{7,5},{8,10},{9,11},{10,... | collective-permute-start | bytes 294920 | tf_op jit(solution)/shard_map/ppermute | solution.py:14
  6.3 0.0 collective-permute-start.2
  6.3 1.7 %collective-permute-start.3 = (f32[32,768]{1,0:T(8,128)}, f32[32,768]{1,0:T(8,128)S(1)}, u32[]{:S(2)}, u32[]{:S(2)}) collective-permute-start(f32[32,768]{1,0:T(8,128)} %param.6), channel_id=1, source_target_pairs={{0,8},{4,12},{8,0},{12,4},{16,24},{20,28},{24,16},{28,20},{1,9},{5... | collective-permute-start | bytes 294920 | tf_op jit(solution)/shard_map/ppermute | solution.py:14
  8.0 0.9 %constant_dynamic-update-slice_fusion.3 = f32[136,768]{1,0:T(8,128)S(1)} fusion(f32[32,768]{1,0:T(8,128)} %param.5), kind=kLoop, calls=%fused_computation.5 | loop fusion | bytes 196608
  8.9 0.0 copy-done.1
  9.0 0.0 copy-done
  9.0 2.2 %collective-permute-done.3 = f32[32,768]{1,0:T(8,128)S(1)} collective-permute-done((f32[32,768]{1,0:T(8,128)}, f32[32,768]{1,0:T(8,128)S(1)}, u32[]{:S(2)}, u32[]{:S(2)}) %collective-permute-start.3) | collective-permute-done | bytes 98336 | tf_op jit(solution)/shard_map/ppermute | solution.py:14
  11.2 1.8 %collective-permute-start.4 = (f32[64,768]{1,0:T(8,128)S(1)}, f32[64,768]{1,0:T(8,128)S(1)}, u32[]{:S(2)}, u32[]{:S(2)}) collective-permute-start(f32[64,768]{1,0:T(8,128)S(1)} %pad_maximum_fusion), channel_id=1, source_target_pairs={{0,16},{4,20},{8,24},{12,28},{16,0},{20,4},{24,8},{28,12},{1,17},{... | collective-permute-start | bytes 589832 | tf_op jit(solution)/shard_map/ppermute | solution.py:14
  13.0 0.0 collective-permute-done
  13.0 1.4 %collective-permute-done.1 = f32[32,768]{1,0:T(8,128)S(1)} collective-permute-done((f32[32,768]{1,0:T(8,128)}, f32[32,768]{1,0:T(8,128)S(1)}, u32[]{:S(2)}, u32[]{:S(2)}) %collective-permute-start.1) | collective-permute-done | bytes 98336 | tf_op jit(solution)/shard_map/ppermute | solution.py:14
  14.4 0.0 collective-permute-done.2
  14.4 2.5 %collective-permute-done.4 = f32[64,768]{1,0:T(8,128)S(1)} collective-permute-done((f32[64,768]{1,0:T(8,128)S(1)}, f32[64,768]{1,0:T(8,128)S(1)}, u32[]{:S(2)}, u32[]{:S(2)}) %collective-permute-start.4) | collective-permute-done | bytes 196640 | tf_op jit(solution)/shard_map/ppermute | solution.py:14
  16.9 0.1 collective-permute-start.5
  17.0 0.5 %collective-permute-start.9 = (f32[136,768]{1,0:T(8,128)S(1)}, f32[136,768]{1,0:T(8,128)S(1)}, u32[]{:S(2)}, u32[]{:S(2)}) collective-permute-start(f32[136,768]{1,0:T(8,128)S(1)} %pad_dynamic-update-slice_fusion.refs_2_), channel_id=1, source_target_pairs={{0,4},{4,0},{8,12},{12,8},{16,20},{20,16},{24,28},{28,24},{1,5},{5... | collective-permute-start | bytes 1253384 | tf_op jit(solution)/shard_map/ppermute | solution.py:14
  18.8 0.0 collective-permute-done.5.refs_4_
  18.8 1.2 %image_terms.1 = (f32[32,768]{1,0:T(8,128)S(1)}, f32[8,128]{1,0:T(8,128)S(1)}, f32[128,128]{1,0:T(8,128)S(1)}, f32[25,8,128]{2,1,0:T(8,128)S(1)}, f32[25,8,128]{2,1,0:T(8,128)S(1)}, /*index=5*/f32[25,8,128]{2,1,0:T(8,128)S(1)}) custom-call(f32[1]{0:T(128)S(6)} %copy.14.refs_0_, f32[1]{0:T(128)S(6)} %copy.15.refs_1_, ...), custom_call_target="tpu_custom_call" | custom-call | tf_op jit(solution)/shard_map/image_terms/pallas_call | solution.py:154
  20.0 1.0 %collective-permute-start.6 = (f32[25,8,128]{2,1,0:T(8,128)S(1)}, f32[25,8,128]{2,1,0:T(8,128)S(1)}, u32[]{:S(2)}, u32[]{:S(2)}) collective-permute-start(f32[25,8,128]{2,1,0:T(8,128)S(1)} %get-tuple-element.17), channel_id=1, source_target_pairs={{0,1},{1,0},{2,3},{3,2},{4,5},{5,4},{6,7},{7,6},{8,9},{9,8},{10,11... | collective-permute-start | bytes 307208 | tf_op jit(solution)/shard_map/ppermute | solution.py:14
  21.0 3.5 %collective-permute-start.7 = (f32[25,8,128]{2,1,0:T(8,128)S(1)}, f32[25,8,128]{2,1,0:T(8,128)S(1)}, u32[]{:S(2)}, u32[]{:S(2)}) collective-permute-start(f32[25,8,128]{2,1,0:T(8,128)S(1)} %get-tuple-element.18), channel_id=1, source_target_pairs={{0,2},{1,3},{2,0},{3,1},{4,6},{5,7},{6,4},{7,5},{8,10},{9,11},{10,... | collective-permute-start | bytes 307208 | tf_op jit(solution)/shard_map/ppermute | solution.py:14
  24.4 0.0 collective-permute-start.8
  24.4 0.0 collective-permute-done.9.refs_3_
  24.5 0.9 %text_terms.1 = (f32[32,768]{1,0:T(8,128)S(1)}, f32[32,768]{1,0:T(8,128)S(1)}, f32[32,768]{1,0:T(8,128)S(1)}, f32[32,768]{1,0:T(8,128)S(1)}) custom-call(f32[1]{0:T(128)S(6)} %copy.14.refs_0_, f32[1]{0:T(128)S(6)} %copy.15.refs_1_, f32[136,768]{1,0:T(8,128)S(1)} %pad_dynamic-update-slice_fusion.refs_2_, f32[136,768]{1,0:T(8,128)S(1)} %collective-permute-done.9.refs_3_, ...), custom_call_target="tpu_custom_call" | custom-call | tf_op jit(solution)/shard_map/text_terms/pallas_call | solution.py:164
  25.3 1.8 %collective-permute-start.10 = (f32[32,768]{1,0:T(8,128)S(1)}, f32[32,768]{1,0:T(8,128)S(1)}, u32[]{:S(2)}, u32[]{:S(2)}) collective-permute-start(f32[32,768]{1,0:T(8,128)S(1)} %get-tuple-element.24), channel_id=1, source_target_pairs={{0,8},{4,12},{8,0},{12,4},{16,24},{20,28},{24,16},{28,20},{1,9},{5... | collective-permute-start | bytes 294920 | tf_op jit(solution)/shard_map/ppermute | solution.py:14
  27.1 1.5 %collective-permute-start.11 = (f32[32,768]{1,0:T(8,128)S(1)}, f32[32,768]{1,0:T(8,128)S(1)}, u32[]{:S(2)}, u32[]{:S(2)}) collective-permute-start(f32[32,768]{1,0:T(8,128)S(1)} %get-tuple-element.25), channel_id=1, source_target_pairs={{0,16},{4,20},{8,24},{12,28},{16,0},{20,4},{24,8},{28,12},{1,17},{... | collective-permute-start | bytes 294920 | tf_op jit(solution)/shard_map/ppermute | solution.py:14
  28.6 0.0 collective-permute-done.6.refs_0_
  28.6 0.3 collective-permute-start.12
  28.9 3.6 %collective-permute-done.7.refs_1_ = f32[25,8,128]{2,1,0:T(8,128)S(1)} collective-permute-done((f32[25,8,128]{2,1,0:T(8,128)S(1)}, f32[25,8,128]{2,1,0:T(8,128)S(1)}, u32[]{:S(2)}, u32[]{:S(2)}) %collective-permute-start.7) | collective-permute-done | bytes 102432 | tf_op jit(solution)/shard_map/ppermute | solution.py:14
  32.5 0.0 collective-permute-done.8.refs_2_
  32.5 0.7 %image_sums.1 = (f32[1,128]{1,0:T(1,128)}, f32[32,768]{1,0:T(8,128)}) custom-call(f32[32,768]{1,0:T(8,128)S(1)} %get-tuple-element.15.own_ref, f32[8,128]{1,0:T(8,128)S(1)} %get-tuple-element.16.loss_ref, f32[25,8,128]{2,1,0:T(8,128)S(1)} %collective-permute-done.6.refs_0_, f32[25,8,128]{2,1,0:T(8,128)S(1)} %collective-permute-done.7.refs_1_, ...), custom_call_target="tpu_custom_call" | custom-call | tf_op jit(solution)/shard_map/image_sums/pallas_call | solution.py:173
  33.2 0.0 collective-permute-done.10.refs_1_
  33.2 0.0 collective-permute-done.11.refs_2_
  33.2 0.9 %collective-permute-done.12.refs_3_ = f32[32,768]{1,0:T(8,128)S(1)} collective-permute-done((f32[32,768]{1,0:T(8,128)S(1)}, f32[32,768]{1,0:T(8,128)S(1)}, u32[]{:S(2)}, u32[]{:S(2)}) %collective-permute-start.12) | collective-permute-done | bytes 98336 | tf_op jit(solution)/shard_map/ppermute | solution.py:14
  34.2 0.7 %text_sums.1 = f32[32,768]{1,0:T(8,128)} custom-call(f32[1,128]{1,0:T(1,128)} %get-tuple-element.20._, f32[32,768]{1,0:T(8,128)S(1)} %get-tuple-element.23.refs_0_, f32[32,768]{1,0:T(8,128)S(1)} %collective-permute-done.10.refs_1_, f32[32,768]{1,0:T(8,128)S(1)} %collective-permute-done.11.refs_2_, f32[32,768]{1,0:T(8,128)S(1)} %collective-permute-done.12.refs_3_), custom_call_target="tpu_custom_call" | custom-call | tf_op jit(solution)/shard_map/text_sums/pallas_call | solution.py:183
  (9 shorter events, 0.1 us)
Async XLA Ops:
  0.6 8.3 %copy-start = (f32[32,768]{1,0:T(8,128)S(1)}, f32[32,768]{1,0:T(8,128)}, u32[]{:S(2)}) copy-start(f32[32,768]{1,0:T(8,128)} %param.6) | copy-start | bytes 294916
  0.6 8.3 %copy-start.1 = (s32[128]{0:T(128)S(1)}, s32[128]{0:T(128)}, u32[]{:S(2)}) copy-start(s32[128]{0:T(128)} %param.7) | copy-start | bytes 1540
  0.7 12.3 %collective-permute-start = (f32[32,768]{1,0:T(8,128)}, f32[32,768]{1,0:T(8,128)S(1)}, u32[]{:S(2)}, u32[]{:S(2)}) collective-permute-start(f32[32,768]{1,0:T(8,128)} %param.5), channel_id=1, source_target_pairs={{0,1},{1,0},{2,3},{3,2},{4,5},{5,4},{6,7},{7,6},{8,9},{9,8},{10,11... | collective-permute-start | bytes 294920 | tf_op jit(solution)/shard_map/ppermute | solution.py:14
  3.7 10.6 %collective-permute-start.1 = (f32[32,768]{1,0:T(8,128)}, f32[32,768]{1,0:T(8,128)S(1)}, u32[]{:S(2)}, u32[]{:S(2)}) collective-permute-start(f32[32,768]{1,0:T(8,128)} %param.5), channel_id=1, source_target_pairs={{0,2},{1,3},{2,0},{3,1},{4,6},{5,7},{6,4},{7,5},{8,10},{9,11},{10,... | collective-permute-start | bytes 294920 | tf_op jit(solution)/shard_map/ppermute | solution.py:14
  6.3 8.1 %collective-permute-start.2 = (f32[32,768]{1,0:T(8,128)}, f32[32,768]{1,0:T(8,128)S(1)}, u32[]{:S(2)}, u32[]{:S(2)}) collective-permute-start(f32[32,768]{1,0:T(8,128)} %param.5), channel_id=1, source_target_pairs={{0,3},{1,2},{2,1},{3,0},{4,7},{5,6},{6,5},{7,4},{8,11},{9,10},{10,... | collective-permute-start | bytes 294920 | tf_op jit(solution)/shard_map/ppermute | solution.py:14
  6.3 4.8 %collective-permute-start.3 = (f32[32,768]{1,0:T(8,128)}, f32[32,768]{1,0:T(8,128)S(1)}, u32[]{:S(2)}, u32[]{:S(2)}) collective-permute-start(f32[32,768]{1,0:T(8,128)} %param.6), channel_id=1, source_target_pairs={{0,8},{4,12},{8,0},{12,4},{16,24},{20,28},{24,16},{28,20},{1,9},{5... | collective-permute-start | bytes 294920 | tf_op jit(solution)/shard_map/ppermute | solution.py:14
  11.2 5.7 %collective-permute-start.4 = (f32[64,768]{1,0:T(8,128)S(1)}, f32[64,768]{1,0:T(8,128)S(1)}, u32[]{:S(2)}, u32[]{:S(2)}) collective-permute-start(f32[64,768]{1,0:T(8,128)S(1)} %pad_maximum_fusion), channel_id=1, source_target_pairs={{0,16},{4,20},{8,24},{12,28},{16,0},{20,4},{24,8},{28,12},{1,17},{... | collective-permute-start | bytes 589832 | tf_op jit(solution)/shard_map/ppermute | solution.py:14
  16.9 1.9 %collective-permute-start.5 = (f32[128,768]{1,0:T(8,128)S(1)}, f32[128,768]{1,0:T(8,128)S(1)}, u32[]{:S(2)}, u32[]{:S(2)}) collective-permute-start(f32[128,768]{1,0:T(8,128)S(1)} %constant_dynamic-update-slice_fusion.4.refs_3_.refs_4_), channel_id=1, source_target_pairs={{0,4},{4,0},{8,12},{12,8},{16,20},{20,16},{24,28},{28,24},{1,5},{5... | collective-permute-start | bytes 1179656 | tf_op jit(solution)/shard_map/ppermute | solution.py:14
  17.0 7.4 %collective-permute-start.9 = (f32[136,768]{1,0:T(8,128)S(1)}, f32[136,768]{1,0:T(8,128)S(1)}, u32[]{:S(2)}, u32[]{:S(2)}) collective-permute-start(f32[136,768]{1,0:T(8,128)S(1)} %pad_dynamic-update-slice_fusion.refs_2_), channel_id=1, source_target_pairs={{0,4},{4,0},{8,12},{12,8},{16,20},{20,16},{24,28},{28,24},{1,5},{5... | collective-permute-start | bytes 1253384 | tf_op jit(solution)/shard_map/ppermute | solution.py:14
  20.0 8.7 %collective-permute-start.6 = (f32[25,8,128]{2,1,0:T(8,128)S(1)}, f32[25,8,128]{2,1,0:T(8,128)S(1)}, u32[]{:S(2)}, u32[]{:S(2)}) collective-permute-start(f32[25,8,128]{2,1,0:T(8,128)S(1)} %get-tuple-element.17), channel_id=1, source_target_pairs={{0,1},{1,0},{2,3},{3,2},{4,5},{5,4},{6,7},{7,6},{8,9},{9,8},{10,11... | collective-permute-start | bytes 307208 | tf_op jit(solution)/shard_map/ppermute | solution.py:14
  21.0 11.6 %collective-permute-start.7 = (f32[25,8,128]{2,1,0:T(8,128)S(1)}, f32[25,8,128]{2,1,0:T(8,128)S(1)}, u32[]{:S(2)}, u32[]{:S(2)}) collective-permute-start(f32[25,8,128]{2,1,0:T(8,128)S(1)} %get-tuple-element.18), channel_id=1, source_target_pairs={{0,2},{1,3},{2,0},{3,1},{4,6},{5,7},{6,4},{7,5},{8,10},{9,11},{10,... | collective-permute-start | bytes 307208 | tf_op jit(solution)/shard_map/ppermute | solution.py:14
  24.4 8.1 %collective-permute-start.8 = (f32[25,8,128]{2,1,0:T(8,128)S(1)}, f32[25,8,128]{2,1,0:T(8,128)S(1)}, u32[]{:S(2)}, u32[]{:S(2)}) collective-permute-start(f32[25,8,128]{2,1,0:T(8,128)S(1)} %get-tuple-element.19), channel_id=1, source_target_pairs={{0,3},{1,2},{2,1},{3,0},{4,7},{5,6},{6,5},{7,4},{8,11},{9,10},{10,... | collective-permute-start | bytes 307208 | tf_op jit(solution)/shard_map/ppermute | solution.py:14
  25.3 7.9 %collective-permute-start.10 = (f32[32,768]{1,0:T(8,128)S(1)}, f32[32,768]{1,0:T(8,128)S(1)}, u32[]{:S(2)}, u32[]{:S(2)}) collective-permute-start(f32[32,768]{1,0:T(8,128)S(1)} %get-tuple-element.24), channel_id=1, source_target_pairs={{0,8},{4,12},{8,0},{12,4},{16,24},{20,28},{24,16},{28,20},{1,9},{5... | collective-permute-start | bytes 294920 | tf_op jit(solution)/shard_map/ppermute | solution.py:14
  27.1 6.1 %collective-permute-start.11 = (f32[32,768]{1,0:T(8,128)S(1)}, f32[32,768]{1,0:T(8,128)S(1)}, u32[]{:S(2)}, u32[]{:S(2)}) collective-permute-start(f32[32,768]{1,0:T(8,128)S(1)} %get-tuple-element.25), channel_id=1, source_target_pairs={{0,16},{4,20},{8,24},{12,28},{16,0},{20,4},{24,8},{28,12},{1,17},{... | collective-permute-start | bytes 294920 | tf_op jit(solution)/shard_map/ppermute | solution.py:14
  28.6 5.5 %collective-permute-start.12 = (f32[32,768]{1,0:T(8,128)S(1)}, f32[32,768]{1,0:T(8,128)S(1)}, u32[]{:S(2)}, u32[]{:S(2)}) collective-permute-start(f32[32,768]{1,0:T(8,128)S(1)} %get-tuple-element.26), channel_id=1, source_target_pairs={{0,24},{4,28},{8,16},{12,20},{16,8},{20,12},{24,0},{28,4},{1,25},{... | collective-permute-start | bytes 294920 | tf_op jit(solution)/shard_map/ppermute | solution.py:14

commit v8 on v7

--- a/solution.py
+++ b/solution.py
@@ -134,18 +134,15 @@
     tiles = rows * width // (8 * LANES)
     smem, whole = pl.BlockSpec(memory_space=pltpu.SMEM), pl.BlockSpec(memory_space=pltpu.VMEM)
 
-    near = text_emb
-    image_blocks = {0: image_emb}
-    order = [k for k in range(2, n_txt)] + [1]
-    step = 1
-    while step < chips:
-        near = jnp.concatenate([near, exchange(near, "img", n_img, 2 * step)])
-        for k in order[:2]:
+    text_blocks, image_blocks = {0: text_emb}, {0: image_emb}
+    for k in range(1, max(n_txt, chips)):
+        if k < chips:
+            text_blocks[k] = exchange(text_emb, "img", n_img, 2 * k)
+        if 1 < k < n_txt:
             image_blocks[k] = exchange(image_emb, "txt", n_txt, k)
-        order = order[2:]
-        step *= 2
-    for k in order:
-        image_blocks[k] = exchange(image_emb, "txt", n_txt, k)
+    late_image, _ = lax.optimization_barrier((image_emb, text_blocks[1]))
+    image_blocks[1] = exchange(late_image, "txt", n_txt, 1)
+    near = jnp.concatenate([text_blocks[k] for k in range(chips)])
     far = exchange(near, "img", n_img, 1)
     pair_row = jnp.pad(pairs.astype(jnp.float32)[None], ((0, 7), (0, width - count)))
     bundle = jnp.concatenate([image_blocks[k] for k in range(n_txt)] + [pair_row])

time: 35 us -> 33.8 us (0.966)
  waiting for transfers between devices: 10.6 us -> 8.61 us
  starting transfers between devices: 17.8 us -> 18.4 us
    ppermute x13 -> x14, waiting for transfers between devices: 10.6 us -> 8.61 us  [exchange(): return lax.ppermute(x, axis, [(i, i ^ k) for i in range(n)])]
    ppermute x13 -> x14, starting transfers between devices: 17.8 us -> 18.4 us  [exchange(): return lax.ppermute(x, axis, [(i, i ^ k) for i in range(n)])]
    unnamed x10 -> x13, local copies, waits for them, and re-layouts: 0.95 us -> 1.08 us
  transfers between devices with their start and end apart: 13 -> 14, of which waited for: 5 -> 7; matrix products, arithmetic and copies ran while one was open for 3% -> 3% of each run, Pallas kernels for 8% -> 8%
where the time goes in v8:
time: 33.8 us; the launch traced here: 33.6 us
  starting transfers between devices  18.4 us (54%)
  waiting for transfers between devices  8.61 us (25%)
  Pallas kernels  3.41 us (10%)
  between operations  2.08 us (6%)
  local copies, waits for them, and re-layouts  1.1 us (3%)
    ppermute x14, starting transfers between devices, exchange(): return lax.ppermute(x, axis, [(i, i ^ k) for i in range(n)])  18.4 us
    ppermute x14, waiting for transfers between devices, exchange(): return lax.ppermute(x, axis, [(i, i ^ k) for i in range(n)])  8.61 us
    pallas_call x1, Pallas kernels, per_device(): pl.pallas_call(functools.partial(image_kernel, n_img, n_txt, rows, cols),...  1.16 us
    unnamed x13, local copies, waits for them, and re-layouts  1.08 us
    pallas_call x1, Pallas kernels, per_device(): pl.pallas_call(functools.partial(text_kernel, n_img, n_txt, rows, cols),...  0.89 us
    pallas_call x1, Pallas kernels, per_device(): pl.pallas_call(functools.partial(image_sum_kernel, n_txt), out_shape=[jax...  0.68 us
  transfers between devices with their start and end apart: 14, of which 7 were waited for; matrix products, arithmetic and copies ran while one was open for 3% of the time, Pallas kernels for 8%

profile of v8, /device:TPU:0, one launch (start us, length us, event | category | flops | bytes accessed | tf_op | source)
XLA Modules:
  0.0 33.6 jit_solution(3454284514377879941)
XLA Ops:
  0.6 0.0 copy-start
  0.6 0.0 copy-start.2
  0.7 4.1 %collective-permute-start.2 = (f32[32,768]{1,0:T(8,128)}, f32[32,768]{1,0:T(8,128)S(1)}, u32[]{:S(2)}, u32[]{:S(2)}) collective-permute-start(f32[32,768]{1,0:T(8,128)} %param.5), channel_id=1, source_target_pairs={{0,2},{1,3},{2,0},{3,1},{4,6},{5,7},{6,4},{7,5},{8,10},{9,11},{10,... | collective-permute-start | bytes 294920 | tf_op jit(solution)/shard_map/ppermute | solution.py:14
  4.8 1.3 %collective-permute-start.3 = (f32[32,768]{1,0:T(8,128)}, f32[32,768]{1,0:T(8,128)S(1)}, u32[]{:S(2)}, u32[]{:S(2)}) collective-permute-start(f32[32,768]{1,0:T(8,128)} %param.5), channel_id=1, source_target_pairs={{0,3},{1,2},{2,1},{3,0},{4,7},{5,6},{6,5},{7,4},{8,11},{9,10},{10,... | collective-permute-start | bytes 294920 | tf_op jit(solution)/shard_map/ppermute | solution.py:14
  6.1 1.5 %collective-permute-start = (f32[32,768]{1,0:T(8,128)}, f32[32,768]{1,0:T(8,128)S(1)}, u32[]{:S(2)}, u32[]{:S(2)}) collective-permute-start(f32[32,768]{1,0:T(8,128)} %param.6), channel_id=1, source_target_pairs={{0,8},{4,12},{8,0},{12,4},{16,24},{20,28},{24,16},{28,20},{1,9},{5... | collective-permute-start | bytes 294920 | tf_op jit(solution)/shard_map/ppermute | solution.py:14
  7.6 1.5 %collective-permute-start.4 = (f32[32,768]{1,0:T(8,128)}, f32[32,768]{1,0:T(8,128)S(1)}, u32[]{:S(2)}, u32[]{:S(2)}) collective-permute-start(f32[32,768]{1,0:T(8,128)} %param.6), channel_id=1, source_target_pairs={{0,16},{4,20},{8,24},{12,28},{16,0},{20,4},{24,8},{28,12},{1,17},{... | collective-permute-start | bytes 294920 | tf_op jit(solution)/shard_map/ppermute | solution.py:14
  9.1 0.5 %collective-permute-start.5 = (f32[32,768]{1,0:T(8,128)}, f32[32,768]{1,0:T(8,128)S(1)}, u32[]{:S(2)}, u32[]{:S(2)}) collective-permute-start(f32[32,768]{1,0:T(8,128)} %param.6), channel_id=1, source_target_pairs={{0,24},{4,28},{8,16},{12,20},{16,8},{20,12},{24,0},{28,4},{1,25},{... | collective-permute-start | bytes 294920 | tf_op jit(solution)/shard_map/ppermute | solution.py:14
  9.6 0.9 %constant_dynamic-update-slice_fusion.3 = f32[136,768]{1,0:T(8,128)S(1)} fusion(f32[32,768]{1,0:T(8,128)} %param.5), kind=kLoop, calls=%fused_computation.4 | loop fusion | bytes 196608
  10.5 0.0 copy-done.2
  10.5 0.0 copy-done
  10.5 0.0 copy-start.1
  10.5 0.7 %collective-permute-done = f32[32,768]{1,0:T(8,128)S(1)} collective-permute-done((f32[32,768]{1,0:T(8,128)}, f32[32,768]{1,0:T(8,128)S(1)}, u32[]{:S(2)}, u32[]{:S(2)}) %collective-permute-start) | collective-permute-done | bytes 98336 | tf_op jit(solution)/shard_map/ppermute | solution.py:14
  11.3 0.1 copy-done.1
  11.4 0.2 collective-permute-start.1
  11.7 1.8 %collective-permute-done.4 = f32[32,768]{1,0:T(8,128)S(1)} collective-permute-done((f32[32,768]{1,0:T(8,128)}, f32[32,768]{1,0:T(8,128)S(1)}, u32[]{:S(2)}, u32[]{:S(2)}) %collective-permute-start.4) | collective-permute-done | bytes 98336 | tf_op jit(solution)/shard_map/ppermute | solution.py:14
  13.5 1.4 %collective-permute-done.5 = f32[32,768]{1,0:T(8,128)S(1)} collective-permute-done((f32[32,768]{1,0:T(8,128)}, f32[32,768]{1,0:T(8,128)S(1)}, u32[]{:S(2)}, u32[]{:S(2)}) %collective-permute-start.5) | collective-permute-done | bytes 98336 | tf_op jit(solution)/shard_map/ppermute | solution.py:14
  14.9 0.1 collective-permute-start.6
  14.9 1.1 %collective-permute-done.1 = f32[32,768]{1,0:T(8,128)S(1)} collective-permute-done((f32[32,768]{1,0:T(8,128)S(1)}, f32[32,768]{1,0:T(8,128)S(1)}, u32[]{:S(2)}, u32[]{:S(2)}) %collective-permute-start.1) | collective-permute-done | bytes 98336 | tf_op jit(solution)/shard_map/ppermute | solution.py:14
  16.0 0.0 collective-permute-done.2
  16.1 0.0 collective-permute-done.3
  16.1 0.1 collective-permute-start.10
  17.5 0.0 collective-permute-done.6.refs_4_
  17.5 1.2 %image_terms.1 = (f32[32,768]{1,0:T(8,128)S(1)}, f32[8,128]{1,0:T(8,128)S(1)}, f32[128,128]{1,0:T(8,128)S(1)}, f32[25,8,128]{2,1,0:T(8,128)S(1)}, f32[25,8,128]{2,1,0:T(8,128)S(1)}, /*index=5*/f32[25,8,128]{2,1,0:T(8,128)S(1)}) custom-call(f32[1]{0:T(128)S(6)} %copy.15.refs_0_, f32[1]{0:T(128)S(6)} %copy.16.refs_1_, ...), custom_call_target="tpu_custom_call" | custom-call | tf_op jit(solution)/shard_map/image_terms/pallas_call | solution.py:151
  18.7 0.3 collective-permute-start.7
  19.0 2.8 %collective-permute-start.8 = (f32[25,8,128]{2,1,0:T(8,128)S(1)}, f32[25,8,128]{2,1,0:T(8,128)S(1)}, u32[]{:S(2)}, u32[]{:S(2)}) collective-permute-start(f32[25,8,128]{2,1,0:T(8,128)S(1)} %get-tuple-element.20), channel_id=1, source_target_pairs={{0,2},{1,3},{2,0},{3,1},{4,6},{5,7},{6,4},{7,5},{8,10},{9,11},{10,... | collective-permute-start | bytes 307208 | tf_op jit(solution)/shard_map/ppermute | solution.py:14
  21.8 1.3 %collective-permute-start.9 = (f32[25,8,128]{2,1,0:T(8,128)S(1)}, f32[25,8,128]{2,1,0:T(8,128)S(1)}, u32[]{:S(2)}, u32[]{:S(2)}) collective-permute-start(f32[25,8,128]{2,1,0:T(8,128)S(1)} %get-tuple-element.21), channel_id=1, source_target_pairs={{0,3},{1,2},{2,1},{3,0},{4,7},{5,6},{6,5},{7,4},{8,11},{9,10},{10,... | collective-permute-start | bytes 307208 | tf_op jit(solution)/shard_map/ppermute | solution.py:14
  23.1 0.0 collective-permute-done.10.refs_3_
  23.1 0.9 %text_terms.1 = (f32[32,768]{1,0:T(8,128)S(1)}, f32[32,768]{1,0:T(8,128)S(1)}, f32[32,768]{1,0:T(8,128)S(1)}, f32[32,768]{1,0:T(8,128)S(1)}) custom-call(f32[1]{0:T(128)S(6)} %copy.15.refs_0_, f32[1]{0:T(128)S(6)} %copy.16.refs_1_, f32[136,768]{1,0:T(8,128)S(1)} %pad_dynamic-update-slice_fusion.refs_2_, f32[136,768]{1,0:T(8,128)S(1)} %collective-permute-done.10.refs_3_, ...), custom_call_target="tpu_custom_call" | custom-call | tf_op jit(solution)/shard_map/text_terms/pallas_call | solution.py:161
  24.0 1.9 %collective-permute-start.11 = (f32[32,768]{1,0:T(8,128)S(1)}, f32[32,768]{1,0:T(8,128)S(1)}, u32[]{:S(2)}, u32[]{:S(2)}) collective-permute-start(f32[32,768]{1,0:T(8,128)S(1)} %get-tuple-element.26), channel_id=1, source_target_pairs={{0,8},{4,12},{8,0},{12,4},{16,24},{20,28},{24,16},{28,20},{1,9},{5... | collective-permute-start | bytes 294920 | tf_op jit(solution)/shard_map/ppermute | solution.py:14
  25.9 1.5 %collective-permute-start.12 = (f32[32,768]{1,0:T(8,128)S(1)}, f32[32,768]{1,0:T(8,128)S(1)}, u32[]{:S(2)}, u32[]{:S(2)}) collective-permute-start(f32[32,768]{1,0:T(8,128)S(1)} %get-tuple-element.27), channel_id=1, source_target_pairs={{0,16},{4,20},{8,24},{12,28},{16,0},{20,4},{24,8},{28,12},{1,17},{... | collective-permute-start | bytes 294920 | tf_op jit(solution)/shard_map/ppermute | solution.py:14
  27.4 0.0 collective-permute-done.7.refs_0_
  27.4 1.3 %collective-permute-start.13 = (f32[32,768]{1,0:T(8,128)S(1)}, f32[32,768]{1,0:T(8,128)S(1)}, u32[]{:S(2)}, u32[]{:S(2)}) collective-permute-start(f32[32,768]{1,0:T(8,128)S(1)} %get-tuple-element.28), channel_id=1, source_target_pairs={{0,24},{4,28},{8,16},{12,20},{16,8},{20,12},{24,0},{28,4},{1,25},{... | collective-permute-start | bytes 294920 | tf_op jit(solution)/shard_map/ppermute | solution.py:14
  28.7 1.3 %collective-permute-done.8.refs_1_ = f32[25,8,128]{2,1,0:T(8,128)S(1)} collective-permute-done((f32[25,8,128]{2,1,0:T(8,128)S(1)}, f32[25,8,128]{2,1,0:T(8,128)S(1)}, u32[]{:S(2)}, u32[]{:S(2)}) %collective-permute-start.8) | collective-permute-done | bytes 102432 | tf_op jit(solution)/shard_map/ppermute | solution.py:14
  30.0 0.0 collective-permute-done.9.refs_2_
  30.0 0.7 %image_sums.1 = (f32[1,128]{1,0:T(1,128)}, f32[32,768]{1,0:T(8,128)}) custom-call(f32[32,768]{1,0:T(8,128)S(1)} %get-tuple-element.17.own_ref, f32[8,128]{1,0:T(8,128)S(1)} %get-tuple-element.18.loss_ref, f32[25,8,128]{2,1,0:T(8,128)S(1)} %collective-permute-done.7.refs_0_, f32[25,8,128]{2,1,0:T(8,128)S(1)} %collective-permute-done.8.refs_1_, ...), custom_call_target="tpu_custom_call" | custom-call | tf_op jit(solution)/shard_map/image_sums/pallas_call | solution.py:170
  30.7 0.0 collective-permute-done.11.refs_1_
  30.7 0.9 %collective-permute-done.12.refs_2_ = f32[32,768]{1,0:T(8,128)S(1)} collective-permute-done((f32[32,768]{1,0:T(8,128)S(1)}, f32[32,768]{1,0:T(8,128)S(1)}, u32[]{:S(2)}, u32[]{:S(2)}) %collective-permute-start.12) | collective-permute-done | bytes 98336 | tf_op jit(solution)/shard_map/ppermute | solution.py:14
  31.6 1.4 %collective-permute-done.13.refs_3_ = f32[32,768]{1,0:T(8,128)S(1)} collective-permute-done((f32[32,768]{1,0:T(8,128)S(1)}, f32[32,768]{1,0:T(8,128)S(1)}, u32[]{:S(2)}, u32[]{:S(2)}) %collective-permute-start.13) | collective-permute-done | bytes 98336 | tf_op jit(solution)/shard_map/ppermute | solution.py:14
  33.0 0.7 %text_sums.1 = f32[32,768]{1,0:T(8,128)} custom-call(f32[1,128]{1,0:T(1,128)} %get-tuple-element.22._, f32[32,768]{1,0:T(8,128)S(1)} %get-tuple-element.25.refs_0_, f32[32,768]{1,0:T(8,128)S(1)} %collective-permute-done.11.refs_1_, f32[32,768]{1,0:T(8,128)S(1)} %collective-permute-done.12.refs_2_, f32[32,768]{1,0:T(8,128)S(1)} %collective-permute-done.13.refs_3_), custom_call_target="tpu_custom_call" | custom-call | tf_op jit(solution)/shard_map/text_sums/pallas_call | solution.py:180
  (9 shorter events, 0.1 us)
Async XLA Ops:
  0.6 9.9 %copy-start = (f32[32,768]{1,0:T(8,128)S(1)}, f32[32,768]{1,0:T(8,128)}, u32[]{:S(2)}) copy-start(f32[32,768]{1,0:T(8,128)} %param.6) | copy-start | bytes 294916
  0.6 9.9 %copy-start.2 = (s32[128]{0:T(128)S(1)}, s32[128]{0:T(128)}, u32[]{:S(2)}) copy-start(s32[128]{0:T(128)} %param.7) | copy-start | bytes 1540
  0.7 15.4 %collective-permute-start.2 = (f32[32,768]{1,0:T(8,128)}, f32[32,768]{1,0:T(8,128)S(1)}, u32[]{:S(2)}, u32[]{:S(2)}) collective-permute-start(f32[32,768]{1,0:T(8,128)} %param.5), channel_id=1, source_target_pairs={{0,2},{1,3},{2,0},{3,1},{4,6},{5,7},{6,4},{7,5},{8,10},{9,11},{10,... | collective-permute-start | bytes 294920 | tf_op jit(solution)/shard_map/ppermute | solution.py:14
  4.8 11.3 %collective-permute-start.3 = (f32[32,768]{1,0:T(8,128)}, f32[32,768]{1,0:T(8,128)S(1)}, u32[]{:S(2)}, u32[]{:S(2)}) collective-permute-start(f32[32,768]{1,0:T(8,128)} %param.5), channel_id=1, source_target_pairs={{0,3},{1,2},{2,1},{3,0},{4,7},{5,6},{6,5},{7,4},{8,11},{9,10},{10,... | collective-permute-start | bytes 294920 | tf_op jit(solution)/shard_map/ppermute | solution.py:14
  6.1 5.2 %collective-permute-start = (f32[32,768]{1,0:T(8,128)}, f32[32,768]{1,0:T(8,128)S(1)}, u32[]{:S(2)}, u32[]{:S(2)}) collective-permute-start(f32[32,768]{1,0:T(8,128)} %param.6), channel_id=1, source_target_pairs={{0,8},{4,12},{8,0},{12,4},{16,24},{20,28},{24,16},{28,20},{1,9},{5... | collective-permute-start | bytes 294920 | tf_op jit(solution)/shard_map/ppermute | solution.py:14
  7.6 5.9 %collective-permute-start.4 = (f32[32,768]{1,0:T(8,128)}, f32[32,768]{1,0:T(8,128)S(1)}, u32[]{:S(2)}, u32[]{:S(2)}) collective-permute-start(f32[32,768]{1,0:T(8,128)} %param.6), channel_id=1, source_target_pairs={{0,16},{4,20},{8,24},{12,28},{16,0},{20,4},{24,8},{28,12},{1,17},{... | collective-permute-start | bytes 294920 | tf_op jit(solution)/shard_map/ppermute | solution.py:14
  9.1 5.7 %collective-permute-start.5 = (f32[32,768]{1,0:T(8,128)}, f32[32,768]{1,0:T(8,128)S(1)}, u32[]{:S(2)}, u32[]{:S(2)}) collective-permute-start(f32[32,768]{1,0:T(8,128)} %param.6), channel_id=1, source_target_pairs={{0,24},{4,28},{8,16},{12,20},{16,8},{20,12},{24,0},{28,4},{1,25},{... | collective-permute-start | bytes 294920 | tf_op jit(solution)/shard_map/ppermute | solution.py:14
  10.5 0.9 %copy-start.1 = (f32[32,768]{1,0:T(8,128)S(1)}, f32[32,768]{1,0:T(8,128)}, u32[]{:S(2)}) copy-start(f32[32,768]{1,0:T(8,128)} %param.5) | copy-start | bytes 294916
  11.4 4.6 %collective-permute-start.1 = (f32[32,768]{1,0:T(8,128)S(1)}, f32[32,768]{1,0:T(8,128)S(1)}, u32[]{:S(2)}, u32[]{:S(2)}) collective-permute-start(f32[32,768]{1,0:T(8,128)S(1)} %copy-done.1), channel_id=1, source_target_pairs={{0,1},{1,0},{2,3},{3,2},{4,5},{5,4},{6,7},{7,6},{8,9},{9,8},{10,11... | collective-permute-start | bytes 294920 | tf_op jit(solution)/shard_map/ppermute | solution.py:14
  14.9 2.6 %collective-permute-start.6 = (f32[128,768]{1,0:T(8,128)S(1)}, f32[128,768]{1,0:T(8,128)S(1)}, u32[]{:S(2)}, u32[]{:S(2)}) collective-permute-start(f32[128,768]{1,0:T(8,128)S(1)} %constant_dynamic-update-slice_fusion.4.refs_3_.refs_4_), channel_id=1, source_target_pairs={{0,4},{4,0},{8,12},{12,8},{16,20},{20,16},{24,28},{28,24},{1,5},{5... | collective-permute-start | bytes 1179656 | tf_op jit(solution)/shard_map/ppermute | solution.py:14
  16.1 7.0 %collective-permute-start.10 = (f32[136,768]{1,0:T(8,128)S(1)}, f32[136,768]{1,0:T(8,128)S(1)}, u32[]{:S(2)}, u32[]{:S(2)}) collective-permute-start(f32[136,768]{1,0:T(8,128)S(1)} %pad_dynamic-update-slice_fusion.refs_2_), channel_id=1, source_target_pairs={{0,4},{4,0},{8,12},{12,8},{16,20},{20,16},{24,28},{28,24},{1,5},{5... | collective-permute-start | bytes 1253384 | tf_op jit(solution)/shard_map/ppermute | solution.py:14
  18.7 8.8 %collective-permute-start.7 = (f32[25,8,128]{2,1,0:T(8,128)S(1)}, f32[25,8,128]{2,1,0:T(8,128)S(1)}, u32[]{:S(2)}, u32[]{:S(2)}) collective-permute-start(f32[25,8,128]{2,1,0:T(8,128)S(1)} %get-tuple-element.19), channel_id=1, source_target_pairs={{0,1},{1,0},{2,3},{3,2},{4,5},{5,4},{6,7},{7,6},{8,9},{9,8},{10,11... | collective-permute-start | bytes 307208 | tf_op jit(solution)/shard_map/ppermute | solution.py:14
  19.0 11.0 %collective-permute-start.8 = (f32[25,8,128]{2,1,0:T(8,128)S(1)}, f32[25,8,128]{2,1,0:T(8,128)S(1)}, u32[]{:S(2)}, u32[]{:S(2)}) collective-permute-start(f32[25,8,128]{2,1,0:T(8,128)S(1)} %get-tuple-element.20), channel_id=1, source_target_pairs={{0,2},{1,3},{2,0},{3,1},{4,6},{5,7},{6,4},{7,5},{8,10},{9,11},{10,... | collective-permute-start | bytes 307208 | tf_op jit(solution)/shard_map/ppermute | solution.py:14
  21.8 8.2 %collective-permute-start.9 = (f32[25,8,128]{2,1,0:T(8,128)S(1)}, f32[25,8,128]{2,1,0:T(8,128)S(1)}, u32[]{:S(2)}, u32[]{:S(2)}) collective-permute-start(f32[25,8,128]{2,1,0:T(8,128)S(1)} %get-tuple-element.21), channel_id=1, source_target_pairs={{0,3},{1,2},{2,1},{3,0},{4,7},{5,6},{6,5},{7,4},{8,11},{9,10},{10,... | collective-permute-start | bytes 307208 | tf_op jit(solution)/shard_map/ppermute | solution.py:14
  24.0 6.7 %collective-permute-start.11 = (f32[32,768]{1,0:T(8,128)S(1)}, f32[32,768]{1,0:T(8,128)S(1)}, u32[]{:S(2)}, u32[]{:S(2)}) collective-permute-start(f32[32,768]{1,0:T(8,128)S(1)} %get-tuple-element.26), channel_id=1, source_target_pairs={{0,8},{4,12},{8,0},{12,4},{16,24},{20,28},{24,16},{28,20},{1,9},{5... | collective-permute-start | bytes 294920 | tf_op jit(solution)/shard_map/ppermute | solution.py:14
  25.9 5.7 %collective-permute-start.12 = (f32[32,768]{1,0:T(8,128)S(1)}, f32[32,768]{1,0:T(8,128)S(1)}, u32[]{:S(2)}, u32[]{:S(2)}) collective-permute-start(f32[32,768]{1,0:T(8,128)S(1)} %get-tuple-element.27), channel_id=1, source_target_pairs={{0,16},{4,20},{8,24},{12,28},{16,0},{20,4},{24,8},{28,12},{1,17},{... | collective-permute-start | bytes 294920 | tf_op jit(solution)/shard_map/ppermute | solution.py:14
  27.4 5.5 %collective-permute-start.13 = (f32[32,768]{1,0:T(8,128)S(1)}, f32[32,768]{1,0:T(8,128)S(1)}, u32[]{:S(2)}, u32[]{:S(2)}) collective-permute-start(f32[32,768]{1,0:T(8,128)S(1)} %get-tuple-element.28), channel_id=1, source_target_pairs={{0,24},{4,28},{8,16},{12,20},{16,8},{20,12},{24,0},{28,4},{1,25},{... | collective-permute-start | bytes 294920 | tf_op jit(solution)/shard_map/ppermute | solution.py:14

commit v9 on v8

--- a/solution.py
+++ b/solution.py
@@ -60,25 +60,30 @@
     return loss, jnp.where(match, -s, s)
 
 
-def image_kernel(n_img, n_txt, rows, cols, *refs):
-    log_scale, bias, bundle, near, far, own_ref, loss_ref, d_ref = refs[:8]
-    message_refs = refs[8:]
+def row_of_numbers(bundle, rows, count):
+    matched = untwist(bundle[count:count + 1, :LANES], rows, lax.axis_index("txt"))
+    scale = jnp.exp(bundle[count:count + 1, LANES:2 * LANES])
+    return matched.astype(jnp.int32), scale, bundle[count:count + 1, 2 * LANES:3 * LANES]
+
+
+def image_kernel(
+    n_img, n_txt, rows, cols, bundle, near, far, own, first, second, third, d_near
+):
     count = n_txt * rows
     me_txt = lax.axis_index("txt")
-    scale = jnp.exp(jnp.full((1, LANES), log_scale[0], jnp.float32))
+    matched, scale, shift = row_of_numbers(bundle, rows, count)
     images = halves(bundle[:count])
     texts = halves(jnp.concatenate([near[...], far[...]]))
-    matched = untwist(bundle[count:count + 1, :LANES], rows, me_txt).astype(jnp.int32)
     ids = text_ids((texts[0].shape[0], count), n_img, cols, True)
-    loss, d = derivative(texts, images, ids, matched, scale, bias[0])
-    d_ref[...] = d[:near.shape[0]]
+    loss, d = derivative(texts, images, ids, matched, scale, shift)
+    d_near[...] = d[:near.shape[0]]
     term = dot(halves(d), texts, (0, 0))
-    own_ref[...] = term[:rows]
+    own[...] = term[:rows]
+    first[...] = term[rows:2 * rows]
     loss_row = untwist(jnp.sum(loss, axis=0, keepdims=True), rows, me_txt)
     loss_tile = jnp.broadcast_to(loss_row, (8, LANES))
-    loss_ref[...] = loss_tile
     across = term.shape[1] // LANES
-    for k, ref in enumerate(message_refs, 1):
+    for k, ref in ((2, second), (3, third)):
         for r in range(rows // 8):
             for c in range(across):
                 ref[r * across + c] = term[
@@ -88,29 +93,27 @@
 
 
 def text_kernel(n_img, n_txt, rows, cols, *refs):
-    log_scale, bias, bundle, pair, near, d_ref = refs[:6]
-    block_refs = refs[6:]
+    bundle, pair, near, d_ref = refs[:4]
+    block_refs = refs[4:]
     count = n_txt * rows
-    scale = jnp.exp(jnp.full((1, LANES), log_scale[0], jnp.float32))
+    matched, scale, shift = row_of_numbers(pair, rows, count)
     others = halves(pair[:count])
     texts = halves(near[...])
-    matched = untwist(pair[count:count + 1, :LANES], rows, lax.axis_index("txt")).astype(jnp.int32)
     ids = text_ids((texts[0].shape[0], count), n_img, cols, False)
-    _, d = derivative(texts, others, ids, matched, scale, bias[0])
+    _, d = derivative(texts, others, ids, matched, scale, shift)
     term = dot(halves(d_ref[...]), halves(bundle[:count]), (1, 0)) + dot(halves(d), others, (1, 0))
     for k, ref in enumerate(block_refs):
         ref[...] = term[k * cols:(k + 1) * cols]
 
 
-def image_sum_kernel(n_txt, own_ref, loss_ref, *refs):
-    messages, (image_loss, image_grad) = refs[:n_txt - 1], refs[n_txt - 1:]
-    rows, width = own_ref.shape
+def image_sum_kernel(own, first, second, got, image_loss, image_grad):
+    rows, width = own.shape
     across = width // LANES
     for r in range(rows // 8):
         for c in range(across):
             at = (slice(r * 8, r * 8 + 8), slice(c * LANES, (c + 1) * LANES))
-            image_grad[at] = own_ref[at] + sum(m[r * across + c] for m in messages)
-    image_loss[...] = (loss_ref[...] + sum(m[rows // 8 * across] for m in messages))[:1]
+            image_grad[at] = own[at] + first[at] + got[r * across + c]
+    image_loss[...] = (second[rows // 8 * across] + got[rows // 8 * across])[:1]
 
 
 def text_sum_kernel(_, *refs):
@@ -132,51 +135,56 @@
     rows, cols, width = image_emb.shape[0], text_emb.shape[0], image_emb.shape[1]
     count = n_txt * rows
     tiles = rows * width // (8 * LANES)
-    smem, whole = pl.BlockSpec(memory_space=pltpu.SMEM), pl.BlockSpec(memory_space=pltpu.VMEM)
-
-    text_blocks, image_blocks = {0: text_emb}, {0: image_emb}
-    for k in range(1, max(n_txt, chips)):
-        if k < chips:
-            text_blocks[k] = exchange(text_emb, "img", n_img, 2 * k)
-        if 1 < k < n_txt:
-            image_blocks[k] = exchange(image_emb, "txt", n_txt, k)
-    late_image, _ = lax.optimization_barrier((image_emb, text_blocks[1]))
-    image_blocks[1] = exchange(late_image, "txt", n_txt, 1)
-    near = jnp.concatenate([text_blocks[k] for k in range(chips)])
+    whole = pl.BlockSpec(memory_space=pltpu.VMEM)
+
+    second_image = exchange(image_emb, "txt", n_txt, 2)
+    text_blocks = [text_emb]
+    for k in range(1, chips):
+        text_blocks.append(exchange(text_emb, "img", n_img, 2 * k))
+    first_image = exchange(image_emb, "txt", n_txt, 1)
+    third_image = exchange(second_image, "txt", n_txt, 1)
+    near = jnp.concatenate(text_blocks)
     far = exchange(near, "img", n_img, 1)
-    pair_row = jnp.pad(pairs.astype(jnp.float32)[None], ((0, 7), (0, width - count)))
-    bundle = jnp.concatenate([image_blocks[k] for k in range(n_txt)] + [pair_row])
+    numbers = jnp.concatenate(
+        [pairs.astype(jnp.float32), jnp.broadcast_to(log_scale, LANES), jnp.broadcast_to(bias, LANES)]
+    )
+    numbers = jnp.pad(numbers[None], ((0, 7), (0, width - numbers.shape[0])))
+    bundle = jnp.concatenate([image_emb, first_image, second_image, third_image, numbers])
     pair = exchange(bundle, "img", n_img, 1)
 
-    own, loss_tile, d_near, *messages = pl.pallas_call(
+    own, first, second, third, d_near = pl.pallas_call(
         functools.partial(image_kernel, n_img, n_txt, rows, cols),
-        out_shape=[vmem((rows, width)), vmem((8, LANES)), vmem((chips * cols, count))]
-        + [vmem((tiles + 1, 8, LANES))] * (n_txt - 1),
-        in_specs=[smem] * 2 + [whole] * 3,
-        out_specs=[whole] * (2 + n_txt),
+        out_shape=[vmem((rows, width))] * 2
+        + [vmem((tiles + 1, 8, LANES))] * 2
+        + [vmem((chips * cols, count))],
+        in_specs=[whole] * 3,
+        out_specs=[whole] * 5,
         name="image_terms",
-    )(log_scale, bias, *in_vmem(bundle, near, far))
-    messages = [exchange(m, "txt", n_txt, k) for k, m in enumerate(messages, 1)]
-
-    blocks = pl.pallas_call(
+    )(*in_vmem(bundle, near, far))
+    blocks = list(pl.pallas_call(
         functools.partial(text_kernel, n_img, n_txt, rows, cols),
         out_shape=[vmem((cols, width))] * chips,
-        in_specs=[smem] * 2 + [whole] * 4,
+        in_specs=[whole] * 4,
         out_specs=[whole] * chips,
         name="text_terms",
-    )(log_scale, bias, *in_vmem(bundle, pair, near, d_near))
-    blocks = [blocks[0]] + [exchange(blocks[k], "img", n_img, 2 * k) for k in range(1, chips)]
+    )(*in_vmem(bundle, pair, near, d_near)))
+    third, _ = lax.optimization_barrier((exchange(third, "txt", n_txt, 1), blocks[0]))
+    second = second + third
+    got = exchange(second, "txt", n_txt, 2)
+    first = exchange(first, "txt", n_txt, 1)
+    for k in range(chips - 1, 0, -1):
+        blocks[k] = exchange(blocks[k], "img", n_img, 2 * k)
 
     image_loss, image_grad = pl.pallas_call(
-        functools.partial(image_sum_kernel, n_txt),
+        image_sum_kernel,
         out_shape=[
             jax.ShapeDtypeStruct((1, LANES), jnp.float32),
             jax.ShapeDtypeStruct(image_emb.shape, jnp.float32),
         ],
-        in_specs=[whole] * (1 + n_txt),
+        in_specs=[whole] * 4,
         out_specs=[whole] * 2,
         name="image_sums",
-    )(*in_vmem(own, loss_tile, *messages))
+    )(*in_vmem(own, first, second, got))
     text_grad = pl.pallas_call(
         text_sum_kernel,
         out_shape=jax.ShapeDtypeStruct(text_emb.shape, jnp.float32),
@@ -225,8 +233,8 @@
     sizes = (mesh.shape["img"], mesh.shape["txt"])
 
     def body(image_emb, *others):
-        small = all(n in (2, 4, 8) for n in sizes)
-        if small and sizes[1] * image_emb.shape[0] == LANES and image_emb.shape[0] % 8 == 0:
+        rows = image_emb.shape[0]
+        if sizes[0] in (4, 8) and sizes[1] == 4 and rows * 4 == LANES:
             return per_device(sizes, image_emb, *others)
         return per_device_large(image_emb, *others)
 

time: 33.8 us -> 36.1 us (1.068)
  waiting for transfers between devices: 8.61 us -> 14.7 us
  starting transfers between devices: 18.4 us -> 14.7 us
    ppermute x14, waiting for transfers between devices: 8.61 us -> 14.7 us  [exchange(): return lax.ppermute(x, axis, [(i, i ^ k) for i in range(n)])]
    ppermute x14, starting transfers between devices: 18.4 us -> 14.7 us  [exchange(): return lax.ppermute(x, axis, [(i, i ^ k) for i in range(n)])]
    unnamed x13 -> x11, local copies, waits for them, and re-layouts: 1.08 us -> 0.99 us
  transfers between devices with their start and end apart: 14 -> 14, of which waited for: 7 -> 6; matrix products, arithmetic and copies ran while one was open for 3% -> 3% of each run, Pallas kernels for 8% -> 8%
where the time goes in v9:
time: 36.1 us; the launch traced here: 35.9 us
  starting transfers between devices  14.7 us (41%)
  waiting for transfers between devices  14.7 us (41%)
  Pallas kernels  3.39 us (9%)
  between operations  2.13 us (6%)
  local copies, waits for them, and re-layouts  1.01 us (3%)
    ppermute x14, starting transfers between devices, exchange(): return lax.ppermute(x, axis, [(i, i ^ k) for i in range(n)])  14.7 us
    ppermute x14, waiting for transfers between devices, exchange(): return lax.ppermute(x, axis, [(i, i ^ k) for i in range(n)])  14.7 us
    pallas_call x1, Pallas kernels, per_device(): pl.pallas_call(functools.partial(image_kernel, n_img, n_txt, rows, cols),...  1.16 us
    unnamed x11, local copies, waits for them, and re-layouts  0.99 us
    pallas_call x1, Pallas kernels, per_device(): pl.pallas_call(functools.partial(text_kernel, n_img, n_txt, rows, cols),...  0.89 us
  transfers between devices with their start and end apart: 14, of which 6 were waited for; matrix products, arithmetic and copies ran while one was open for 3% of the time, Pallas kernels for 8%

profile of v9, /device:TPU:0, one launch (start us, length us, event | category | flops | bytes accessed | tf_op | source)
XLA Modules:
  0.0 35.9 jit_solution(17282175578773530485)
XLA Ops:
  0.6 0.0 copy-start
  0.6 3.1 %collective-permute-start = (f32[32,768]{1,0:T(8,128)}, f32[32,768]{1,0:T(8,128)S(1)}, u32[]{:S(2)}, u32[]{:S(2)}) collective-permute-start(f32[32,768]{1,0:T(8,128)} %param.5), channel_id=1, source_target_pairs={{0,1},{1,0},{2,3},{3,2},{4,5},{5,4},{6,7},{7,6},{8,9},{9,8},{10,11... | collective-permute-start | bytes 294920 | tf_op jit(solution)/shard_map/ppermute | solution.py:14
  3.7 2.6 %collective-permute-start.1 = (f32[32,768]{1,0:T(8,128)}, f32[32,768]{1,0:T(8,128)S(1)}, u32[]{:S(2)}, u32[]{:S(2)}) collective-permute-start(f32[32,768]{1,0:T(8,128)} %param.5), channel_id=1, source_target_pairs={{0,2},{1,3},{2,0},{3,1},{4,6},{5,7},{6,4},{7,5},{8,10},{9,11},{10,... | collective-permute-start | bytes 294920 | tf_op jit(solution)/shard_map/ppermute | solution.py:14
  6.3 1.5 %collective-permute-start.4 = (f32[32,768]{1,0:T(8,128)}, f32[32,768]{1,0:T(8,128)S(1)}, u32[]{:S(2)}, u32[]{:S(2)}) collective-permute-start(f32[32,768]{1,0:T(8,128)} %param.6), channel_id=1, source_target_pairs={{0,16},{4,20},{8,24},{12,28},{16,0},{20,4},{24,8},{28,12},{1,17},{... | collective-permute-start | bytes 294920 | tf_op jit(solution)/shard_map/ppermute | solution.py:14
  7.8 1.5 %collective-permute-start.3 = (f32[32,768]{1,0:T(8,128)}, f32[32,768]{1,0:T(8,128)S(1)}, u32[]{:S(2)}, u32[]{:S(2)}) collective-permute-start(f32[32,768]{1,0:T(8,128)} %param.6), channel_id=1, source_target_pairs={{0,8},{4,12},{8,0},{12,4},{16,24},{20,28},{24,16},{28,20},{1,9},{5... | collective-permute-start | bytes 294920 | tf_op jit(solution)/shard_map/ppermute | solution.py:14
  9.3 0.5 %collective-permute-start.5 = (f32[32,768]{1,0:T(8,128)}, f32[32,768]{1,0:T(8,128)S(1)}, u32[]{:S(2)}, u32[]{:S(2)}) collective-permute-start(f32[32,768]{1,0:T(8,128)} %param.6), channel_id=1, source_target_pairs={{0,24},{4,28},{8,16},{12,20},{16,8},{20,12},{24,0},{28,4},{1,25},{... | collective-permute-start | bytes 294920 | tf_op jit(solution)/shard_map/ppermute | solution.py:14
  9.8 0.9 %constant_dynamic-update-slice_fusion.7 = f32[128,768]{1,0:T(8,128)S(1)} fusion(f32[32,768]{1,0:T(8,128)} %param.6), kind=kLoop, calls=%fused_computation.8 | loop fusion | bytes 196608
  11.4 0.0 copy-start.1
  12.1 0.0 copy-done.1
  12.1 0.0 copy-done
  12.2 0.7 %collective-permute-done.3 = f32[32,768]{1,0:T(8,128)S(1)} collective-permute-done((f32[32,768]{1,0:T(8,128)}, f32[32,768]{1,0:T(8,128)S(1)}, u32[]{:S(2)}, u32[]{:S(2)}) %collective-permute-start.3) | collective-permute-done | bytes 98336 | tf_op jit(solution)/shard_map/ppermute | solution.py:14
  12.9 0.0 collective-permute-done.4
  12.9 2.1 %collective-permute-done.5 = f32[32,768]{1,0:T(8,128)S(1)} collective-permute-done((f32[32,768]{1,0:T(8,128)}, f32[32,768]{1,0:T(8,128)S(1)}, u32[]{:S(2)}, u32[]{:S(2)}) %collective-permute-start.5) | collective-permute-done | bytes 98336 | tf_op jit(solution)/shard_map/ppermute | solution.py:14
  15.1 0.1 collective-permute-start.6
  15.1 0.0 collective-permute-done.1
  15.2 0.5 %collective-permute-start.2 = (f32[32,768]{1,0:T(8,128)S(1)}, f32[32,768]{1,0:T(8,128)S(1)}, u32[]{:S(2)}, u32[]{:S(2)}) collective-permute-start(f32[32,768]{1,0:T(8,128)S(1)} %collective-permute-done.1), channel_id=1, source_target_pairs={{0,1},{1,0},{2,3},{3,2},{4,5},{5,4},{6,7},{7,6},{8,9},{9,8},{10,11... | collective-permute-start | bytes 294920 | tf_op jit(solution)/shard_map/ppermute | solution.py:14
  15.7 0.0 collective-permute-done
  15.7 4.7 %collective-permute-done.2 = f32[32,768]{1,0:T(8,128)S(1)} collective-permute-done((f32[32,768]{1,0:T(8,128)S(1)}, f32[32,768]{1,0:T(8,128)S(1)}, u32[]{:S(2)}, u32[]{:S(2)}) %collective-permute-start.2) | collective-permute-done | bytes 98336 | tf_op jit(solution)/shard_map/ppermute | solution.py:14
  20.4 0.1 collective-permute-start.9
  20.5 0.0 collective-permute-done.6.far
  20.5 1.2 %image_terms.1 = (f32[32,768]{1,0:T(8,128)S(1)}, f32[32,768]{1,0:T(8,128)S(1)}, f32[25,8,128]{2,1,0:T(8,128)S(1)}, f32[25,8,128]{2,1,0:T(8,128)S(1)}, f32[128,128]{1,0:T(8,128)S(1)}) custom-call(f32[136,768]{1,0:T(8,128)S(1)} %pad_dynamic-update-slice_fusion.bundle.refs_0_, f32[128,768]{1,0:T(8,128)S(1)} %constant_dynamic-update-slice_fusion.4.near.refs_2_, ...), custom_call_target="tpu_custom_call" | custom-call | tf_op jit(solution)/shard_map/image_terms/pallas_call | solution.py:155
  21.6 0.5 %collective-permute-start.8 = (f32[25,8,128]{2,1,0:T(8,128)S(1)}, f32[25,8,128]{2,1,0:T(8,128)S(1)}, u32[]{:S(2)}, u32[]{:S(2)}) collective-permute-start(f32[25,8,128]{2,1,0:T(8,128)S(1)} %get-tuple-element.18), channel_id=1, source_target_pairs={{0,1},{1,0},{2,3},{3,2},{4,5},{5,4},{6,7},{7,6},{8,9},{9,8},{10,11... | collective-permute-start | bytes 307208 | tf_op jit(solution)/shard_map/ppermute | solution.py:14
  22.2 0.0 collective-permute-done.9.refs_1_
  22.2 0.9 %text_terms.1 = (f32[32,768]{1,0:T(8,128)S(1)}, f32[32,768]{1,0:T(8,128)S(1)}, f32[32,768]{1,0:T(8,128)S(1)}, f32[32,768]{1,0:T(8,128)S(1)}) custom-call(f32[136,768]{1,0:T(8,128)S(1)} %pad_dynamic-update-slice_fusion.bundle.refs_0_, f32[136,768]{1,0:T(8,128)S(1)} %collective-permute-done.9.refs_1_, ...), custom_call_target="tpu_custom_call" | custom-call | tf_op jit(solution)/shard_map/text_terms/pallas_call | solution.py:164
  23.1 3.9 %collective-permute-done.8 = f32[25,8,128]{2,1,0:T(8,128)S(1)} collective-permute-done((f32[25,8,128]{2,1,0:T(8,128)S(1)}, f32[25,8,128]{2,1,0:T(8,128)S(1)}, u32[]{:S(2)}, u32[]{:S(2)}) %collective-permute-start.8) | collective-permute-done | bytes 102432 | tf_op jit(solution)/shard_map/ppermute | solution.py:14
  27.0 0.4 %collective-permute-start.10 = (f32[25,8,128]{2,1,0:T(8,128)S(1)}, f32[25,8,128]{2,1,0:T(8,128)S(1)}, u32[]{:S(2)}, u32[]{:S(2)}) collective-permute-start(f32[25,8,128]{2,1,0:T(8,128)S(1)} %add.5.second), channel_id=1, source_target_pairs={{0,2},{1,3},{2,0},{3,1},{4,6},{5,7},{6,4},{7,5},{8,10},{9,11},{10,... | collective-permute-start | bytes 307208 | tf_op jit(solution)/shard_map/ppermute | solution.py:14
  27.4 0.4 %collective-permute-start.7 = (f32[32,768]{1,0:T(8,128)S(1)}, f32[32,768]{1,0:T(8,128)S(1)}, u32[]{:S(2)}, u32[]{:S(2)}) collective-permute-start(f32[32,768]{1,0:T(8,128)S(1)} %get-tuple-element.16), channel_id=1, source_target_pairs={{0,1},{1,0},{2,3},{3,2},{4,5},{5,4},{6,7},{7,6},{8,9},{9,8},{10,11... | collective-permute-start | bytes 294920 | tf_op jit(solution)/shard_map/ppermute | solution.py:14
  27.9 0.5 %collective-permute-start.11 = (f32[32,768]{1,0:T(8,128)S(1)}, f32[32,768]{1,0:T(8,128)S(1)}, u32[]{:S(2)}, u32[]{:S(2)}) collective-permute-start(f32[32,768]{1,0:T(8,128)S(1)} %get-tuple-element.24), channel_id=1, source_target_pairs={{0,8},{4,12},{8,0},{12,4},{16,24},{20,28},{24,16},{28,20},{1,9},{5... | collective-permute-start | bytes 294920 | tf_op jit(solution)/shard_map/ppermute | solution.py:14
  28.4 1.3 %collective-permute-start.12 = (f32[32,768]{1,0:T(8,128)S(1)}, f32[32,768]{1,0:T(8,128)S(1)}, u32[]{:S(2)}, u32[]{:S(2)}) collective-permute-start(f32[32,768]{1,0:T(8,128)S(1)} %get-tuple-element.25), channel_id=1, source_target_pairs={{0,16},{4,20},{8,24},{12,28},{16,0},{20,4},{24,8},{28,12},{1,17},{... | collective-permute-start | bytes 294920 | tf_op jit(solution)/shard_map/ppermute | solution.py:14
  29.6 1.7 %collective-permute-start.13 = (f32[32,768]{1,0:T(8,128)S(1)}, f32[32,768]{1,0:T(8,128)S(1)}, u32[]{:S(2)}, u32[]{:S(2)}) collective-permute-start(f32[32,768]{1,0:T(8,128)S(1)} %get-tuple-element.26), channel_id=1, source_target_pairs={{0,24},{4,28},{8,16},{12,20},{16,8},{20,12},{24,0},{28,4},{1,25},{... | collective-permute-start | bytes 294920 | tf_op jit(solution)/shard_map/ppermute | solution.py:14
  31.3 1.5 %collective-permute-done.7.first = f32[32,768]{1,0:T(8,128)S(1)} collective-permute-done((f32[32,768]{1,0:T(8,128)S(1)}, f32[32,768]{1,0:T(8,128)S(1)}, u32[]{:S(2)}, u32[]{:S(2)}) %collective-permute-start.7) | collective-permute-done | bytes 98336 | tf_op jit(solution)/shard_map/ppermute | solution.py:14
  32.8 1.7 %collective-permute-done.10.got = f32[25,8,128]{2,1,0:T(8,128)S(1)} collective-permute-done((f32[25,8,128]{2,1,0:T(8,128)S(1)}, f32[25,8,128]{2,1,0:T(8,128)S(1)}, u32[]{:S(2)}, u32[]{:S(2)}) %collective-permute-start.10) | collective-permute-done | bytes 102432 | tf_op jit(solution)/shard_map/ppermute | solution.py:14
  34.5 0.7 %image_sums.1 = (f32[1,128]{1,0:T(1,128)}, f32[32,768]{1,0:T(8,128)}) custom-call(f32[32,768]{1,0:T(8,128)S(1)} %get-tuple-element.15.own, f32[32,768]{1,0:T(8,128)S(1)} %collective-permute-done.7.first, f32[25,8,128]{2,1,0:T(8,128)S(1)} %add.5.second, f32[25,8,128]{2,1,0:T(8,128)S(1)} %collective-permute-done.10.got), custom_call_target="tpu_custom_call" | custom-call | tf_op jit(solution)/shard_map/image_sums/pallas_call | solution.py:178
  35.2 0.0 collective-permute-done.11.refs_1_
  35.2 0.0 collective-permute-done.12.refs_2_
  35.2 0.0 collective-permute-done.13.refs_3_
  35.2 0.7 %text_sums.1 = f32[32,768]{1,0:T(8,128)} custom-call(f32[1,128]{1,0:T(1,128)} %get-tuple-element.22._, f32[32,768]{1,0:T(8,128)S(1)} %get-tuple-element.20.refs_0_, f32[32,768]{1,0:T(8,128)S(1)} %collective-permute-done.11.refs_1_, f32[32,768]{1,0:T(8,128)S(1)} %collective-permute-done.12.refs_2_, f32[32,768]{1,0:T(8,128)S(1)} %collective-permute-done.13.refs_3_), custom_call_target="tpu_custom_call" | custom-call | tf_op jit(solution)/shard_map/text_sums/pallas_call | solution.py:188
  (14 shorter events, 0.1 us)
Async XLA Ops:
  0.6 11.5 %copy-start = (f32[32,768]{1,0:T(8,128)S(1)}, f32[32,768]{1,0:T(8,128)}, u32[]{:S(2)}) copy-start(f32[32,768]{1,0:T(8,128)} %param.5) | copy-start | bytes 294916
  0.6 15.0 %collective-permute-start = (f32[32,768]{1,0:T(8,128)}, f32[32,768]{1,0:T(8,128)S(1)}, u32[]{:S(2)}, u32[]{:S(2)}) collective-permute-start(f32[32,768]{1,0:T(8,128)} %param.5), channel_id=1, source_target_pairs={{0,1},{1,0},{2,3},{3,2},{4,5},{5,4},{6,7},{7,6},{8,9},{9,8},{10,11... | collective-permute-start | bytes 294920 | tf_op jit(solution)/shard_map/ppermute | solution.py:14
  3.7 11.4 %collective-permute-start.1 = (f32[32,768]{1,0:T(8,128)}, f32[32,768]{1,0:T(8,128)S(1)}, u32[]{:S(2)}, u32[]{:S(2)}) collective-permute-start(f32[32,768]{1,0:T(8,128)} %param.5), channel_id=1, source_target_pairs={{0,2},{1,3},{2,0},{3,1},{4,6},{5,7},{6,4},{7,5},{8,10},{9,11},{10,... | collective-permute-start | bytes 294920 | tf_op jit(solution)/shard_map/ppermute | solution.py:14
  6.3 6.6 %collective-permute-start.4 = (f32[32,768]{1,0:T(8,128)}, f32[32,768]{1,0:T(8,128)S(1)}, u32[]{:S(2)}, u32[]{:S(2)}) collective-permute-start(f32[32,768]{1,0:T(8,128)} %param.6), channel_id=1, source_target_pairs={{0,16},{4,20},{8,24},{12,28},{16,0},{20,4},{24,8},{28,12},{1,17},{... | collective-permute-start | bytes 294920 | tf_op jit(solution)/shard_map/ppermute | solution.py:14
  7.8 5.1 %collective-permute-start.3 = (f32[32,768]{1,0:T(8,128)}, f32[32,768]{1,0:T(8,128)S(1)}, u32[]{:S(2)}, u32[]{:S(2)}) collective-permute-start(f32[32,768]{1,0:T(8,128)} %param.6), channel_id=1, source_target_pairs={{0,8},{4,12},{8,0},{12,4},{16,24},{20,28},{24,16},{28,20},{1,9},{5... | collective-permute-start | bytes 294920 | tf_op jit(solution)/shard_map/ppermute | solution.py:14
  9.3 5.7 %collective-permute-start.5 = (f32[32,768]{1,0:T(8,128)}, f32[32,768]{1,0:T(8,128)S(1)}, u32[]{:S(2)}, u32[]{:S(2)}) collective-permute-start(f32[32,768]{1,0:T(8,128)} %param.6), channel_id=1, source_target_pairs={{0,24},{4,28},{8,16},{12,20},{16,8},{20,12},{24,0},{28,4},{1,25},{... | collective-permute-start | bytes 294920 | tf_op jit(solution)/shard_map/ppermute | solution.py:14
  11.4 0.7 %copy-start.1 = (s32[128]{0:T(128)S(1)}, s32[128]{0:T(128)}, u32[]{:S(2)}) copy-start(s32[128]{0:T(128)} %param.7) | copy-start | bytes 1540
  15.1 5.4 %collective-permute-start.6 = (f32[128,768]{1,0:T(8,128)S(1)}, f32[128,768]{1,0:T(8,128)S(1)}, u32[]{:S(2)}, u32[]{:S(2)}) collective-permute-start(f32[128,768]{1,0:T(8,128)S(1)} %constant_dynamic-update-slice_fusion.4.near.refs_2_), channel_id=1, source_target_pairs={{0,4},{4,0},{8,12},{12,8},{16,20},{20,16},{24,28},{28,24},{1,5},{5... | collective-permute-start | bytes 1179656 | tf_op jit(solution)/shard_map/ppermute | solution.py:14
  15.2 5.2 %collective-permute-start.2 = (f32[32,768]{1,0:T(8,128)S(1)}, f32[32,768]{1,0:T(8,128)S(1)}, u32[]{:S(2)}, u32[]{:S(2)}) collective-permute-start(f32[32,768]{1,0:T(8,128)S(1)} %collective-permute-done.1), channel_id=1, source_target_pairs={{0,1},{1,0},{2,3},{3,2},{4,5},{5,4},{6,7},{7,6},{8,9},{9,8},{10,11... | collective-permute-start | bytes 294920 | tf_op jit(solution)/shard_map/ppermute | solution.py:14
  20.4 1.8 %collective-permute-start.9 = (f32[136,768]{1,0:T(8,128)S(1)}, f32[136,768]{1,0:T(8,128)S(1)}, u32[]{:S(2)}, u32[]{:S(2)}) collective-permute-start(f32[136,768]{1,0:T(8,128)S(1)} %pad_dynamic-update-slice_fusion.bundle.refs_0_), channel_id=1, source_target_pairs={{0,4},{4,0},{8,12},{12,8},{16,20},{20,16},{24,28},{28,24},{1,5},{5... | collective-permute-start | bytes 1253384 | tf_op jit(solution)/shard_map/ppermute | solution.py:14
  21.6 5.3 %collective-permute-start.8 = (f32[25,8,128]{2,1,0:T(8,128)S(1)}, f32[25,8,128]{2,1,0:T(8,128)S(1)}, u32[]{:S(2)}, u32[]{:S(2)}) collective-permute-start(f32[25,8,128]{2,1,0:T(8,128)S(1)} %get-tuple-element.18), channel_id=1, source_target_pairs={{0,1},{1,0},{2,3},{3,2},{4,5},{5,4},{6,7},{7,6},{8,9},{9,8},{10,11... | collective-permute-start | bytes 307208 | tf_op jit(solution)/shard_map/ppermute | solution.py:14
  27.0 7.5 %collective-permute-start.10 = (f32[25,8,128]{2,1,0:T(8,128)S(1)}, f32[25,8,128]{2,1,0:T(8,128)S(1)}, u32[]{:S(2)}, u32[]{:S(2)}) collective-permute-start(f32[25,8,128]{2,1,0:T(8,128)S(1)} %add.5.second), channel_id=1, source_target_pairs={{0,2},{1,3},{2,0},{3,1},{4,6},{5,7},{6,4},{7,5},{8,10},{9,11},{10,... | collective-permute-start | bytes 307208 | tf_op jit(solution)/shard_map/ppermute | solution.py:14
  27.4 5.4 %collective-permute-start.7 = (f32[32,768]{1,0:T(8,128)S(1)}, f32[32,768]{1,0:T(8,128)S(1)}, u32[]{:S(2)}, u32[]{:S(2)}) collective-permute-start(f32[32,768]{1,0:T(8,128)S(1)} %get-tuple-element.16), channel_id=1, source_target_pairs={{0,1},{1,0},{2,3},{3,2},{4,5},{5,4},{6,7},{7,6},{8,9},{9,8},{10,11... | collective-permute-start | bytes 294920 | tf_op jit(solution)/shard_map/ppermute | solution.py:14
  27.9 7.4 %collective-permute-start.11 = (f32[32,768]{1,0:T(8,128)S(1)}, f32[32,768]{1,0:T(8,128)S(1)}, u32[]{:S(2)}, u32[]{:S(2)}) collective-permute-start(f32[32,768]{1,0:T(8,128)S(1)} %get-tuple-element.24), channel_id=1, source_target_pairs={{0,8},{4,12},{8,0},{12,4},{16,24},{20,28},{24,16},{28,20},{1,9},{5... | collective-permute-start | bytes 294920 | tf_op jit(solution)/shard_map/ppermute | solution.py:14
  28.4 6.8 %collective-permute-start.12 = (f32[32,768]{1,0:T(8,128)S(1)}, f32[32,768]{1,0:T(8,128)S(1)}, u32[]{:S(2)}, u32[]{:S(2)}) collective-permute-start(f32[32,768]{1,0:T(8,128)S(1)} %get-tuple-element.25), channel_id=1, source_target_pairs={{0,16},{4,20},{8,24},{12,28},{16,0},{20,4},{24,8},{28,12},{1,17},{... | collective-permute-start | bytes 294920 | tf_op jit(solution)/shard_map/ppermute | solution.py:14
  29.6 5.6 %collective-permute-start.13 = (f32[32,768]{1,0:T(8,128)S(1)}, f32[32,768]{1,0:T(8,128)S(1)}, u32[]{:S(2)}, u32[]{:S(2)}) collective-permute-start(f32[32,768]{1,0:T(8,128)S(1)} %get-tuple-element.26), channel_id=1, source_target_pairs={{0,24},{4,28},{8,16},{12,20},{16,8},{20,12},{24,0},{28,4},{1,25},{... | collective-permute-start | bytes 294920 | tf_op jit(solution)/shard_map/ppermute | solution.py:14

commit v10 on v9

--- a/solution.py
+++ b/solution.py
@@ -12,6 +12,10 @@
 
 def exchange(x, axis, n, k):
     return lax.ppermute(x, axis, [(i, i ^ k) for i in range(n)])
+
+
+def after(x, other):
+    return lax.optimization_barrier((x, other))[0]
 
 
 def halves(x):
@@ -66,11 +70,8 @@
     return matched.astype(jnp.int32), scale, bundle[count:count + 1, 2 * LANES:3 * LANES]
 
 
-def image_kernel(
-    n_img, n_txt, rows, cols, bundle, near, far, own, first, second, third, d_near
-):
+def image_kernel(n_img, n_txt, rows, cols, bundle, near, far, own, loss_ref, d_near, *messages):
     count = n_txt * rows
-    me_txt = lax.axis_index("txt")
     matched, scale, shift = row_of_numbers(bundle, rows, count)
     images = halves(bundle[:count])
     texts = halves(jnp.concatenate([near[...], far[...]]))
@@ -79,11 +80,11 @@
     d_near[...] = d[:near.shape[0]]
     term = dot(halves(d), texts, (0, 0))
     own[...] = term[:rows]
-    first[...] = term[rows:2 * rows]
-    loss_row = untwist(jnp.sum(loss, axis=0, keepdims=True), rows, me_txt)
+    loss_row = untwist(jnp.sum(loss, axis=0, keepdims=True), rows, lax.axis_index("txt"))
     loss_tile = jnp.broadcast_to(loss_row, (8, LANES))
+    loss_ref[...] = loss_tile
     across = term.shape[1] // LANES
-    for k, ref in ((2, second), (3, third)):
+    for k, ref in enumerate(messages, 1):
         for r in range(rows // 8):
             for c in range(across):
                 ref[r * across + c] = term[
@@ -106,14 +107,15 @@
         ref[...] = term[k * cols:(k + 1) * cols]
 
 
-def image_sum_kernel(own, first, second, got, image_loss, image_grad):
-    rows, width = own.shape
+def image_sum_kernel(n_txt, own_ref, loss_ref, *refs):
+    messages, (image_loss, image_grad) = refs[:n_txt - 1], refs[n_txt - 1:]
+    rows, width = own_ref.shape
     across = width // LANES
     for r in range(rows // 8):
         for c in range(across):
             at = (slice(r * 8, r * 8 + 8), slice(c * LANES, (c + 1) * LANES))
-            image_grad[at] = own[at] + first[at] + got[r * across + c]
-    image_loss[...] = (second[rows // 8 * across] + got[rows // 8 * across])[:1]
+            image_grad[at] = own_ref[at] + sum(m[r * across + c] for m in messages)
+    image_loss[...] = (loss_ref[...] + sum(m[rows // 8 * across] for m in messages))[:1]
 
 
 def text_sum_kernel(_, *refs):
@@ -137,54 +139,53 @@
     tiles = rows * width // (8 * LANES)
     whole = pl.BlockSpec(memory_space=pltpu.VMEM)
 
-    second_image = exchange(image_emb, "txt", n_txt, 2)
-    text_blocks = [text_emb]
-    for k in range(1, chips):
-        text_blocks.append(exchange(text_emb, "img", n_img, 2 * k))
-    first_image = exchange(image_emb, "txt", n_txt, 1)
-    third_image = exchange(second_image, "txt", n_txt, 1)
+    text_blocks, image_blocks = [text_emb], {0: image_emb}
+    for k in range(1, max(n_txt, chips)):
+        if k < chips:
+            text_blocks.append(exchange(text_emb, "img", n_img, 2 * k))
+        if 1 < k < n_txt:
+            image_blocks[k] = exchange(image_emb, "txt", n_txt, k)
+    image_blocks[1] = exchange(after(image_emb, text_blocks[1]), "txt", n_txt, 1)
     near = jnp.concatenate(text_blocks)
     far = exchange(near, "img", n_img, 1)
     numbers = jnp.concatenate(
         [pairs.astype(jnp.float32), jnp.broadcast_to(log_scale, LANES), jnp.broadcast_to(bias, LANES)]
     )
     numbers = jnp.pad(numbers[None], ((0, 7), (0, width - numbers.shape[0])))
-    bundle = jnp.concatenate([image_emb, first_image, second_image, third_image, numbers])
-    pair = exchange(bundle, "img", n_img, 1)
-
-    own, first, second, third, d_near = pl.pallas_call(
+    bundle = jnp.concatenate([image_blocks[k] for k in range(n_txt)] + [numbers])
+
+    own, loss_tile, d_near, *messages = pl.pallas_call(
         functools.partial(image_kernel, n_img, n_txt, rows, cols),
-        out_shape=[vmem((rows, width))] * 2
-        + [vmem((tiles + 1, 8, LANES))] * 2
-        + [vmem((chips * cols, count))],
+        out_shape=[vmem((rows, width)), vmem((8, LANES)), vmem((chips * cols, count))]
+        + [vmem((tiles + 1, 8, LANES))] * (n_txt - 1),
         in_specs=[whole] * 3,
-        out_specs=[whole] * 5,
+        out_specs=[whole] * (2 + n_txt),
         name="image_terms",
     )(*in_vmem(bundle, near, far))
-    blocks = list(pl.pallas_call(
+    messages = [exchange(messages[k - 1], "txt", n_txt, k) for k in range(n_txt - 1, 0, -1)]
+
+    pair = exchange(after(bundle, own), "img", n_img, 1)
+    blocks = pl.pallas_call(
         functools.partial(text_kernel, n_img, n_txt, rows, cols),
         out_shape=[vmem((cols, width))] * chips,
         in_specs=[whole] * 4,
         out_specs=[whole] * chips,
         name="text_terms",
-    )(*in_vmem(bundle, pair, near, d_near)))
-    third, _ = lax.optimization_barrier((exchange(third, "txt", n_txt, 1), blocks[0]))
-    second = second + third
-    got = exchange(second, "txt", n_txt, 2)
-    first = exchange(first, "txt", n_txt, 1)
-    for k in range(chips - 1, 0, -1):
-        blocks[k] = exchange(blocks[k], "img", n_img, 2 * k)
+    )(*in_vmem(bundle, pair, near, d_near))
+    blocks = list(blocks)
+    blocks[1] = after(blocks[1], messages[-1])
+    blocks = [exchange(blocks[k], "img", n_img, 2 * k) for k in range(chips - 1, 0, -1)] + [blocks[0]]
 
     image_loss, image_grad = pl.pallas_call(
-        image_sum_kernel,
+        functools.partial(image_sum_kernel, n_txt),
         out_shape=[
             jax.ShapeDtypeStruct((1, LANES), jnp.float32),
             jax.ShapeDtypeStruct(image_emb.shape, jnp.float32),
         ],
-        in_specs=[whole] * 4,
+        in_specs=[whole] * (1 + n_txt),
         out_specs=[whole] * 2,
         name="image_sums",
-    )(*in_vmem(own, first, second, got))
+    )(*in_vmem(own, loss_tile, *messages))
     text_grad = pl.pallas_call(
         text_sum_kernel,
         out_shape=jax.ShapeDtypeStruct(text_emb.shape, jnp.float32),

time: 36.1 us -> 33.4 us (0.925)
  waiting for transfers between devices: 14.7 us -> 9.34 us
  starting transfers between devices: 14.7 us -> 16.4 us
  local copies, waits for them, and re-layouts: 1.01 us -> 1.84 us
    ppermute x14, waiting for transfers between devices: 14.7 us -> 9.34 us  [exchange(): return lax.ppermute(x, axis, [(i, i ^ k) for i in range(n)])]
    ppermute x14, starting transfers between devices: 14.7 us -> 16.4 us  [exchange(): return lax.ppermute(x, axis, [(i, i ^ k) for i in range(n)])]
    unnamed x11 -> x13, local copies, waits for them, and re-layouts: 0.99 us -> 1.82 us
  transfers between devices with their start and end apart: 14 -> 14, of which waited for: 6 -> 5; matrix products, arithmetic and copies ran while one was open for 3% -> 3% of each run, Pallas kernels for 8% -> 5%
where the time goes in v10:
time: 33.4 us; the launch traced here: 33.2 us
  starting transfers between devices  16.4 us (49%)
  waiting for transfers between devices  9.34 us (28%)
  Pallas kernels  3.41 us (10%)
  between operations  2.14 us (6%)
  local copies, waits for them, and re-layouts  1.84 us (6%)
    ppermute x14, starting transfers between devices, exchange(): return lax.ppermute(x, axis, [(i, i ^ k) for i in range(n)])  16.4 us
    ppermute x14, waiting for transfers between devices, exchange(): return lax.ppermute(x, axis, [(i, i ^ k) for i in range(n)])  9.34 us
    unnamed x13, local copies, waits for them, and re-layouts  1.82 us
    pallas_call x1, Pallas kernels, per_device(): pl.pallas_call(functools.partial(image_kernel, n_img, n_txt, rows, cols),...  1.16 us
    pallas_call x1, Pallas kernels, per_device(): pl.pallas_call(functools.partial(text_kernel, n_img, n_txt, rows, cols),...  0.89 us
    pallas_call x1, Pallas kernels, per_device(): pl.pallas_call(text_sum_kernel, out_shape=jax.ShapeDtypeStruct(text_emb.s...  0.68 us
    pallas_call x1, Pallas kernels, per_device(): pl.pallas_call(functools.partial(image_sum_kernel, n_txt), out_shape=[jax...  0.67 us
  transfers between devices with their start and end apart: 14, of which 5 were waited for; matrix products, arithmetic and copies ran while one was open for 3% of the time, Pallas kernels for 5%

profile of v10, /device:TPU:0, one launch (start us, length us, event | category | flops | bytes accessed | tf_op | source)
XLA Modules:
  0.0 33.2 jit_solution(1977489158291626657)
XLA Ops:
  0.6 0.0 copy-start
  0.6 4.1 %collective-permute-start.2 = (f32[32,768]{1,0:T(8,128)}, f32[32,768]{1,0:T(8,128)S(1)}, u32[]{:S(2)}, u32[]{:S(2)}) collective-permute-start(f32[32,768]{1,0:T(8,128)} %param.5), channel_id=1, source_target_pairs={{0,2},{1,3},{2,0},{3,1},{4,6},{5,7},{6,4},{7,5},{8,10},{9,11},{10,... | collective-permute-start | bytes 294920 | tf_op jit(solution)/shard_map/ppermute | solution.py:14
  4.7 1.3 %collective-permute-start.3 = (f32[32,768]{1,0:T(8,128)}, f32[32,768]{1,0:T(8,128)S(1)}, u32[]{:S(2)}, u32[]{:S(2)}) collective-permute-start(f32[32,768]{1,0:T(8,128)} %param.5), channel_id=1, source_target_pairs={{0,3},{1,2},{2,1},{3,0},{4,7},{5,6},{6,5},{7,4},{8,11},{9,10},{10,... | collective-permute-start | bytes 294920 | tf_op jit(solution)/shard_map/ppermute | solution.py:14
  6.1 1.5 %collective-permute-start = (f32[32,768]{1,0:T(8,128)}, f32[32,768]{1,0:T(8,128)S(1)}, u32[]{:S(2)}, u32[]{:S(2)}) collective-permute-start(f32[32,768]{1,0:T(8,128)} %param.6), channel_id=1, source_target_pairs={{0,8},{4,12},{8,0},{12,4},{16,24},{20,28},{24,16},{28,20},{1,9},{5... | collective-permute-start | bytes 294920 | tf_op jit(solution)/shard_map/ppermute | solution.py:14
  7.6 1.5 %collective-permute-start.4 = (f32[32,768]{1,0:T(8,128)}, f32[32,768]{1,0:T(8,128)S(1)}, u32[]{:S(2)}, u32[]{:S(2)}) collective-permute-start(f32[32,768]{1,0:T(8,128)} %param.6), channel_id=1, source_target_pairs={{0,16},{4,20},{8,24},{12,28},{16,0},{20,4},{24,8},{28,12},{1,17},{... | collective-permute-start | bytes 294920 | tf_op jit(solution)/shard_map/ppermute | solution.py:14
  9.1 0.5 %collective-permute-start.5 = (f32[32,768]{1,0:T(8,128)}, f32[32,768]{1,0:T(8,128)S(1)}, u32[]{:S(2)}, u32[]{:S(2)}) collective-permute-start(f32[32,768]{1,0:T(8,128)} %param.6), channel_id=1, source_target_pairs={{0,24},{4,28},{8,16},{12,20},{16,8},{20,12},{24,0},{28,4},{1,25},{... | collective-permute-start | bytes 294920 | tf_op jit(solution)/shard_map/ppermute | solution.py:14
  9.6 0.9 %constant_dynamic-update-slice_fusion.3 = f32[136,768]{1,0:T(8,128)S(1)} fusion(f32[32,768]{1,0:T(8,128)} %param.5), kind=kLoop, calls=%fused_computation.4 | loop fusion | bytes 196608
  11.1 0.0 copy-start.2
  11.8 0.0 copy-done.2
  11.9 0.0 copy-done
  11.9 0.0 copy-start.1
  11.9 0.0 collective-permute-done
  11.9 0.9 %copy-done.1 = f32[32,768]{1,0:T(8,128)S(1)} copy-done((f32[32,768]{1,0:T(8,128)S(1)}, f32[32,768]{1,0:T(8,128)}, u32[]{:S(2)}) %copy-start.1) | copy-done | bytes 98328
  12.8 0.2 collective-permute-start.1
  13.0 0.4 %collective-permute-done.4 = f32[32,768]{1,0:T(8,128)S(1)} collective-permute-done((f32[32,768]{1,0:T(8,128)}, f32[32,768]{1,0:T(8,128)S(1)}, u32[]{:S(2)}, u32[]{:S(2)}) %collective-permute-start.4) | collective-permute-done | bytes 98336 | tf_op jit(solution)/shard_map/ppermute | solution.py:14
  13.5 1.4 %collective-permute-done.5 = f32[32,768]{1,0:T(8,128)S(1)} collective-permute-done((f32[32,768]{1,0:T(8,128)}, f32[32,768]{1,0:T(8,128)S(1)}, u32[]{:S(2)}, u32[]{:S(2)}) %collective-permute-start.5) | collective-permute-done | bytes 98336 | tf_op jit(solution)/shard_map/ppermute | solution.py:14
  14.8 0.1 collective-permute-start.6
  14.9 2.5 %collective-permute-done.1 = f32[32,768]{1,0:T(8,128)S(1)} collective-permute-done((f32[32,768]{1,0:T(8,128)S(1)}, f32[32,768]{1,0:T(8,128)S(1)}, u32[]{:S(2)}, u32[]{:S(2)}) %collective-permute-start.1) | collective-permute-done | bytes 98336 | tf_op jit(solution)/shard_map/ppermute | solution.py:14
  17.4 0.0 collective-permute-done.2
  17.4 0.0 collective-permute-done.3
  17.5 0.0 collective-permute-done.6.far
  17.5 1.2 %image_terms.1 = (f32[32,768]{1,0:T(8,128)S(1)}, f32[8,128]{1,0:T(8,128)S(1)}, f32[128,128]{1,0:T(8,128)S(1)}, f32[25,8,128]{2,1,0:T(8,128)S(1)}, f32[25,8,128]{2,1,0:T(8,128)S(1)}, /*index=5*/f32[25,8,128]{2,1,0:T(8,128)S(1)}) custom-call(f32[136,768]{1,0:T(8,128)S(1)} %pad_dynamic-update-slice_fusion.bundle.refs_0_, ...), custom_call_target="tpu_custom_call" | custom-call | tf_op jit(solution)/shard_map/image_terms/pallas_call | solution.py:157
  18.7 0.1 collective-permute-start.10
  18.7 0.3 collective-permute-start.9
  19.0 2.9 %collective-permute-start.7 = (f32[25,8,128]{2,1,0:T(8,128)S(1)}, f32[25,8,128]{2,1,0:T(8,128)S(1)}, u32[]{:S(2)}, u32[]{:S(2)}) collective-permute-start(f32[25,8,128]{2,1,0:T(8,128)S(1)} %get-tuple-element.21), channel_id=1, source_target_pairs={{0,3},{1,2},{2,1},{3,0},{4,7},{5,6},{6,5},{7,4},{8,11},{9,10},{10,... | collective-permute-start | bytes 307208 | tf_op jit(solution)/shard_map/ppermute | solution.py:14
  22.0 0.3 %collective-permute-start.8 = (f32[25,8,128]{2,1,0:T(8,128)S(1)}, f32[25,8,128]{2,1,0:T(8,128)S(1)}, u32[]{:S(2)}, u32[]{:S(2)}) collective-permute-start(f32[25,8,128]{2,1,0:T(8,128)S(1)} %get-tuple-element.22), channel_id=1, source_target_pairs={{0,2},{1,3},{2,0},{3,1},{4,6},{5,7},{6,4},{7,5},{8,10},{9,11},{10,... | collective-permute-start | bytes 307208 | tf_op jit(solution)/shard_map/ppermute | solution.py:14
  22.3 0.0 collective-permute-done.10.refs_1_
  22.3 0.9 %text_terms.1 = (f32[32,768]{1,0:T(8,128)S(1)}, f32[32,768]{1,0:T(8,128)S(1)}, f32[32,768]{1,0:T(8,128)S(1)}, f32[32,768]{1,0:T(8,128)S(1)}) custom-call(f32[136,768]{1,0:T(8,128)S(1)} %pad_dynamic-update-slice_fusion.bundle.refs_0_, f32[136,768]{1,0:T(8,128)S(1)} %collective-permute-done.10.refs_1_, ...), custom_call_target="tpu_custom_call" | custom-call | tf_op jit(solution)/shard_map/text_terms/pallas_call | solution.py:168
  23.2 2.5 %collective-permute-start.11 = (f32[32,768]{1,0:T(8,128)S(1)}, f32[32,768]{1,0:T(8,128)S(1)}, u32[]{:S(2)}, u32[]{:S(2)}) collective-permute-start(f32[32,768]{1,0:T(8,128)S(1)} %get-tuple-element.28), channel_id=1, source_target_pairs={{0,24},{4,28},{8,16},{12,20},{16,8},{20,12},{24,0},{28,4},{1,25},{... | collective-permute-start | bytes 294920 | tf_op jit(solution)/shard_map/ppermute | solution.py:14
  25.7 0.5 %collective-permute-start.12 = (f32[32,768]{1,0:T(8,128)S(1)}, f32[32,768]{1,0:T(8,128)S(1)}, u32[]{:S(2)}, u32[]{:S(2)}) collective-permute-start(f32[32,768]{1,0:T(8,128)S(1)} %get-tuple-element.29), channel_id=1, source_target_pairs={{0,16},{4,20},{8,24},{12,28},{16,0},{20,4},{24,8},{28,12},{1,17},{... | collective-permute-start | bytes 294920 | tf_op jit(solution)/shard_map/ppermute | solution.py:14
  26.2 0.0 collective-permute-done.9.refs_2_
  26.2 0.5 %collective-permute-start.13 = (f32[32,768]{1,0:T(8,128)S(1)}, f32[32,768]{1,0:T(8,128)S(1)}, u32[]{:S(2)}, u32[]{:S(2)}) collective-permute-start(f32[32,768]{1,0:T(8,128)S(1)} %get-tuple-element.31), channel_id=1, source_target_pairs={{0,8},{4,12},{8,0},{12,4},{16,24},{20,28},{24,16},{28,20},{1,9},{5... | collective-permute-start | bytes 294920 | tf_op jit(solution)/shard_map/ppermute | solution.py:14
  26.8 1.2 %collective-permute-done.7.refs_0_ = f32[25,8,128]{2,1,0:T(8,128)S(1)} collective-permute-done((f32[25,8,128]{2,1,0:T(8,128)S(1)}, f32[25,8,128]{2,1,0:T(8,128)S(1)}, u32[]{:S(2)}, u32[]{:S(2)}) %collective-permute-start.7) | collective-permute-done | bytes 102432 | tf_op jit(solution)/shard_map/ppermute | solution.py:14
  27.9 3.9 %collective-permute-done.8.refs_1_ = f32[25,8,128]{2,1,0:T(8,128)S(1)} collective-permute-done((f32[25,8,128]{2,1,0:T(8,128)S(1)}, f32[25,8,128]{2,1,0:T(8,128)S(1)}, u32[]{:S(2)}, u32[]{:S(2)}) %collective-permute-start.8) | collective-permute-done | bytes 102432 | tf_op jit(solution)/shard_map/ppermute | solution.py:14
  31.8 0.7 %image_sums.1 = (f32[1,128]{1,0:T(1,128)}, f32[32,768]{1,0:T(8,128)}) custom-call(f32[32,768]{1,0:T(8,128)S(1)} %get-tuple-element.19.own_ref, f32[8,128]{1,0:T(8,128)S(1)} %get-tuple-element.20.loss_ref, f32[25,8,128]{2,1,0:T(8,128)S(1)} %collective-permute-done.7.refs_0_, f32[25,8,128]{2,1,0:T(8,128)S(1)} %collective-permute-done.8.refs_1_, ...), custom_call_target="tpu_custom_call" | custom-call | tf_op jit(solution)/shard_map/image_sums/pallas_call | solution.py:179
  32.5 0.0 collective-permute-done.11.refs_0_
  32.5 0.0 collective-permute-done.12.refs_1_
  32.5 0.0 collective-permute-done.13.refs_2_
  32.5 0.7 %text_sums.1 = f32[32,768]{1,0:T(8,128)} custom-call(f32[1,128]{1,0:T(1,128)} %get-tuple-element.24._, f32[32,768]{1,0:T(8,128)S(1)} %collective-permute-done.11.refs_0_, f32[32,768]{1,0:T(8,128)S(1)} %collective-permute-done.12.refs_1_, f32[32,768]{1,0:T(8,128)S(1)} %collective-permute-done.13.refs_2_, f32[32,768]{1,0:T(8,128)S(1)} %get-tuple-element.32.refs_3_), custom_call_target="tpu_custom_call" | custom-call | tf_op jit(solution)/shard_map/text_sums/pallas_call | solution.py:189
  (13 shorter events, 0.1 us)
Async XLA Ops:
  0.6 11.2 %copy-start = (f32[32,768]{1,0:T(8,128)S(1)}, f32[32,768]{1,0:T(8,128)}, u32[]{:S(2)}) copy-start(f32[32,768]{1,0:T(8,128)} %param.6) | copy-start | bytes 294916
  0.6 16.8 %collective-permute-start.2 = (f32[32,768]{1,0:T(8,128)}, f32[32,768]{1,0:T(8,128)S(1)}, u32[]{:S(2)}, u32[]{:S(2)}) collective-permute-start(f32[32,768]{1,0:T(8,128)} %param.5), channel_id=1, source_target_pairs={{0,2},{1,3},{2,0},{3,1},{4,6},{5,7},{6,4},{7,5},{8,10},{9,11},{10,... | collective-permute-start | bytes 294920 | tf_op jit(solution)/shard_map/ppermute | solution.py:14
  4.7 12.7 %collective-permute-start.3 = (f32[32,768]{1,0:T(8,128)}, f32[32,768]{1,0:T(8,128)S(1)}, u32[]{:S(2)}, u32[]{:S(2)}) collective-permute-start(f32[32,768]{1,0:T(8,128)} %param.5), channel_id=1, source_target_pairs={{0,3},{1,2},{2,1},{3,0},{4,7},{5,6},{6,5},{7,4},{8,11},{9,10},{10,... | collective-permute-start | bytes 294920 | tf_op jit(solution)/shard_map/ppermute | solution.py:14
  6.1 5.8 %collective-permute-start = (f32[32,768]{1,0:T(8,128)}, f32[32,768]{1,0:T(8,128)S(1)}, u32[]{:S(2)}, u32[]{:S(2)}) collective-permute-start(f32[32,768]{1,0:T(8,128)} %param.6), channel_id=1, source_target_pairs={{0,8},{4,12},{8,0},{12,4},{16,24},{20,28},{24,16},{28,20},{1,9},{5... | collective-permute-start | bytes 294920 | tf_op jit(solution)/shard_map/ppermute | solution.py:14
  7.6 5.9 %collective-permute-start.4 = (f32[32,768]{1,0:T(8,128)}, f32[32,768]{1,0:T(8,128)S(1)}, u32[]{:S(2)}, u32[]{:S(2)}) collective-permute-start(f32[32,768]{1,0:T(8,128)} %param.6), channel_id=1, source_target_pairs={{0,16},{4,20},{8,24},{12,28},{16,0},{20,4},{24,8},{28,12},{1,17},{... | collective-permute-start | bytes 294920 | tf_op jit(solution)/shard_map/ppermute | solution.py:14
  9.1 5.7 %collective-permute-start.5 = (f32[32,768]{1,0:T(8,128)}, f32[32,768]{1,0:T(8,128)S(1)}, u32[]{:S(2)}, u32[]{:S(2)}) collective-permute-start(f32[32,768]{1,0:T(8,128)} %param.6), channel_id=1, source_target_pairs={{0,24},{4,28},{8,16},{12,20},{16,8},{20,12},{24,0},{28,4},{1,25},{... | collective-permute-start | bytes 294920 | tf_op jit(solution)/shard_map/ppermute | solution.py:14
  11.1 0.7 %copy-start.2 = (s32[128]{0:T(128)S(1)}, s32[128]{0:T(128)}, u32[]{:S(2)}) copy-start(s32[128]{0:T(128)} %param.7) | copy-start | bytes 1540
  11.9 0.9 %copy-start.1 = (f32[32,768]{1,0:T(8,128)S(1)}, f32[32,768]{1,0:T(8,128)}, u32[]{:S(2)}) copy-start(f32[32,768]{1,0:T(8,128)} %param.5) | copy-start | bytes 294916
  12.8 4.6 %collective-permute-start.1 = (f32[32,768]{1,0:T(8,128)S(1)}, f32[32,768]{1,0:T(8,128)S(1)}, u32[]{:S(2)}, u32[]{:S(2)}) collective-permute-start(f32[32,768]{1,0:T(8,128)S(1)} %copy-done.1), channel_id=1, source_target_pairs={{0,1},{1,0},{2,3},{3,2},{4,5},{5,4},{6,7},{7,6},{8,9},{9,8},{10,11... | collective-permute-start | bytes 294920 | tf_op jit(solution)/shard_map/ppermute | solution.py:14
  14.8 2.6 %collective-permute-start.6 = (f32[128,768]{1,0:T(8,128)S(1)}, f32[128,768]{1,0:T(8,128)S(1)}, u32[]{:S(2)}, u32[]{:S(2)}) collective-permute-start(f32[128,768]{1,0:T(8,128)S(1)} %constant_dynamic-update-slice_fusion.4.near.refs_2_), channel_id=1, source_target_pairs={{0,4},{4,0},{8,12},{12,8},{16,20},{20,16},{24,28},{28,24},{1,5},{5... | collective-permute-start | bytes 1179656 | tf_op jit(solution)/shard_map/ppermute | solution.py:14
  18.7 3.6 %collective-permute-start.10 = (f32[136,768]{1,0:T(8,128)S(1)}, f32[136,768]{1,0:T(8,128)S(1)}, u32[]{:S(2)}, u32[]{:S(2)}) collective-permute-start(f32[136,768]{1,0:T(8,128)S(1)} %pad_dynamic-update-slice_fusion.bundle.refs_0_), channel_id=1, source_target_pairs={{0,4},{4,0},{8,12},{12,8},{16,20},{20,16},{24,28},{28,24},{1,5},{5... | collective-permute-start | bytes 1253384 | tf_op jit(solution)/shard_map/ppermute | solution.py:14
  18.7 7.5 %collective-permute-start.9 = (f32[25,8,128]{2,1,0:T(8,128)S(1)}, f32[25,8,128]{2,1,0:T(8,128)S(1)}, u32[]{:S(2)}, u32[]{:S(2)}) collective-permute-start(f32[25,8,128]{2,1,0:T(8,128)S(1)} %get-tuple-element.23), channel_id=1, source_target_pairs={{0,1},{1,0},{2,3},{3,2},{4,5},{5,4},{6,7},{7,6},{8,9},{9,8},{10,11... | collective-permute-start | bytes 307208 | tf_op jit(solution)/shard_map/ppermute | solution.py:14
  19.0 8.9 %collective-permute-start.7 = (f32[25,8,128]{2,1,0:T(8,128)S(1)}, f32[25,8,128]{2,1,0:T(8,128)S(1)}, u32[]{:S(2)}, u32[]{:S(2)}) collective-permute-start(f32[25,8,128]{2,1,0:T(8,128)S(1)} %get-tuple-element.21), channel_id=1, source_target_pairs={{0,3},{1,2},{2,1},{3,0},{4,7},{5,6},{6,5},{7,4},{8,11},{9,10},{10,... | collective-permute-start | bytes 307208 | tf_op jit(solution)/shard_map/ppermute | solution.py:14
  22.0 9.8 %collective-permute-start.8 = (f32[25,8,128]{2,1,0:T(8,128)S(1)}, f32[25,8,128]{2,1,0:T(8,128)S(1)}, u32[]{:S(2)}, u32[]{:S(2)}) collective-permute-start(f32[25,8,128]{2,1,0:T(8,128)S(1)} %get-tuple-element.22), channel_id=1, source_target_pairs={{0,2},{1,3},{2,0},{3,1},{4,6},{5,7},{6,4},{7,5},{8,10},{9,11},{10,... | collective-permute-start | bytes 307208 | tf_op jit(solution)/shard_map/ppermute | solution.py:14
  23.2 9.3 %collective-permute-start.11 = (f32[32,768]{1,0:T(8,128)S(1)}, f32[32,768]{1,0:T(8,128)S(1)}, u32[]{:S(2)}, u32[]{:S(2)}) collective-permute-start(f32[32,768]{1,0:T(8,128)S(1)} %get-tuple-element.28), channel_id=1, source_target_pairs={{0,24},{4,28},{8,16},{12,20},{16,8},{20,12},{24,0},{28,4},{1,25},{... | collective-permute-start | bytes 294920 | tf_op jit(solution)/shard_map/ppermute | solution.py:14
  25.7 6.8 %collective-permute-start.12 = (f32[32,768]{1,0:T(8,128)S(1)}, f32[32,768]{1,0:T(8,128)S(1)}, u32[]{:S(2)}, u32[]{:S(2)}) collective-permute-start(f32[32,768]{1,0:T(8,128)S(1)} %get-tuple-element.29), channel_id=1, source_target_pairs={{0,16},{4,20},{8,24},{12,28},{16,0},{20,4},{24,8},{28,12},{1,17},{... | collective-permute-start | bytes 294920 | tf_op jit(solution)/shard_map/ppermute | solution.py:14
  26.2 6.3 %collective-permute-start.13 = (f32[32,768]{1,0:T(8,128)S(1)}, f32[32,768]{1,0:T(8,128)S(1)}, u32[]{:S(2)}, u32[]{:S(2)}) collective-permute-start(f32[32,768]{1,0:T(8,128)S(1)} %get-tuple-element.31), channel_id=1, source_target_pairs={{0,8},{4,12},{8,0},{12,4},{16,24},{20,28},{24,16},{28,20},{1,9},{5... | collective-permute-start | bytes 294920 | tf_op jit(solution)/shard_map/ppermute | solution.py:14

commit v11 on v10

--- a/solution.py
+++ b/solution.py
@@ -42,6 +42,10 @@
     return row
 
 
+def far_first(n):
+    return [0] + sorted(range(1, n), key=lambda k: -k.bit_count())
+
+
 def text_ids(shape, n_img, cols, far):
     me_img, me_txt = lax.axis_index("img"), lax.axis_index("txt")
     place = lax.broadcasted_iota(jnp.int32, shape, 0)
@@ -50,7 +54,8 @@
     if far:
         core = core ^ (place // half)
         place = place % half
-    chip = (me_img // 2) ^ (place // cols)
+    distance = sum(jnp.where(place // cols == p, k, 0) for p, k in enumerate(far_first(n_img // 2)))
+    chip = (me_img // 2) ^ distance
     return (me_txt * n_img + 2 * chip + core) * cols + place % cols
 
 
@@ -107,8 +112,10 @@
         ref[...] = term[k * cols:(k + 1) * cols]
 
 
-def image_sum_kernel(n_txt, own_ref, loss_ref, *refs):
-    messages, (image_loss, image_grad) = refs[:n_txt - 1], refs[n_txt - 1:]
+def sum_kernel(n_txt, n_chips, own_ref, loss_ref, *refs):
+    messages, blocks = refs[:n_txt - 1], refs[n_txt - 1:n_txt - 1 + n_chips]
+    image_loss, image_grad, text_grad = refs[n_txt - 1 + n_chips:]
+    text_grad[...] = sum(b[...] for b in blocks)
     rows, width = own_ref.shape
     across = width // LANES
     for r in range(rows // 8):
@@ -118,11 +125,6 @@
     image_loss[...] = (loss_ref[...] + sum(m[rows // 8 * across] for m in messages))[:1]
 
 
-def text_sum_kernel(_, *refs):
-    blocks, text_grad = refs[:-1], refs[-1]
-    text_grad[...] = sum(b[...] for b in blocks)
-
-
 def in_vmem(*arrays):
     return [pltpu.with_memory_space_constraint(x, pltpu.VMEM) for x in arrays]
 
@@ -139,13 +141,11 @@
     tiles = rows * width // (8 * LANES)
     whole = pl.BlockSpec(memory_space=pltpu.VMEM)
 
-    text_blocks, image_blocks = [text_emb], {0: image_emb}
-    for k in range(1, max(n_txt, chips)):
-        if k < chips:
-            text_blocks.append(exchange(text_emb, "img", n_img, 2 * k))
-        if 1 < k < n_txt:
-            image_blocks[k] = exchange(image_emb, "txt", n_txt, k)
-    image_blocks[1] = exchange(after(image_emb, text_blocks[1]), "txt", n_txt, 1)
+    text_order = far_first(chips)
+    text_blocks = [text_emb] + [exchange(text_emb, "img", n_img, 2 * k) for k in text_order[1:]]
+    image_blocks = {k: exchange(image_emb, "txt", n_txt, k) for k in range(2, n_txt)}
+    image_blocks[0] = image_emb
+    image_blocks[1] = exchange(after(image_emb, text_blocks[min(2, chips - 1)]), "txt", n_txt, 1)
     near = jnp.concatenate(text_blocks)
     far = exchange(near, "img", n_img, 1)
     numbers = jnp.concatenate(
@@ -162,7 +162,7 @@
         out_specs=[whole] * (2 + n_txt),
         name="image_terms",
     )(*in_vmem(bundle, near, far))
-    messages = [exchange(messages[k - 1], "txt", n_txt, k) for k in range(n_txt - 1, 0, -1)]
+    messages = [exchange(messages[k - 1], "txt", n_txt, k) for k in (1, 3, 2)]
 
     pair = exchange(after(bundle, own), "img", n_img, 1)
     blocks = pl.pallas_call(
@@ -173,26 +173,20 @@
         name="text_terms",
     )(*in_vmem(bundle, pair, near, d_near))
     blocks = list(blocks)
-    blocks[1] = after(blocks[1], messages[-1])
-    blocks = [exchange(blocks[k], "img", n_img, 2 * k) for k in range(chips - 1, 0, -1)] + [blocks[0]]
-
-    image_loss, image_grad = pl.pallas_call(
-        functools.partial(image_sum_kernel, n_txt),
+    for p, k in enumerate(text_order):
+        if k:
+            blocks[p] = exchange(blocks[p], "img", n_img, 2 * k)
+
+    image_loss, image_grad, text_grad = pl.pallas_call(
+        functools.partial(sum_kernel, n_txt, chips),
         out_shape=[
-            jax.ShapeDtypeStruct((1, LANES), jnp.float32),
-            jax.ShapeDtypeStruct(image_emb.shape, jnp.float32),
+            jax.ShapeDtypeStruct(shape, jnp.float32)
+            for shape in ((1, LANES), image_emb.shape, text_emb.shape)
         ],
-        in_specs=[whole] * (1 + n_txt),
-        out_specs=[whole] * 2,
-        name="image_sums",
-    )(*in_vmem(own, loss_tile, *messages))
-    text_grad = pl.pallas_call(
-        text_sum_kernel,
-        out_shape=jax.ShapeDtypeStruct(text_emb.shape, jnp.float32),
-        in_specs=[pl.BlockSpec(memory_space=pl.ANY)] + [whole] * chips,
-        out_specs=whole,
-        name="text_sums",
-    )(image_loss, *in_vmem(*blocks))
+        in_specs=[whole] * (1 + n_txt + chips),
+        out_specs=[whole] * 3,
+        name="sums",
+    )(*in_vmem(own, loss_tile, *messages, *blocks))
     return (image_loss.reshape(count), image_grad, text_grad)
 
 

time: 33.4 us -> 33.5 us (level)
  waiting for transfers between devices: 9.34 us -> 10.7 us
  local copies, waits for them, and re-layouts: 1.84 us -> 1.02 us
  Pallas kernels: 3.41 us -> 2.79 us
    ppermute x14, waiting for transfers between devices: 9.34 us -> 10.7 us  [exchange(): return lax.ppermute(x, axis, [(i, i ^ k) for i in range(n)])]
    unnamed x13 -> x11, local copies, waits for them, and re-layouts: 1.82 us -> 1 us
    pallas_call x2 -> x1, Pallas kernels: 1.35 us -> 0.74 us  [per_device(): pl.pallas_call(functools.partial(sum_kernel, n_txt, chips), out_shape=[ja...]
  transfers between devices with their start and end apart: 14 -> 14, of which waited for: 5 -> 4; matrix products, arithmetic and copies ran while one was open for 3% -> 3% of each run, Pallas kernels for 5% -> 3%
where the time goes in v11:
time: 33.5 us; the launch traced here: 33.3 us
  starting transfers between devices  16.7 us (50%)
  waiting for transfers between devices  10.7 us (32%)
  Pallas kernels  2.79 us (8%)
  between operations  2.14 us (6%)
  local copies, waits for them, and re-layouts  1.02 us (3%)
    ppermute x14, starting transfers between devices, exchange(): return lax.ppermute(x, axis, [(i, i ^ k) for i in range(n)])  16.7 us
    ppermute x14, waiting for transfers between devices, exchange(): return lax.ppermute(x, axis, [(i, i ^ k) for i in range(n)])  10.7 us
    pallas_call x1, Pallas kernels, per_device(): pl.pallas_call(functools.partial(image_kernel, n_img, n_txt, rows, cols),...  1.16 us
    unnamed x11, local copies, waits for them, and re-layouts  1 us
    pallas_call x1, Pallas kernels, per_device(): pl.pallas_call(functools.partial(text_kernel, n_img, n_txt, rows, cols),...  0.89 us
    pallas_call x1, Pallas kernels, per_device(): pl.pallas_call(functools.partial(sum_kernel, n_txt, chips), out_shape=[ja...  0.74 us
  transfers between devices with their start and end apart: 14, of which 4 were waited for; matrix products, arithmetic and copies ran while one was open for 3% of the time, Pallas kernels for 3%

profile of v11, /device:TPU:0, one launch (start us, length us, event | category | flops | bytes accessed | tf_op | source)
XLA Modules:
  0.0 33.3 jit_solution(9708220429982098469)
XLA Ops:
  0.6 0.0 copy-start
  0.6 4.1 %collective-permute-start.2 = (f32[32,768]{1,0:T(8,128)}, f32[32,768]{1,0:T(8,128)S(1)}, u32[]{:S(2)}, u32[]{:S(2)}) collective-permute-start(f32[32,768]{1,0:T(8,128)} %param.5), channel_id=1, source_target_pairs={{0,2},{1,3},{2,0},{3,1},{4,6},{5,7},{6,4},{7,5},{8,10},{9,11},{10,... | collective-permute-start | bytes 294920 | tf_op jit(solution)/shard_map/ppermute | solution.py:14
  4.7 1.3 %collective-permute-start.3 = (f32[32,768]{1,0:T(8,128)}, f32[32,768]{1,0:T(8,128)S(1)}, u32[]{:S(2)}, u32[]{:S(2)}) collective-permute-start(f32[32,768]{1,0:T(8,128)} %param.5), channel_id=1, source_target_pairs={{0,3},{1,2},{2,1},{3,0},{4,7},{5,6},{6,5},{7,4},{8,11},{9,10},{10,... | collective-permute-start | bytes 294920 | tf_op jit(solution)/shard_map/ppermute | solution.py:14
  6.1 2.4 %collective-permute-start.4 = (f32[32,768]{1,0:T(8,128)}, f32[32,768]{1,0:T(8,128)S(1)}, u32[]{:S(2)}, u32[]{:S(2)}) collective-permute-start(f32[32,768]{1,0:T(8,128)} %param.6), channel_id=1, source_target_pairs={{0,24},{4,28},{8,16},{12,20},{16,8},{20,12},{24,0},{28,4},{1,25},{... | collective-permute-start | bytes 294920 | tf_op jit(solution)/shard_map/ppermute | solution.py:14
  8.5 0.5 %collective-permute-start = (f32[32,768]{1,0:T(8,128)}, f32[32,768]{1,0:T(8,128)S(1)}, u32[]{:S(2)}, u32[]{:S(2)}) collective-permute-start(f32[32,768]{1,0:T(8,128)} %param.6), channel_id=1, source_target_pairs={{0,8},{4,12},{8,0},{12,4},{16,24},{20,28},{24,16},{28,20},{1,9},{5... | collective-permute-start | bytes 294920 | tf_op jit(solution)/shard_map/ppermute | solution.py:14
  9.1 0.5 %collective-permute-start.5 = (f32[32,768]{1,0:T(8,128)}, f32[32,768]{1,0:T(8,128)S(1)}, u32[]{:S(2)}, u32[]{:S(2)}) collective-permute-start(f32[32,768]{1,0:T(8,128)} %param.6), channel_id=1, source_target_pairs={{0,16},{4,20},{8,24},{12,28},{16,0},{20,4},{24,8},{28,12},{1,17},{... | collective-permute-start | bytes 294920 | tf_op jit(solution)/shard_map/ppermute | solution.py:14
  9.6 0.9 %constant_dynamic-update-slice_fusion.7 = f32[128,768]{1,0:T(8,128)S(1)} fusion(f32[32,768]{1,0:T(8,128)} %param.6), kind=kLoop, calls=%fused_computation.8 | loop fusion | bytes 196608
  11.2 0.0 copy-start.1
  11.8 0.0 copy-done.1
  11.9 0.0 copy-done
  11.9 1.6 %collective-permute-done = f32[32,768]{1,0:T(8,128)S(1)} collective-permute-done((f32[32,768]{1,0:T(8,128)}, f32[32,768]{1,0:T(8,128)S(1)}, u32[]{:S(2)}, u32[]{:S(2)}) %collective-permute-start) | collective-permute-done | bytes 98336 | tf_op jit(solution)/shard_map/ppermute | solution.py:14
  13.5 0.5 %collective-permute-start.1 = (f32[32,768]{1,0:T(8,128)S(1)}, f32[32,768]{1,0:T(8,128)S(1)}, u32[]{:S(2)}, u32[]{:S(2)}) collective-permute-start(f32[32,768]{1,0:T(8,128)S(1)} %copy-done), channel_id=1, source_target_pairs={{0,1},{1,0},{2,3},{3,2},{4,5},{5,4},{6,7},{7,6},{8,9},{9,8},{10,11... | collective-permute-start | bytes 294920 | tf_op jit(solution)/shard_map/ppermute | solution.py:14
  14.0 0.0 collective-permute-done.4
  14.0 0.0 collective-permute-done.5
  14.1 0.1 collective-permute-start.6
  14.1 4.0 %collective-permute-done.1 = f32[32,768]{1,0:T(8,128)S(1)} collective-permute-done((f32[32,768]{1,0:T(8,128)S(1)}, f32[32,768]{1,0:T(8,128)S(1)}, u32[]{:S(2)}, u32[]{:S(2)}) %collective-permute-start.1) | collective-permute-done | bytes 98336 | tf_op jit(solution)/shard_map/ppermute | solution.py:14
  18.1 0.0 collective-permute-done.2
  18.2 0.0 collective-permute-done.3
  18.2 0.0 collective-permute-done.6.far
  18.2 1.2 %image_terms.1 = (f32[32,768]{1,0:T(8,128)S(1)}, f32[8,128]{1,0:T(8,128)S(1)}, f32[128,128]{1,0:T(8,128)S(1)}, f32[25,8,128]{2,1,0:T(8,128)S(1)}, f32[25,8,128]{2,1,0:T(8,128)S(1)}, /*index=5*/f32[25,8,128]{2,1,0:T(8,128)S(1)}) custom-call(f32[136,768]{1,0:T(8,128)S(1)} %pad_dynamic-update-slice_fusion.bundle.refs_0_, ...), custom_call_target="tpu_custom_call" | custom-call | tf_op jit(solution)/shard_map/image_terms/pallas_call | solution.py:157
  19.4 0.1 collective-permute-start.10
  19.5 0.6 %collective-permute-start.7 = (f32[25,8,128]{2,1,0:T(8,128)S(1)}, f32[25,8,128]{2,1,0:T(8,128)S(1)}, u32[]{:S(2)}, u32[]{:S(2)}) collective-permute-start(f32[25,8,128]{2,1,0:T(8,128)S(1)} %get-tuple-element.21), channel_id=1, source_target_pairs={{0,1},{1,0},{2,3},{3,2},{4,5},{5,4},{6,7},{7,6},{8,9},{9,8},{10,11... | collective-permute-start | bytes 307208 | tf_op jit(solution)/shard_map/ppermute | solution.py:14
  20.0 2.6 %collective-permute-start.8 = (f32[25,8,128]{2,1,0:T(8,128)S(1)}, f32[25,8,128]{2,1,0:T(8,128)S(1)}, u32[]{:S(2)}, u32[]{:S(2)}) collective-permute-start(f32[25,8,128]{2,1,0:T(8,128)S(1)} %get-tuple-element.22), channel_id=1, source_target_pairs={{0,3},{1,2},{2,1},{3,0},{4,7},{5,6},{6,5},{7,4},{8,11},{9,10},{10,... | collective-permute-start | bytes 307208 | tf_op jit(solution)/shard_map/ppermute | solution.py:14
  22.7 0.4 %collective-permute-start.9 = (f32[25,8,128]{2,1,0:T(8,128)S(1)}, f32[25,8,128]{2,1,0:T(8,128)S(1)}, u32[]{:S(2)}, u32[]{:S(2)}) collective-permute-start(f32[25,8,128]{2,1,0:T(8,128)S(1)} %get-tuple-element.23), channel_id=1, source_target_pairs={{0,2},{1,3},{2,0},{3,1},{4,6},{5,7},{6,4},{7,5},{8,10},{9,11},{10,... | collective-permute-start | bytes 307208 | tf_op jit(solution)/shard_map/ppermute | solution.py:14
  23.0 0.0 collective-permute-done.10.refs_1_
  23.0 0.9 %text_terms.1 = (f32[32,768]{1,0:T(8,128)S(1)}, f32[32,768]{1,0:T(8,128)S(1)}, f32[32,768]{1,0:T(8,128)S(1)}, f32[32,768]{1,0:T(8,128)S(1)}) custom-call(f32[136,768]{1,0:T(8,128)S(1)} %pad_dynamic-update-slice_fusion.bundle.refs_0_, f32[136,768]{1,0:T(8,128)S(1)} %collective-permute-done.10.refs_1_, ...), custom_call_target="tpu_custom_call" | custom-call | tf_op jit(solution)/shard_map/text_terms/pallas_call | solution.py:168
  23.9 1.3 %collective-permute-start.11 = (f32[32,768]{1,0:T(8,128)S(1)}, f32[32,768]{1,0:T(8,128)S(1)}, u32[]{:S(2)}, u32[]{:S(2)}) collective-permute-start(f32[32,768]{1,0:T(8,128)S(1)} %get-tuple-element.27), channel_id=1, source_target_pairs={{0,24},{4,28},{8,16},{12,20},{16,8},{20,12},{24,0},{28,4},{1,25},{... | collective-permute-start | bytes 294920 | tf_op jit(solution)/shard_map/ppermute | solution.py:14
  25.3 0.7 %collective-permute-start.12 = (f32[32,768]{1,0:T(8,128)S(1)}, f32[32,768]{1,0:T(8,128)S(1)}, u32[]{:S(2)}, u32[]{:S(2)}) collective-permute-start(f32[32,768]{1,0:T(8,128)S(1)} %get-tuple-element.28), channel_id=1, source_target_pairs={{0,8},{4,12},{8,0},{12,4},{16,24},{20,28},{24,16},{28,20},{1,9},{5... | collective-permute-start | bytes 294920 | tf_op jit(solution)/shard_map/ppermute | solution.py:14
  26.0 0.0 collective-permute-done.7.refs_0_
  26.0 1.5 %collective-permute-start.13 = (f32[32,768]{1,0:T(8,128)S(1)}, f32[32,768]{1,0:T(8,128)S(1)}, u32[]{:S(2)}, u32[]{:S(2)}) collective-permute-start(f32[32,768]{1,0:T(8,128)S(1)} %get-tuple-element.29), channel_id=1, source_target_pairs={{0,16},{4,20},{8,24},{12,28},{16,0},{20,4},{24,8},{28,12},{1,17},{... | collective-permute-start | bytes 294920 | tf_op jit(solution)/shard_map/ppermute | solution.py:14
  27.5 1.1 %collective-permute-done.8.refs_1_ = f32[25,8,128]{2,1,0:T(8,128)S(1)} collective-permute-done((f32[25,8,128]{2,1,0:T(8,128)S(1)}, f32[25,8,128]{2,1,0:T(8,128)S(1)}, u32[]{:S(2)}, u32[]{:S(2)}) %collective-permute-start.8) | collective-permute-done | bytes 102432 | tf_op jit(solution)/shard_map/ppermute | solution.py:14
  28.6 3.9 %collective-permute-done.9.refs_2_ = f32[25,8,128]{2,1,0:T(8,128)S(1)} collective-permute-done((f32[25,8,128]{2,1,0:T(8,128)S(1)}, f32[25,8,128]{2,1,0:T(8,128)S(1)}, u32[]{:S(2)}, u32[]{:S(2)}) %collective-permute-start.9) | collective-permute-done | bytes 102432 | tf_op jit(solution)/shard_map/ppermute | solution.py:14
  32.5 0.0 collective-permute-done.11.refs_4_
  32.5 0.0 collective-permute-done.12.refs_5_
  32.5 0.0 collective-permute-done.13.refs_6_
  32.6 0.7 %sums.1 = (f32[1,128]{1,0:T(1,128)}, f32[32,768]{1,0:T(8,128)}, f32[32,768]{1,0:T(8,128)}) custom-call(f32[32,768]{1,0:T(8,128)S(1)} %get-tuple-element.19.own_ref, f32[8,128]{1,0:T(8,128)S(1)} %get-tuple-element.20.loss_ref, f32[25,8,128]{2,1,0:T(8,128)S(1)} %collective-permute-done.7.refs_0_, f32[25,8,128]{2,1,0:T(8,128)S(1)} %collective-permute-done.8.refs_1_, ...), custom_call_target="tpu_custom_call" | custom-call | tf_op jit(solution)/shard_map/sums/pallas_call | solution.py:180
  (13 shorter events, 0.1 us)
Async XLA Ops:
  0.6 11.3 %copy-start = (f32[32,768]{1,0:T(8,128)S(1)}, f32[32,768]{1,0:T(8,128)}, u32[]{:S(2)}) copy-start(f32[32,768]{1,0:T(8,128)} %param.5) | copy-start | bytes 294916
  0.6 17.5 %collective-permute-start.2 = (f32[32,768]{1,0:T(8,128)}, f32[32,768]{1,0:T(8,128)S(1)}, u32[]{:S(2)}, u32[]{:S(2)}) collective-permute-start(f32[32,768]{1,0:T(8,128)} %param.5), channel_id=1, source_target_pairs={{0,2},{1,3},{2,0},{3,1},{4,6},{5,7},{6,4},{7,5},{8,10},{9,11},{10,... | collective-permute-start | bytes 294920 | tf_op jit(solution)/shard_map/ppermute | solution.py:14
  4.7 13.4 %collective-permute-start.3 = (f32[32,768]{1,0:T(8,128)}, f32[32,768]{1,0:T(8,128)S(1)}, u32[]{:S(2)}, u32[]{:S(2)}) collective-permute-start(f32[32,768]{1,0:T(8,128)} %param.5), channel_id=1, source_target_pairs={{0,3},{1,2},{2,1},{3,0},{4,7},{5,6},{6,5},{7,4},{8,11},{9,10},{10,... | collective-permute-start | bytes 294920 | tf_op jit(solution)/shard_map/ppermute | solution.py:14
  6.1 7.9 %collective-permute-start.4 = (f32[32,768]{1,0:T(8,128)}, f32[32,768]{1,0:T(8,128)S(1)}, u32[]{:S(2)}, u32[]{:S(2)}) collective-permute-start(f32[32,768]{1,0:T(8,128)} %param.6), channel_id=1, source_target_pairs={{0,24},{4,28},{8,16},{12,20},{16,8},{20,12},{24,0},{28,4},{1,25},{... | collective-permute-start | bytes 294920 | tf_op jit(solution)/shard_map/ppermute | solution.py:14
  8.5 5.0 %collective-permute-start = (f32[32,768]{1,0:T(8,128)}, f32[32,768]{1,0:T(8,128)S(1)}, u32[]{:S(2)}, u32[]{:S(2)}) collective-permute-start(f32[32,768]{1,0:T(8,128)} %param.6), channel_id=1, source_target_pairs={{0,8},{4,12},{8,0},{12,4},{16,24},{20,28},{24,16},{28,20},{1,9},{5... | collective-permute-start | bytes 294920 | tf_op jit(solution)/shard_map/ppermute | solution.py:14
  9.1 5.0 %collective-permute-start.5 = (f32[32,768]{1,0:T(8,128)}, f32[32,768]{1,0:T(8,128)S(1)}, u32[]{:S(2)}, u32[]{:S(2)}) collective-permute-start(f32[32,768]{1,0:T(8,128)} %param.6), channel_id=1, source_target_pairs={{0,16},{4,20},{8,24},{12,28},{16,0},{20,4},{24,8},{28,12},{1,17},{... | collective-permute-start | bytes 294920 | tf_op jit(solution)/shard_map/ppermute | solution.py:14
  11.2 0.7 %copy-start.1 = (s32[128]{0:T(128)S(1)}, s32[128]{0:T(128)}, u32[]{:S(2)}) copy-start(s32[128]{0:T(128)} %param.7) | copy-start | bytes 1540
  13.5 4.6 %collective-permute-start.1 = (f32[32,768]{1,0:T(8,128)S(1)}, f32[32,768]{1,0:T(8,128)S(1)}, u32[]{:S(2)}, u32[]{:S(2)}) collective-permute-start(f32[32,768]{1,0:T(8,128)S(1)} %copy-done), channel_id=1, source_target_pairs={{0,1},{1,0},{2,3},{3,2},{4,5},{5,4},{6,7},{7,6},{8,9},{9,8},{10,11... | collective-permute-start | bytes 294920 | tf_op jit(solution)/shard_map/ppermute | solution.py:14
  14.1 4.2 %collective-permute-start.6 = (f32[128,768]{1,0:T(8,128)S(1)}, f32[128,768]{1,0:T(8,128)S(1)}, u32[]{:S(2)}, u32[]{:S(2)}) collective-permute-start(f32[128,768]{1,0:T(8,128)S(1)} %constant_dynamic-update-slice_fusion.4.near.refs_2_), channel_id=1, source_target_pairs={{0,4},{4,0},{8,12},{12,8},{16,20},{20,16},{24,28},{28,24},{1,5},{5... | collective-permute-start | bytes 1179656 | tf_op jit(solution)/shard_map/ppermute | solution.py:14
  19.4 3.6 %collective-permute-start.10 = (f32[136,768]{1,0:T(8,128)S(1)}, f32[136,768]{1,0:T(8,128)S(1)}, u32[]{:S(2)}, u32[]{:S(2)}) collective-permute-start(f32[136,768]{1,0:T(8,128)S(1)} %pad_dynamic-update-slice_fusion.bundle.refs_0_), channel_id=1, source_target_pairs={{0,4},{4,0},{8,12},{12,8},{16,20},{20,16},{24,28},{28,24},{1,5},{5... | collective-permute-start | bytes 1253384 | tf_op jit(solution)/shard_map/ppermute | solution.py:14
  19.5 6.5 %collective-permute-start.7 = (f32[25,8,128]{2,1,0:T(8,128)S(1)}, f32[25,8,128]{2,1,0:T(8,128)S(1)}, u32[]{:S(2)}, u32[]{:S(2)}) collective-permute-start(f32[25,8,128]{2,1,0:T(8,128)S(1)} %get-tuple-element.21), channel_id=1, source_target_pairs={{0,1},{1,0},{2,3},{3,2},{4,5},{5,4},{6,7},{7,6},{8,9},{9,8},{10,11... | collective-permute-start | bytes 307208 | tf_op jit(solution)/shard_map/ppermute | solution.py:14
  20.0 8.6 %collective-permute-start.8 = (f32[25,8,128]{2,1,0:T(8,128)S(1)}, f32[25,8,128]{2,1,0:T(8,128)S(1)}, u32[]{:S(2)}, u32[]{:S(2)}) collective-permute-start(f32[25,8,128]{2,1,0:T(8,128)S(1)} %get-tuple-element.22), channel_id=1, source_target_pairs={{0,3},{1,2},{2,1},{3,0},{4,7},{5,6},{6,5},{7,4},{8,11},{9,10},{10,... | collective-permute-start | bytes 307208 | tf_op jit(solution)/shard_map/ppermute | solution.py:14
  22.7 9.9 %collective-permute-start.9 = (f32[25,8,128]{2,1,0:T(8,128)S(1)}, f32[25,8,128]{2,1,0:T(8,128)S(1)}, u32[]{:S(2)}, u32[]{:S(2)}) collective-permute-start(f32[25,8,128]{2,1,0:T(8,128)S(1)} %get-tuple-element.23), channel_id=1, source_target_pairs={{0,2},{1,3},{2,0},{3,1},{4,6},{5,7},{6,4},{7,5},{8,10},{9,11},{10,... | collective-permute-start | bytes 307208 | tf_op jit(solution)/shard_map/ppermute | solution.py:14
  23.9 8.6 %collective-permute-start.11 = (f32[32,768]{1,0:T(8,128)S(1)}, f32[32,768]{1,0:T(8,128)S(1)}, u32[]{:S(2)}, u32[]{:S(2)}) collective-permute-start(f32[32,768]{1,0:T(8,128)S(1)} %get-tuple-element.27), channel_id=1, source_target_pairs={{0,24},{4,28},{8,16},{12,20},{16,8},{20,12},{24,0},{28,4},{1,25},{... | collective-permute-start | bytes 294920 | tf_op jit(solution)/shard_map/ppermute | solution.py:14
  25.3 7.3 %collective-permute-start.12 = (f32[32,768]{1,0:T(8,128)S(1)}, f32[32,768]{1,0:T(8,128)S(1)}, u32[]{:S(2)}, u32[]{:S(2)}) collective-permute-start(f32[32,768]{1,0:T(8,128)S(1)} %get-tuple-element.28), channel_id=1, source_target_pairs={{0,8},{4,12},{8,0},{12,4},{16,24},{20,28},{24,16},{28,20},{1,9},{5... | collective-permute-start | bytes 294920 | tf_op jit(solution)/shard_map/ppermute | solution.py:14
  26.0 6.6 %collective-permute-start.13 = (f32[32,768]{1,0:T(8,128)S(1)}, f32[32,768]{1,0:T(8,128)S(1)}, u32[]{:S(2)}, u32[]{:S(2)}) collective-permute-start(f32[32,768]{1,0:T(8,128)S(1)} %get-tuple-element.29), channel_id=1, source_target_pairs={{0,16},{4,20},{8,24},{12,28},{16,0},{20,4},{24,8},{28,12},{1,17},{... | collective-permute-start | bytes 294920 | tf_op jit(solution)/shard_map/ppermute | solution.py:14

commit v12 on v11

--- a/solution.py
+++ b/solution.py
@@ -9,6 +9,8 @@
 
 LANES = 128
 
+IMAGE_ORDER = (0, 2, 3, 1)
+
 
 def exchange(x, axis, n, k):
     return lax.ppermute(x, axis, [(i, i ^ k) for i in range(n)])
@@ -16,6 +18,10 @@
 
 def after(x, other):
     return lax.optimization_barrier((x, other))[0]
+
+
+def chip_exchange(x, n_img, distances):
+    return lax.ppermute(x, "img", [(i, i ^ (2 * distances[i % 2])) for i in range(n_img)])
 
 
 def halves(x):
@@ -42,25 +48,43 @@
     return row
 
 
-def far_first(n):
-    return [0] + sorted(range(1, n), key=lambda k: -k.bit_count())
+def shuffle(row, block, sources):
+    place = lax.broadcasted_iota(jnp.int32, row.shape, 1) // block
+    result = row
+    for step in range(1, len(sources)):
+        moved = pltpu.roll(row, LANES - step * block, 1)
+        for p, source in enumerate(sources):
+            if (source - p) % len(sources) == step:
+                result = jnp.where(place == p, moved, result)
+    return result
 
 
 def text_ids(shape, n_img, cols, far):
     me_img, me_txt = lax.axis_index("img"), lax.axis_index("txt")
     place = lax.broadcasted_iota(jnp.int32, shape, 0)
     half = n_img // 2 * cols
-    core = me_img % 2
+    me_core = me_img % 2
+    core = me_core
     if far:
         core = core ^ (place // half)
         place = place % half
-    distance = sum(jnp.where(place // cols == p, k, 0) for p, k in enumerate(far_first(n_img // 2)))
+    turn = place // cols
+    distance = jnp.where(turn == 1, 1 + me_core, jnp.where(turn == 2, 2 - me_core, turn))
     chip = (me_img // 2) ^ distance
     return (me_txt * n_img + 2 * chip + core) * cols + place % cols
 
 
-def derivative(texts, images, ids, matched, scale, shift):
-    logits = scale * dot(texts, images, (1, 1)) + shift
+def own_core_texts(cols, both, sent, got):
+    return [both[:cols], sent[:cols], got[cols:2 * cols], sent[2 * cols:]]
+
+
+def other_core_texts(cols, both, sent, got):
+    return [both[cols:], sent[cols:2 * cols], got[:cols], got[2 * cols:]]
+
+
+def derivative(texts, images, ids, matched, log_scale, bias):
+    scale = jnp.exp(jnp.full((1, LANES), log_scale[0], jnp.float32))
+    logits = scale * dot(texts, images, (1, 1)) + bias[0]
     match = ids == matched
     v = jnp.where(match, -logits, logits)
     e = jnp.exp(-jnp.abs(v))
@@ -69,44 +93,49 @@
     return loss, jnp.where(match, -s, s)
 
 
-def row_of_numbers(bundle, rows, count):
+def matched_texts(bundle, rows, count):
     matched = untwist(bundle[count:count + 1, :LANES], rows, lax.axis_index("txt"))
-    scale = jnp.exp(bundle[count:count + 1, LANES:2 * LANES])
-    return matched.astype(jnp.int32), scale, bundle[count:count + 1, 2 * LANES:3 * LANES]
-
-
-def image_kernel(n_img, n_txt, rows, cols, bundle, near, far, own, loss_ref, d_near, *messages):
+    return shuffle(matched, rows, IMAGE_ORDER).astype(jnp.int32)
+
+
+def image_kernel(
+    n_img, n_txt, rows, cols, log_scale, bias, bundle, both, sent, got,
+    own, loss_ref, d_near, *messages
+):
     count = n_txt * rows
-    matched, scale, shift = row_of_numbers(bundle, rows, count)
+    matched = matched_texts(bundle, rows, count)
     images = halves(bundle[:count])
-    texts = halves(jnp.concatenate([near[...], far[...]]))
+    near = own_core_texts(cols, both, sent, got)
+    texts = halves(jnp.concatenate(near + other_core_texts(cols, both, sent, got)))
     ids = text_ids((texts[0].shape[0], count), n_img, cols, True)
-    loss, d = derivative(texts, images, ids, matched, scale, shift)
-    d_near[...] = d[:near.shape[0]]
+    loss, d = derivative(texts, images, ids, matched, log_scale, bias)
+    d_near[...] = d[:len(near) * cols]
     term = dot(halves(d), texts, (0, 0))
     own[...] = term[:rows]
-    loss_row = untwist(jnp.sum(loss, axis=0, keepdims=True), rows, lax.axis_index("txt"))
+    back = [IMAGE_ORDER.index(k) for k in range(n_txt)]
+    loss_row = shuffle(jnp.sum(loss, axis=0, keepdims=True), rows, back)
+    loss_row = untwist(loss_row, rows, lax.axis_index("txt"))
     loss_tile = jnp.broadcast_to(loss_row, (8, LANES))
     loss_ref[...] = loss_tile
     across = term.shape[1] // LANES
-    for k, ref in enumerate(messages, 1):
+    for p, ref in enumerate(messages, 1):
         for r in range(rows // 8):
             for c in range(across):
                 ref[r * across + c] = term[
-                    k * rows + r * 8:k * rows + r * 8 + 8, c * LANES:(c + 1) * LANES
+                    p * rows + r * 8:p * rows + r * 8 + 8, c * LANES:(c + 1) * LANES
                 ]
         ref[rows // 8 * across] = loss_tile
 
 
 def text_kernel(n_img, n_txt, rows, cols, *refs):
-    bundle, pair, near, d_ref = refs[:4]
-    block_refs = refs[4:]
+    log_scale, bias, bundle, pair, both, sent, got, d_ref = refs[:8]
+    block_refs = refs[8:]
     count = n_txt * rows
-    matched, scale, shift = row_of_numbers(pair, rows, count)
+    matched = matched_texts(pair, rows, count)
     others = halves(pair[:count])
-    texts = halves(near[...])
+    texts = halves(jnp.concatenate(own_core_texts(cols, both, sent, got)))
     ids = text_ids((texts[0].shape[0], count), n_img, cols, False)
-    _, d = derivative(texts, others, ids, matched, scale, shift)
+    _, d = derivative(texts, others, ids, matched, log_scale, bias)
     term = dot(halves(d_ref[...]), halves(bundle[:count]), (1, 0)) + dot(halves(d), others, (1, 0))
     for k, ref in enumerate(block_refs):
         ref[...] = term[k * cols:(k + 1) * cols]
@@ -139,43 +168,41 @@
     rows, cols, width = image_emb.shape[0], text_emb.shape[0], image_emb.shape[1]
     count = n_txt * rows
     tiles = rows * width // (8 * LANES)
-    whole = pl.BlockSpec(memory_space=pltpu.VMEM)
-
-    text_order = far_first(chips)
-    text_blocks = [text_emb] + [exchange(text_emb, "img", n_img, 2 * k) for k in text_order[1:]]
-    image_blocks = {k: exchange(image_emb, "txt", n_txt, k) for k in range(2, n_txt)}
-    image_blocks[0] = image_emb
-    image_blocks[1] = exchange(after(image_emb, text_blocks[min(2, chips - 1)]), "txt", n_txt, 1)
-    near = jnp.concatenate(text_blocks)
-    far = exchange(near, "img", n_img, 1)
-    numbers = jnp.concatenate(
-        [pairs.astype(jnp.float32), jnp.broadcast_to(log_scale, LANES), jnp.broadcast_to(bias, LANES)]
-    )
-    numbers = jnp.pad(numbers[None], ((0, 7), (0, width - numbers.shape[0])))
-    bundle = jnp.concatenate([image_blocks[k] for k in range(n_txt)] + [numbers])
+    smem, whole = pl.BlockSpec(memory_space=pltpu.SMEM), pl.BlockSpec(memory_space=pltpu.VMEM)
+
+    both = jnp.concatenate([text_emb, exchange(text_emb, "img", n_img, 1)])
+    image_blocks = [image_emb] + [None] * (n_txt - 1)
+    for k in (2, 3):
+        image_blocks[k] = exchange(image_emb, "txt", n_txt, k)
+    beside = chip_exchange(both, n_img, (1, 2))
+    diagonal = chip_exchange(after(text_emb, both), n_img, (3, 3))
+    image_blocks[1] = exchange(after(image_emb, both), "txt", n_txt, 1)
+    sent = jnp.concatenate([beside, diagonal])
+    got = exchange(sent, "img", n_img, 1)
+    numbers = jnp.pad(after(pairs, sent).astype(jnp.float32)[None], ((0, 7), (0, width - count)))
+    bundle = jnp.concatenate([image_blocks[k] for k in IMAGE_ORDER] + [numbers])
 
     own, loss_tile, d_near, *messages = pl.pallas_call(
         functools.partial(image_kernel, n_img, n_txt, rows, cols),
         out_shape=[vmem((rows, width)), vmem((8, LANES)), vmem((chips * cols, count))]
         + [vmem((tiles + 1, 8, LANES))] * (n_txt - 1),
-        in_specs=[whole] * 3,
+        in_specs=[smem] * 2 + [whole] * 4,
         out_specs=[whole] * (2 + n_txt),
         name="image_terms",
-    )(*in_vmem(bundle, near, far))
-    messages = [exchange(messages[k - 1], "txt", n_txt, k) for k in (1, 3, 2)]
+    )(log_scale, bias, *in_vmem(bundle, both, sent, got))
+    messages = [exchange(messages[p - 1], "txt", n_txt, IMAGE_ORDER[p]) for p in (3, 2, 1)]
 
     pair = exchange(after(bundle, own), "img", n_img, 1)
     blocks = pl.pallas_call(
         functools.partial(text_kernel, n_img, n_txt, rows, cols),
         out_shape=[vmem((cols, width))] * chips,
-        in_specs=[whole] * 4,
+        in_specs=[smem] * 2 + [whole] * 6,
         out_specs=[whole] * chips,
         name="text_terms",
-    )(*in_vmem(bundle, pair, near, d_near))
+    )(log_scale, bias, *in_vmem(bundle, pair, both, sent, got, d_near))
     blocks = list(blocks)
-    for p, k in enumerate(text_order):
-        if k:
-            blocks[p] = exchange(blocks[p], "img", n_img, 2 * k)
+    for k, distances in ((3, (3, 3)), (1, (1, 2)), (2, (2, 1))):
+        blocks[k] = chip_exchange(blocks[k], n_img, distances)
 
     image_loss, image_grad, text_grad = pl.pallas_call(
         functools.partial(sum_kernel, n_txt, chips),
@@ -186,7 +213,7 @@
         in_specs=[whole] * (1 + n_txt + chips),
         out_specs=[whole] * 3,
         name="sums",
-    )(*in_vmem(own, loss_tile, *messages, *blocks))
+    )(*in_vmem(own, loss_tile, *messages, blocks[3], *blocks[:3]))
     return (image_loss.reshape(count), image_grad, text_grad)
 
 
@@ -229,7 +256,7 @@
 
     def body(image_emb, *others):
         rows = image_emb.shape[0]
-        if sizes[0] in (4, 8) and sizes[1] == 4 and rows * 4 == LANES:
+        if sizes == (8, 4) and rows * sizes[1] == LANES:
             return per_device(sizes, image_emb, *others)
         return per_device_large(image_emb, *others)
 

time: 33.5 us -> 34.7 us (1.036)
  waiting for transfers between devices: 10.7 us -> 11.5 us
  starting transfers between devices: 16.7 us -> 17.2 us
    ppermute x0 -> x5, starting transfers between devices: none -> 6.6 us  [chip_exchange(): lax.ppermute(x, 'img', [(i, i ^ 2 * distances[i % 2]) for i in range(n_im...]
    ppermute x14 -> x9, starting transfers between devices: 16.7 us -> 10.6 us  [exchange(): return lax.ppermute(x, axis, [(i, i ^ k) for i in range(n)])]
    ppermute x0 -> x5, waiting for transfers between devices: none -> 0.77 us  [chip_exchange(): lax.ppermute(x, 'img', [(i, i ^ 2 * distances[i % 2]) for i in range(n_im...]
    ppermute x14 -> x9, waiting for transfers between devices: 10.7 us -> 10.7 us  [exchange(): return lax.ppermute(x, axis, [(i, i ^ k) for i in range(n)])]
    unnamed x11 -> x12, local copies, waits for them, and re-layouts: 1 us -> 0.97 us
  transfers between devices with their start and end apart: 14 -> 14, of which waited for: 4 -> 6; matrix products, arithmetic and copies ran while one was open for 3% -> 3% of each run, Pallas kernels for 3% -> 3%
where the time goes in v12:
time: 34.7 us; the launch traced here: 34.5 us
  starting transfers between devices  17.2 us (50%)
  waiting for transfers between devices  11.5 us (33%)
  Pallas kernels  2.8 us (8%)
  between operations  2.09 us (6%)
  local copies, waits for them, and re-layouts  0.99 us (3%)
    ppermute x9, waiting for transfers between devices, exchange(): return lax.ppermute(x, axis, [(i, i ^ k) for i in range(n)])  10.7 us
    ppermute x9, starting transfers between devices, exchange(): return lax.ppermute(x, axis, [(i, i ^ k) for i in range(n)])  10.6 us
    ppermute x5, starting transfers between devices, chip_exchange(): lax.ppermute(x, 'img', [(i, i ^ 2 * distances[i % 2]) for i in range(n_im...  6.6 us
    pallas_call x1, Pallas kernels, per_device(): pl.pallas_call(functools.partial(image_kernel, n_img, n_txt, rows, cols),...  1.17 us
    unnamed x12, local copies, waits for them, and re-layouts  0.97 us
    pallas_call x1, Pallas kernels, per_device(): pl.pallas_call(functools.partial(text_kernel, n_img, n_txt, rows, cols),...  0.89 us
    ppermute x5, waiting for transfers between devices, chip_exchange(): lax.ppermute(x, 'img', [(i, i ^ 2 * distances[i % 2]) for i in range(n_im...  0.77 us
    pallas_call x1, Pallas kernels, per_device(): pl.pallas_call(functools.partial(sum_kernel, n_txt, chips), out_shape=[ja...  0.74 us
  transfers between devices with their start and end apart: 14, of which 6 were waited for; matrix products, arithmetic and copies ran while one was open for 3% of the time, Pallas kernels for 3%

profile of v12, /device:TPU:0, one launch (start us, length us, event | category | flops | bytes accessed | tf_op | source)
XLA Modules:
  0.0 34.5 jit_solution(9841697738816776169)
XLA Ops:
  0.6 0.0 copy-start
  0.6 5.1 %collective-permute-start.1 = (f32[32,768]{1,0:T(8,128)}, f32[32,768]{1,0:T(8,128)S(1)}, u32[]{:S(2)}, u32[]{:S(2)}) collective-permute-start(f32[32,768]{1,0:T(8,128)} %param.5), channel_id=1, source_target_pairs={{0,3},{1,2},{2,1},{3,0},{4,7},{5,6},{6,5},{7,4},{8,11},{9,10},{10,... | collective-permute-start | bytes 294920 | tf_op jit(solution)/shard_map/ppermute | solution.py:16
  5.8 0.0 collective-permute-start
  5.8 0.0 collective-permute-start.2
  5.8 0.9 %constant_dynamic-update-slice_fusion.1 = f32[64,768]{1,0:T(8,128)S(1)} fusion(f32[32,768]{1,0:T(8,128)} %param.6), kind=kLoop, calls=%fused_computation.2 | loop fusion | bytes 196608
  8.0 0.0 copy-done
  8.0 0.0 copy-start.1
  8.0 0.0 collective-permute-done.2
  8.0 1.6 %collective-permute-start.4 = (f32[64,768]{1,0:T(8,128)S(1)}, f32[64,768]{1,0:T(8,128)S(1)}, u32[]{:S(2)}, u32[]{:S(2)}) collective-permute-start(f32[64,768]{1,0:T(8,128)S(1)} %constant_dynamic-update-slice_fusion.both.refs_4_), channel_id=1, source_target_pairs={{0,8},{4,20},{8,0},{12,28},{16,24},{20,4},{24,16},{28,12},{1,9},{5... | collective-permute-start | bytes 589832 | tf_op jit(solution)/shard_map/ppermute | solution.py:24
  9.6 0.8 %collective-permute-start.3 = (f32[32,768]{1,0:T(8,128)S(1)}, f32[32,768]{1,0:T(8,128)S(1)}, u32[]{:S(2)}, u32[]{:S(2)}) collective-permute-start(f32[32,768]{1,0:T(8,128)S(1)} %copy-done), channel_id=1, source_target_pairs={{0,1},{1,0},{2,3},{3,2},{4,5},{5,4},{6,7},{7,6},{8,9},{9,8},{10,11... | collective-permute-start | bytes 294920 | tf_op jit(solution)/shard_map/ppermute | solution.py:16
  10.4 0.0 copy-done.1
  10.4 1.5 %collective-permute-start.5 = (f32[32,768]{1,0:T(8,128)S(1)}, f32[32,768]{1,0:T(8,128)S(1)}, u32[]{:S(2)}, u32[]{:S(2)}) collective-permute-start(f32[32,768]{1,0:T(8,128)S(1)} %copy-done.1), channel_id=1, source_target_pairs={{0,24},{4,28},{8,16},{12,20},{16,8},{20,12},{24,0},{28,4},{1,25},{... | collective-permute-start | bytes 294920 | tf_op jit(solution)/shard_map/ppermute | solution.py:24
  11.9 2.5 %collective-permute-done = f32[32,768]{1,0:T(8,128)S(1)} collective-permute-done((f32[32,768]{1,0:T(8,128)}, f32[32,768]{1,0:T(8,128)S(1)}, u32[]{:S(2)}, u32[]{:S(2)}) %collective-permute-start) | collective-permute-done | bytes 98336 | tf_op jit(solution)/shard_map/ppermute | solution.py:16
  14.3 0.0 collective-permute-done.1
  14.4 1.6 %collective-permute-done.3 = f32[32,768]{1,0:T(8,128)S(1)} collective-permute-done((f32[32,768]{1,0:T(8,128)S(1)}, f32[32,768]{1,0:T(8,128)S(1)}, u32[]{:S(2)}, u32[]{:S(2)}) %collective-permute-start.3) | collective-permute-done | bytes 98336 | tf_op jit(solution)/shard_map/ppermute | solution.py:16
  16.0 0.0 collective-permute-done.4
  16.1 0.0 copy-start.2
  16.1 0.8 %collective-permute-done.5 = f32[32,768]{1,0:T(8,128)S(1)} collective-permute-done((f32[32,768]{1,0:T(8,128)S(1)}, f32[32,768]{1,0:T(8,128)S(1)}, u32[]{:S(2)}, u32[]{:S(2)}) %collective-permute-start.5) | collective-permute-done | bytes 98336 | tf_op jit(solution)/shard_map/ppermute | solution.py:24
  16.8 0.1 collective-permute-start.6
  16.9 0.0 copy-done.2
  16.9 1.5 %collective-permute-done.6.got.refs_6_ = f32[96,768]{1,0:T(8,128)S(1)} collective-permute-done((f32[96,768]{1,0:T(8,128)S(1)}, f32[96,768]{1,0:T(8,128)S(1)}, u32[]{:S(2)}, u32[]{:S(2)}) %collective-permute-start.6) | collective-permute-done | bytes 294944 | tf_op jit(solution)/shard_map/ppermute | solution.py:16
  18.5 1.2 %image_terms.1 = (f32[32,768]{1,0:T(8,128)S(1)}, f32[8,128]{1,0:T(8,128)S(1)}, f32[128,128]{1,0:T(8,128)S(1)}, f32[25,8,128]{2,1,0:T(8,128)S(1)}, f32[25,8,128]{2,1,0:T(8,128)S(1)}, /*index=5*/f32[25,8,128]{2,1,0:T(8,128)S(1)}) custom-call(f32[1]{0:T(128)S(6)} %copy.14.log_scale.refs_0_, f32[1]{0:T(128)S(6)} %copy.15.bias.refs_1_, ...), custom_call_target="tpu_custom_call" | custom-call | tf_op jit(solution)/shard_map/image_terms/pallas_call | solution.py:185
  19.7 0.2 collective-permute-start.10
  19.9 0.8 %collective-permute-start.7 = (f32[25,8,128]{2,1,0:T(8,128)S(1)}, f32[25,8,128]{2,1,0:T(8,128)S(1)}, u32[]{:S(2)}, u32[]{:S(2)}) collective-permute-start(f32[25,8,128]{2,1,0:T(8,128)S(1)} %get-tuple-element.25), channel_id=1, source_target_pairs={{0,1},{1,0},{2,3},{3,2},{4,5},{5,4},{6,7},{7,6},{8,9},{9,8},{10,11... | collective-permute-start | bytes 307208 | tf_op jit(solution)/shard_map/ppermute | solution.py:16
  20.7 3.6 %collective-permute-start.8 = (f32[25,8,128]{2,1,0:T(8,128)S(1)}, f32[25,8,128]{2,1,0:T(8,128)S(1)}, u32[]{:S(2)}, u32[]{:S(2)}) collective-permute-start(f32[25,8,128]{2,1,0:T(8,128)S(1)} %get-tuple-element.26), channel_id=1, source_target_pairs={{0,3},{1,2},{2,1},{3,0},{4,7},{5,6},{6,5},{7,4},{8,11},{9,10},{10,... | collective-permute-start | bytes 307208 | tf_op jit(solution)/shard_map/ppermute | solution.py:16
  24.3 0.0 collective-permute-start.9
  24.3 0.0 collective-permute-done.10.refs_3_
  24.3 0.9 %text_terms.1 = (f32[32,768]{1,0:T(8,128)S(1)}, f32[32,768]{1,0:T(8,128)S(1)}, f32[32,768]{1,0:T(8,128)S(1)}, f32[32,768]{1,0:T(8,128)S(1)}) custom-call(f32[1]{0:T(128)S(6)} %copy.14.log_scale.refs_0_, f32[1]{0:T(128)S(6)} %copy.15.bias.refs_1_, f32[136,768]{1,0:T(8,128)S(1)} %pad_dynamic-update-slice_fusion.bundle.refs_2_, ...), custom_call_target="tpu_custom_call" | custom-call | tf_op jit(solution)/shard_map/text_terms/pallas_call | solution.py:196
  25.2 1.5 %collective-permute-start.11 = (f32[32,768]{1,0:T(8,128)S(1)}, f32[32,768]{1,0:T(8,128)S(1)}, u32[]{:S(2)}, u32[]{:S(2)}) collective-permute-start(f32[32,768]{1,0:T(8,128)S(1)} %get-tuple-element.30), channel_id=1, source_target_pairs={{0,24},{4,28},{8,16},{12,20},{16,8},{20,12},{24,0},{28,4},{1,25},{... | collective-permute-start | bytes 294920 | tf_op jit(solution)/shard_map/ppermute | solution.py:24
  26.7 0.5 %collective-permute-start.12 = (f32[32,768]{1,0:T(8,128)S(1)}, f32[32,768]{1,0:T(8,128)S(1)}, u32[]{:S(2)}, u32[]{:S(2)}) collective-permute-start(f32[32,768]{1,0:T(8,128)S(1)} %get-tuple-element.32), channel_id=1, source_target_pairs={{0,8},{4,20},{8,0},{12,28},{16,24},{20,4},{24,16},{28,12},{1,9},{5... | collective-permute-start | bytes 294920 | tf_op jit(solution)/shard_map/ppermute | solution.py:24
  27.2 0.0 collective-permute-done.7.refs_0_
  27.2 1.5 %collective-permute-start.13 = (f32[32,768]{1,0:T(8,128)S(1)}, f32[32,768]{1,0:T(8,128)S(1)}, u32[]{:S(2)}, u32[]{:S(2)}) collective-permute-start(f32[32,768]{1,0:T(8,128)S(1)} %get-tuple-element.33), channel_id=1, source_target_pairs={{0,16},{4,12},{8,24},{12,4},{16,0},{20,28},{24,8},{28,20},{1,17},{... | collective-permute-start | bytes 294920 | tf_op jit(solution)/shard_map/ppermute | solution.py:24
  28.7 1.5 %collective-permute-done.8.refs_1_ = f32[25,8,128]{2,1,0:T(8,128)S(1)} collective-permute-done((f32[25,8,128]{2,1,0:T(8,128)S(1)}, f32[25,8,128]{2,1,0:T(8,128)S(1)}, u32[]{:S(2)}, u32[]{:S(2)}) %collective-permute-start.8) | collective-permute-done | bytes 102432 | tf_op jit(solution)/shard_map/ppermute | solution.py:16
  30.2 3.5 %collective-permute-done.9.refs_2_ = f32[25,8,128]{2,1,0:T(8,128)S(1)} collective-permute-done((f32[25,8,128]{2,1,0:T(8,128)S(1)}, f32[25,8,128]{2,1,0:T(8,128)S(1)}, u32[]{:S(2)}, u32[]{:S(2)}) %collective-permute-start.9) | collective-permute-done | bytes 102432 | tf_op jit(solution)/shard_map/ppermute | solution.py:16
  33.8 0.0 collective-permute-done.11.refs_3_
  33.8 0.0 collective-permute-done.12.refs_5_
  33.8 0.0 collective-permute-done.13.refs_6_
  33.8 0.7 %sums.1 = (f32[1,128]{1,0:T(1,128)}, f32[32,768]{1,0:T(8,128)}, f32[32,768]{1,0:T(8,128)}) custom-call(f32[32,768]{1,0:T(8,128)S(1)} %get-tuple-element.23.own_ref, f32[8,128]{1,0:T(8,128)S(1)} %get-tuple-element.24.loss_ref, f32[25,8,128]{2,1,0:T(8,128)S(1)} %collective-permute-done.7.refs_0_, f32[25,8,128]{2,1,0:T(8,128)S(1)} %collective-permute-done.8.refs_1_, ...), custom_call_target="tpu_custom_call" | custom-call | tf_op jit(solution)/shard_map/sums/pallas_call | solution.py:207
  (9 shorter events, 0.1 us)
Async XLA Ops:
  0.6 7.3 %copy-start = (f32[32,768]{1,0:T(8,128)S(1)}, f32[32,768]{1,0:T(8,128)}, u32[]{:S(2)}) copy-start(f32[32,768]{1,0:T(8,128)} %param.5) | copy-start | bytes 294916
  0.6 13.7 %collective-permute-start.1 = (f32[32,768]{1,0:T(8,128)}, f32[32,768]{1,0:T(8,128)S(1)}, u32[]{:S(2)}, u32[]{:S(2)}) collective-permute-start(f32[32,768]{1,0:T(8,128)} %param.5), channel_id=1, source_target_pairs={{0,3},{1,2},{2,1},{3,0},{4,7},{5,6},{6,5},{7,4},{8,11},{9,10},{10,... | collective-permute-start | bytes 294920 | tf_op jit(solution)/shard_map/ppermute | solution.py:16
  5.8 8.6 %collective-permute-start = (f32[32,768]{1,0:T(8,128)}, f32[32,768]{1,0:T(8,128)S(1)}, u32[]{:S(2)}, u32[]{:S(2)}) collective-permute-start(f32[32,768]{1,0:T(8,128)} %param.5), channel_id=1, source_target_pairs={{0,2},{1,3},{2,0},{3,1},{4,6},{5,7},{6,4},{7,5},{8,10},{9,11},{10,... | collective-permute-start | bytes 294920 | tf_op jit(solution)/shard_map/ppermute | solution.py:16
  5.8 2.2 %collective-permute-start.2 = (f32[32,768]{1,0:T(8,128)}, f32[32,768]{1,0:T(8,128)S(1)}, u32[]{:S(2)}, u32[]{:S(2)}) collective-permute-start(f32[32,768]{1,0:T(8,128)} %param.6), channel_id=1, source_target_pairs={{0,4},{4,0},{8,12},{12,8},{16,20},{20,16},{24,28},{28,24},{1,5},{5... | collective-permute-start | bytes 294920 | tf_op jit(solution)/shard_map/ppermute | solution.py:16
  8.0 2.4 %copy-start.1 = (f32[32,768]{1,0:T(8,128)S(1)}, f32[32,768]{1,0:T(8,128)}, u32[]{:S(2)}) copy-start(f32[32,768]{1,0:T(8,128)} %param.6) | copy-start | bytes 294916
  8.0 8.0 %collective-permute-start.4 = (f32[64,768]{1,0:T(8,128)S(1)}, f32[64,768]{1,0:T(8,128)S(1)}, u32[]{:S(2)}, u32[]{:S(2)}) collective-permute-start(f32[64,768]{1,0:T(8,128)S(1)} %constant_dynamic-update-slice_fusion.both.refs_4_), channel_id=1, source_target_pairs={{0,8},{4,20},{8,0},{12,28},{16,24},{20,4},{24,16},{28,12},{1,9},{5... | collective-permute-start | bytes 589832 | tf_op jit(solution)/shard_map/ppermute | solution.py:24
  9.6 6.4 %collective-permute-start.3 = (f32[32,768]{1,0:T(8,128)S(1)}, f32[32,768]{1,0:T(8,128)S(1)}, u32[]{:S(2)}, u32[]{:S(2)}) collective-permute-start(f32[32,768]{1,0:T(8,128)S(1)} %copy-done), channel_id=1, source_target_pairs={{0,1},{1,0},{2,3},{3,2},{4,5},{5,4},{6,7},{7,6},{8,9},{9,8},{10,11... | collective-permute-start | bytes 294920 | tf_op jit(solution)/shard_map/ppermute | solution.py:16
  10.4 6.5 %collective-permute-start.5 = (f32[32,768]{1,0:T(8,128)S(1)}, f32[32,768]{1,0:T(8,128)S(1)}, u32[]{:S(2)}, u32[]{:S(2)}) collective-permute-start(f32[32,768]{1,0:T(8,128)S(1)} %copy-done.1), channel_id=1, source_target_pairs={{0,24},{4,28},{8,16},{12,20},{16,8},{20,12},{24,0},{28,4},{1,25},{... | collective-permute-start | bytes 294920 | tf_op jit(solution)/shard_map/ppermute | solution.py:24
  16.1 0.9 %copy-start.2 = (s32[128]{0:T(128)S(1)}, s32[128]{0:T(128)}, u32[]{:S(2)}) copy-start(s32[128]{0:T(128)} %param.7) | copy-start | bytes 1540
  16.8 1.6 %collective-permute-start.6 = (f32[96,768]{1,0:T(8,128)S(1)}, f32[96,768]{1,0:T(8,128)S(1)}, u32[]{:S(2)}, u32[]{:S(2)}) collective-permute-start(f32[96,768]{1,0:T(8,128)S(1)} %constant_dynamic-update-slice_fusion.2.sent.refs_5_), channel_id=1, source_target_pairs={{0,4},{4,0},{8,12},{12,8},{16,20},{20,16},{24,28},{28,24},{1,5},{5... | collective-permute-start | bytes 884744 | tf_op jit(solution)/shard_map/ppermute | solution.py:16
  19.7 4.6 %collective-permute-start.10 = (f32[136,768]{1,0:T(8,128)S(1)}, f32[136,768]{1,0:T(8,128)S(1)}, u32[]{:S(2)}, u32[]{:S(2)}) collective-permute-start(f32[136,768]{1,0:T(8,128)S(1)} %pad_dynamic-update-slice_fusion.bundle.refs_2_), channel_id=1, source_target_pairs={{0,4},{4,0},{8,12},{12,8},{16,20},{20,16},{24,28},{28,24},{1,5},{5... | collective-permute-start | bytes 1253384 | tf_op jit(solution)/shard_map/ppermute | solution.py:16
  19.9 7.3 %collective-permute-start.7 = (f32[25,8,128]{2,1,0:T(8,128)S(1)}, f32[25,8,128]{2,1,0:T(8,128)S(1)}, u32[]{:S(2)}, u32[]{:S(2)}) collective-permute-start(f32[25,8,128]{2,1,0:T(8,128)S(1)} %get-tuple-element.25), channel_id=1, source_target_pairs={{0,1},{1,0},{2,3},{3,2},{4,5},{5,4},{6,7},{7,6},{8,9},{9,8},{10,11... | collective-permute-start | bytes 307208 | tf_op jit(solution)/shard_map/ppermute | solution.py:16
  20.7 9.6 %collective-permute-start.8 = (f32[25,8,128]{2,1,0:T(8,128)S(1)}, f32[25,8,128]{2,1,0:T(8,128)S(1)}, u32[]{:S(2)}, u32[]{:S(2)}) collective-permute-start(f32[25,8,128]{2,1,0:T(8,128)S(1)} %get-tuple-element.26), channel_id=1, source_target_pairs={{0,3},{1,2},{2,1},{3,0},{4,7},{5,6},{6,5},{7,4},{8,11},{9,10},{10,... | collective-permute-start | bytes 307208 | tf_op jit(solution)/shard_map/ppermute | solution.py:16
  24.3 9.5 %collective-permute-start.9 = (f32[25,8,128]{2,1,0:T(8,128)S(1)}, f32[25,8,128]{2,1,0:T(8,128)S(1)}, u32[]{:S(2)}, u32[]{:S(2)}) collective-permute-start(f32[25,8,128]{2,1,0:T(8,128)S(1)} %get-tuple-element.27), channel_id=1, source_target_pairs={{0,2},{1,3},{2,0},{3,1},{4,6},{5,7},{6,4},{7,5},{8,10},{9,11},{10,... | collective-permute-start | bytes 307208 | tf_op jit(solution)/shard_map/ppermute | solution.py:16
  25.2 8.6 %collective-permute-start.11 = (f32[32,768]{1,0:T(8,128)S(1)}, f32[32,768]{1,0:T(8,128)S(1)}, u32[]{:S(2)}, u32[]{:S(2)}) collective-permute-start(f32[32,768]{1,0:T(8,128)S(1)} %get-tuple-element.30), channel_id=1, source_target_pairs={{0,24},{4,28},{8,16},{12,20},{16,8},{20,12},{24,0},{28,4},{1,25},{... | collective-permute-start | bytes 294920 | tf_op jit(solution)/shard_map/ppermute | solution.py:24
  26.7 7.1 %collective-permute-start.12 = (f32[32,768]{1,0:T(8,128)S(1)}, f32[32,768]{1,0:T(8,128)S(1)}, u32[]{:S(2)}, u32[]{:S(2)}) collective-permute-start(f32[32,768]{1,0:T(8,128)S(1)} %get-tuple-element.32), channel_id=1, source_target_pairs={{0,8},{4,20},{8,0},{12,28},{16,24},{20,4},{24,16},{28,12},{1,9},{5... | collective-permute-start | bytes 294920 | tf_op jit(solution)/shard_map/ppermute | solution.py:24
  27.2 6.6 %collective-permute-start.13 = (f32[32,768]{1,0:T(8,128)S(1)}, f32[32,768]{1,0:T(8,128)S(1)}, u32[]{:S(2)}, u32[]{:S(2)}) collective-permute-start(f32[32,768]{1,0:T(8,128)S(1)} %get-tuple-element.33), channel_id=1, source_target_pairs={{0,16},{4,12},{8,24},{12,4},{16,0},{20,28},{24,8},{28,20},{1,17},{... | collective-permute-start | bytes 294920 | tf_op jit(solution)/shard_map/ppermute | solution.py:24

commit v13 on v12

--- a/solution.py
+++ b/solution.py
@@ -175,7 +175,7 @@
     for k in (2, 3):
         image_blocks[k] = exchange(image_emb, "txt", n_txt, k)
     beside = chip_exchange(both, n_img, (1, 2))
-    diagonal = chip_exchange(after(text_emb, both), n_img, (3, 3))
+    diagonal = chip_exchange(text_emb, n_img, (3, 3))
     image_blocks[1] = exchange(after(image_emb, both), "txt", n_txt, 1)
     sent = jnp.concatenate([beside, diagonal])
     got = exchange(sent, "img", n_img, 1)
@@ -192,7 +192,7 @@
     )(log_scale, bias, *in_vmem(bundle, both, sent, got))
     messages = [exchange(messages[p - 1], "txt", n_txt, IMAGE_ORDER[p]) for p in (3, 2, 1)]
 
-    pair = exchange(after(bundle, own), "img", n_img, 1)
+    pair = exchange(bundle, "img", n_img, 1)
     blocks = pl.pallas_call(
         functools.partial(text_kernel, n_img, n_txt, rows, cols),
         out_shape=[vmem((cols, width))] * chips,

time: 34.7 us -> 33.1 us (0.954)
  waiting for transfers between devices: 11.5 us -> 9.8 us
  starting transfers between devices: 17.2 us -> 16.3 us
  local copies, waits for them, and re-layouts: 0.99 us -> 1.86 us
    ppermute x9, waiting for transfers between devices: 10.7 us -> 9.79 us  [exchange(): return lax.ppermute(x, axis, [(i, i ^ k) for i in range(n)])]
    unnamed x12, local copies, waits for them, and re-layouts: 0.97 us -> 1.83 us
    ppermute x9, starting transfers between devices: 10.6 us -> 9.75 us  [exchange(): return lax.ppermute(x, axis, [(i, i ^ k) for i in range(n)])]
    ppermute x5, waiting for transfers between devices: 0.77 us -> 0.01 us  [chip_exchange(): lax.ppermute(x, 'img', [(i, i ^ 2 * distances[i % 2]) for i in range(n_im...]
  transfers between devices with their start and end apart: 14 -> 14, of which waited for: 6 -> 5; matrix products, arithmetic and copies ran while one was open for 3% -> 3% of each run, Pallas kernels for 3% -> 6%
where the time goes in v13:
time: 33.1 us; the launch traced here: 32.9 us
  starting transfers between devices  16.3 us (49%)
  waiting for transfers between devices  9.8 us (30%)
  Pallas kernels  2.8 us (8%)
  between operations  2.07 us (6%)
  local copies, waits for them, and re-layouts  1.86 us (6%)
    ppermute x9, waiting for transfers between devices, exchange(): return lax.ppermute(x, axis, [(i, i ^ k) for i in range(n)])  9.79 us
    ppermute x9, starting transfers between devices, exchange(): return lax.ppermute(x, axis, [(i, i ^ k) for i in range(n)])  9.75 us
    ppermute x5, starting transfers between devices, chip_exchange(): lax.ppermute(x, 'img', [(i, i ^ 2 * distances[i % 2]) for i in range(n_im...  6.6 us
    unnamed x12, local copies, waits for them, and re-layouts  1.83 us
    pallas_call x1, Pallas kernels, per_device(): pl.pallas_call(functools.partial(image_kernel, n_img, n_txt, rows, cols),...  1.17 us
    pallas_call x1, Pallas kernels, per_device(): pl.pallas_call(functools.partial(text_kernel, n_img, n_txt, rows, cols),...  0.9 us
    pallas_call x1, Pallas kernels, per_device(): pl.pallas_call(functools.partial(sum_kernel, n_txt, chips), out_shape=[ja...  0.74 us
  transfers between devices with their start and end apart: 14, of which 5 were waited for; matrix products, arithmetic and copies ran while one was open for 3% of the time, Pallas kernels for 6%

profile of v13, /device:TPU:0, one launch (start us, length us, event | category | flops | bytes accessed | tf_op | source)
XLA Modules:
  0.0 32.9 jit_solution(11765817888886854518)
XLA Ops:
  0.6 0.0 copy-start.1
  0.6 4.1 %collective-permute-start = (f32[32,768]{1,0:T(8,128)}, f32[32,768]{1,0:T(8,128)S(1)}, u32[]{:S(2)}, u32[]{:S(2)}) collective-permute-start(f32[32,768]{1,0:T(8,128)} %param.5), channel_id=1, source_target_pairs={{0,2},{1,3},{2,0},{3,1},{4,6},{5,7},{6,4},{7,5},{8,10},{9,11},{10,... | collective-permute-start | bytes 294920 | tf_op jit(solution)/shard_map/ppermute | solution.py:16
  4.7 1.3 %collective-permute-start.1 = (f32[32,768]{1,0:T(8,128)}, f32[32,768]{1,0:T(8,128)S(1)}, u32[]{:S(2)}, u32[]{:S(2)}) collective-permute-start(f32[32,768]{1,0:T(8,128)} %param.5), channel_id=1, source_target_pairs={{0,3},{1,2},{2,1},{3,0},{4,7},{5,6},{6,5},{7,4},{8,11},{9,10},{10,... | collective-permute-start | bytes 294920 | tf_op jit(solution)/shard_map/ppermute | solution.py:16
  6.1 0.0 collective-permute-start.2
  6.1 2.4 %collective-permute-start.5 = (f32[32,768]{1,0:T(8,128)}, f32[32,768]{1,0:T(8,128)S(1)}, u32[]{:S(2)}, u32[]{:S(2)}) collective-permute-start(f32[32,768]{1,0:T(8,128)} %param.6), channel_id=1, source_target_pairs={{0,24},{4,28},{8,16},{12,20},{16,8},{20,12},{24,0},{28,4},{1,25},{... | collective-permute-start | bytes 294920 | tf_op jit(solution)/shard_map/ppermute | solution.py:24
  8.5 0.9 %constant_dynamic-update-slice_fusion.7 = f32[136,768]{1,0:T(8,128)S(1)} fusion(f32[32,768]{1,0:T(8,128)} %param.5), kind=kLoop, calls=%fused_computation.8 | loop fusion | bytes 196608
  9.4 0.0 copy-done.1
  9.5 0.0 copy-start
  9.5 0.0 collective-permute-done.2
  9.5 0.6 %collective-permute-start.4 = (f32[64,768]{1,0:T(8,128)S(1)}, f32[64,768]{1,0:T(8,128)S(1)}, u32[]{:S(2)}, u32[]{:S(2)}) collective-permute-start(f32[64,768]{1,0:T(8,128)S(1)} %constant_dynamic-update-slice_fusion.both.refs_4_), channel_id=1, source_target_pairs={{0,8},{4,20},{8,0},{12,28},{16,24},{20,4},{24,16},{28,12},{1,9},{5... | collective-permute-start | bytes 589832 | tf_op jit(solution)/shard_map/ppermute | solution.py:24
  10.1 0.3 copy-done
  10.4 0.2 collective-permute-start.3
  10.6 2.2 %collective-permute-done = f32[32,768]{1,0:T(8,128)S(1)} collective-permute-done((f32[32,768]{1,0:T(8,128)}, f32[32,768]{1,0:T(8,128)S(1)}, u32[]{:S(2)}, u32[]{:S(2)}) %collective-permute-start) | collective-permute-done | bytes 98336 | tf_op jit(solution)/shard_map/ppermute | solution.py:16
  12.8 0.0 collective-permute-done.1
  12.8 2.5 %collective-permute-done.3 = f32[32,768]{1,0:T(8,128)S(1)} collective-permute-done((f32[32,768]{1,0:T(8,128)S(1)}, f32[32,768]{1,0:T(8,128)S(1)}, u32[]{:S(2)}, u32[]{:S(2)}) %collective-permute-start.3) | collective-permute-done | bytes 98336 | tf_op jit(solution)/shard_map/ppermute | solution.py:16
  15.3 0.0 collective-permute-done.4
  15.3 0.0 copy-start.2
  15.3 0.0 collective-permute-done.5
  15.4 0.6 %copy-done.2 = s32[128]{0:T(128)S(1)} copy-done((s32[128]{0:T(128)S(1)}, s32[128]{0:T(128)}, u32[]{:S(2)}) %copy-start.2) | copy-done | bytes 536
  16.0 0.0 collective-permute-start.10
  16.0 0.5 %collective-permute-start.6 = (f32[96,768]{1,0:T(8,128)S(1)}, f32[96,768]{1,0:T(8,128)S(1)}, u32[]{:S(2)}, u32[]{:S(2)}) collective-permute-start(f32[96,768]{1,0:T(8,128)S(1)} %constant_dynamic-update-slice_fusion.2.sent.refs_5_), channel_id=1, source_target_pairs={{0,4},{4,0},{8,12},{12,8},{16,20},{20,16},{24,28},{28,24},{1,5},{5... | collective-permute-start | bytes 884744 | tf_op jit(solution)/shard_map/ppermute | solution.py:16
  17.8 0.4 %collective-permute-done.6.got.refs_6_ = f32[96,768]{1,0:T(8,128)S(1)} collective-permute-done((f32[96,768]{1,0:T(8,128)S(1)}, f32[96,768]{1,0:T(8,128)S(1)}, u32[]{:S(2)}, u32[]{:S(2)}) %collective-permute-start.6) | collective-permute-done | bytes 294944 | tf_op jit(solution)/shard_map/ppermute | solution.py:16
  18.2 1.2 %image_terms.1 = (f32[32,768]{1,0:T(8,128)S(1)}, f32[8,128]{1,0:T(8,128)S(1)}, f32[128,128]{1,0:T(8,128)S(1)}, f32[25,8,128]{2,1,0:T(8,128)S(1)}, f32[25,8,128]{2,1,0:T(8,128)S(1)}, /*index=5*/f32[25,8,128]{2,1,0:T(8,128)S(1)}) custom-call(f32[1]{0:T(128)S(6)} %copy.14.log_scale.refs_0_, f32[1]{0:T(128)S(6)} %copy.15.bias.refs_1_, ...), custom_call_target="tpu_custom_call" | custom-call | tf_op jit(solution)/shard_map/image_terms/pallas_call | solution.py:185
  19.4 0.3 %collective-permute-start.7 = (f32[25,8,128]{2,1,0:T(8,128)S(1)}, f32[25,8,128]{2,1,0:T(8,128)S(1)}, u32[]{:S(2)}, u32[]{:S(2)}) collective-permute-start(f32[25,8,128]{2,1,0:T(8,128)S(1)} %get-tuple-element.22), channel_id=1, source_target_pairs={{0,1},{1,0},{2,3},{3,2},{4,5},{5,4},{6,7},{7,6},{8,9},{9,8},{10,11... | collective-permute-start | bytes 307208 | tf_op jit(solution)/shard_map/ppermute | solution.py:16
  19.7 2.9 %collective-permute-start.8 = (f32[25,8,128]{2,1,0:T(8,128)S(1)}, f32[25,8,128]{2,1,0:T(8,128)S(1)}, u32[]{:S(2)}, u32[]{:S(2)}) collective-permute-start(f32[25,8,128]{2,1,0:T(8,128)S(1)} %get-tuple-element.23), channel_id=1, source_target_pairs={{0,3},{1,2},{2,1},{3,0},{4,7},{5,6},{6,5},{7,4},{8,11},{9,10},{10,... | collective-permute-start | bytes 307208 | tf_op jit(solution)/shard_map/ppermute | solution.py:16
  22.6 0.3 %collective-permute-start.9 = (f32[25,8,128]{2,1,0:T(8,128)S(1)}, f32[25,8,128]{2,1,0:T(8,128)S(1)}, u32[]{:S(2)}, u32[]{:S(2)}) collective-permute-start(f32[25,8,128]{2,1,0:T(8,128)S(1)} %get-tuple-element.24), channel_id=1, source_target_pairs={{0,2},{1,3},{2,0},{3,1},{4,6},{5,7},{6,4},{7,5},{8,10},{9,11},{10,... | collective-permute-start | bytes 307208 | tf_op jit(solution)/shard_map/ppermute | solution.py:16
  22.9 0.0 collective-permute-done.10.refs_3_
  22.9 0.9 %text_terms.1 = (f32[32,768]{1,0:T(8,128)S(1)}, f32[32,768]{1,0:T(8,128)S(1)}, f32[32,768]{1,0:T(8,128)S(1)}, f32[32,768]{1,0:T(8,128)S(1)}) custom-call(f32[1]{0:T(128)S(6)} %copy.14.log_scale.refs_0_, f32[1]{0:T(128)S(6)} %copy.15.bias.refs_1_, f32[136,768]{1,0:T(8,128)S(1)} %pad_dynamic-update-slice_fusion.bundle.refs_2_, ...), custom_call_target="tpu_custom_call" | custom-call | tf_op jit(solution)/shard_map/text_terms/pallas_call | solution.py:196
  23.8 1.9 %collective-permute-start.11 = (f32[32,768]{1,0:T(8,128)S(1)}, f32[32,768]{1,0:T(8,128)S(1)}, u32[]{:S(2)}, u32[]{:S(2)}) collective-permute-start(f32[32,768]{1,0:T(8,128)S(1)} %get-tuple-element.26), channel_id=1, source_target_pairs={{0,24},{4,28},{8,16},{12,20},{16,8},{20,12},{24,0},{28,4},{1,25},{... | collective-permute-start | bytes 294920 | tf_op jit(solution)/shard_map/ppermute | solution.py:24
  25.8 0.7 %collective-permute-start.12 = (f32[32,768]{1,0:T(8,128)S(1)}, f32[32,768]{1,0:T(8,128)S(1)}, u32[]{:S(2)}, u32[]{:S(2)}) collective-permute-start(f32[32,768]{1,0:T(8,128)S(1)} %get-tuple-element.28), channel_id=1, source_target_pairs={{0,8},{4,20},{8,0},{12,28},{16,24},{20,4},{24,16},{28,12},{1,9},{5... | collective-permute-start | bytes 294920 | tf_op jit(solution)/shard_map/ppermute | solution.py:24
  26.5 0.0 collective-permute-done.7.refs_0_
  26.5 0.9 %collective-permute-start.13 = (f32[32,768]{1,0:T(8,128)S(1)}, f32[32,768]{1,0:T(8,128)S(1)}, u32[]{:S(2)}, u32[]{:S(2)}) collective-permute-start(f32[32,768]{1,0:T(8,128)S(1)} %get-tuple-element.29), channel_id=1, source_target_pairs={{0,16},{4,12},{8,24},{12,4},{16,0},{20,28},{24,8},{28,20},{1,17},{... | collective-permute-start | bytes 294920 | tf_op jit(solution)/shard_map/ppermute | solution.py:24
  27.4 1.2 %collective-permute-done.8.refs_1_ = f32[25,8,128]{2,1,0:T(8,128)S(1)} collective-permute-done((f32[25,8,128]{2,1,0:T(8,128)S(1)}, f32[25,8,128]{2,1,0:T(8,128)S(1)}, u32[]{:S(2)}, u32[]{:S(2)}) %collective-permute-start.8) | collective-permute-done | bytes 102432 | tf_op jit(solution)/shard_map/ppermute | solution.py:16
  28.6 3.6 %collective-permute-done.9.refs_2_ = f32[25,8,128]{2,1,0:T(8,128)S(1)} collective-permute-done((f32[25,8,128]{2,1,0:T(8,128)S(1)}, f32[25,8,128]{2,1,0:T(8,128)S(1)}, u32[]{:S(2)}, u32[]{:S(2)}) %collective-permute-start.9) | collective-permute-done | bytes 102432 | tf_op jit(solution)/shard_map/ppermute | solution.py:16
  32.1 0.0 collective-permute-done.11.refs_3_
  32.1 0.0 collective-permute-done.12.refs_5_
  32.1 0.0 collective-permute-done.13.refs_6_
  32.1 0.7 %sums.1 = (f32[1,128]{1,0:T(1,128)}, f32[32,768]{1,0:T(8,128)}, f32[32,768]{1,0:T(8,128)}) custom-call(f32[32,768]{1,0:T(8,128)S(1)} %get-tuple-element.20.own_ref, f32[8,128]{1,0:T(8,128)S(1)} %get-tuple-element.21.loss_ref, f32[25,8,128]{2,1,0:T(8,128)S(1)} %collective-permute-done.7.refs_0_, f32[25,8,128]{2,1,0:T(8,128)S(1)} %collective-permute-done.8.refs_1_, ...), custom_call_target="tpu_custom_call" | custom-call | tf_op jit(solution)/shard_map/sums/pallas_call | solution.py:207
  (9 shorter events, 0.1 us)
Async XLA Ops:
  0.6 8.8 %copy-start.1 = (f32[32,768]{1,0:T(8,128)S(1)}, f32[32,768]{1,0:T(8,128)}, u32[]{:S(2)}) copy-start(f32[32,768]{1,0:T(8,128)} %param.6) | copy-start | bytes 294916
  0.6 12.2 %collective-permute-start = (f32[32,768]{1,0:T(8,128)}, f32[32,768]{1,0:T(8,128)S(1)}, u32[]{:S(2)}, u32[]{:S(2)}) collective-permute-start(f32[32,768]{1,0:T(8,128)} %param.5), channel_id=1, source_target_pairs={{0,2},{1,3},{2,0},{3,1},{4,6},{5,7},{6,4},{7,5},{8,10},{9,11},{10,... | collective-permute-start | bytes 294920 | tf_op jit(solution)/shard_map/ppermute | solution.py:16
  4.7 8.1 %collective-permute-start.1 = (f32[32,768]{1,0:T(8,128)}, f32[32,768]{1,0:T(8,128)S(1)}, u32[]{:S(2)}, u32[]{:S(2)}) collective-permute-start(f32[32,768]{1,0:T(8,128)} %param.5), channel_id=1, source_target_pairs={{0,3},{1,2},{2,1},{3,0},{4,7},{5,6},{6,5},{7,4},{8,11},{9,10},{10,... | collective-permute-start | bytes 294920 | tf_op jit(solution)/shard_map/ppermute | solution.py:16
  6.1 3.4 %collective-permute-start.2 = (f32[32,768]{1,0:T(8,128)}, f32[32,768]{1,0:T(8,128)S(1)}, u32[]{:S(2)}, u32[]{:S(2)}) collective-permute-start(f32[32,768]{1,0:T(8,128)} %param.6), channel_id=1, source_target_pairs={{0,4},{4,0},{8,12},{12,8},{16,20},{20,16},{24,28},{28,24},{1,5},{5... | collective-permute-start | bytes 294920 | tf_op jit(solution)/shard_map/ppermute | solution.py:16
  6.1 9.3 %collective-permute-start.5 = (f32[32,768]{1,0:T(8,128)}, f32[32,768]{1,0:T(8,128)S(1)}, u32[]{:S(2)}, u32[]{:S(2)}) collective-permute-start(f32[32,768]{1,0:T(8,128)} %param.6), channel_id=1, source_target_pairs={{0,24},{4,28},{8,16},{12,20},{16,8},{20,12},{24,0},{28,4},{1,25},{... | collective-permute-start | bytes 294920 | tf_op jit(solution)/shard_map/ppermute | solution.py:24
  9.5 0.9 %copy-start = (f32[32,768]{1,0:T(8,128)S(1)}, f32[32,768]{1,0:T(8,128)}, u32[]{:S(2)}) copy-start(f32[32,768]{1,0:T(8,128)} %param.5) | copy-start | bytes 294916
  9.5 5.8 %collective-permute-start.4 = (f32[64,768]{1,0:T(8,128)S(1)}, f32[64,768]{1,0:T(8,128)S(1)}, u32[]{:S(2)}, u32[]{:S(2)}) collective-permute-start(f32[64,768]{1,0:T(8,128)S(1)} %constant_dynamic-update-slice_fusion.both.refs_4_), channel_id=1, source_target_pairs={{0,8},{4,20},{8,0},{12,28},{16,24},{20,4},{24,16},{28,12},{1,9},{5... | collective-permute-start | bytes 589832 | tf_op jit(solution)/shard_map/ppermute | solution.py:24
  10.4 4.9 %collective-permute-start.3 = (f32[32,768]{1,0:T(8,128)S(1)}, f32[32,768]{1,0:T(8,128)S(1)}, u32[]{:S(2)}, u32[]{:S(2)}) collective-permute-start(f32[32,768]{1,0:T(8,128)S(1)} %copy-done), channel_id=1, source_target_pairs={{0,1},{1,0},{2,3},{3,2},{4,5},{5,4},{6,7},{7,6},{8,9},{9,8},{10,11... | collective-permute-start | bytes 294920 | tf_op jit(solution)/shard_map/ppermute | solution.py:16
  15.3 0.7 %copy-start.2 = (s32[128]{0:T(128)S(1)}, s32[128]{0:T(128)}, u32[]{:S(2)}) copy-start(s32[128]{0:T(128)} %param.7) | copy-start | bytes 1540
  16.0 6.9 %collective-permute-start.10 = (f32[136,768]{1,0:T(8,128)S(1)}, f32[136,768]{1,0:T(8,128)S(1)}, u32[]{:S(2)}, u32[]{:S(2)}) collective-permute-start(f32[136,768]{1,0:T(8,128)S(1)} %pad_dynamic-update-slice_fusion.bundle.refs_2_), channel_id=1, source_target_pairs={{0,4},{4,0},{8,12},{12,8},{16,20},{20,16},{24,28},{28,24},{1,5},{5... | collective-permute-start | bytes 1253384 | tf_op jit(solution)/shard_map/ppermute | solution.py:16
  16.0 2.2 %collective-permute-start.6 = (f32[96,768]{1,0:T(8,128)S(1)}, f32[96,768]{1,0:T(8,128)S(1)}, u32[]{:S(2)}, u32[]{:S(2)}) collective-permute-start(f32[96,768]{1,0:T(8,128)S(1)} %constant_dynamic-update-slice_fusion.2.sent.refs_5_), channel_id=1, source_target_pairs={{0,4},{4,0},{8,12},{12,8},{16,20},{20,16},{24,28},{28,24},{1,5},{5... | collective-permute-start | bytes 884744 | tf_op jit(solution)/shard_map/ppermute | solution.py:16
  19.4 7.1 %collective-permute-start.7 = (f32[25,8,128]{2,1,0:T(8,128)S(1)}, f32[25,8,128]{2,1,0:T(8,128)S(1)}, u32[]{:S(2)}, u32[]{:S(2)}) collective-permute-start(f32[25,8,128]{2,1,0:T(8,128)S(1)} %get-tuple-element.22), channel_id=1, source_target_pairs={{0,1},{1,0},{2,3},{3,2},{4,5},{5,4},{6,7},{7,6},{8,9},{9,8},{10,11... | collective-permute-start | bytes 307208 | tf_op jit(solution)/shard_map/ppermute | solution.py:16
  19.7 8.9 %collective-permute-start.8 = (f32[25,8,128]{2,1,0:T(8,128)S(1)}, f32[25,8,128]{2,1,0:T(8,128)S(1)}, u32[]{:S(2)}, u32[]{:S(2)}) collective-permute-start(f32[25,8,128]{2,1,0:T(8,128)S(1)} %get-tuple-element.23), channel_id=1, source_target_pairs={{0,3},{1,2},{2,1},{3,0},{4,7},{5,6},{6,5},{7,4},{8,11},{9,10},{10,... | collective-permute-start | bytes 307208 | tf_op jit(solution)/shard_map/ppermute | solution.py:16
  22.6 9.6 %collective-permute-start.9 = (f32[25,8,128]{2,1,0:T(8,128)S(1)}, f32[25,8,128]{2,1,0:T(8,128)S(1)}, u32[]{:S(2)}, u32[]{:S(2)}) collective-permute-start(f32[25,8,128]{2,1,0:T(8,128)S(1)} %get-tuple-element.24), channel_id=1, source_target_pairs={{0,2},{1,3},{2,0},{3,1},{4,6},{5,7},{6,4},{7,5},{8,10},{9,11},{10,... | collective-permute-start | bytes 307208 | tf_op jit(solution)/shard_map/ppermute | solution.py:16
  23.8 8.3 %collective-permute-start.11 = (f32[32,768]{1,0:T(8,128)S(1)}, f32[32,768]{1,0:T(8,128)S(1)}, u32[]{:S(2)}, u32[]{:S(2)}) collective-permute-start(f32[32,768]{1,0:T(8,128)S(1)} %get-tuple-element.26), channel_id=1, source_target_pairs={{0,24},{4,28},{8,16},{12,20},{16,8},{20,12},{24,0},{28,4},{1,25},{... | collective-permute-start | bytes 294920 | tf_op jit(solution)/shard_map/ppermute | solution.py:24
  25.8 6.4 %collective-permute-start.12 = (f32[32,768]{1,0:T(8,128)S(1)}, f32[32,768]{1,0:T(8,128)S(1)}, u32[]{:S(2)}, u32[]{:S(2)}) collective-permute-start(f32[32,768]{1,0:T(8,128)S(1)} %get-tuple-element.28), channel_id=1, source_target_pairs={{0,8},{4,20},{8,0},{12,28},{16,24},{20,4},{24,16},{28,12},{1,9},{5... | collective-permute-start | bytes 294920 | tf_op jit(solution)/shard_map/ppermute | solution.py:24
  26.5 5.6 %collective-permute-start.13 = (f32[32,768]{1,0:T(8,128)S(1)}, f32[32,768]{1,0:T(8,128)S(1)}, u32[]{:S(2)}, u32[]{:S(2)}) collective-permute-start(f32[32,768]{1,0:T(8,128)S(1)} %get-tuple-element.29), channel_id=1, source_target_pairs={{0,16},{4,12},{8,24},{12,4},{16,0},{20,28},{24,8},{28,20},{1,17},{... | collective-permute-start | bytes 294920 | tf_op jit(solution)/shard_map/ppermute | solution.py:24

commit v14 on v13

--- a/solution.py
+++ b/solution.py
@@ -179,7 +179,7 @@
     image_blocks[1] = exchange(after(image_emb, both), "txt", n_txt, 1)
     sent = jnp.concatenate([beside, diagonal])
     got = exchange(sent, "img", n_img, 1)
-    numbers = jnp.pad(after(pairs, sent).astype(jnp.float32)[None], ((0, 7), (0, width - count)))
+    numbers = jnp.pad(pairs.astype(jnp.float32)[None], ((0, 7), (0, width - count)))
     bundle = jnp.concatenate([image_blocks[k] for k in IMAGE_ORDER] + [numbers])
 
     own, loss_tile, d_near, *messages = pl.pallas_call(
@@ -192,7 +192,7 @@
     )(log_scale, bias, *in_vmem(bundle, both, sent, got))
     messages = [exchange(messages[p - 1], "txt", n_txt, IMAGE_ORDER[p]) for p in (3, 2, 1)]
 
-    pair = exchange(bundle, "img", n_img, 1)
+    pair = exchange(after(bundle, own), "img", n_img, 1)
     blocks = pl.pallas_call(
         functools.partial(text_kernel, n_img, n_txt, rows, cols),
         out_shape=[vmem((cols, width))] * chips,

time: 33.1 us -> 34.2 us (1.033)
  waiting for transfers between devices: 9.8 us -> 11.5 us
  local copies, waits for them, and re-layouts: 1.86 us -> 1.24 us
    ppermute x9, waiting for transfers between devices: 9.79 us -> 11.5 us  [exchange(): return lax.ppermute(x, axis, [(i, i ^ k) for i in range(n)])]
    ppermute x5, starting transfers between devices: 6.6 us -> 7.68 us  [chip_exchange(): lax.ppermute(x, 'img', [(i, i ^ 2 * distances[i % 2]) for i in range(n_im...]
    ppermute x9, starting transfers between devices: 9.75 us -> 8.74 us  [exchange(): return lax.ppermute(x, axis, [(i, i ^ k) for i in range(n)])]
    unnamed x12 -> x10, local copies, waits for them, and re-layouts: 1.83 us -> 1.21 us
  transfers between devices with their start and end apart: 14 -> 14, of which waited for: 5 -> 5; matrix products, arithmetic and copies ran while one was open for 3% -> 3% of each run, Pallas kernels for 6% -> 3%
where the time goes in v14:
time: 34.2 us; the launch traced here: 34 us
  starting transfers between devices  16.4 us (48%)
  waiting for transfers between devices  11.5 us (34%)
  Pallas kernels  2.8 us (8%)
  between operations  2.09 us (6%)
  local copies, waits for them, and re-layouts  1.24 us (4%)
    ppermute x9, waiting for transfers between devices, exchange(): return lax.ppermute(x, axis, [(i, i ^ k) for i in range(n)])  11.5 us
    ppermute x9, starting transfers between devices, exchange(): return lax.ppermute(x, axis, [(i, i ^ k) for i in range(n)])  8.74 us
    ppermute x5, starting transfers between devices, chip_exchange(): lax.ppermute(x, 'img', [(i, i ^ 2 * distances[i % 2]) for i in range(n_im...  7.68 us
    unnamed x10, local copies, waits for them, and re-layouts  1.21 us
    pallas_call x1, Pallas kernels, per_device(): pl.pallas_call(functools.partial(image_kernel, n_img, n_txt, rows, cols),...  1.17 us
    pallas_call x1, Pallas kernels, per_device(): pl.pallas_call(functools.partial(text_kernel, n_img, n_txt, rows, cols),...  0.89 us
    pallas_call x1, Pallas kernels, per_device(): pl.pallas_call(functools.partial(sum_kernel, n_txt, chips), out_shape=[ja...  0.74 us
  transfers between devices with their start and end apart: 14, of which 5 were waited for; matrix products, arithmetic and copies ran while one was open for 3% of the time, Pallas kernels for 3%

profile of v14, /device:TPU:0, one launch (start us, length us, event | category | flops | bytes accessed | tf_op | source)
XLA Modules:
  0.0 34.0 jit_solution(7643809937383294671)
XLA Ops:
  0.6 0.5 %collective-permute-start.2 = (f32[32,768]{1,0:T(8,128)}, f32[32,768]{1,0:T(8,128)S(1)}, u32[]{:S(2)}, u32[]{:S(2)}) collective-permute-start(f32[32,768]{1,0:T(8,128)} %param.6), channel_id=1, source_target_pairs={{0,4},{4,0},{8,12},{12,8},{16,20},{20,16},{24,28},{28,24},{1,5},{5... | collective-permute-start | bytes 294920 | tf_op jit(solution)/shard_map/ppermute | solution.py:16
  1.1 3.5 %collective-permute-start.5 = (f32[32,768]{1,0:T(8,128)}, f32[32,768]{1,0:T(8,128)S(1)}, u32[]{:S(2)}, u32[]{:S(2)}) collective-permute-start(f32[32,768]{1,0:T(8,128)} %param.6), channel_id=1, source_target_pairs={{0,24},{4,28},{8,16},{12,20},{16,8},{20,12},{24,0},{28,4},{1,25},{... | collective-permute-start | bytes 294920 | tf_op jit(solution)/shard_map/ppermute | solution.py:24
  4.7 3.6 %collective-permute-start.1 = (f32[32,768]{1,0:T(8,128)}, f32[32,768]{1,0:T(8,128)S(1)}, u32[]{:S(2)}, u32[]{:S(2)}) collective-permute-start(f32[32,768]{1,0:T(8,128)} %param.5), channel_id=1, source_target_pairs={{0,3},{1,2},{2,1},{3,0},{4,7},{5,6},{6,5},{7,4},{8,11},{9,10},{10,... | collective-permute-start | bytes 294920 | tf_op jit(solution)/shard_map/ppermute | solution.py:16
  8.3 0.0 collective-permute-start
  8.9 0.0 copy-start.1
  9.6 0.0 copy-done.1
  9.6 0.9 %constant_dynamic-update-slice_fusion.1 = f32[64,768]{1,0:T(8,128)S(1)} fusion(f32[32,768]{1,0:T(8,128)} %param.6), kind=kLoop, calls=%fused_computation.2 | loop fusion | bytes 196608
  10.5 0.0 copy-start
  10.5 0.0 collective-permute-done.2
  10.6 0.6 %collective-permute-start.4 = (f32[64,768]{1,0:T(8,128)S(1)}, f32[64,768]{1,0:T(8,128)S(1)}, u32[]{:S(2)}, u32[]{:S(2)}) collective-permute-start(f32[64,768]{1,0:T(8,128)S(1)} %constant_dynamic-update-slice_fusion.both.refs_4_), channel_id=1, source_target_pairs={{0,8},{4,20},{8,0},{12,28},{16,24},{20,4},{24,16},{28,12},{1,9},{5... | collective-permute-start | bytes 589832 | tf_op jit(solution)/shard_map/ppermute | solution.py:24
  11.2 0.3 copy-done
  11.4 0.8 %collective-permute-start.3 = (f32[32,768]{1,0:T(8,128)S(1)}, f32[32,768]{1,0:T(8,128)S(1)}, u32[]{:S(2)}, u32[]{:S(2)}) collective-permute-start(f32[32,768]{1,0:T(8,128)S(1)} %copy-done), channel_id=1, source_target_pairs={{0,1},{1,0},{2,3},{3,2},{4,5},{5,4},{6,7},{7,6},{8,9},{9,8},{10,11... | collective-permute-start | bytes 294920 | tf_op jit(solution)/shard_map/ppermute | solution.py:16
  12.3 4.9 %collective-permute-done = f32[32,768]{1,0:T(8,128)S(1)} collective-permute-done((f32[32,768]{1,0:T(8,128)}, f32[32,768]{1,0:T(8,128)S(1)}, u32[]{:S(2)}, u32[]{:S(2)}) %collective-permute-start) | collective-permute-done | bytes 98336 | tf_op jit(solution)/shard_map/ppermute | solution.py:16
  17.2 0.0 collective-permute-done.4
  17.2 0.0 collective-permute-done.5
  17.3 0.1 collective-permute-start.6
  17.3 0.0 collective-permute-done.1
  17.4 0.8 %collective-permute-done.3 = f32[32,768]{1,0:T(8,128)S(1)} collective-permute-done((f32[32,768]{1,0:T(8,128)S(1)}, f32[32,768]{1,0:T(8,128)S(1)}, u32[]{:S(2)}, u32[]{:S(2)}) %collective-permute-start.3) | collective-permute-done | bytes 98336 | tf_op jit(solution)/shard_map/ppermute | solution.py:16
  18.2 0.7 %collective-permute-done.6.got.refs_6_ = f32[96,768]{1,0:T(8,128)S(1)} collective-permute-done((f32[96,768]{1,0:T(8,128)S(1)}, f32[96,768]{1,0:T(8,128)S(1)}, u32[]{:S(2)}, u32[]{:S(2)}) %collective-permute-start.6) | collective-permute-done | bytes 294944 | tf_op jit(solution)/shard_map/ppermute | solution.py:16
  18.9 1.2 %image_terms.1 = (f32[32,768]{1,0:T(8,128)S(1)}, f32[8,128]{1,0:T(8,128)S(1)}, f32[128,128]{1,0:T(8,128)S(1)}, f32[25,8,128]{2,1,0:T(8,128)S(1)}, f32[25,8,128]{2,1,0:T(8,128)S(1)}, /*index=5*/f32[25,8,128]{2,1,0:T(8,128)S(1)}) custom-call(f32[1]{0:T(128)S(6)} %copy.14.log_scale.refs_0_, f32[1]{0:T(128)S(6)} %copy.15.bias.refs_1_, ...), custom_call_target="tpu_custom_call" | custom-call | tf_op jit(solution)/shard_map/image_terms/pallas_call | solution.py:185
  20.1 0.2 collective-permute-start.10
  20.3 0.0 collective-permute-start.7
  20.3 3.5 %collective-permute-start.8 = (f32[25,8,128]{2,1,0:T(8,128)S(1)}, f32[25,8,128]{2,1,0:T(8,128)S(1)}, u32[]{:S(2)}, u32[]{:S(2)}) collective-permute-start(f32[25,8,128]{2,1,0:T(8,128)S(1)} %get-tuple-element.22), channel_id=1, source_target_pairs={{0,3},{1,2},{2,1},{3,0},{4,7},{5,6},{6,5},{7,4},{8,11},{9,10},{10,... | collective-permute-start | bytes 307208 | tf_op jit(solution)/shard_map/ppermute | solution.py:16
  23.8 0.0 collective-permute-start.9
  23.8 0.0 collective-permute-done.10.refs_3_
  23.8 0.9 %text_terms.1 = (f32[32,768]{1,0:T(8,128)S(1)}, f32[32,768]{1,0:T(8,128)S(1)}, f32[32,768]{1,0:T(8,128)S(1)}, f32[32,768]{1,0:T(8,128)S(1)}) custom-call(f32[1]{0:T(128)S(6)} %copy.14.log_scale.refs_0_, f32[1]{0:T(128)S(6)} %copy.15.bias.refs_1_, f32[136,768]{1,0:T(8,128)S(1)} %pad_dynamic-update-slice_fusion.bundle.refs_2_, ...), custom_call_target="tpu_custom_call" | custom-call | tf_op jit(solution)/shard_map/text_terms/pallas_call | solution.py:196
  24.7 0.5 %collective-permute-start.11 = (f32[32,768]{1,0:T(8,128)S(1)}, f32[32,768]{1,0:T(8,128)S(1)}, u32[]{:S(2)}, u32[]{:S(2)}) collective-permute-start(f32[32,768]{1,0:T(8,128)S(1)} %get-tuple-element.26), channel_id=1, source_target_pairs={{0,24},{4,28},{8,16},{12,20},{16,8},{20,12},{24,0},{28,4},{1,25},{... | collective-permute-start | bytes 294920 | tf_op jit(solution)/shard_map/ppermute | solution.py:24
  25.2 1.5 %collective-permute-start.12 = (f32[32,768]{1,0:T(8,128)S(1)}, f32[32,768]{1,0:T(8,128)S(1)}, u32[]{:S(2)}, u32[]{:S(2)}) collective-permute-start(f32[32,768]{1,0:T(8,128)S(1)} %get-tuple-element.28), channel_id=1, source_target_pairs={{0,8},{4,20},{8,0},{12,28},{16,24},{20,4},{24,16},{28,12},{1,9},{5... | collective-permute-start | bytes 294920 | tf_op jit(solution)/shard_map/ppermute | solution.py:24
  26.7 0.0 collective-permute-done.7.refs_0_
  26.7 1.5 %collective-permute-start.13 = (f32[32,768]{1,0:T(8,128)S(1)}, f32[32,768]{1,0:T(8,128)S(1)}, u32[]{:S(2)}, u32[]{:S(2)}) collective-permute-start(f32[32,768]{1,0:T(8,128)S(1)} %get-tuple-element.29), channel_id=1, source_target_pairs={{0,16},{4,12},{8,24},{12,4},{16,0},{20,28},{24,8},{28,20},{1,17},{... | collective-permute-start | bytes 294920 | tf_op jit(solution)/shard_map/ppermute | solution.py:24
  28.2 1.5 %collective-permute-done.8.refs_1_ = f32[25,8,128]{2,1,0:T(8,128)S(1)} collective-permute-done((f32[25,8,128]{2,1,0:T(8,128)S(1)}, f32[25,8,128]{2,1,0:T(8,128)S(1)}, u32[]{:S(2)}, u32[]{:S(2)}) %collective-permute-start.8) | collective-permute-done | bytes 102432 | tf_op jit(solution)/shard_map/ppermute | solution.py:16
  29.7 3.5 %collective-permute-done.9.refs_2_ = f32[25,8,128]{2,1,0:T(8,128)S(1)} collective-permute-done((f32[25,8,128]{2,1,0:T(8,128)S(1)}, f32[25,8,128]{2,1,0:T(8,128)S(1)}, u32[]{:S(2)}, u32[]{:S(2)}) %collective-permute-start.9) | collective-permute-done | bytes 102432 | tf_op jit(solution)/shard_map/ppermute | solution.py:16
  33.3 0.0 collective-permute-done.11.refs_3_
  33.3 0.0 collective-permute-done.12.refs_5_
  33.3 0.0 collective-permute-done.13.refs_6_
  33.3 0.7 %sums.1 = (f32[1,128]{1,0:T(1,128)}, f32[32,768]{1,0:T(8,128)}, f32[32,768]{1,0:T(8,128)}) custom-call(f32[32,768]{1,0:T(8,128)S(1)} %get-tuple-element.19.own_ref, f32[8,128]{1,0:T(8,128)S(1)} %get-tuple-element.20.loss_ref, f32[25,8,128]{2,1,0:T(8,128)S(1)} %collective-permute-done.7.refs_0_, f32[25,8,128]{2,1,0:T(8,128)S(1)} %collective-permute-done.8.refs_1_, ...), custom_call_target="tpu_custom_call" | custom-call | tf_op jit(solution)/shard_map/sums/pallas_call | solution.py:207
  (9 shorter events, 0.1 us)
Async XLA Ops:
  0.6 9.9 %collective-permute-start.2 = (f32[32,768]{1,0:T(8,128)}, f32[32,768]{1,0:T(8,128)S(1)}, u32[]{:S(2)}, u32[]{:S(2)}) collective-permute-start(f32[32,768]{1,0:T(8,128)} %param.6), channel_id=1, source_target_pairs={{0,4},{4,0},{8,12},{12,8},{16,20},{20,16},{24,28},{28,24},{1,5},{5... | collective-permute-start | bytes 294920 | tf_op jit(solution)/shard_map/ppermute | solution.py:16
  1.1 16.1 %collective-permute-start.5 = (f32[32,768]{1,0:T(8,128)}, f32[32,768]{1,0:T(8,128)S(1)}, u32[]{:S(2)}, u32[]{:S(2)}) collective-permute-start(f32[32,768]{1,0:T(8,128)} %param.6), channel_id=1, source_target_pairs={{0,24},{4,28},{8,16},{12,20},{16,8},{20,12},{24,0},{28,4},{1,25},{... | collective-permute-start | bytes 294920 | tf_op jit(solution)/shard_map/ppermute | solution.py:24
  4.7 12.7 %collective-permute-start.1 = (f32[32,768]{1,0:T(8,128)}, f32[32,768]{1,0:T(8,128)S(1)}, u32[]{:S(2)}, u32[]{:S(2)}) collective-permute-start(f32[32,768]{1,0:T(8,128)} %param.5), channel_id=1, source_target_pairs={{0,3},{1,2},{2,1},{3,0},{4,7},{5,6},{6,5},{7,4},{8,11},{9,10},{10,... | collective-permute-start | bytes 294920 | tf_op jit(solution)/shard_map/ppermute | solution.py:16
  8.3 8.9 %collective-permute-start = (f32[32,768]{1,0:T(8,128)}, f32[32,768]{1,0:T(8,128)S(1)}, u32[]{:S(2)}, u32[]{:S(2)}) collective-permute-start(f32[32,768]{1,0:T(8,128)} %param.5), channel_id=1, source_target_pairs={{0,2},{1,3},{2,0},{3,1},{4,6},{5,7},{6,4},{7,5},{8,10},{9,11},{10,... | collective-permute-start | bytes 294920 | tf_op jit(solution)/shard_map/ppermute | solution.py:16
  8.9 0.7 %copy-start.1 = (s32[128]{0:T(128)S(1)}, s32[128]{0:T(128)}, u32[]{:S(2)}) copy-start(s32[128]{0:T(128)} %param.7) | copy-start | bytes 1540
  10.5 0.9 %copy-start = (f32[32,768]{1,0:T(8,128)S(1)}, f32[32,768]{1,0:T(8,128)}, u32[]{:S(2)}) copy-start(f32[32,768]{1,0:T(8,128)} %param.5) | copy-start | bytes 294916
  10.6 6.6 %collective-permute-start.4 = (f32[64,768]{1,0:T(8,128)S(1)}, f32[64,768]{1,0:T(8,128)S(1)}, u32[]{:S(2)}, u32[]{:S(2)}) collective-permute-start(f32[64,768]{1,0:T(8,128)S(1)} %constant_dynamic-update-slice_fusion.both.refs_4_), channel_id=1, source_target_pairs={{0,8},{4,20},{8,0},{12,28},{16,24},{20,4},{24,16},{28,12},{1,9},{5... | collective-permute-start | bytes 589832 | tf_op jit(solution)/shard_map/ppermute | solution.py:24
  11.4 6.8 %collective-permute-start.3 = (f32[32,768]{1,0:T(8,128)S(1)}, f32[32,768]{1,0:T(8,128)S(1)}, u32[]{:S(2)}, u32[]{:S(2)}) collective-permute-start(f32[32,768]{1,0:T(8,128)S(1)} %copy-done), channel_id=1, source_target_pairs={{0,1},{1,0},{2,3},{3,2},{4,5},{5,4},{6,7},{7,6},{8,9},{9,8},{10,11... | collective-permute-start | bytes 294920 | tf_op jit(solution)/shard_map/ppermute | solution.py:16
  17.3 1.6 %collective-permute-start.6 = (f32[96,768]{1,0:T(8,128)S(1)}, f32[96,768]{1,0:T(8,128)S(1)}, u32[]{:S(2)}, u32[]{:S(2)}) collective-permute-start(f32[96,768]{1,0:T(8,128)S(1)} %constant_dynamic-update-slice_fusion.6.sent.refs_5_), channel_id=1, source_target_pairs={{0,4},{4,0},{8,12},{12,8},{16,20},{20,16},{24,28},{28,24},{1,5},{5... | collective-permute-start | bytes 884744 | tf_op jit(solution)/shard_map/ppermute | solution.py:16
  20.1 3.7 %collective-permute-start.10 = (f32[136,768]{1,0:T(8,128)S(1)}, f32[136,768]{1,0:T(8,128)S(1)}, u32[]{:S(2)}, u32[]{:S(2)}) collective-permute-start(f32[136,768]{1,0:T(8,128)S(1)} %pad_dynamic-update-slice_fusion.bundle.refs_2_), channel_id=1, source_target_pairs={{0,4},{4,0},{8,12},{12,8},{16,20},{20,16},{24,28},{28,24},{1,5},{5... | collective-permute-start | bytes 1253384 | tf_op jit(solution)/shard_map/ppermute | solution.py:16
  20.3 6.5 %collective-permute-start.7 = (f32[25,8,128]{2,1,0:T(8,128)S(1)}, f32[25,8,128]{2,1,0:T(8,128)S(1)}, u32[]{:S(2)}, u32[]{:S(2)}) collective-permute-start(f32[25,8,128]{2,1,0:T(8,128)S(1)} %get-tuple-element.21), channel_id=1, source_target_pairs={{0,1},{1,0},{2,3},{3,2},{4,5},{5,4},{6,7},{7,6},{8,9},{9,8},{10,11... | collective-permute-start | bytes 307208 | tf_op jit(solution)/shard_map/ppermute | solution.py:16
  20.3 9.4 %collective-permute-start.8 = (f32[25,8,128]{2,1,0:T(8,128)S(1)}, f32[25,8,128]{2,1,0:T(8,128)S(1)}, u32[]{:S(2)}, u32[]{:S(2)}) collective-permute-start(f32[25,8,128]{2,1,0:T(8,128)S(1)} %get-tuple-element.22), channel_id=1, source_target_pairs={{0,3},{1,2},{2,1},{3,0},{4,7},{5,6},{6,5},{7,4},{8,11},{9,10},{10,... | collective-permute-start | bytes 307208 | tf_op jit(solution)/shard_map/ppermute | solution.py:16
  23.8 9.5 %collective-permute-start.9 = (f32[25,8,128]{2,1,0:T(8,128)S(1)}, f32[25,8,128]{2,1,0:T(8,128)S(1)}, u32[]{:S(2)}, u32[]{:S(2)}) collective-permute-start(f32[25,8,128]{2,1,0:T(8,128)S(1)} %get-tuple-element.23), channel_id=1, source_target_pairs={{0,2},{1,3},{2,0},{3,1},{4,6},{5,7},{6,4},{7,5},{8,10},{9,11},{10,... | collective-permute-start | bytes 307208 | tf_op jit(solution)/shard_map/ppermute | solution.py:16
  24.7 8.6 %collective-permute-start.11 = (f32[32,768]{1,0:T(8,128)S(1)}, f32[32,768]{1,0:T(8,128)S(1)}, u32[]{:S(2)}, u32[]{:S(2)}) collective-permute-start(f32[32,768]{1,0:T(8,128)S(1)} %get-tuple-element.26), channel_id=1, source_target_pairs={{0,24},{4,28},{8,16},{12,20},{16,8},{20,12},{24,0},{28,4},{1,25},{... | collective-permute-start | bytes 294920 | tf_op jit(solution)/shard_map/ppermute | solution.py:24
  25.2 8.0 %collective-permute-start.12 = (f32[32,768]{1,0:T(8,128)S(1)}, f32[32,768]{1,0:T(8,128)S(1)}, u32[]{:S(2)}, u32[]{:S(2)}) collective-permute-start(f32[32,768]{1,0:T(8,128)S(1)} %get-tuple-element.28), channel_id=1, source_target_pairs={{0,8},{4,20},{8,0},{12,28},{16,24},{20,4},{24,16},{28,12},{1,9},{5... | collective-permute-start | bytes 294920 | tf_op jit(solution)/shard_map/ppermute | solution.py:24
  26.7 6.5 %collective-permute-start.13 = (f32[32,768]{1,0:T(8,128)S(1)}, f32[32,768]{1,0:T(8,128)S(1)}, u32[]{:S(2)}, u32[]{:S(2)}) collective-permute-start(f32[32,768]{1,0:T(8,128)S(1)} %get-tuple-element.29), channel_id=1, source_target_pairs={{0,16},{4,12},{8,24},{12,4},{16,0},{20,28},{24,8},{28,20},{1,17},{... | collective-permute-start | bytes 294920 | tf_op jit(solution)/shard_map/ppermute | solution.py:24

commit v15 on v14

--- a/solution.py
+++ b/solution.py
@@ -192,7 +192,7 @@
     )(log_scale, bias, *in_vmem(bundle, both, sent, got))
     messages = [exchange(messages[p - 1], "txt", n_txt, IMAGE_ORDER[p]) for p in (3, 2, 1)]
 
-    pair = exchange(after(bundle, own), "img", n_img, 1)
+    pair = exchange(bundle, "img", n_img, 1)
     blocks = pl.pallas_call(
         functools.partial(text_kernel, n_img, n_txt, rows, cols),
         out_shape=[vmem((cols, width))] * chips,

time: 34.2 us -> 32.5 us (0.950)
  waiting for transfers between devices: 11.5 us -> 9.69 us
    ppermute x9, waiting for transfers between devices: 11.5 us -> 9.68 us  [exchange(): return lax.ppermute(x, axis, [(i, i ^ k) for i in range(n)])]
    ppermute x9, starting transfers between devices: 8.74 us -> 9.86 us  [exchange(): return lax.ppermute(x, axis, [(i, i ^ k) for i in range(n)])]
    ppermute x5, starting transfers between devices: 7.68 us -> 6.6 us  [chip_exchange(): lax.ppermute(x, 'img', [(i, i ^ 2 * distances[i % 2]) for i in range(n_im...]
    unnamed x10 -> x12, local copies, waits for them, and re-layouts: 1.21 us -> 1.21 us
  transfers between devices with their start and end apart: 14 -> 14, of which waited for: 5 -> 5; matrix products, arithmetic and copies ran while one was open for 3% -> 3% of each run, Pallas kernels for 3% -> 6%
where the time goes in v15:
time: 32.5 us; the launch traced here: 32.3 us
  starting transfers between devices  16.5 us (51%)
  waiting for transfers between devices  9.69 us (30%)
  Pallas kernels  2.8 us (9%)
  between operations  2.1 us (6%)
  local copies, waits for them, and re-layouts  1.24 us (4%)
    ppermute x9, starting transfers between devices, exchange(): return lax.ppermute(x, axis, [(i, i ^ k) for i in range(n)])  9.86 us
    ppermute x9, waiting for transfers between devices, exchange(): return lax.ppermute(x, axis, [(i, i ^ k) for i in range(n)])  9.68 us
    ppermute x5, starting transfers between devices, chip_exchange(): lax.ppermute(x, 'img', [(i, i ^ 2 * distances[i % 2]) for i in range(n_im...  6.6 us
    unnamed x12, local copies, waits for them, and re-layouts  1.21 us
    pallas_call x1, Pallas kernels, per_device(): pl.pallas_call(functools.partial(image_kernel, n_img, n_txt, rows, cols),...  1.17 us
    pallas_call x1, Pallas kernels, per_device(): pl.pallas_call(functools.partial(text_kernel, n_img, n_txt, rows, cols),...  0.89 us
    pallas_call x1, Pallas kernels, per_device(): pl.pallas_call(functools.partial(sum_kernel, n_txt, chips), out_shape=[ja...  0.74 us
  transfers between devices with their start and end apart: 14, of which 5 were waited for; matrix products, arithmetic and copies ran while one was open for 3% of the time, Pallas kernels for 6%

profile of v15, /device:TPU:0, one launch (start us, length us, event | category | flops | bytes accessed | tf_op | source)
XLA Modules:
  0.0 32.3 jit_solution(11241564784978020064)
XLA Ops:
  0.6 0.0 copy-start.1
  0.6 0.0 copy-start.2
  0.7 4.1 %collective-permute-start = (f32[32,768]{1,0:T(8,128)}, f32[32,768]{1,0:T(8,128)S(1)}, u32[]{:S(2)}, u32[]{:S(2)}) collective-permute-start(f32[32,768]{1,0:T(8,128)} %param.5), channel_id=1, source_target_pairs={{0,2},{1,3},{2,0},{3,1},{4,6},{5,7},{6,4},{7,5},{8,10},{9,11},{10,... | collective-permute-start | bytes 294920 | tf_op jit(solution)/shard_map/ppermute | solution.py:16
  4.8 1.3 %collective-permute-start.1 = (f32[32,768]{1,0:T(8,128)}, f32[32,768]{1,0:T(8,128)S(1)}, u32[]{:S(2)}, u32[]{:S(2)}) collective-permute-start(f32[32,768]{1,0:T(8,128)} %param.5), channel_id=1, source_target_pairs={{0,3},{1,2},{2,1},{3,0},{4,7},{5,6},{6,5},{7,4},{8,11},{9,10},{10,... | collective-permute-start | bytes 294920 | tf_op jit(solution)/shard_map/ppermute | solution.py:16
  6.1 0.0 collective-permute-start.2
  6.1 2.4 %collective-permute-start.5 = (f32[32,768]{1,0:T(8,128)}, f32[32,768]{1,0:T(8,128)S(1)}, u32[]{:S(2)}, u32[]{:S(2)}) collective-permute-start(f32[32,768]{1,0:T(8,128)} %param.6), channel_id=1, source_target_pairs={{0,24},{4,28},{8,16},{12,20},{16,8},{20,12},{24,0},{28,4},{1,25},{... | collective-permute-start | bytes 294920 | tf_op jit(solution)/shard_map/ppermute | solution.py:24
  8.6 0.9 %constant_dynamic-update-slice_fusion.5 = f32[136,768]{1,0:T(8,128)S(1)} fusion(f32[32,768]{1,0:T(8,128)} %param.5), kind=kLoop, calls=%fused_computation.6 | loop fusion | bytes 196608
  9.5 0.0 copy-done.2
  9.5 0.0 copy-done.1
  9.5 0.0 copy-start
  9.5 0.0 collective-permute-done.2
  9.5 0.6 %collective-permute-start.4 = (f32[64,768]{1,0:T(8,128)S(1)}, f32[64,768]{1,0:T(8,128)S(1)}, u32[]{:S(2)}, u32[]{:S(2)}) collective-permute-start(f32[64,768]{1,0:T(8,128)S(1)} %constant_dynamic-update-slice_fusion.both.refs_4_), channel_id=1, source_target_pairs={{0,8},{4,20},{8,0},{12,28},{16,24},{20,4},{24,16},{28,12},{1,9},{5... | collective-permute-start | bytes 589832 | tf_op jit(solution)/shard_map/ppermute | solution.py:24
  10.1 0.3 copy-done
  10.4 0.2 collective-permute-start.3
  10.6 2.2 %collective-permute-done = f32[32,768]{1,0:T(8,128)S(1)} collective-permute-done((f32[32,768]{1,0:T(8,128)}, f32[32,768]{1,0:T(8,128)S(1)}, u32[]{:S(2)}, u32[]{:S(2)}) %collective-permute-start) | collective-permute-done | bytes 98336 | tf_op jit(solution)/shard_map/ppermute | solution.py:16
  12.8 0.0 collective-permute-done.1
  12.8 2.5 %collective-permute-done.3 = f32[32,768]{1,0:T(8,128)S(1)} collective-permute-done((f32[32,768]{1,0:T(8,128)S(1)}, f32[32,768]{1,0:T(8,128)S(1)}, u32[]{:S(2)}, u32[]{:S(2)}) %collective-permute-start.3) | collective-permute-done | bytes 98336 | tf_op jit(solution)/shard_map/ppermute | solution.py:16
  15.3 0.1 collective-permute-start.10
  15.4 0.0 collective-permute-done.4
  15.5 0.0 collective-permute-done.5
  15.5 0.6 %collective-permute-start.6 = (f32[96,768]{1,0:T(8,128)S(1)}, f32[96,768]{1,0:T(8,128)S(1)}, u32[]{:S(2)}, u32[]{:S(2)}) collective-permute-start(f32[96,768]{1,0:T(8,128)S(1)} %constant_dynamic-update-slice_fusion.6.sent.refs_5_), channel_id=1, source_target_pairs={{0,4},{4,0},{8,12},{12,8},{16,20},{20,16},{24,28},{28,24},{1,5},{5... | collective-permute-start | bytes 884744 | tf_op jit(solution)/shard_map/ppermute | solution.py:16
  17.3 0.3 collective-permute-done.6.got.refs_6_
  17.6 1.2 %image_terms.1 = (f32[32,768]{1,0:T(8,128)S(1)}, f32[8,128]{1,0:T(8,128)S(1)}, f32[128,128]{1,0:T(8,128)S(1)}, f32[25,8,128]{2,1,0:T(8,128)S(1)}, f32[25,8,128]{2,1,0:T(8,128)S(1)}, /*index=5*/f32[25,8,128]{2,1,0:T(8,128)S(1)}) custom-call(f32[1]{0:T(128)S(6)} %copy.14.log_scale.refs_0_, f32[1]{0:T(128)S(6)} %copy.15.bias.refs_1_, ...), custom_call_target="tpu_custom_call" | custom-call | tf_op jit(solution)/shard_map/image_terms/pallas_call | solution.py:185
  18.8 0.3 %collective-permute-start.7 = (f32[25,8,128]{2,1,0:T(8,128)S(1)}, f32[25,8,128]{2,1,0:T(8,128)S(1)}, u32[]{:S(2)}, u32[]{:S(2)}) collective-permute-start(f32[25,8,128]{2,1,0:T(8,128)S(1)} %get-tuple-element.20), channel_id=1, source_target_pairs={{0,1},{1,0},{2,3},{3,2},{4,5},{5,4},{6,7},{7,6},{8,9},{9,8},{10,11... | collective-permute-start | bytes 307208 | tf_op jit(solution)/shard_map/ppermute | solution.py:16
  19.1 2.9 %collective-permute-start.8 = (f32[25,8,128]{2,1,0:T(8,128)S(1)}, f32[25,8,128]{2,1,0:T(8,128)S(1)}, u32[]{:S(2)}, u32[]{:S(2)}) collective-permute-start(f32[25,8,128]{2,1,0:T(8,128)S(1)} %get-tuple-element.21), channel_id=1, source_target_pairs={{0,3},{1,2},{2,1},{3,0},{4,7},{5,6},{6,5},{7,4},{8,11},{9,10},{10,... | collective-permute-start | bytes 307208 | tf_op jit(solution)/shard_map/ppermute | solution.py:16
  22.0 0.3 %collective-permute-start.9 = (f32[25,8,128]{2,1,0:T(8,128)S(1)}, f32[25,8,128]{2,1,0:T(8,128)S(1)}, u32[]{:S(2)}, u32[]{:S(2)}) collective-permute-start(f32[25,8,128]{2,1,0:T(8,128)S(1)} %get-tuple-element.22), channel_id=1, source_target_pairs={{0,2},{1,3},{2,0},{3,1},{4,6},{5,7},{6,4},{7,5},{8,10},{9,11},{10,... | collective-permute-start | bytes 307208 | tf_op jit(solution)/shard_map/ppermute | solution.py:16
  22.3 0.0 collective-permute-done.10.refs_3_
  22.3 0.9 %text_terms.1 = (f32[32,768]{1,0:T(8,128)S(1)}, f32[32,768]{1,0:T(8,128)S(1)}, f32[32,768]{1,0:T(8,128)S(1)}, f32[32,768]{1,0:T(8,128)S(1)}) custom-call(f32[1]{0:T(128)S(6)} %copy.14.log_scale.refs_0_, f32[1]{0:T(128)S(6)} %copy.15.bias.refs_1_, f32[136,768]{1,0:T(8,128)S(1)} %pad_dynamic-update-slice_fusion.bundle.refs_2_, ...), custom_call_target="tpu_custom_call" | custom-call | tf_op jit(solution)/shard_map/text_terms/pallas_call | solution.py:196
  23.2 1.9 %collective-permute-start.11 = (f32[32,768]{1,0:T(8,128)S(1)}, f32[32,768]{1,0:T(8,128)S(1)}, u32[]{:S(2)}, u32[]{:S(2)}) collective-permute-start(f32[32,768]{1,0:T(8,128)S(1)} %get-tuple-element.24), channel_id=1, source_target_pairs={{0,24},{4,28},{8,16},{12,20},{16,8},{20,12},{24,0},{28,4},{1,25},{... | collective-permute-start | bytes 294920 | tf_op jit(solution)/shard_map/ppermute | solution.py:24
  25.1 0.7 %collective-permute-start.12 = (f32[32,768]{1,0:T(8,128)S(1)}, f32[32,768]{1,0:T(8,128)S(1)}, u32[]{:S(2)}, u32[]{:S(2)}) collective-permute-start(f32[32,768]{1,0:T(8,128)S(1)} %get-tuple-element.26), channel_id=1, source_target_pairs={{0,8},{4,20},{8,0},{12,28},{16,24},{20,4},{24,16},{28,12},{1,9},{5... | collective-permute-start | bytes 294920 | tf_op jit(solution)/shard_map/ppermute | solution.py:24
  25.9 0.0 collective-permute-done.7.refs_0_
  25.9 0.9 %collective-permute-start.13 = (f32[32,768]{1,0:T(8,128)S(1)}, f32[32,768]{1,0:T(8,128)S(1)}, u32[]{:S(2)}, u32[]{:S(2)}) collective-permute-start(f32[32,768]{1,0:T(8,128)S(1)} %get-tuple-element.27), channel_id=1, source_target_pairs={{0,16},{4,12},{8,24},{12,4},{16,0},{20,28},{24,8},{28,20},{1,17},{... | collective-permute-start | bytes 294920 | tf_op jit(solution)/shard_map/ppermute | solution.py:24
  26.8 1.2 %collective-permute-done.8.refs_1_ = f32[25,8,128]{2,1,0:T(8,128)S(1)} collective-permute-done((f32[25,8,128]{2,1,0:T(8,128)S(1)}, f32[25,8,128]{2,1,0:T(8,128)S(1)}, u32[]{:S(2)}, u32[]{:S(2)}) %collective-permute-start.8) | collective-permute-done | bytes 102432 | tf_op jit(solution)/shard_map/ppermute | solution.py:16
  28.0 3.6 %collective-permute-done.9.refs_2_ = f32[25,8,128]{2,1,0:T(8,128)S(1)} collective-permute-done((f32[25,8,128]{2,1,0:T(8,128)S(1)}, f32[25,8,128]{2,1,0:T(8,128)S(1)}, u32[]{:S(2)}, u32[]{:S(2)}) %collective-permute-start.9) | collective-permute-done | bytes 102432 | tf_op jit(solution)/shard_map/ppermute | solution.py:16
  31.5 0.0 collective-permute-done.11.refs_3_
  31.5 0.0 collective-permute-done.12.refs_5_
  31.5 0.0 collective-permute-done.13.refs_6_
  31.5 0.7 %sums.1 = (f32[1,128]{1,0:T(1,128)}, f32[32,768]{1,0:T(8,128)}, f32[32,768]{1,0:T(8,128)}) custom-call(f32[32,768]{1,0:T(8,128)S(1)} %get-tuple-element.18.own_ref, f32[8,128]{1,0:T(8,128)S(1)} %get-tuple-element.19.loss_ref, f32[25,8,128]{2,1,0:T(8,128)S(1)} %collective-permute-done.7.refs_0_, f32[25,8,128]{2,1,0:T(8,128)S(1)} %collective-permute-done.8.refs_1_, ...), custom_call_target="tpu_custom_call" | custom-call | tf_op jit(solution)/shard_map/sums/pallas_call | solution.py:207
  (9 shorter events, 0.1 us)
Async XLA Ops:
  0.6 8.8 %copy-start.1 = (f32[32,768]{1,0:T(8,128)S(1)}, f32[32,768]{1,0:T(8,128)}, u32[]{:S(2)}) copy-start(f32[32,768]{1,0:T(8,128)} %param.6) | copy-start | bytes 294916
  0.6 8.8 %copy-start.2 = (s32[128]{0:T(128)S(1)}, s32[128]{0:T(128)}, u32[]{:S(2)}) copy-start(s32[128]{0:T(128)} %param.7) | copy-start | bytes 1540
  0.7 12.2 %collective-permute-start = (f32[32,768]{1,0:T(8,128)}, f32[32,768]{1,0:T(8,128)S(1)}, u32[]{:S(2)}, u32[]{:S(2)}) collective-permute-start(f32[32,768]{1,0:T(8,128)} %param.5), channel_id=1, source_target_pairs={{0,2},{1,3},{2,0},{3,1},{4,6},{5,7},{6,4},{7,5},{8,10},{9,11},{10,... | collective-permute-start | bytes 294920 | tf_op jit(solution)/shard_map/ppermute | solution.py:16
  4.8 8.1 %collective-permute-start.1 = (f32[32,768]{1,0:T(8,128)}, f32[32,768]{1,0:T(8,128)S(1)}, u32[]{:S(2)}, u32[]{:S(2)}) collective-permute-start(f32[32,768]{1,0:T(8,128)} %param.5), channel_id=1, source_target_pairs={{0,3},{1,2},{2,1},{3,0},{4,7},{5,6},{6,5},{7,4},{8,11},{9,10},{10,... | collective-permute-start | bytes 294920 | tf_op jit(solution)/shard_map/ppermute | solution.py:16
  6.1 3.4 %collective-permute-start.2 = (f32[32,768]{1,0:T(8,128)}, f32[32,768]{1,0:T(8,128)S(1)}, u32[]{:S(2)}, u32[]{:S(2)}) collective-permute-start(f32[32,768]{1,0:T(8,128)} %param.6), channel_id=1, source_target_pairs={{0,4},{4,0},{8,12},{12,8},{16,20},{20,16},{24,28},{28,24},{1,5},{5... | collective-permute-start | bytes 294920 | tf_op jit(solution)/shard_map/ppermute | solution.py:16
  6.1 9.4 %collective-permute-start.5 = (f32[32,768]{1,0:T(8,128)}, f32[32,768]{1,0:T(8,128)S(1)}, u32[]{:S(2)}, u32[]{:S(2)}) collective-permute-start(f32[32,768]{1,0:T(8,128)} %param.6), channel_id=1, source_target_pairs={{0,24},{4,28},{8,16},{12,20},{16,8},{20,12},{24,0},{28,4},{1,25},{... | collective-permute-start | bytes 294920 | tf_op jit(solution)/shard_map/ppermute | solution.py:24
  9.5 0.9 %copy-start = (f32[32,768]{1,0:T(8,128)S(1)}, f32[32,768]{1,0:T(8,128)}, u32[]{:S(2)}) copy-start(f32[32,768]{1,0:T(8,128)} %param.5) | copy-start | bytes 294916
  9.5 5.9 %collective-permute-start.4 = (f32[64,768]{1,0:T(8,128)S(1)}, f32[64,768]{1,0:T(8,128)S(1)}, u32[]{:S(2)}, u32[]{:S(2)}) collective-permute-start(f32[64,768]{1,0:T(8,128)S(1)} %constant_dynamic-update-slice_fusion.both.refs_4_), channel_id=1, source_target_pairs={{0,8},{4,20},{8,0},{12,28},{16,24},{20,4},{24,16},{28,12},{1,9},{5... | collective-permute-start | bytes 589832 | tf_op jit(solution)/shard_map/ppermute | solution.py:24
  10.4 4.9 %collective-permute-start.3 = (f32[32,768]{1,0:T(8,128)S(1)}, f32[32,768]{1,0:T(8,128)S(1)}, u32[]{:S(2)}, u32[]{:S(2)}) collective-permute-start(f32[32,768]{1,0:T(8,128)S(1)} %copy-done), channel_id=1, source_target_pairs={{0,1},{1,0},{2,3},{3,2},{4,5},{5,4},{6,7},{7,6},{8,9},{9,8},{10,11... | collective-permute-start | bytes 294920 | tf_op jit(solution)/shard_map/ppermute | solution.py:16
  15.3 7.0 %collective-permute-start.10 = (f32[136,768]{1,0:T(8,128)S(1)}, f32[136,768]{1,0:T(8,128)S(1)}, u32[]{:S(2)}, u32[]{:S(2)}) collective-permute-start(f32[136,768]{1,0:T(8,128)S(1)} %pad_dynamic-update-slice_fusion.bundle.refs_2_), channel_id=1, source_target_pairs={{0,4},{4,0},{8,12},{12,8},{16,20},{20,16},{24,28},{28,24},{1,5},{5... | collective-permute-start | bytes 1253384 | tf_op jit(solution)/shard_map/ppermute | solution.py:16
  15.5 2.1 %collective-permute-start.6 = (f32[96,768]{1,0:T(8,128)S(1)}, f32[96,768]{1,0:T(8,128)S(1)}, u32[]{:S(2)}, u32[]{:S(2)}) collective-permute-start(f32[96,768]{1,0:T(8,128)S(1)} %constant_dynamic-update-slice_fusion.6.sent.refs_5_), channel_id=1, source_target_pairs={{0,4},{4,0},{8,12},{12,8},{16,20},{20,16},{24,28},{28,24},{1,5},{5... | collective-permute-start | bytes 884744 | tf_op jit(solution)/shard_map/ppermute | solution.py:16
  18.8 7.1 %collective-permute-start.7 = (f32[25,8,128]{2,1,0:T(8,128)S(1)}, f32[25,8,128]{2,1,0:T(8,128)S(1)}, u32[]{:S(2)}, u32[]{:S(2)}) collective-permute-start(f32[25,8,128]{2,1,0:T(8,128)S(1)} %get-tuple-element.20), channel_id=1, source_target_pairs={{0,1},{1,0},{2,3},{3,2},{4,5},{5,4},{6,7},{7,6},{8,9},{9,8},{10,11... | collective-permute-start | bytes 307208 | tf_op jit(solution)/shard_map/ppermute | solution.py:16
  19.1 8.9 %collective-permute-start.8 = (f32[25,8,128]{2,1,0:T(8,128)S(1)}, f32[25,8,128]{2,1,0:T(8,128)S(1)}, u32[]{:S(2)}, u32[]{:S(2)}) collective-permute-start(f32[25,8,128]{2,1,0:T(8,128)S(1)} %get-tuple-element.21), channel_id=1, source_target_pairs={{0,3},{1,2},{2,1},{3,0},{4,7},{5,6},{6,5},{7,4},{8,11},{9,10},{10,... | collective-permute-start | bytes 307208 | tf_op jit(solution)/shard_map/ppermute | solution.py:16
  22.0 9.6 %collective-permute-start.9 = (f32[25,8,128]{2,1,0:T(8,128)S(1)}, f32[25,8,128]{2,1,0:T(8,128)S(1)}, u32[]{:S(2)}, u32[]{:S(2)}) collective-permute-start(f32[25,8,128]{2,1,0:T(8,128)S(1)} %get-tuple-element.22), channel_id=1, source_target_pairs={{0,2},{1,3},{2,0},{3,1},{4,6},{5,7},{6,4},{7,5},{8,10},{9,11},{10,... | collective-permute-start | bytes 307208 | tf_op jit(solution)/shard_map/ppermute | solution.py:16
  23.2 8.3 %collective-permute-start.11 = (f32[32,768]{1,0:T(8,128)S(1)}, f32[32,768]{1,0:T(8,128)S(1)}, u32[]{:S(2)}, u32[]{:S(2)}) collective-permute-start(f32[32,768]{1,0:T(8,128)S(1)} %get-tuple-element.24), channel_id=1, source_target_pairs={{0,24},{4,28},{8,16},{12,20},{16,8},{20,12},{24,0},{28,4},{1,25},{... | collective-permute-start | bytes 294920 | tf_op jit(solution)/shard_map/ppermute | solution.py:24
  25.1 6.4 %collective-permute-start.12 = (f32[32,768]{1,0:T(8,128)S(1)}, f32[32,768]{1,0:T(8,128)S(1)}, u32[]{:S(2)}, u32[]{:S(2)}) collective-permute-start(f32[32,768]{1,0:T(8,128)S(1)} %get-tuple-element.26), channel_id=1, source_target_pairs={{0,8},{4,20},{8,0},{12,28},{16,24},{20,4},{24,16},{28,12},{1,9},{5... | collective-permute-start | bytes 294920 | tf_op jit(solution)/shard_map/ppermute | solution.py:24
  25.9 5.6 %collective-permute-start.13 = (f32[32,768]{1,0:T(8,128)S(1)}, f32[32,768]{1,0:T(8,128)S(1)}, u32[]{:S(2)}, u32[]{:S(2)}) collective-permute-start(f32[32,768]{1,0:T(8,128)S(1)} %get-tuple-element.27), channel_id=1, source_target_pairs={{0,16},{4,12},{8,24},{12,4},{16,0},{20,28},{24,8},{28,20},{1,17},{... | collective-permute-start | bytes 294920 | tf_op jit(solution)/shard_map/ppermute | solution.py:24

commit v16 on v15

--- a/solution.py
+++ b/solution.py
@@ -29,12 +29,11 @@
     return high, (x - high.astype(jnp.float32)).astype(jnp.bfloat16)
 
 
-def dot(a, b, contract):
-    def part(x, y):
-        dims = ((contract[:1], contract[1:]), ((), ()))
-        return lax.dot_general(x, y, dims, preferred_element_type=jnp.float32)
-
-    return part(a[0], b[0]) + (part(a[0], b[1]) + part(a[1], b[0]))
+def dot(pairs, contract):
+    left = jnp.concatenate([part for a, _ in pairs for part in (a[0], a[0], a[1])], contract[0])
+    right = jnp.concatenate([part for _, b in pairs for part in (b[0], b[1], b[0])], contract[1])
+    dims = ((contract[:1], contract[1:]), ((), ()))
+    return lax.dot_general(left, right, dims, preferred_element_type=jnp.float32)
 
 
 def untwist(row, block, me):
@@ -84,7 +83,7 @@
 
 def derivative(texts, images, ids, matched, log_scale, bias):
     scale = jnp.exp(jnp.full((1, LANES), log_scale[0], jnp.float32))
-    logits = scale * dot(texts, images, (1, 1)) + bias[0]
+    logits = scale * dot([(texts, images)], (1, 1)) + bias[0]
     match = ids == matched
     v = jnp.where(match, -logits, logits)
     e = jnp.exp(-jnp.abs(v))
@@ -110,7 +109,7 @@
     ids = text_ids((texts[0].shape[0], count), n_img, cols, True)
     loss, d = derivative(texts, images, ids, matched, log_scale, bias)
     d_near[...] = d[:len(near) * cols]
-    term = dot(halves(d), texts, (0, 0))
+    term = dot([(halves(d), texts)], (0, 0))
     own[...] = term[:rows]
     back = [IMAGE_ORDER.index(k) for k in range(n_txt)]
     loss_row = shuffle(jnp.sum(loss, axis=0, keepdims=True), rows, back)
@@ -136,7 +135,8 @@
     texts = halves(jnp.concatenate(own_core_texts(cols, both, sent, got)))
     ids = text_ids((texts[0].shape[0], count), n_img, cols, False)
     _, d = derivative(texts, others, ids, matched, log_scale, bias)
-    term = dot(halves(d_ref[...]), halves(bundle[:count]), (1, 0)) + dot(halves(d), others, (1, 0))
+    near = halves(d_ref[...]), halves(bundle[:count])
+    term = dot([near, (halves(d), others)], (1, 0))
     for k, ref in enumerate(block_refs):
         ref[...] = term[k * cols:(k + 1) * cols]
 

time: 32.5 us -> 32.5 us (level)
  no operation moved by 1% of the time
where the time goes in v16:
time: 32.5 us; the launch traced here: 32.3 us
  starting transfers between devices  16.5 us (51%)
  waiting for transfers between devices  9.74 us (30%)
  Pallas kernels  2.76 us (8%)
  between operations  2.08 us (6%)
  local copies, waits for them, and re-layouts  1.24 us (4%)
    ppermute x9, starting transfers between devices, exchange(): return lax.ppermute(x, axis, [(i, i ^ k) for i in range(n)])  9.86 us
    ppermute x9, waiting for transfers between devices, exchange(): return lax.ppermute(x, axis, [(i, i ^ k) for i in range(n)])  9.73 us
    ppermute x5, starting transfers between devices, chip_exchange(): lax.ppermute(x, 'img', [(i, i ^ 2 * distances[i % 2]) for i in range(n_im...  6.6 us
    unnamed x12, local copies, waits for them, and re-layouts  1.21 us
    pallas_call x1, Pallas kernels, per_device(): pl.pallas_call(functools.partial(image_kernel, n_img, n_txt, rows, cols),...  1.17 us
    pallas_call x1, Pallas kernels, per_device(): pl.pallas_call(functools.partial(text_kernel, n_img, n_txt, rows, cols),...  0.84 us
    pallas_call x1, Pallas kernels, per_device(): pl.pallas_call(functools.partial(sum_kernel, n_txt, chips), out_shape=[ja...  0.74 us
  transfers between devices with their start and end apart: 14, of which 5 were waited for; matrix products, arithmetic and copies ran while one was open for 3% of the time, Pallas kernels for 6%

profile of v16, /device:TPU:0, one launch (start us, length us, event | category | flops | bytes accessed | tf_op | source)
XLA Modules:
  0.0 32.3 jit_solution(16668997649118604162)
XLA Ops:
  0.6 0.0 copy-start.1
  0.6 0.0 copy-start.2
  0.7 4.1 %collective-permute-start = (f32[32,768]{1,0:T(8,128)}, f32[32,768]{1,0:T(8,128)S(1)}, u32[]{:S(2)}, u32[]{:S(2)}) collective-permute-start(f32[32,768]{1,0:T(8,128)} %param.5), channel_id=1, source_target_pairs={{0,2},{1,3},{2,0},{3,1},{4,6},{5,7},{6,4},{7,5},{8,10},{9,11},{10,... | collective-permute-start | bytes 294920 | tf_op jit(solution)/shard_map/ppermute | solution.py:16
  4.8 1.3 %collective-permute-start.1 = (f32[32,768]{1,0:T(8,128)}, f32[32,768]{1,0:T(8,128)S(1)}, u32[]{:S(2)}, u32[]{:S(2)}) collective-permute-start(f32[32,768]{1,0:T(8,128)} %param.5), channel_id=1, source_target_pairs={{0,3},{1,2},{2,1},{3,0},{4,7},{5,6},{6,5},{7,4},{8,11},{9,10},{10,... | collective-permute-start | bytes 294920 | tf_op jit(solution)/shard_map/ppermute | solution.py:16
  6.1 0.0 collective-permute-start.2
  6.1 2.4 %collective-permute-start.5 = (f32[32,768]{1,0:T(8,128)}, f32[32,768]{1,0:T(8,128)S(1)}, u32[]{:S(2)}, u32[]{:S(2)}) collective-permute-start(f32[32,768]{1,0:T(8,128)} %param.6), channel_id=1, source_target_pairs={{0,24},{4,28},{8,16},{12,20},{16,8},{20,12},{24,0},{28,4},{1,25},{... | collective-permute-start | bytes 294920 | tf_op jit(solution)/shard_map/ppermute | solution.py:24
  8.6 0.9 %constant_dynamic-update-slice_fusion.5 = f32[136,768]{1,0:T(8,128)S(1)} fusion(f32[32,768]{1,0:T(8,128)} %param.5), kind=kLoop, calls=%fused_computation.6 | loop fusion | bytes 196608
  9.5 0.0 copy-done.2
  9.5 0.0 copy-done.1
  9.5 0.0 copy-start
  9.5 0.0 collective-permute-done.2
  9.5 0.6 %collective-permute-start.4 = (f32[64,768]{1,0:T(8,128)S(1)}, f32[64,768]{1,0:T(8,128)S(1)}, u32[]{:S(2)}, u32[]{:S(2)}) collective-permute-start(f32[64,768]{1,0:T(8,128)S(1)} %constant_dynamic-update-slice_fusion.both.refs_4_), channel_id=1, source_target_pairs={{0,8},{4,20},{8,0},{12,28},{16,24},{20,4},{24,16},{28,12},{1,9},{5... | collective-permute-start | bytes 589832 | tf_op jit(solution)/shard_map/ppermute | solution.py:24
  10.1 0.3 copy-done
  10.4 0.2 collective-permute-start.3
  10.6 2.2 %collective-permute-done = f32[32,768]{1,0:T(8,128)S(1)} collective-permute-done((f32[32,768]{1,0:T(8,128)}, f32[32,768]{1,0:T(8,128)S(1)}, u32[]{:S(2)}, u32[]{:S(2)}) %collective-permute-start) | collective-permute-done | bytes 98336 | tf_op jit(solution)/shard_map/ppermute | solution.py:16
  12.8 0.0 collective-permute-done.1
  12.8 2.5 %collective-permute-done.3 = f32[32,768]{1,0:T(8,128)S(1)} collective-permute-done((f32[32,768]{1,0:T(8,128)S(1)}, f32[32,768]{1,0:T(8,128)S(1)}, u32[]{:S(2)}, u32[]{:S(2)}) %collective-permute-start.3) | collective-permute-done | bytes 98336 | tf_op jit(solution)/shard_map/ppermute | solution.py:16
  15.3 0.1 collective-permute-start.10
  15.4 0.0 collective-permute-done.4
  15.5 0.0 collective-permute-done.5
  15.5 0.6 %collective-permute-start.6 = (f32[96,768]{1,0:T(8,128)S(1)}, f32[96,768]{1,0:T(8,128)S(1)}, u32[]{:S(2)}, u32[]{:S(2)}) collective-permute-start(f32[96,768]{1,0:T(8,128)S(1)} %constant_dynamic-update-slice_fusion.6.sent.refs_5_), channel_id=1, source_target_pairs={{0,4},{4,0},{8,12},{12,8},{16,20},{20,16},{24,28},{28,24},{1,5},{5... | collective-permute-start | bytes 884744 | tf_op jit(solution)/shard_map/ppermute | solution.py:16
  17.3 0.3 collective-permute-done.6.got.refs_6_
  17.6 1.2 %image_terms.1 = (f32[32,768]{1,0:T(8,128)S(1)}, f32[8,128]{1,0:T(8,128)S(1)}, f32[128,128]{1,0:T(8,128)S(1)}, f32[25,8,128]{2,1,0:T(8,128)S(1)}, f32[25,8,128]{2,1,0:T(8,128)S(1)}, /*index=5*/f32[25,8,128]{2,1,0:T(8,128)S(1)}) custom-call(f32[1]{0:T(128)S(6)} %copy.14.log_scale.refs_0_, f32[1]{0:T(128)S(6)} %copy.15.bias.refs_1_, ...), custom_call_target="tpu_custom_call" | custom-call | tf_op jit(solution)/shard_map/image_terms/pallas_call | solution.py:185
  18.8 0.4 %collective-permute-start.7 = (f32[25,8,128]{2,1,0:T(8,128)S(1)}, f32[25,8,128]{2,1,0:T(8,128)S(1)}, u32[]{:S(2)}, u32[]{:S(2)}) collective-permute-start(f32[25,8,128]{2,1,0:T(8,128)S(1)} %get-tuple-element.20), channel_id=1, source_target_pairs={{0,1},{1,0},{2,3},{3,2},{4,5},{5,4},{6,7},{7,6},{8,9},{9,8},{10,11... | collective-permute-start | bytes 307208 | tf_op jit(solution)/shard_map/ppermute | solution.py:16
  19.1 2.9 %collective-permute-start.8 = (f32[25,8,128]{2,1,0:T(8,128)S(1)}, f32[25,8,128]{2,1,0:T(8,128)S(1)}, u32[]{:S(2)}, u32[]{:S(2)}) collective-permute-start(f32[25,8,128]{2,1,0:T(8,128)S(1)} %get-tuple-element.21), channel_id=1, source_target_pairs={{0,3},{1,2},{2,1},{3,0},{4,7},{5,6},{6,5},{7,4},{8,11},{9,10},{10,... | collective-permute-start | bytes 307208 | tf_op jit(solution)/shard_map/ppermute | solution.py:16
  22.0 0.3 %collective-permute-start.9 = (f32[25,8,128]{2,1,0:T(8,128)S(1)}, f32[25,8,128]{2,1,0:T(8,128)S(1)}, u32[]{:S(2)}, u32[]{:S(2)}) collective-permute-start(f32[25,8,128]{2,1,0:T(8,128)S(1)} %get-tuple-element.22), channel_id=1, source_target_pairs={{0,2},{1,3},{2,0},{3,1},{4,6},{5,7},{6,4},{7,5},{8,10},{9,11},{10,... | collective-permute-start | bytes 307208 | tf_op jit(solution)/shard_map/ppermute | solution.py:16
  22.3 0.0 collective-permute-done.10.refs_3_
  22.3 0.8 %text_terms.1 = (f32[32,768]{1,0:T(8,128)S(1)}, f32[32,768]{1,0:T(8,128)S(1)}, f32[32,768]{1,0:T(8,128)S(1)}, f32[32,768]{1,0:T(8,128)S(1)}) custom-call(f32[1]{0:T(128)S(6)} %copy.14.log_scale.refs_0_, f32[1]{0:T(128)S(6)} %copy.15.bias.refs_1_, f32[136,768]{1,0:T(8,128)S(1)} %pad_dynamic-update-slice_fusion.bundle.refs_2_, ...), custom_call_target="tpu_custom_call" | custom-call | tf_op jit(solution)/shard_map/text_terms/pallas_call | solution.py:196
  23.2 1.9 %collective-permute-start.11 = (f32[32,768]{1,0:T(8,128)S(1)}, f32[32,768]{1,0:T(8,128)S(1)}, u32[]{:S(2)}, u32[]{:S(2)}) collective-permute-start(f32[32,768]{1,0:T(8,128)S(1)} %get-tuple-element.24), channel_id=1, source_target_pairs={{0,24},{4,28},{8,16},{12,20},{16,8},{20,12},{24,0},{28,4},{1,25},{... | collective-permute-start | bytes 294920 | tf_op jit(solution)/shard_map/ppermute | solution.py:24
  25.1 0.8 %collective-permute-start.12 = (f32[32,768]{1,0:T(8,128)S(1)}, f32[32,768]{1,0:T(8,128)S(1)}, u32[]{:S(2)}, u32[]{:S(2)}) collective-permute-start(f32[32,768]{1,0:T(8,128)S(1)} %get-tuple-element.26), channel_id=1, source_target_pairs={{0,8},{4,20},{8,0},{12,28},{16,24},{20,4},{24,16},{28,12},{1,9},{5... | collective-permute-start | bytes 294920 | tf_op jit(solution)/shard_map/ppermute | solution.py:24
  25.8 0.0 collective-permute-done.7.refs_0_
  25.8 0.9 %collective-permute-start.13 = (f32[32,768]{1,0:T(8,128)S(1)}, f32[32,768]{1,0:T(8,128)S(1)}, u32[]{:S(2)}, u32[]{:S(2)}) collective-permute-start(f32[32,768]{1,0:T(8,128)S(1)} %get-tuple-element.27), channel_id=1, source_target_pairs={{0,16},{4,12},{8,24},{12,4},{16,0},{20,28},{24,8},{28,20},{1,17},{... | collective-permute-start | bytes 294920 | tf_op jit(solution)/shard_map/ppermute | solution.py:24
  26.7 1.3 %collective-permute-done.8.refs_1_ = f32[25,8,128]{2,1,0:T(8,128)S(1)} collective-permute-done((f32[25,8,128]{2,1,0:T(8,128)S(1)}, f32[25,8,128]{2,1,0:T(8,128)S(1)}, u32[]{:S(2)}, u32[]{:S(2)}) %collective-permute-start.8) | collective-permute-done | bytes 102432 | tf_op jit(solution)/shard_map/ppermute | solution.py:16
  28.0 3.6 %collective-permute-done.9.refs_2_ = f32[25,8,128]{2,1,0:T(8,128)S(1)} collective-permute-done((f32[25,8,128]{2,1,0:T(8,128)S(1)}, f32[25,8,128]{2,1,0:T(8,128)S(1)}, u32[]{:S(2)}, u32[]{:S(2)}) %collective-permute-start.9) | collective-permute-done | bytes 102432 | tf_op jit(solution)/shard_map/ppermute | solution.py:16
  31.5 0.0 collective-permute-done.11.refs_3_
  31.5 0.0 collective-permute-done.12.refs_5_
  31.5 0.0 collective-permute-done.13.refs_6_
  31.5 0.7 %sums.1 = (f32[1,128]{1,0:T(1,128)}, f32[32,768]{1,0:T(8,128)}, f32[32,768]{1,0:T(8,128)}) custom-call(f32[32,768]{1,0:T(8,128)S(1)} %get-tuple-element.18.own_ref, f32[8,128]{1,0:T(8,128)S(1)} %get-tuple-element.19.loss_ref, f32[25,8,128]{2,1,0:T(8,128)S(1)} %collective-permute-done.7.refs_0_, f32[25,8,128]{2,1,0:T(8,128)S(1)} %collective-permute-done.8.refs_1_, ...), custom_call_target="tpu_custom_call" | custom-call | tf_op jit(solution)/shard_map/sums/pallas_call | solution.py:207
  (9 shorter events, 0.1 us)
Async XLA Ops:
  0.6 8.8 %copy-start.1 = (f32[32,768]{1,0:T(8,128)S(1)}, f32[32,768]{1,0:T(8,128)}, u32[]{:S(2)}) copy-start(f32[32,768]{1,0:T(8,128)} %param.6) | copy-start | bytes 294916
  0.6 8.8 %copy-start.2 = (s32[128]{0:T(128)S(1)}, s32[128]{0:T(128)}, u32[]{:S(2)}) copy-start(s32[128]{0:T(128)} %param.7) | copy-start | bytes 1540
  0.7 12.2 %collective-permute-start = (f32[32,768]{1,0:T(8,128)}, f32[32,768]{1,0:T(8,128)S(1)}, u32[]{:S(2)}, u32[]{:S(2)}) collective-permute-start(f32[32,768]{1,0:T(8,128)} %param.5), channel_id=1, source_target_pairs={{0,2},{1,3},{2,0},{3,1},{4,6},{5,7},{6,4},{7,5},{8,10},{9,11},{10,... | collective-permute-start | bytes 294920 | tf_op jit(solution)/shard_map/ppermute | solution.py:16
  4.8 8.1 %collective-permute-start.1 = (f32[32,768]{1,0:T(8,128)}, f32[32,768]{1,0:T(8,128)S(1)}, u32[]{:S(2)}, u32[]{:S(2)}) collective-permute-start(f32[32,768]{1,0:T(8,128)} %param.5), channel_id=1, source_target_pairs={{0,3},{1,2},{2,1},{3,0},{4,7},{5,6},{6,5},{7,4},{8,11},{9,10},{10,... | collective-permute-start | bytes 294920 | tf_op jit(solution)/shard_map/ppermute | solution.py:16
  6.1 3.4 %collective-permute-start.2 = (f32[32,768]{1,0:T(8,128)}, f32[32,768]{1,0:T(8,128)S(1)}, u32[]{:S(2)}, u32[]{:S(2)}) collective-permute-start(f32[32,768]{1,0:T(8,128)} %param.6), channel_id=1, source_target_pairs={{0,4},{4,0},{8,12},{12,8},{16,20},{20,16},{24,28},{28,24},{1,5},{5... | collective-permute-start | bytes 294920 | tf_op jit(solution)/shard_map/ppermute | solution.py:16
  6.1 9.4 %collective-permute-start.5 = (f32[32,768]{1,0:T(8,128)}, f32[32,768]{1,0:T(8,128)S(1)}, u32[]{:S(2)}, u32[]{:S(2)}) collective-permute-start(f32[32,768]{1,0:T(8,128)} %param.6), channel_id=1, source_target_pairs={{0,24},{4,28},{8,16},{12,20},{16,8},{20,12},{24,0},{28,4},{1,25},{... | collective-permute-start | bytes 294920 | tf_op jit(solution)/shard_map/ppermute | solution.py:24
  9.5 0.9 %copy-start = (f32[32,768]{1,0:T(8,128)S(1)}, f32[32,768]{1,0:T(8,128)}, u32[]{:S(2)}) copy-start(f32[32,768]{1,0:T(8,128)} %param.5) | copy-start | bytes 294916
  9.5 5.9 %collective-permute-start.4 = (f32[64,768]{1,0:T(8,128)S(1)}, f32[64,768]{1,0:T(8,128)S(1)}, u32[]{:S(2)}, u32[]{:S(2)}) collective-permute-start(f32[64,768]{1,0:T(8,128)S(1)} %constant_dynamic-update-slice_fusion.both.refs_4_), channel_id=1, source_target_pairs={{0,8},{4,20},{8,0},{12,28},{16,24},{20,4},{24,16},{28,12},{1,9},{5... | collective-permute-start | bytes 589832 | tf_op jit(solution)/shard_map/ppermute | solution.py:24
  10.4 4.9 %collective-permute-start.3 = (f32[32,768]{1,0:T(8,128)S(1)}, f32[32,768]{1,0:T(8,128)S(1)}, u32[]{:S(2)}, u32[]{:S(2)}) collective-permute-start(f32[32,768]{1,0:T(8,128)S(1)} %copy-done), channel_id=1, source_target_pairs={{0,1},{1,0},{2,3},{3,2},{4,5},{5,4},{6,7},{7,6},{8,9},{9,8},{10,11... | collective-permute-start | bytes 294920 | tf_op jit(solution)/shard_map/ppermute | solution.py:16
  15.3 7.0 %collective-permute-start.10 = (f32[136,768]{1,0:T(8,128)S(1)}, f32[136,768]{1,0:T(8,128)S(1)}, u32[]{:S(2)}, u32[]{:S(2)}) collective-permute-start(f32[136,768]{1,0:T(8,128)S(1)} %pad_dynamic-update-slice_fusion.bundle.refs_2_), channel_id=1, source_target_pairs={{0,4},{4,0},{8,12},{12,8},{16,20},{20,16},{24,28},{28,24},{1,5},{5... | collective-permute-start | bytes 1253384 | tf_op jit(solution)/shard_map/ppermute | solution.py:16
  15.5 2.1 %collective-permute-start.6 = (f32[96,768]{1,0:T(8,128)S(1)}, f32[96,768]{1,0:T(8,128)S(1)}, u32[]{:S(2)}, u32[]{:S(2)}) collective-permute-start(f32[96,768]{1,0:T(8,128)S(1)} %constant_dynamic-update-slice_fusion.6.sent.refs_5_), channel_id=1, source_target_pairs={{0,4},{4,0},{8,12},{12,8},{16,20},{20,16},{24,28},{28,24},{1,5},{5... | collective-permute-start | bytes 884744 | tf_op jit(solution)/shard_map/ppermute | solution.py:16
  18.8 7.1 %collective-permute-start.7 = (f32[25,8,128]{2,1,0:T(8,128)S(1)}, f32[25,8,128]{2,1,0:T(8,128)S(1)}, u32[]{:S(2)}, u32[]{:S(2)}) collective-permute-start(f32[25,8,128]{2,1,0:T(8,128)S(1)} %get-tuple-element.20), channel_id=1, source_target_pairs={{0,1},{1,0},{2,3},{3,2},{4,5},{5,4},{6,7},{7,6},{8,9},{9,8},{10,11... | collective-permute-start | bytes 307208 | tf_op jit(solution)/shard_map/ppermute | solution.py:16
  19.1 8.9 %collective-permute-start.8 = (f32[25,8,128]{2,1,0:T(8,128)S(1)}, f32[25,8,128]{2,1,0:T(8,128)S(1)}, u32[]{:S(2)}, u32[]{:S(2)}) collective-permute-start(f32[25,8,128]{2,1,0:T(8,128)S(1)} %get-tuple-element.21), channel_id=1, source_target_pairs={{0,3},{1,2},{2,1},{3,0},{4,7},{5,6},{6,5},{7,4},{8,11},{9,10},{10,... | collective-permute-start | bytes 307208 | tf_op jit(solution)/shard_map/ppermute | solution.py:16
  22.0 9.6 %collective-permute-start.9 = (f32[25,8,128]{2,1,0:T(8,128)S(1)}, f32[25,8,128]{2,1,0:T(8,128)S(1)}, u32[]{:S(2)}, u32[]{:S(2)}) collective-permute-start(f32[25,8,128]{2,1,0:T(8,128)S(1)} %get-tuple-element.22), channel_id=1, source_target_pairs={{0,2},{1,3},{2,0},{3,1},{4,6},{5,7},{6,4},{7,5},{8,10},{9,11},{10,... | collective-permute-start | bytes 307208 | tf_op jit(solution)/shard_map/ppermute | solution.py:16
  23.2 8.4 %collective-permute-start.11 = (f32[32,768]{1,0:T(8,128)S(1)}, f32[32,768]{1,0:T(8,128)S(1)}, u32[]{:S(2)}, u32[]{:S(2)}) collective-permute-start(f32[32,768]{1,0:T(8,128)S(1)} %get-tuple-element.24), channel_id=1, source_target_pairs={{0,24},{4,28},{8,16},{12,20},{16,8},{20,12},{24,0},{28,4},{1,25},{... | collective-permute-start | bytes 294920 | tf_op jit(solution)/shard_map/ppermute | solution.py:24
  25.1 6.5 %collective-permute-start.12 = (f32[32,768]{1,0:T(8,128)S(1)}, f32[32,768]{1,0:T(8,128)S(1)}, u32[]{:S(2)}, u32[]{:S(2)}) collective-permute-start(f32[32,768]{1,0:T(8,128)S(1)} %get-tuple-element.26), channel_id=1, source_target_pairs={{0,8},{4,20},{8,0},{12,28},{16,24},{20,4},{24,16},{28,12},{1,9},{5... | collective-permute-start | bytes 294920 | tf_op jit(solution)/shard_map/ppermute | solution.py:24
  25.8 5.7 %collective-permute-start.13 = (f32[32,768]{1,0:T(8,128)S(1)}, f32[32,768]{1,0:T(8,128)S(1)}, u32[]{:S(2)}, u32[]{:S(2)}) collective-permute-start(f32[32,768]{1,0:T(8,128)S(1)} %get-tuple-element.27), channel_id=1, source_target_pairs={{0,16},{4,12},{8,24},{12,4},{16,0},{20,28},{24,8},{28,20},{1,17},{... | collective-permute-start | bytes 294920 | tf_op jit(solution)/shard_map/ppermute | solution.py:24

commit v17 on v16

--- a/solution.py
+++ b/solution.py
@@ -81,9 +81,9 @@
     return [both[cols:], sent[cols:2 * cols], got[:cols], got[2 * cols:]]
 
 
-def derivative(texts, images, ids, matched, log_scale, bias):
-    scale = jnp.exp(jnp.full((1, LANES), log_scale[0], jnp.float32))
-    logits = scale * dot([(texts, images)], (1, 1)) + bias[0]
+def derivative(texts, images, ids, matched, scalars):
+    scale = jnp.exp(scalars[0:1])
+    logits = scale * dot([(texts, images)], (1, 1)) + scalars[1:2]
     match = ids == matched
     v = jnp.where(match, -logits, logits)
     e = jnp.exp(-jnp.abs(v))
@@ -98,7 +98,7 @@
 
 
 def image_kernel(
-    n_img, n_txt, rows, cols, log_scale, bias, bundle, both, sent, got,
+    n_img, n_txt, rows, cols, scalars, bundle, both, sent, got,
     own, loss_ref, d_near, *messages
 ):
     count = n_txt * rows
@@ -107,7 +107,7 @@
     near = own_core_texts(cols, both, sent, got)
     texts = halves(jnp.concatenate(near + other_core_texts(cols, both, sent, got)))
     ids = text_ids((texts[0].shape[0], count), n_img, cols, True)
-    loss, d = derivative(texts, images, ids, matched, log_scale, bias)
+    loss, d = derivative(texts, images, ids, matched, scalars)
     d_near[...] = d[:len(near) * cols]
     term = dot([(halves(d), texts)], (0, 0))
     own[...] = term[:rows]
@@ -127,14 +127,14 @@
 
 
 def text_kernel(n_img, n_txt, rows, cols, *refs):
-    log_scale, bias, bundle, pair, both, sent, got, d_ref = refs[:8]
-    block_refs = refs[8:]
+    scalars, bundle, pair, both, sent, got, d_ref = refs[:7]
+    block_refs = refs[7:]
     count = n_txt * rows
     matched = matched_texts(pair, rows, count)
     others = halves(pair[:count])
     texts = halves(jnp.concatenate(own_core_texts(cols, both, sent, got)))
     ids = text_ids((texts[0].shape[0], count), n_img, cols, False)
-    _, d = derivative(texts, others, ids, matched, log_scale, bias)
+    _, d = derivative(texts, others, ids, matched, scalars)
     near = halves(d_ref[...]), halves(bundle[:count])
     term = dot([near, (halves(d), others)], (1, 0))
     for k, ref in enumerate(block_refs):
@@ -168,7 +168,7 @@
     rows, cols, width = image_emb.shape[0], text_emb.shape[0], image_emb.shape[1]
     count = n_txt * rows
     tiles = rows * width // (8 * LANES)
-    smem, whole = pl.BlockSpec(memory_space=pltpu.SMEM), pl.BlockSpec(memory_space=pltpu.VMEM)
+    whole = pl.BlockSpec(memory_space=pltpu.VMEM)
 
     both = jnp.concatenate([text_emb, exchange(text_emb, "img", n_img, 1)])
     image_blocks = [image_emb] + [None] * (n_txt - 1)
@@ -178,6 +178,9 @@
     diagonal = chip_exchange(text_emb, n_img, (3, 3))
     image_blocks[1] = exchange(after(image_emb, both), "txt", n_txt, 1)
     sent = jnp.concatenate([beside, diagonal])
+    scalars = jnp.stack([jnp.broadcast_to(log_scale, LANES), jnp.broadcast_to(bias, LANES)])
+    scalars = jnp.pad(scalars, ((0, 6), (0, 0)))
+    image_blocks[1], scalars = lax.optimization_barrier((image_blocks[1], scalars))
     got = exchange(sent, "img", n_img, 1)
     numbers = jnp.pad(pairs.astype(jnp.float32)[None], ((0, 7), (0, width - count)))
     bundle = jnp.concatenate([image_blocks[k] for k in IMAGE_ORDER] + [numbers])
@@ -186,20 +189,20 @@
         functools.partial(image_kernel, n_img, n_txt, rows, cols),
         out_shape=[vmem((rows, width)), vmem((8, LANES)), vmem((chips * cols, count))]
         + [vmem((tiles + 1, 8, LANES))] * (n_txt - 1),
-        in_specs=[smem] * 2 + [whole] * 4,
+        in_specs=[whole] * 5,
         out_specs=[whole] * (2 + n_txt),
         name="image_terms",
-    )(log_scale, bias, *in_vmem(bundle, both, sent, got))
+    )(*in_vmem(scalars, bundle, both, sent, got))
     messages = [exchange(messages[p - 1], "txt", n_txt, IMAGE_ORDER[p]) for p in (3, 2, 1)]
 
-    pair = exchange(bundle, "img", n_img, 1)
+    pair = exchange(after(bundle, got), "img", n_img, 1)
     blocks = pl.pallas_call(
         functools.partial(text_kernel, n_img, n_txt, rows, cols),
         out_shape=[vmem((cols, width))] * chips,
-        in_specs=[smem] * 2 + [whole] * 6,
+        in_specs=[whole] * 7,
         out_specs=[whole] * chips,
         name="text_terms",
-    )(log_scale, bias, *in_vmem(bundle, pair, both, sent, got, d_near))
+    )(*in_vmem(scalars, bundle, pair, both, sent, got, d_near))
     blocks = list(blocks)
     for k, distances in ((3, (3, 3)), (1, (1, 2)), (2, (2, 1))):
         blocks[k] = chip_exchange(blocks[k], n_img, distances)

time: 32.5 us -> 33.5 us (1.031)
  waiting for transfers between devices: 9.74 us -> 11.4 us
  starting transfers between devices: 16.5 us -> 16.1 us
    ppermute x5, waiting for transfers between devices: 0.01 us -> 3.82 us  [chip_exchange(): lax.ppermute(x, 'img', [(i, i ^ 2 * distances[i % 2]) for i in range(n_im...]
    ppermute x9, waiting for transfers between devices: 9.73 us -> 7.54 us  [exchange(): return lax.ppermute(x, axis, [(i, i ^ k) for i in range(n)])]
    ppermute x9, starting transfers between devices: 9.86 us -> 9.46 us  [exchange(): return lax.ppermute(x, axis, [(i, i ^ k) for i in range(n)])]
    unnamed x12 -> x10, local copies, waits for them, and re-layouts: 1.21 us -> 0.99 us
where the time goes in v17:
time: 33.5 us; the launch traced here: 33.4 us
  starting transfers between devices  16.1 us (48%)
  waiting for transfers between devices  11.4 us (34%)
  Pallas kernels  2.78 us (8%)
  between operations  2.08 us (6%)
  local copies, waits for them, and re-layouts  1.08 us (3%)
    ppermute x9, starting transfers between devices, exchange(): return lax.ppermute(x, axis, [(i, i ^ k) for i in range(n)])  9.46 us
    ppermute x9, waiting for transfers between devices, exchange(): return lax.ppermute(x, axis, [(i, i ^ k) for i in range(n)])  7.54 us
    ppermute x5, starting transfers between devices, chip_exchange(): lax.ppermute(x, 'img', [(i, i ^ 2 * distances[i % 2]) for i in range(n_im...  6.6 us
    ppermute x5, waiting for transfers between devices, chip_exchange(): lax.ppermute(x, 'img', [(i, i ^ 2 * distances[i % 2]) for i in range(n_im...  3.82 us
    pallas_call x1, Pallas kernels, per_device(): pl.pallas_call(functools.partial(image_kernel, n_img, n_txt, rows, cols),...  1.18 us
    unnamed x10, local copies, waits for them, and re-layouts  0.99 us
    pallas_call x1, Pallas kernels, per_device(): pl.pallas_call(functools.partial(text_kernel, n_img, n_txt, rows, cols),...  0.85 us
    pallas_call x1, Pallas kernels, per_device(): pl.pallas_call(functools.partial(sum_kernel, n_txt, chips), out_shape=[ja...  0.75 us
  transfers between devices with their start and end apart: 14, of which 5 were waited for; matrix products, arithmetic and copies ran while one was open for 3% of the time, Pallas kernels for 6%

profile of v17, /device:TPU:0, one launch (start us, length us, event | category | flops | bytes accessed | tf_op | source)
XLA Modules:
  0.0 33.4 jit_solution(13753503055096812008)
XLA Ops:
  0.6 0.0 copy-start
  0.6 4.1 %collective-permute-start.2 = (f32[32,768]{1,0:T(8,128)}, f32[32,768]{1,0:T(8,128)S(1)}, u32[]{:S(2)}, u32[]{:S(2)}) collective-permute-start(f32[32,768]{1,0:T(8,128)} %param.5), channel_id=1, source_target_pairs={{0,2},{1,3},{2,0},{3,1},{4,6},{5,7},{6,4},{7,5},{8,10},{9,11},{10,... | collective-permute-start | bytes 294920 | tf_op jit(solution)/shard_map/ppermute | solution.py:16
  4.7 1.3 %collective-permute-start.3 = (f32[32,768]{1,0:T(8,128)}, f32[32,768]{1,0:T(8,128)S(1)}, u32[]{:S(2)}, u32[]{:S(2)}) collective-permute-start(f32[32,768]{1,0:T(8,128)} %param.5), channel_id=1, source_target_pairs={{0,3},{1,2},{2,1},{3,0},{4,7},{5,6},{6,5},{7,4},{8,11},{9,10},{10,... | collective-permute-start | bytes 294920 | tf_op jit(solution)/shard_map/ppermute | solution.py:16
  6.1 0.0 collective-permute-start
  6.1 2.4 %collective-permute-start.5 = (f32[32,768]{1,0:T(8,128)}, f32[32,768]{1,0:T(8,128)S(1)}, u32[]{:S(2)}, u32[]{:S(2)}) collective-permute-start(f32[32,768]{1,0:T(8,128)} %param.6), channel_id=1, source_target_pairs={{0,24},{4,28},{8,16},{12,20},{16,8},{20,12},{24,0},{28,4},{1,25},{... | collective-permute-start | bytes 294920 | tf_op jit(solution)/shard_map/ppermute | solution.py:24
  8.5 0.9 %constant_dynamic-update-slice_fusion.1 = f32[64,768]{1,0:T(8,128)S(1)} fusion(f32[32,768]{1,0:T(8,128)} %param.6), kind=kLoop, calls=%fused_computation.2 | loop fusion | bytes 196608
  10.1 0.0 copy-start.1
  10.8 0.0 copy-done.1
  10.8 0.0 copy-done
  10.8 0.0 collective-permute-done
  10.9 0.6 %collective-permute-start.4 = (f32[64,768]{1,0:T(8,128)S(1)}, f32[64,768]{1,0:T(8,128)S(1)}, u32[]{:S(2)}, u32[]{:S(2)}) collective-permute-start(f32[64,768]{1,0:T(8,128)S(1)} %constant_dynamic-update-slice_fusion.both.refs_3_), channel_id=1, source_target_pairs={{0,8},{4,20},{8,0},{12,28},{16,24},{20,4},{24,16},{28,12},{1,9},{5... | collective-permute-start | bytes 589832 | tf_op jit(solution)/shard_map/ppermute | solution.py:24
  11.5 0.2 collective-permute-start.1
  11.7 1.1 %collective-permute-done.2 = f32[32,768]{1,0:T(8,128)S(1)} collective-permute-done((f32[32,768]{1,0:T(8,128)}, f32[32,768]{1,0:T(8,128)S(1)}, u32[]{:S(2)}, u32[]{:S(2)}) %collective-permute-start.2) | collective-permute-done | bytes 98336 | tf_op jit(solution)/shard_map/ppermute | solution.py:16
  12.8 3.8 %collective-permute-done.4 = f32[64,768]{1,0:T(8,128)S(1)} collective-permute-done((f32[64,768]{1,0:T(8,128)S(1)}, f32[64,768]{1,0:T(8,128)S(1)}, u32[]{:S(2)}, u32[]{:S(2)}) %collective-permute-start.4) | collective-permute-done | bytes 196640 | tf_op jit(solution)/shard_map/ppermute | solution.py:24
  16.6 0.0 collective-permute-done.5
  16.7 0.1 collective-permute-start.6
  16.7 0.0 collective-permute-done.3
  16.8 0.0 collective-permute-done.1
  16.8 0.1 pad.12.scalars.refs_0_
  16.9 1.4 %collective-permute-done.6.got.refs_5_ = f32[96,768]{1,0:T(8,128)S(1)} collective-permute-done((f32[96,768]{1,0:T(8,128)S(1)}, f32[96,768]{1,0:T(8,128)S(1)}, u32[]{:S(2)}, u32[]{:S(2)}) %collective-permute-start.6) | collective-permute-done | bytes 294944 | tf_op jit(solution)/shard_map/ppermute | solution.py:16
  18.3 0.1 collective-permute-start.10
  18.4 1.2 %image_terms.1 = (f32[32,768]{1,0:T(8,128)S(1)}, f32[8,128]{1,0:T(8,128)S(1)}, f32[128,128]{1,0:T(8,128)S(1)}, f32[25,8,128]{2,1,0:T(8,128)S(1)}, f32[25,8,128]{2,1,0:T(8,128)S(1)}, /*index=5*/f32[25,8,128]{2,1,0:T(8,128)S(1)}) custom-call(f32[8,128]{1,0:T(8,128)S(1)} %pad.12.scalars.refs_0_, f32[136,768]{1,0:T(8,128)S(1)} %pad_dynamic-update-slice_fusion.bundle.refs_1_, ...), custom_call_target="tpu_custom_call" | custom-call | tf_op jit(solution)/shard_map/image_terms/pallas_call | solution.py:188
  19.6 0.3 collective-permute-start.7
  19.9 2.9 %collective-permute-start.8 = (f32[25,8,128]{2,1,0:T(8,128)S(1)}, f32[25,8,128]{2,1,0:T(8,128)S(1)}, u32[]{:S(2)}, u32[]{:S(2)}) collective-permute-start(f32[25,8,128]{2,1,0:T(8,128)S(1)} %get-tuple-element.26), channel_id=1, source_target_pairs={{0,3},{1,2},{2,1},{3,0},{4,7},{5,6},{6,5},{7,4},{8,11},{9,10},{10,... | collective-permute-start | bytes 307208 | tf_op jit(solution)/shard_map/ppermute | solution.py:16
  22.9 0.3 %collective-permute-start.9 = (f32[25,8,128]{2,1,0:T(8,128)S(1)}, f32[25,8,128]{2,1,0:T(8,128)S(1)}, u32[]{:S(2)}, u32[]{:S(2)}) collective-permute-start(f32[25,8,128]{2,1,0:T(8,128)S(1)} %get-tuple-element.27), channel_id=1, source_target_pairs={{0,2},{1,3},{2,0},{3,1},{4,6},{5,7},{6,4},{7,5},{8,10},{9,11},{10,... | collective-permute-start | bytes 307208 | tf_op jit(solution)/shard_map/ppermute | solution.py:16
  23.2 0.0 collective-permute-done.10.refs_2_
  23.2 0.8 %text_terms.1 = (f32[32,768]{1,0:T(8,128)S(1)}, f32[32,768]{1,0:T(8,128)S(1)}, f32[32,768]{1,0:T(8,128)S(1)}, f32[32,768]{1,0:T(8,128)S(1)}) custom-call(f32[8,128]{1,0:T(8,128)S(1)} %pad.12.scalars.refs_0_, f32[136,768]{1,0:T(8,128)S(1)} %pad_dynamic-update-slice_fusion.bundle.refs_1_, f32[136,768]{1,0:T(8,128)S(1)} %collective-permute-done.10.refs_2_, ...), custom_call_target="tpu_custom_call" | custom-call | tf_op jit(solution)/shard_map/text_terms/pallas_call | solution.py:199
  24.0 0.5 %collective-permute-start.11 = (f32[32,768]{1,0:T(8,128)S(1)}, f32[32,768]{1,0:T(8,128)S(1)}, u32[]{:S(2)}, u32[]{:S(2)}) collective-permute-start(f32[32,768]{1,0:T(8,128)S(1)} %get-tuple-element.30), channel_id=1, source_target_pairs={{0,24},{4,28},{8,16},{12,20},{16,8},{20,12},{24,0},{28,4},{1,25},{... | collective-permute-start | bytes 294920 | tf_op jit(solution)/shard_map/ppermute | solution.py:24
  24.6 1.5 %collective-permute-start.12 = (f32[32,768]{1,0:T(8,128)S(1)}, f32[32,768]{1,0:T(8,128)S(1)}, u32[]{:S(2)}, u32[]{:S(2)}) collective-permute-start(f32[32,768]{1,0:T(8,128)S(1)} %get-tuple-element.32), channel_id=1, source_target_pairs={{0,8},{4,20},{8,0},{12,28},{16,24},{20,4},{24,16},{28,12},{1,9},{5... | collective-permute-start | bytes 294920 | tf_op jit(solution)/shard_map/ppermute | solution.py:24
  26.1 0.0 collective-permute-done.7.refs_0_
  26.1 1.5 %collective-permute-start.13 = (f32[32,768]{1,0:T(8,128)S(1)}, f32[32,768]{1,0:T(8,128)S(1)}, u32[]{:S(2)}, u32[]{:S(2)}) collective-permute-start(f32[32,768]{1,0:T(8,128)S(1)} %get-tuple-element.33), channel_id=1, source_target_pairs={{0,16},{4,12},{8,24},{12,4},{16,0},{20,28},{24,8},{28,20},{1,17},{... | collective-permute-start | bytes 294920 | tf_op jit(solution)/shard_map/ppermute | solution.py:24
  27.6 1.2 %collective-permute-done.8.refs_1_ = f32[25,8,128]{2,1,0:T(8,128)S(1)} collective-permute-done((f32[25,8,128]{2,1,0:T(8,128)S(1)}, f32[25,8,128]{2,1,0:T(8,128)S(1)}, u32[]{:S(2)}, u32[]{:S(2)}) %collective-permute-start.8) | collective-permute-done | bytes 102432 | tf_op jit(solution)/shard_map/ppermute | solution.py:16
  28.8 3.8 %collective-permute-done.9.refs_2_ = f32[25,8,128]{2,1,0:T(8,128)S(1)} collective-permute-done((f32[25,8,128]{2,1,0:T(8,128)S(1)}, f32[25,8,128]{2,1,0:T(8,128)S(1)}, u32[]{:S(2)}, u32[]{:S(2)}) %collective-permute-start.9) | collective-permute-done | bytes 102432 | tf_op jit(solution)/shard_map/ppermute | solution.py:16
  32.6 0.0 collective-permute-done.11.refs_3_
  32.6 0.0 collective-permute-done.12.refs_5_
  32.6 0.0 collective-permute-done.13.refs_6_
  32.6 0.7 %sums.1 = (f32[1,128]{1,0:T(1,128)}, f32[32,768]{1,0:T(8,128)}, f32[32,768]{1,0:T(8,128)}) custom-call(f32[32,768]{1,0:T(8,128)S(1)} %get-tuple-element.23.own_ref, f32[8,128]{1,0:T(8,128)S(1)} %get-tuple-element.24.loss_ref, f32[25,8,128]{2,1,0:T(8,128)S(1)} %collective-permute-done.7.refs_0_, f32[25,8,128]{2,1,0:T(8,128)S(1)} %collective-permute-done.8.refs_1_, ...), custom_call_target="tpu_custom_call" | custom-call | tf_op jit(solution)/shard_map/sums/pallas_call | solution.py:210
  (10 shorter events, 0.1 us)
Async XLA Ops:
  0.6 10.2 %copy-start = (f32[32,768]{1,0:T(8,128)S(1)}, f32[32,768]{1,0:T(8,128)}, u32[]{:S(2)}) copy-start(f32[32,768]{1,0:T(8,128)} %param.5) | copy-start | bytes 294916
  0.6 12.1 %collective-permute-start.2 = (f32[32,768]{1,0:T(8,128)}, f32[32,768]{1,0:T(8,128)S(1)}, u32[]{:S(2)}, u32[]{:S(2)}) collective-permute-start(f32[32,768]{1,0:T(8,128)} %param.5), channel_id=1, source_target_pairs={{0,2},{1,3},{2,0},{3,1},{4,6},{5,7},{6,4},{7,5},{8,10},{9,11},{10,... | collective-permute-start | bytes 294920 | tf_op jit(solution)/shard_map/ppermute | solution.py:16
  4.7 12.0 %collective-permute-start.3 = (f32[32,768]{1,0:T(8,128)}, f32[32,768]{1,0:T(8,128)S(1)}, u32[]{:S(2)}, u32[]{:S(2)}) collective-permute-start(f32[32,768]{1,0:T(8,128)} %param.5), channel_id=1, source_target_pairs={{0,3},{1,2},{2,1},{3,0},{4,7},{5,6},{6,5},{7,4},{8,11},{9,10},{10,... | collective-permute-start | bytes 294920 | tf_op jit(solution)/shard_map/ppermute | solution.py:16
  6.1 4.8 %collective-permute-start = (f32[32,768]{1,0:T(8,128)}, f32[32,768]{1,0:T(8,128)S(1)}, u32[]{:S(2)}, u32[]{:S(2)}) collective-permute-start(f32[32,768]{1,0:T(8,128)} %param.6), channel_id=1, source_target_pairs={{0,4},{4,0},{8,12},{12,8},{16,20},{20,16},{24,28},{28,24},{1,5},{5... | collective-permute-start | bytes 294920 | tf_op jit(solution)/shard_map/ppermute | solution.py:16
  6.1 10.5 %collective-permute-start.5 = (f32[32,768]{1,0:T(8,128)}, f32[32,768]{1,0:T(8,128)S(1)}, u32[]{:S(2)}, u32[]{:S(2)}) collective-permute-start(f32[32,768]{1,0:T(8,128)} %param.6), channel_id=1, source_target_pairs={{0,24},{4,28},{8,16},{12,20},{16,8},{20,12},{24,0},{28,4},{1,25},{... | collective-permute-start | bytes 294920 | tf_op jit(solution)/shard_map/ppermute | solution.py:24
  10.1 0.7 %copy-start.1 = (s32[128]{0:T(128)S(1)}, s32[128]{0:T(128)}, u32[]{:S(2)}) copy-start(s32[128]{0:T(128)} %param.7) | copy-start | bytes 1540
  10.9 5.7 %collective-permute-start.4 = (f32[64,768]{1,0:T(8,128)S(1)}, f32[64,768]{1,0:T(8,128)S(1)}, u32[]{:S(2)}, u32[]{:S(2)}) collective-permute-start(f32[64,768]{1,0:T(8,128)S(1)} %constant_dynamic-update-slice_fusion.both.refs_3_), channel_id=1, source_target_pairs={{0,8},{4,20},{8,0},{12,28},{16,24},{20,4},{24,16},{28,12},{1,9},{5... | collective-permute-start | bytes 589832 | tf_op jit(solution)/shard_map/ppermute | solution.py:24
  11.5 5.3 %collective-permute-start.1 = (f32[32,768]{1,0:T(8,128)S(1)}, f32[32,768]{1,0:T(8,128)S(1)}, u32[]{:S(2)}, u32[]{:S(2)}) collective-permute-start(f32[32,768]{1,0:T(8,128)S(1)} %copy-done), channel_id=1, source_target_pairs={{0,1},{1,0},{2,3},{3,2},{4,5},{5,4},{6,7},{7,6},{8,9},{9,8},{10,11... | collective-permute-start | bytes 294920 | tf_op jit(solution)/shard_map/ppermute | solution.py:16
  16.7 1.6 %collective-permute-start.6 = (f32[96,768]{1,0:T(8,128)S(1)}, f32[96,768]{1,0:T(8,128)S(1)}, u32[]{:S(2)}, u32[]{:S(2)}) collective-permute-start(f32[96,768]{1,0:T(8,128)S(1)} %constant_dynamic-update-slice_fusion.6.sent.refs_4_), channel_id=1, source_target_pairs={{0,4},{4,0},{8,12},{12,8},{16,20},{20,16},{24,28},{28,24},{1,5},{5... | collective-permute-start | bytes 884744 | tf_op jit(solution)/shard_map/ppermute | solution.py:16
  18.3 4.9 %collective-permute-start.10 = (f32[136,768]{1,0:T(8,128)S(1)}, f32[136,768]{1,0:T(8,128)S(1)}, u32[]{:S(2)}, u32[]{:S(2)}) collective-permute-start(f32[136,768]{1,0:T(8,128)S(1)} %pad_dynamic-update-slice_fusion.bundle.refs_1_), channel_id=1, source_target_pairs={{0,4},{4,0},{8,12},{12,8},{16,20},{20,16},{24,28},{28,24},{1,5},{5... | collective-permute-start | bytes 1253384 | tf_op jit(solution)/shard_map/ppermute | solution.py:16
  19.6 6.5 %collective-permute-start.7 = (f32[25,8,128]{2,1,0:T(8,128)S(1)}, f32[25,8,128]{2,1,0:T(8,128)S(1)}, u32[]{:S(2)}, u32[]{:S(2)}) collective-permute-start(f32[25,8,128]{2,1,0:T(8,128)S(1)} %get-tuple-element.25), channel_id=1, source_target_pairs={{0,1},{1,0},{2,3},{3,2},{4,5},{5,4},{6,7},{7,6},{8,9},{9,8},{10,11... | collective-permute-start | bytes 307208 | tf_op jit(solution)/shard_map/ppermute | solution.py:16
  19.9 8.9 %collective-permute-start.8 = (f32[25,8,128]{2,1,0:T(8,128)S(1)}, f32[25,8,128]{2,1,0:T(8,128)S(1)}, u32[]{:S(2)}, u32[]{:S(2)}) collective-permute-start(f32[25,8,128]{2,1,0:T(8,128)S(1)} %get-tuple-element.26), channel_id=1, source_target_pairs={{0,3},{1,2},{2,1},{3,0},{4,7},{5,6},{6,5},{7,4},{8,11},{9,10},{10,... | collective-permute-start | bytes 307208 | tf_op jit(solution)/shard_map/ppermute | solution.py:16
  22.9 9.8 %collective-permute-start.9 = (f32[25,8,128]{2,1,0:T(8,128)S(1)}, f32[25,8,128]{2,1,0:T(8,128)S(1)}, u32[]{:S(2)}, u32[]{:S(2)}) collective-permute-start(f32[25,8,128]{2,1,0:T(8,128)S(1)} %get-tuple-element.27), channel_id=1, source_target_pairs={{0,2},{1,3},{2,0},{3,1},{4,6},{5,7},{6,4},{7,5},{8,10},{9,11},{10,... | collective-permute-start | bytes 307208 | tf_op jit(solution)/shard_map/ppermute | solution.py:16
  24.0 8.6 %collective-permute-start.11 = (f32[32,768]{1,0:T(8,128)S(1)}, f32[32,768]{1,0:T(8,128)S(1)}, u32[]{:S(2)}, u32[]{:S(2)}) collective-permute-start(f32[32,768]{1,0:T(8,128)S(1)} %get-tuple-element.30), channel_id=1, source_target_pairs={{0,24},{4,28},{8,16},{12,20},{16,8},{20,12},{24,0},{28,4},{1,25},{... | collective-permute-start | bytes 294920 | tf_op jit(solution)/shard_map/ppermute | solution.py:24
  24.6 8.0 %collective-permute-start.12 = (f32[32,768]{1,0:T(8,128)S(1)}, f32[32,768]{1,0:T(8,128)S(1)}, u32[]{:S(2)}, u32[]{:S(2)}) collective-permute-start(f32[32,768]{1,0:T(8,128)S(1)} %get-tuple-element.32), channel_id=1, source_target_pairs={{0,8},{4,20},{8,0},{12,28},{16,24},{20,4},{24,16},{28,12},{1,9},{5... | collective-permute-start | bytes 294920 | tf_op jit(solution)/shard_map/ppermute | solution.py:24
  26.1 6.5 %collective-permute-start.13 = (f32[32,768]{1,0:T(8,128)S(1)}, f32[32,768]{1,0:T(8,128)S(1)}, u32[]{:S(2)}, u32[]{:S(2)}) collective-permute-start(f32[32,768]{1,0:T(8,128)S(1)} %get-tuple-element.33), channel_id=1, source_target_pairs={{0,16},{4,12},{8,24},{12,4},{16,0},{20,28},{24,8},{28,20},{1,17},{... | collective-permute-start | bytes 294920 | tf_op jit(solution)/shard_map/ppermute | solution.py:24

commit v18 on v16

--- a/solution.py
+++ b/solution.py
@@ -58,9 +58,9 @@
     return result
 
 
-def text_ids(shape, n_img, cols, far):
+def text_ids(shape, n_img, cols, far, along):
     me_img, me_txt = lax.axis_index("img"), lax.axis_index("txt")
-    place = lax.broadcasted_iota(jnp.int32, shape, 0)
+    place = lax.broadcasted_iota(jnp.int32, shape, along)
     half = n_img // 2 * cols
     me_core = me_img % 2
     core = me_core
@@ -81,9 +81,9 @@
     return [both[cols:], sent[cols:2 * cols], got[:cols], got[2 * cols:]]
 
 
-def derivative(texts, images, ids, matched, log_scale, bias):
-    scale = jnp.exp(jnp.full((1, LANES), log_scale[0], jnp.float32))
-    logits = scale * dot([(texts, images)], (1, 1)) + bias[0]
+def derivative(left, right, ids, matched, log_scale, bias):
+    scale = jnp.exp(jnp.full((1, 1), log_scale[0], jnp.float32))
+    logits = scale * dot([(left, right)], (1, 1)) + bias[0]
     match = ids == matched
     v = jnp.where(match, -logits, logits)
     e = jnp.exp(-jnp.abs(v))
@@ -95,6 +95,10 @@
 def matched_texts(bundle, rows, count):
     matched = untwist(bundle[count:count + 1, :LANES], rows, lax.axis_index("txt"))
     return shuffle(matched, rows, IMAGE_ORDER).astype(jnp.int32)
+
+
+def turned(line):
+    return jnp.broadcast_to(line, (LANES, LANES)).T
 
 
 def image_kernel(
@@ -106,13 +110,15 @@
     images = halves(bundle[:count])
     near = own_core_texts(cols, both, sent, got)
     texts = halves(jnp.concatenate(near + other_core_texts(cols, both, sent, got)))
-    ids = text_ids((texts[0].shape[0], count), n_img, cols, True)
-    loss, d = derivative(texts, images, ids, matched, log_scale, bias)
-    d_near[...] = d[:len(near) * cols]
-    term = dot([(halves(d), texts)], (0, 0))
+    ids = text_ids((count, texts[0].shape[0]), n_img, cols, True, 1)
+    matched = turned(matched.astype(jnp.float32)).astype(jnp.int32)
+    matched = jnp.concatenate([matched] * (ids.shape[1] // LANES), axis=1)
+    loss, d = derivative(images, texts, ids, matched, log_scale, bias)
+    term = dot([(halves(d), texts)], (1, 0))
+    d_near[...] = d[:, :len(near) * cols].T
     own[...] = term[:rows]
     back = [IMAGE_ORDER.index(k) for k in range(n_txt)]
-    loss_row = shuffle(jnp.sum(loss, axis=0, keepdims=True), rows, back)
+    loss_row = shuffle(turned(jnp.sum(loss, axis=1, keepdims=True))[:1], rows, back)
     loss_row = untwist(loss_row, rows, lax.axis_index("txt"))
     loss_tile = jnp.broadcast_to(loss_row, (8, LANES))
     loss_ref[...] = loss_tile
@@ -133,7 +139,7 @@
     matched = matched_texts(pair, rows, count)
     others = halves(pair[:count])
     texts = halves(jnp.concatenate(own_core_texts(cols, both, sent, got)))
-    ids = text_ids((texts[0].shape[0], count), n_img, cols, False)
+    ids = text_ids((texts[0].shape[0], count), n_img, cols, False, 0)
     _, d = derivative(texts, others, ids, matched, log_scale, bias)
     near = halves(d_ref[...]), halves(bundle[:count])
     term = dot([near, (halves(d), others)], (1, 0))

time: 32.5 us -> 32.4 us (level)
  no operation moved by 1% of the time
where the time goes in v18:
time: 32.4 us; the launch traced here: 32.2 us
  starting transfers between devices  16.5 us (51%)
  waiting for transfers between devices  9.74 us (30%)
  Pallas kernels  2.7 us (8%)
  between operations  2.09 us (6%)
  local copies, waits for them, and re-layouts  1.24 us (4%)
    ppermute x9, starting transfers between devices, exchange(): return lax.ppermute(x, axis, [(i, i ^ k) for i in range(n)])  9.86 us
    ppermute x9, waiting for transfers between devices, exchange(): return lax.ppermute(x, axis, [(i, i ^ k) for i in range(n)])  9.73 us
    ppermute x5, starting transfers between devices, chip_exchange(): lax.ppermute(x, 'img', [(i, i ^ 2 * distances[i % 2]) for i in range(n_im...  6.6 us
    unnamed x12, local copies, waits for them, and re-layouts  1.21 us
    pallas_call x1, Pallas kernels, per_device(): pl.pallas_call(functools.partial(image_kernel, n_img, n_txt, rows, cols),...  1.12 us
    pallas_call x1, Pallas kernels, per_device(): pl.pallas_call(functools.partial(text_kernel, n_img, n_txt, rows, cols),...  0.84 us
    pallas_call x1, Pallas kernels, per_device(): pl.pallas_call(functools.partial(sum_kernel, n_txt, chips), out_shape=[ja...  0.74 us
  transfers between devices with their start and end apart: 14, of which 5 were waited for; matrix products, arithmetic and copies ran while one was open for 3% of the time, Pallas kernels for 6%

profile of v18, /device:TPU:0, one launch (start us, length us, event | category | flops | bytes accessed | tf_op | source)
XLA Modules:
  0.0 32.2 jit_solution(14597556875111759315)
XLA Ops:
  0.6 0.0 copy-start.1
  0.6 0.0 copy-start.2
  0.7 4.1 %collective-permute-start = (f32[32,768]{1,0:T(8,128)}, f32[32,768]{1,0:T(8,128)S(1)}, u32[]{:S(2)}, u32[]{:S(2)}) collective-permute-start(f32[32,768]{1,0:T(8,128)} %param.5), channel_id=1, source_target_pairs={{0,2},{1,3},{2,0},{3,1},{4,6},{5,7},{6,4},{7,5},{8,10},{9,11},{10,... | collective-permute-start | bytes 294920 | tf_op jit(solution)/shard_map/ppermute | solution.py:16
  4.8 1.3 %collective-permute-start.1 = (f32[32,768]{1,0:T(8,128)}, f32[32,768]{1,0:T(8,128)S(1)}, u32[]{:S(2)}, u32[]{:S(2)}) collective-permute-start(f32[32,768]{1,0:T(8,128)} %param.5), channel_id=1, source_target_pairs={{0,3},{1,2},{2,1},{3,0},{4,7},{5,6},{6,5},{7,4},{8,11},{9,10},{10,... | collective-permute-start | bytes 294920 | tf_op jit(solution)/shard_map/ppermute | solution.py:16
  6.1 0.0 collective-permute-start.2
  6.1 2.4 %collective-permute-start.5 = (f32[32,768]{1,0:T(8,128)}, f32[32,768]{1,0:T(8,128)S(1)}, u32[]{:S(2)}, u32[]{:S(2)}) collective-permute-start(f32[32,768]{1,0:T(8,128)} %param.6), channel_id=1, source_target_pairs={{0,24},{4,28},{8,16},{12,20},{16,8},{20,12},{24,0},{28,4},{1,25},{... | collective-permute-start | bytes 294920 | tf_op jit(solution)/shard_map/ppermute | solution.py:24
  8.6 0.9 %constant_dynamic-update-slice_fusion.5 = f32[136,768]{1,0:T(8,128)S(1)} fusion(f32[32,768]{1,0:T(8,128)} %param.5), kind=kLoop, calls=%fused_computation.6 | loop fusion | bytes 196608
  9.5 0.0 copy-done.2
  9.5 0.0 copy-done.1
  9.5 0.0 copy-start
  9.5 0.0 collective-permute-done.2
  9.5 0.6 %collective-permute-start.4 = (f32[64,768]{1,0:T(8,128)S(1)}, f32[64,768]{1,0:T(8,128)S(1)}, u32[]{:S(2)}, u32[]{:S(2)}) collective-permute-start(f32[64,768]{1,0:T(8,128)S(1)} %constant_dynamic-update-slice_fusion.both.refs_4_), channel_id=1, source_target_pairs={{0,8},{4,20},{8,0},{12,28},{16,24},{20,4},{24,16},{28,12},{1,9},{5... | collective-permute-start | bytes 589832 | tf_op jit(solution)/shard_map/ppermute | solution.py:24
  10.1 0.3 copy-done
  10.4 0.2 collective-permute-start.3
  10.6 2.2 %collective-permute-done = f32[32,768]{1,0:T(8,128)S(1)} collective-permute-done((f32[32,768]{1,0:T(8,128)}, f32[32,768]{1,0:T(8,128)S(1)}, u32[]{:S(2)}, u32[]{:S(2)}) %collective-permute-start) | collective-permute-done | bytes 98336 | tf_op jit(solution)/shard_map/ppermute | solution.py:16
  12.8 0.0 collective-permute-done.1
  12.8 2.5 %collective-permute-done.3 = f32[32,768]{1,0:T(8,128)S(1)} collective-permute-done((f32[32,768]{1,0:T(8,128)S(1)}, f32[32,768]{1,0:T(8,128)S(1)}, u32[]{:S(2)}, u32[]{:S(2)}) %collective-permute-start.3) | collective-permute-done | bytes 98336 | tf_op jit(solution)/shard_map/ppermute | solution.py:16
  15.3 0.1 collective-permute-start.10
  15.4 0.0 collective-permute-done.4
  15.5 0.0 collective-permute-done.5
  15.5 0.6 %collective-permute-start.6 = (f32[96,768]{1,0:T(8,128)S(1)}, f32[96,768]{1,0:T(8,128)S(1)}, u32[]{:S(2)}, u32[]{:S(2)}) collective-permute-start(f32[96,768]{1,0:T(8,128)S(1)} %constant_dynamic-update-slice_fusion.6.sent.refs_5_), channel_id=1, source_target_pairs={{0,4},{4,0},{8,12},{12,8},{16,20},{20,16},{24,28},{28,24},{1,5},{5... | collective-permute-start | bytes 884744 | tf_op jit(solution)/shard_map/ppermute | solution.py:16
  17.3 0.3 collective-permute-done.6.got.refs_6_
  17.6 1.1 %image_terms.1 = (f32[32,768]{1,0:T(8,128)S(1)}, f32[8,128]{1,0:T(8,128)S(1)}, f32[128,128]{1,0:T(8,128)S(1)}, f32[25,8,128]{2,1,0:T(8,128)S(1)}, f32[25,8,128]{2,1,0:T(8,128)S(1)}, /*index=5*/f32[25,8,128]{2,1,0:T(8,128)S(1)}) custom-call(f32[1]{0:T(128)S(6)} %copy.14.log_scale.refs_0_, f32[1]{0:T(128)S(6)} %copy.15.bias.refs_1_, ...), custom_call_target="tpu_custom_call" | custom-call | tf_op jit(solution)/shard_map/image_terms/pallas_call | solution.py:191
  18.7 0.3 %collective-permute-start.7 = (f32[25,8,128]{2,1,0:T(8,128)S(1)}, f32[25,8,128]{2,1,0:T(8,128)S(1)}, u32[]{:S(2)}, u32[]{:S(2)}) collective-permute-start(f32[25,8,128]{2,1,0:T(8,128)S(1)} %get-tuple-element.20), channel_id=1, source_target_pairs={{0,1},{1,0},{2,3},{3,2},{4,5},{5,4},{6,7},{7,6},{8,9},{9,8},{10,11... | collective-permute-start | bytes 307208 | tf_op jit(solution)/shard_map/ppermute | solution.py:16
  19.1 2.9 %collective-permute-start.8 = (f32[25,8,128]{2,1,0:T(8,128)S(1)}, f32[25,8,128]{2,1,0:T(8,128)S(1)}, u32[]{:S(2)}, u32[]{:S(2)}) collective-permute-start(f32[25,8,128]{2,1,0:T(8,128)S(1)} %get-tuple-element.21), channel_id=1, source_target_pairs={{0,3},{1,2},{2,1},{3,0},{4,7},{5,6},{6,5},{7,4},{8,11},{9,10},{10,... | collective-permute-start | bytes 307208 | tf_op jit(solution)/shard_map/ppermute | solution.py:16
  21.9 0.3 %collective-permute-start.9 = (f32[25,8,128]{2,1,0:T(8,128)S(1)}, f32[25,8,128]{2,1,0:T(8,128)S(1)}, u32[]{:S(2)}, u32[]{:S(2)}) collective-permute-start(f32[25,8,128]{2,1,0:T(8,128)S(1)} %get-tuple-element.22), channel_id=1, source_target_pairs={{0,2},{1,3},{2,0},{3,1},{4,6},{5,7},{6,4},{7,5},{8,10},{9,11},{10,... | collective-permute-start | bytes 307208 | tf_op jit(solution)/shard_map/ppermute | solution.py:16
  22.3 0.0 collective-permute-done.10.refs_3_
  22.3 0.8 %text_terms.1 = (f32[32,768]{1,0:T(8,128)S(1)}, f32[32,768]{1,0:T(8,128)S(1)}, f32[32,768]{1,0:T(8,128)S(1)}, f32[32,768]{1,0:T(8,128)S(1)}) custom-call(f32[1]{0:T(128)S(6)} %copy.14.log_scale.refs_0_, f32[1]{0:T(128)S(6)} %copy.15.bias.refs_1_, f32[136,768]{1,0:T(8,128)S(1)} %pad_dynamic-update-slice_fusion.bundle.refs_2_, ...), custom_call_target="tpu_custom_call" | custom-call | tf_op jit(solution)/shard_map/text_terms/pallas_call | solution.py:202
  23.1 1.9 %collective-permute-start.11 = (f32[32,768]{1,0:T(8,128)S(1)}, f32[32,768]{1,0:T(8,128)S(1)}, u32[]{:S(2)}, u32[]{:S(2)}) collective-permute-start(f32[32,768]{1,0:T(8,128)S(1)} %get-tuple-element.24), channel_id=1, source_target_pairs={{0,24},{4,28},{8,16},{12,20},{16,8},{20,12},{24,0},{28,4},{1,25},{... | collective-permute-start | bytes 294920 | tf_op jit(solution)/shard_map/ppermute | solution.py:24
  25.0 0.8 %collective-permute-start.12 = (f32[32,768]{1,0:T(8,128)S(1)}, f32[32,768]{1,0:T(8,128)S(1)}, u32[]{:S(2)}, u32[]{:S(2)}) collective-permute-start(f32[32,768]{1,0:T(8,128)S(1)} %get-tuple-element.26), channel_id=1, source_target_pairs={{0,8},{4,20},{8,0},{12,28},{16,24},{20,4},{24,16},{28,12},{1,9},{5... | collective-permute-start | bytes 294920 | tf_op jit(solution)/shard_map/ppermute | solution.py:24
  25.8 0.0 collective-permute-done.7.refs_0_
  25.8 0.9 %collective-permute-start.13 = (f32[32,768]{1,0:T(8,128)S(1)}, f32[32,768]{1,0:T(8,128)S(1)}, u32[]{:S(2)}, u32[]{:S(2)}) collective-permute-start(f32[32,768]{1,0:T(8,128)S(1)} %get-tuple-element.27), channel_id=1, source_target_pairs={{0,16},{4,12},{8,24},{12,4},{16,0},{20,28},{24,8},{28,20},{1,17},{... | collective-permute-start | bytes 294920 | tf_op jit(solution)/shard_map/ppermute | solution.py:24
  26.7 1.3 %collective-permute-done.8.refs_1_ = f32[25,8,128]{2,1,0:T(8,128)S(1)} collective-permute-done((f32[25,8,128]{2,1,0:T(8,128)S(1)}, f32[25,8,128]{2,1,0:T(8,128)S(1)}, u32[]{:S(2)}, u32[]{:S(2)}) %collective-permute-start.8) | collective-permute-done | bytes 102432 | tf_op jit(solution)/shard_map/ppermute | solution.py:16
  27.9 3.6 %collective-permute-done.9.refs_2_ = f32[25,8,128]{2,1,0:T(8,128)S(1)} collective-permute-done((f32[25,8,128]{2,1,0:T(8,128)S(1)}, f32[25,8,128]{2,1,0:T(8,128)S(1)}, u32[]{:S(2)}, u32[]{:S(2)}) %collective-permute-start.9) | collective-permute-done | bytes 102432 | tf_op jit(solution)/shard_map/ppermute | solution.py:16
  31.5 0.0 collective-permute-done.11.refs_3_
  31.5 0.0 collective-permute-done.12.refs_5_
  31.5 0.0 collective-permute-done.13.refs_6_
  31.5 0.7 %sums.1 = (f32[1,128]{1,0:T(1,128)}, f32[32,768]{1,0:T(8,128)}, f32[32,768]{1,0:T(8,128)}) custom-call(f32[32,768]{1,0:T(8,128)S(1)} %get-tuple-element.18.own_ref, f32[8,128]{1,0:T(8,128)S(1)} %get-tuple-element.19.loss_ref, f32[25,8,128]{2,1,0:T(8,128)S(1)} %collective-permute-done.7.refs_0_, f32[25,8,128]{2,1,0:T(8,128)S(1)} %collective-permute-done.8.refs_1_, ...), custom_call_target="tpu_custom_call" | custom-call | tf_op jit(solution)/shard_map/sums/pallas_call | solution.py:213
  (9 shorter events, 0.1 us)
Async XLA Ops:
  0.6 8.8 %copy-start.1 = (f32[32,768]{1,0:T(8,128)S(1)}, f32[32,768]{1,0:T(8,128)}, u32[]{:S(2)}) copy-start(f32[32,768]{1,0:T(8,128)} %param.6) | copy-start | bytes 294916
  0.6 8.8 %copy-start.2 = (s32[128]{0:T(128)S(1)}, s32[128]{0:T(128)}, u32[]{:S(2)}) copy-start(s32[128]{0:T(128)} %param.7) | copy-start | bytes 1540
  0.7 12.2 %collective-permute-start = (f32[32,768]{1,0:T(8,128)}, f32[32,768]{1,0:T(8,128)S(1)}, u32[]{:S(2)}, u32[]{:S(2)}) collective-permute-start(f32[32,768]{1,0:T(8,128)} %param.5), channel_id=1, source_target_pairs={{0,2},{1,3},{2,0},{3,1},{4,6},{5,7},{6,4},{7,5},{8,10},{9,11},{10,... | collective-permute-start | bytes 294920 | tf_op jit(solution)/shard_map/ppermute | solution.py:16
  4.8 8.1 %collective-permute-start.1 = (f32[32,768]{1,0:T(8,128)}, f32[32,768]{1,0:T(8,128)S(1)}, u32[]{:S(2)}, u32[]{:S(2)}) collective-permute-start(f32[32,768]{1,0:T(8,128)} %param.5), channel_id=1, source_target_pairs={{0,3},{1,2},{2,1},{3,0},{4,7},{5,6},{6,5},{7,4},{8,11},{9,10},{10,... | collective-permute-start | bytes 294920 | tf_op jit(solution)/shard_map/ppermute | solution.py:16
  6.1 3.4 %collective-permute-start.2 = (f32[32,768]{1,0:T(8,128)}, f32[32,768]{1,0:T(8,128)S(1)}, u32[]{:S(2)}, u32[]{:S(2)}) collective-permute-start(f32[32,768]{1,0:T(8,128)} %param.6), channel_id=1, source_target_pairs={{0,4},{4,0},{8,12},{12,8},{16,20},{20,16},{24,28},{28,24},{1,5},{5... | collective-permute-start | bytes 294920 | tf_op jit(solution)/shard_map/ppermute | solution.py:16
  6.1 9.4 %collective-permute-start.5 = (f32[32,768]{1,0:T(8,128)}, f32[32,768]{1,0:T(8,128)S(1)}, u32[]{:S(2)}, u32[]{:S(2)}) collective-permute-start(f32[32,768]{1,0:T(8,128)} %param.6), channel_id=1, source_target_pairs={{0,24},{4,28},{8,16},{12,20},{16,8},{20,12},{24,0},{28,4},{1,25},{... | collective-permute-start | bytes 294920 | tf_op jit(solution)/shard_map/ppermute | solution.py:24
  9.5 0.9 %copy-start = (f32[32,768]{1,0:T(8,128)S(1)}, f32[32,768]{1,0:T(8,128)}, u32[]{:S(2)}) copy-start(f32[32,768]{1,0:T(8,128)} %param.5) | copy-start | bytes 294916
  9.5 5.9 %collective-permute-start.4 = (f32[64,768]{1,0:T(8,128)S(1)}, f32[64,768]{1,0:T(8,128)S(1)}, u32[]{:S(2)}, u32[]{:S(2)}) collective-permute-start(f32[64,768]{1,0:T(8,128)S(1)} %constant_dynamic-update-slice_fusion.both.refs_4_), channel_id=1, source_target_pairs={{0,8},{4,20},{8,0},{12,28},{16,24},{20,4},{24,16},{28,12},{1,9},{5... | collective-permute-start | bytes 589832 | tf_op jit(solution)/shard_map/ppermute | solution.py:24
  10.4 4.9 %collective-permute-start.3 = (f32[32,768]{1,0:T(8,128)S(1)}, f32[32,768]{1,0:T(8,128)S(1)}, u32[]{:S(2)}, u32[]{:S(2)}) collective-permute-start(f32[32,768]{1,0:T(8,128)S(1)} %copy-done), channel_id=1, source_target_pairs={{0,1},{1,0},{2,3},{3,2},{4,5},{5,4},{6,7},{7,6},{8,9},{9,8},{10,11... | collective-permute-start | bytes 294920 | tf_op jit(solution)/shard_map/ppermute | solution.py:16
  15.3 6.9 %collective-permute-start.10 = (f32[136,768]{1,0:T(8,128)S(1)}, f32[136,768]{1,0:T(8,128)S(1)}, u32[]{:S(2)}, u32[]{:S(2)}) collective-permute-start(f32[136,768]{1,0:T(8,128)S(1)} %pad_dynamic-update-slice_fusion.bundle.refs_2_), channel_id=1, source_target_pairs={{0,4},{4,0},{8,12},{12,8},{16,20},{20,16},{24,28},{28,24},{1,5},{5... | collective-permute-start | bytes 1253384 | tf_op jit(solution)/shard_map/ppermute | solution.py:16
  15.5 2.1 %collective-permute-start.6 = (f32[96,768]{1,0:T(8,128)S(1)}, f32[96,768]{1,0:T(8,128)S(1)}, u32[]{:S(2)}, u32[]{:S(2)}) collective-permute-start(f32[96,768]{1,0:T(8,128)S(1)} %constant_dynamic-update-slice_fusion.6.sent.refs_5_), channel_id=1, source_target_pairs={{0,4},{4,0},{8,12},{12,8},{16,20},{20,16},{24,28},{28,24},{1,5},{5... | collective-permute-start | bytes 884744 | tf_op jit(solution)/shard_map/ppermute | solution.py:16
  18.7 7.1 %collective-permute-start.7 = (f32[25,8,128]{2,1,0:T(8,128)S(1)}, f32[25,8,128]{2,1,0:T(8,128)S(1)}, u32[]{:S(2)}, u32[]{:S(2)}) collective-permute-start(f32[25,8,128]{2,1,0:T(8,128)S(1)} %get-tuple-element.20), channel_id=1, source_target_pairs={{0,1},{1,0},{2,3},{3,2},{4,5},{5,4},{6,7},{7,6},{8,9},{9,8},{10,11... | collective-permute-start | bytes 307208 | tf_op jit(solution)/shard_map/ppermute | solution.py:16
  19.1 8.9 %collective-permute-start.8 = (f32[25,8,128]{2,1,0:T(8,128)S(1)}, f32[25,8,128]{2,1,0:T(8,128)S(1)}, u32[]{:S(2)}, u32[]{:S(2)}) collective-permute-start(f32[25,8,128]{2,1,0:T(8,128)S(1)} %get-tuple-element.21), channel_id=1, source_target_pairs={{0,3},{1,2},{2,1},{3,0},{4,7},{5,6},{6,5},{7,4},{8,11},{9,10},{10,... | collective-permute-start | bytes 307208 | tf_op jit(solution)/shard_map/ppermute | solution.py:16
  21.9 9.6 %collective-permute-start.9 = (f32[25,8,128]{2,1,0:T(8,128)S(1)}, f32[25,8,128]{2,1,0:T(8,128)S(1)}, u32[]{:S(2)}, u32[]{:S(2)}) collective-permute-start(f32[25,8,128]{2,1,0:T(8,128)S(1)} %get-tuple-element.22), channel_id=1, source_target_pairs={{0,2},{1,3},{2,0},{3,1},{4,6},{5,7},{6,4},{7,5},{8,10},{9,11},{10,... | collective-permute-start | bytes 307208 | tf_op jit(solution)/shard_map/ppermute | solution.py:16
  23.1 8.4 %collective-permute-start.11 = (f32[32,768]{1,0:T(8,128)S(1)}, f32[32,768]{1,0:T(8,128)S(1)}, u32[]{:S(2)}, u32[]{:S(2)}) collective-permute-start(f32[32,768]{1,0:T(8,128)S(1)} %get-tuple-element.24), channel_id=1, source_target_pairs={{0,24},{4,28},{8,16},{12,20},{16,8},{20,12},{24,0},{28,4},{1,25},{... | collective-permute-start | bytes 294920 | tf_op jit(solution)/shard_map/ppermute | solution.py:24
  25.0 6.5 %collective-permute-start.12 = (f32[32,768]{1,0:T(8,128)S(1)}, f32[32,768]{1,0:T(8,128)S(1)}, u32[]{:S(2)}, u32[]{:S(2)}) collective-permute-start(f32[32,768]{1,0:T(8,128)S(1)} %get-tuple-element.26), channel_id=1, source_target_pairs={{0,8},{4,20},{8,0},{12,28},{16,24},{20,4},{24,16},{28,12},{1,9},{5... | collective-permute-start | bytes 294920 | tf_op jit(solution)/shard_map/ppermute | solution.py:24
  25.8 5.7 %collective-permute-start.13 = (f32[32,768]{1,0:T(8,128)S(1)}, f32[32,768]{1,0:T(8,128)S(1)}, u32[]{:S(2)}, u32[]{:S(2)}) collective-permute-start(f32[32,768]{1,0:T(8,128)S(1)} %get-tuple-element.27), channel_id=1, source_target_pairs={{0,16},{4,12},{8,24},{12,4},{16,0},{20,28},{24,8},{28,20},{1,17},{... | collective-permute-start | bytes 294920 | tf_op jit(solution)/shard_map/ppermute | solution.py:24

commit v19 on v18

--- a/solution.py
+++ b/solution.py
@@ -181,7 +181,7 @@
     for k in (2, 3):
         image_blocks[k] = exchange(image_emb, "txt", n_txt, k)
     beside = chip_exchange(both, n_img, (1, 2))
-    diagonal = chip_exchange(text_emb, n_img, (3, 3))
+    diagonal = chip_exchange(after(text_emb, both), n_img, (3, 3))
     image_blocks[1] = exchange(after(image_emb, both), "txt", n_txt, 1)
     sent = jnp.concatenate([beside, diagonal])
     got = exchange(sent, "img", n_img, 1)

time: 32.4 us -> 33 us (1.019)
  waiting for transfers between devices: 9.74 us -> 11.1 us
  starting transfers between devices: 16.5 us -> 16 us
    ppermute x5, waiting for transfers between devices: 0.01 us -> 1.95 us  [chip_exchange(): lax.ppermute(x, 'img', [(i, i ^ 2 * distances[i % 2]) for i in range(n_im...]
    ppermute x9, waiting for transfers between devices: 9.73 us -> 9.1 us  [exchange(): return lax.ppermute(x, axis, [(i, i ^ k) for i in range(n)])]
    ppermute x9, starting transfers between devices: 9.86 us -> 9.38 us  [exchange(): return lax.ppermute(x, axis, [(i, i ^ k) for i in range(n)])]
  transfers between devices with their start and end apart: 14 -> 14, of which waited for: 5 -> 7; matrix products, arithmetic and copies ran while one was open for 3% -> 3% of each run, Pallas kernels for 6% -> 6%
where the time goes in v19:
time: 33 us; the launch traced here: 32.8 us
  starting transfers between devices  16 us (48%)
  waiting for transfers between devices  11.1 us (34%)
  Pallas kernels  2.7 us (8%)
  between operations  2.07 us (6%)
  local copies, waits for them, and re-layouts  1.01 us (3%)
    ppermute x9, starting transfers between devices, exchange(): return lax.ppermute(x, axis, [(i, i ^ k) for i in range(n)])  9.38 us
    ppermute x9, waiting for transfers between devices, exchange(): return lax.ppermute(x, axis, [(i, i ^ k) for i in range(n)])  9.1 us
    ppermute x5, starting transfers between devices, chip_exchange(): lax.ppermute(x, 'img', [(i, i ^ 2 * distances[i % 2]) for i in range(n_im...  6.6 us
    ppermute x5, waiting for transfers between devices, chip_exchange(): lax.ppermute(x, 'img', [(i, i ^ 2 * distances[i % 2]) for i in range(n_im...  1.95 us
    pallas_call x1, Pallas kernels, per_device(): pl.pallas_call(functools.partial(image_kernel, n_img, n_txt, rows, cols),...  1.12 us
    unnamed x12, local copies, waits for them, and re-layouts  0.99 us
    pallas_call x1, Pallas kernels, per_device(): pl.pallas_call(functools.partial(text_kernel, n_img, n_txt, rows, cols),...  0.84 us
    pallas_call x1, Pallas kernels, per_device(): pl.pallas_call(functools.partial(sum_kernel, n_txt, chips), out_shape=[ja...  0.74 us
  transfers between devices with their start and end apart: 14, of which 7 were waited for; matrix products, arithmetic and copies ran while one was open for 3% of the time, Pallas kernels for 6%

profile of v19, /device:TPU:0, one launch (start us, length us, event | category | flops | bytes accessed | tf_op | source)
XLA Modules:
  0.0 32.8 jit_solution(18314510699651106667)
XLA Ops:
  0.6 0.0 copy-start.1
  0.6 0.0 copy-start.2
  0.7 4.1 %collective-permute-start = (f32[32,768]{1,0:T(8,128)}, f32[32,768]{1,0:T(8,128)S(1)}, u32[]{:S(2)}, u32[]{:S(2)}) collective-permute-start(f32[32,768]{1,0:T(8,128)} %param.5), channel_id=1, source_target_pairs={{0,2},{1,3},{2,0},{3,1},{4,6},{5,7},{6,4},{7,5},{8,10},{9,11},{10,... | collective-permute-start | bytes 294920 | tf_op jit(solution)/shard_map/ppermute | solution.py:16
  4.8 1.3 %collective-permute-start.1 = (f32[32,768]{1,0:T(8,128)}, f32[32,768]{1,0:T(8,128)S(1)}, u32[]{:S(2)}, u32[]{:S(2)}) collective-permute-start(f32[32,768]{1,0:T(8,128)} %param.5), channel_id=1, source_target_pairs={{0,3},{1,2},{2,1},{3,0},{4,7},{5,6},{6,5},{7,4},{8,11},{9,10},{10,... | collective-permute-start | bytes 294920 | tf_op jit(solution)/shard_map/ppermute | solution.py:16
  6.1 0.0 collective-permute-start.2
  6.1 0.9 %constant_dynamic-update-slice_fusion.5 = f32[136,768]{1,0:T(8,128)S(1)} fusion(f32[32,768]{1,0:T(8,128)} %param.5), kind=kLoop, calls=%fused_computation.6 | loop fusion | bytes 196608
  7.0 0.0 copy-done.2
  7.1 0.0 copy-done.1
  7.1 0.0 copy-start
  7.1 0.5 %collective-permute-done.2 = f32[32,768]{1,0:T(8,128)S(1)} collective-permute-done((f32[32,768]{1,0:T(8,128)}, f32[32,768]{1,0:T(8,128)S(1)}, u32[]{:S(2)}, u32[]{:S(2)}) %collective-permute-start.2) | collective-permute-done | bytes 98336 | tf_op jit(solution)/shard_map/ppermute | solution.py:16
  7.6 1.6 %collective-permute-start.4 = (f32[64,768]{1,0:T(8,128)S(1)}, f32[64,768]{1,0:T(8,128)S(1)}, u32[]{:S(2)}, u32[]{:S(2)}) collective-permute-start(f32[64,768]{1,0:T(8,128)S(1)} %constant_dynamic-update-slice_fusion.both.refs_4_), channel_id=1, source_target_pairs={{0,8},{4,20},{8,0},{12,28},{16,24},{20,4},{24,16},{28,12},{1,9},{5... | collective-permute-start | bytes 589832 | tf_op jit(solution)/shard_map/ppermute | solution.py:24
  9.2 0.0 copy-done
  9.2 0.2 collective-permute-start.3
  9.4 1.5 %collective-permute-start.5 = (f32[32,768]{1,0:T(8,128)S(1)}, f32[32,768]{1,0:T(8,128)S(1)}, u32[]{:S(2)}, u32[]{:S(2)}) collective-permute-start(f32[32,768]{1,0:T(8,128)S(1)} %copy-done.1), channel_id=1, source_target_pairs={{0,24},{4,28},{8,16},{12,20},{16,8},{20,12},{24,0},{28,4},{1,25},{... | collective-permute-start | bytes 294920 | tf_op jit(solution)/shard_map/ppermute | solution.py:24
  10.9 1.9 %collective-permute-done = f32[32,768]{1,0:T(8,128)S(1)} collective-permute-done((f32[32,768]{1,0:T(8,128)}, f32[32,768]{1,0:T(8,128)S(1)}, u32[]{:S(2)}, u32[]{:S(2)}) %collective-permute-start) | collective-permute-done | bytes 98336 | tf_op jit(solution)/shard_map/ppermute | solution.py:16
  12.8 0.0 collective-permute-done.1
  12.8 1.5 %collective-permute-done.3 = f32[32,768]{1,0:T(8,128)S(1)} collective-permute-done((f32[32,768]{1,0:T(8,128)S(1)}, f32[32,768]{1,0:T(8,128)S(1)}, u32[]{:S(2)}, u32[]{:S(2)}) %collective-permute-start.3) | collective-permute-done | bytes 98336 | tf_op jit(solution)/shard_map/ppermute | solution.py:16
  14.4 0.1 collective-permute-start.10
  14.4 0.0 collective-permute-done.4
  14.5 1.9 %collective-permute-done.5 = f32[32,768]{1,0:T(8,128)S(1)} collective-permute-done((f32[32,768]{1,0:T(8,128)S(1)}, f32[32,768]{1,0:T(8,128)S(1)}, u32[]{:S(2)}, u32[]{:S(2)}) %collective-permute-start.5) | collective-permute-done | bytes 98336 | tf_op jit(solution)/shard_map/ppermute | solution.py:24
  16.4 0.1 collective-permute-start.6
  17.8 0.3 collective-permute-done.6.got.refs_6_
  18.1 1.1 %image_terms.1 = (f32[32,768]{1,0:T(8,128)S(1)}, f32[8,128]{1,0:T(8,128)S(1)}, f32[128,128]{1,0:T(8,128)S(1)}, f32[25,8,128]{2,1,0:T(8,128)S(1)}, f32[25,8,128]{2,1,0:T(8,128)S(1)}, /*index=5*/f32[25,8,128]{2,1,0:T(8,128)S(1)}) custom-call(f32[1]{0:T(128)S(6)} %copy.14.log_scale.refs_0_, f32[1]{0:T(128)S(6)} %copy.15.bias.refs_1_, ...), custom_call_target="tpu_custom_call" | custom-call | tf_op jit(solution)/shard_map/image_terms/pallas_call | solution.py:191
  19.2 0.4 %collective-permute-start.7 = (f32[25,8,128]{2,1,0:T(8,128)S(1)}, f32[25,8,128]{2,1,0:T(8,128)S(1)}, u32[]{:S(2)}, u32[]{:S(2)}) collective-permute-start(f32[25,8,128]{2,1,0:T(8,128)S(1)} %get-tuple-element.22), channel_id=1, source_target_pairs={{0,1},{1,0},{2,3},{3,2},{4,5},{5,4},{6,7},{7,6},{8,9},{9,8},{10,11... | collective-permute-start | bytes 307208 | tf_op jit(solution)/shard_map/ppermute | solution.py:16
  19.6 2.8 %collective-permute-start.8 = (f32[25,8,128]{2,1,0:T(8,128)S(1)}, f32[25,8,128]{2,1,0:T(8,128)S(1)}, u32[]{:S(2)}, u32[]{:S(2)}) collective-permute-start(f32[25,8,128]{2,1,0:T(8,128)S(1)} %get-tuple-element.23), channel_id=1, source_target_pairs={{0,3},{1,2},{2,1},{3,0},{4,7},{5,6},{6,5},{7,4},{8,11},{9,10},{10,... | collective-permute-start | bytes 307208 | tf_op jit(solution)/shard_map/ppermute | solution.py:16
  22.4 0.3 %collective-permute-start.9 = (f32[25,8,128]{2,1,0:T(8,128)S(1)}, f32[25,8,128]{2,1,0:T(8,128)S(1)}, u32[]{:S(2)}, u32[]{:S(2)}) collective-permute-start(f32[25,8,128]{2,1,0:T(8,128)S(1)} %get-tuple-element.24), channel_id=1, source_target_pairs={{0,2},{1,3},{2,0},{3,1},{4,6},{5,7},{6,4},{7,5},{8,10},{9,11},{10,... | collective-permute-start | bytes 307208 | tf_op jit(solution)/shard_map/ppermute | solution.py:16
  22.8 0.0 collective-permute-done.10.refs_3_
  22.8 0.8 %text_terms.1 = (f32[32,768]{1,0:T(8,128)S(1)}, f32[32,768]{1,0:T(8,128)S(1)}, f32[32,768]{1,0:T(8,128)S(1)}, f32[32,768]{1,0:T(8,128)S(1)}) custom-call(f32[1]{0:T(128)S(6)} %copy.14.log_scale.refs_0_, f32[1]{0:T(128)S(6)} %copy.15.bias.refs_1_, f32[136,768]{1,0:T(8,128)S(1)} %pad_dynamic-update-slice_fusion.bundle.refs_2_, ...), custom_call_target="tpu_custom_call" | custom-call | tf_op jit(solution)/shard_map/text_terms/pallas_call | solution.py:202
  23.6 1.5 %collective-permute-start.11 = (f32[32,768]{1,0:T(8,128)S(1)}, f32[32,768]{1,0:T(8,128)S(1)}, u32[]{:S(2)}, u32[]{:S(2)}) collective-permute-start(f32[32,768]{1,0:T(8,128)S(1)} %get-tuple-element.26), channel_id=1, source_target_pairs={{0,24},{4,28},{8,16},{12,20},{16,8},{20,12},{24,0},{28,4},{1,25},{... | collective-permute-start | bytes 294920 | tf_op jit(solution)/shard_map/ppermute | solution.py:24
  25.1 0.8 %collective-permute-start.12 = (f32[32,768]{1,0:T(8,128)S(1)}, f32[32,768]{1,0:T(8,128)S(1)}, u32[]{:S(2)}, u32[]{:S(2)}) collective-permute-start(f32[32,768]{1,0:T(8,128)S(1)} %get-tuple-element.28), channel_id=1, source_target_pairs={{0,8},{4,20},{8,0},{12,28},{16,24},{20,4},{24,16},{28,12},{1,9},{5... | collective-permute-start | bytes 294920 | tf_op jit(solution)/shard_map/ppermute | solution.py:24
  26.0 0.0 collective-permute-done.7.refs_0_
  26.0 1.2 %collective-permute-start.13 = (f32[32,768]{1,0:T(8,128)S(1)}, f32[32,768]{1,0:T(8,128)S(1)}, u32[]{:S(2)}, u32[]{:S(2)}) collective-permute-start(f32[32,768]{1,0:T(8,128)S(1)} %get-tuple-element.29), channel_id=1, source_target_pairs={{0,16},{4,12},{8,24},{12,4},{16,0},{20,28},{24,8},{28,20},{1,17},{... | collective-permute-start | bytes 294920 | tf_op jit(solution)/shard_map/ppermute | solution.py:24
  27.2 1.2 %collective-permute-done.8.refs_1_ = f32[25,8,128]{2,1,0:T(8,128)S(1)} collective-permute-done((f32[25,8,128]{2,1,0:T(8,128)S(1)}, f32[25,8,128]{2,1,0:T(8,128)S(1)}, u32[]{:S(2)}, u32[]{:S(2)}) %collective-permute-start.8) | collective-permute-done | bytes 102432 | tf_op jit(solution)/shard_map/ppermute | solution.py:16
  28.4 3.7 %collective-permute-done.9.refs_2_ = f32[25,8,128]{2,1,0:T(8,128)S(1)} collective-permute-done((f32[25,8,128]{2,1,0:T(8,128)S(1)}, f32[25,8,128]{2,1,0:T(8,128)S(1)}, u32[]{:S(2)}, u32[]{:S(2)}) %collective-permute-start.9) | collective-permute-done | bytes 102432 | tf_op jit(solution)/shard_map/ppermute | solution.py:16
  32.1 0.0 collective-permute-done.11.refs_3_
  32.1 0.0 collective-permute-done.12.refs_5_
  32.1 0.0 collective-permute-done.13.refs_6_
  32.1 0.7 %sums.1 = (f32[1,128]{1,0:T(1,128)}, f32[32,768]{1,0:T(8,128)}, f32[32,768]{1,0:T(8,128)}) custom-call(f32[32,768]{1,0:T(8,128)S(1)} %get-tuple-element.20.own_ref, f32[8,128]{1,0:T(8,128)S(1)} %get-tuple-element.21.loss_ref, f32[25,8,128]{2,1,0:T(8,128)S(1)} %collective-permute-done.7.refs_0_, f32[25,8,128]{2,1,0:T(8,128)S(1)} %collective-permute-done.8.refs_1_, ...), custom_call_target="tpu_custom_call" | custom-call | tf_op jit(solution)/shard_map/sums/pallas_call | solution.py:213
  (9 shorter events, 0.1 us)
Async XLA Ops:
  0.6 6.4 %copy-start.1 = (f32[32,768]{1,0:T(8,128)S(1)}, f32[32,768]{1,0:T(8,128)}, u32[]{:S(2)}) copy-start(f32[32,768]{1,0:T(8,128)} %param.6) | copy-start | bytes 294916
  0.6 6.4 %copy-start.2 = (s32[128]{0:T(128)S(1)}, s32[128]{0:T(128)}, u32[]{:S(2)}) copy-start(s32[128]{0:T(128)} %param.7) | copy-start | bytes 1540
  0.7 12.2 %collective-permute-start = (f32[32,768]{1,0:T(8,128)}, f32[32,768]{1,0:T(8,128)S(1)}, u32[]{:S(2)}, u32[]{:S(2)}) collective-permute-start(f32[32,768]{1,0:T(8,128)} %param.5), channel_id=1, source_target_pairs={{0,2},{1,3},{2,0},{3,1},{4,6},{5,7},{6,4},{7,5},{8,10},{9,11},{10,... | collective-permute-start | bytes 294920 | tf_op jit(solution)/shard_map/ppermute | solution.py:16
  4.8 8.1 %collective-permute-start.1 = (f32[32,768]{1,0:T(8,128)}, f32[32,768]{1,0:T(8,128)S(1)}, u32[]{:S(2)}, u32[]{:S(2)}) collective-permute-start(f32[32,768]{1,0:T(8,128)} %param.5), channel_id=1, source_target_pairs={{0,3},{1,2},{2,1},{3,0},{4,7},{5,6},{6,5},{7,4},{8,11},{9,10},{10,... | collective-permute-start | bytes 294920 | tf_op jit(solution)/shard_map/ppermute | solution.py:16
  6.1 1.5 %collective-permute-start.2 = (f32[32,768]{1,0:T(8,128)}, f32[32,768]{1,0:T(8,128)S(1)}, u32[]{:S(2)}, u32[]{:S(2)}) collective-permute-start(f32[32,768]{1,0:T(8,128)} %param.6), channel_id=1, source_target_pairs={{0,4},{4,0},{8,12},{12,8},{16,20},{20,16},{24,28},{28,24},{1,5},{5... | collective-permute-start | bytes 294920 | tf_op jit(solution)/shard_map/ppermute | solution.py:16
  7.1 2.1 %copy-start = (f32[32,768]{1,0:T(8,128)S(1)}, f32[32,768]{1,0:T(8,128)}, u32[]{:S(2)}) copy-start(f32[32,768]{1,0:T(8,128)} %param.5) | copy-start | bytes 294916
  7.6 6.8 %collective-permute-start.4 = (f32[64,768]{1,0:T(8,128)S(1)}, f32[64,768]{1,0:T(8,128)S(1)}, u32[]{:S(2)}, u32[]{:S(2)}) collective-permute-start(f32[64,768]{1,0:T(8,128)S(1)} %constant_dynamic-update-slice_fusion.both.refs_4_), channel_id=1, source_target_pairs={{0,8},{4,20},{8,0},{12,28},{16,24},{20,4},{24,16},{28,12},{1,9},{5... | collective-permute-start | bytes 589832 | tf_op jit(solution)/shard_map/ppermute | solution.py:24
  9.2 5.2 %collective-permute-start.3 = (f32[32,768]{1,0:T(8,128)S(1)}, f32[32,768]{1,0:T(8,128)S(1)}, u32[]{:S(2)}, u32[]{:S(2)}) collective-permute-start(f32[32,768]{1,0:T(8,128)S(1)} %copy-done), channel_id=1, source_target_pairs={{0,1},{1,0},{2,3},{3,2},{4,5},{5,4},{6,7},{7,6},{8,9},{9,8},{10,11... | collective-permute-start | bytes 294920 | tf_op jit(solution)/shard_map/ppermute | solution.py:16
  9.4 7.0 %collective-permute-start.5 = (f32[32,768]{1,0:T(8,128)S(1)}, f32[32,768]{1,0:T(8,128)S(1)}, u32[]{:S(2)}, u32[]{:S(2)}) collective-permute-start(f32[32,768]{1,0:T(8,128)S(1)} %copy-done.1), channel_id=1, source_target_pairs={{0,24},{4,28},{8,16},{12,20},{16,8},{20,12},{24,0},{28,4},{1,25},{... | collective-permute-start | bytes 294920 | tf_op jit(solution)/shard_map/ppermute | solution.py:24
  14.4 8.4 %collective-permute-start.10 = (f32[136,768]{1,0:T(8,128)S(1)}, f32[136,768]{1,0:T(8,128)S(1)}, u32[]{:S(2)}, u32[]{:S(2)}) collective-permute-start(f32[136,768]{1,0:T(8,128)S(1)} %pad_dynamic-update-slice_fusion.bundle.refs_2_), channel_id=1, source_target_pairs={{0,4},{4,0},{8,12},{12,8},{16,20},{20,16},{24,28},{28,24},{1,5},{5... | collective-permute-start | bytes 1253384 | tf_op jit(solution)/shard_map/ppermute | solution.py:16
  16.4 1.6 %collective-permute-start.6 = (f32[96,768]{1,0:T(8,128)S(1)}, f32[96,768]{1,0:T(8,128)S(1)}, u32[]{:S(2)}, u32[]{:S(2)}) collective-permute-start(f32[96,768]{1,0:T(8,128)S(1)} %constant_dynamic-update-slice_fusion.6.sent.refs_5_), channel_id=1, source_target_pairs={{0,4},{4,0},{8,12},{12,8},{16,20},{20,16},{24,28},{28,24},{1,5},{5... | collective-permute-start | bytes 884744 | tf_op jit(solution)/shard_map/ppermute | solution.py:16
  19.2 6.7 %collective-permute-start.7 = (f32[25,8,128]{2,1,0:T(8,128)S(1)}, f32[25,8,128]{2,1,0:T(8,128)S(1)}, u32[]{:S(2)}, u32[]{:S(2)}) collective-permute-start(f32[25,8,128]{2,1,0:T(8,128)S(1)} %get-tuple-element.22), channel_id=1, source_target_pairs={{0,1},{1,0},{2,3},{3,2},{4,5},{5,4},{6,7},{7,6},{8,9},{9,8},{10,11... | collective-permute-start | bytes 307208 | tf_op jit(solution)/shard_map/ppermute | solution.py:16
  19.6 8.8 %collective-permute-start.8 = (f32[25,8,128]{2,1,0:T(8,128)S(1)}, f32[25,8,128]{2,1,0:T(8,128)S(1)}, u32[]{:S(2)}, u32[]{:S(2)}) collective-permute-start(f32[25,8,128]{2,1,0:T(8,128)S(1)} %get-tuple-element.23), channel_id=1, source_target_pairs={{0,3},{1,2},{2,1},{3,0},{4,7},{5,6},{6,5},{7,4},{8,11},{9,10},{10,... | collective-permute-start | bytes 307208 | tf_op jit(solution)/shard_map/ppermute | solution.py:16
  22.4 9.6 %collective-permute-start.9 = (f32[25,8,128]{2,1,0:T(8,128)S(1)}, f32[25,8,128]{2,1,0:T(8,128)S(1)}, u32[]{:S(2)}, u32[]{:S(2)}) collective-permute-start(f32[25,8,128]{2,1,0:T(8,128)S(1)} %get-tuple-element.24), channel_id=1, source_target_pairs={{0,2},{1,3},{2,0},{3,1},{4,6},{5,7},{6,4},{7,5},{8,10},{9,11},{10,... | collective-permute-start | bytes 307208 | tf_op jit(solution)/shard_map/ppermute | solution.py:16
  23.6 8.5 %collective-permute-start.11 = (f32[32,768]{1,0:T(8,128)S(1)}, f32[32,768]{1,0:T(8,128)S(1)}, u32[]{:S(2)}, u32[]{:S(2)}) collective-permute-start(f32[32,768]{1,0:T(8,128)S(1)} %get-tuple-element.26), channel_id=1, source_target_pairs={{0,24},{4,28},{8,16},{12,20},{16,8},{20,12},{24,0},{28,4},{1,25},{... | collective-permute-start | bytes 294920 | tf_op jit(solution)/shard_map/ppermute | solution.py:24
  25.1 7.0 %collective-permute-start.12 = (f32[32,768]{1,0:T(8,128)S(1)}, f32[32,768]{1,0:T(8,128)S(1)}, u32[]{:S(2)}, u32[]{:S(2)}) collective-permute-start(f32[32,768]{1,0:T(8,128)S(1)} %get-tuple-element.28), channel_id=1, source_target_pairs={{0,8},{4,20},{8,0},{12,28},{16,24},{20,4},{24,16},{28,12},{1,9},{5... | collective-permute-start | bytes 294920 | tf_op jit(solution)/shard_map/ppermute | solution.py:24
  26.0 6.1 %collective-permute-start.13 = (f32[32,768]{1,0:T(8,128)S(1)}, f32[32,768]{1,0:T(8,128)S(1)}, u32[]{:S(2)}, u32[]{:S(2)}) collective-permute-start(f32[32,768]{1,0:T(8,128)S(1)} %get-tuple-element.29), channel_id=1, source_target_pairs={{0,16},{4,12},{8,24},{12,4},{16,0},{20,28},{24,8},{28,20},{1,17},{... | collective-permute-start | bytes 294920 | tf_op jit(solution)/shard_map/ppermute | solution.py:24

commit v20 on v15

--- a/solution.py
+++ b/solution.py
@@ -9,7 +9,7 @@
 
 LANES = 128
 
-IMAGE_ORDER = (0, 2, 3, 1)
+IMAGE_ORDER = (0, 3, 2, 1)
 
 
 def exchange(x, axis, n, k):

time: 32.5 us -> 33.5 us (1.031)
  starting transfers between devices: 16.5 us -> 17.6 us
    ppermute x9, waiting for transfers between devices: 9.68 us -> 7.95 us  [exchange(): return lax.ppermute(x, axis, [(i, i ^ k) for i in range(n)])]
    ppermute x5, waiting for transfers between devices: 0.01 us -> 1.66 us  [chip_exchange(): lax.ppermute(x, 'img', [(i, i ^ 2 * distances[i % 2]) for i in range(n_im...]
    ppermute x9, starting transfers between devices: 9.86 us -> 11 us  [exchange(): return lax.ppermute(x, axis, [(i, i ^ k) for i in range(n)])]
  transfers between devices with their start and end apart: 14 -> 14, of which waited for: 5 -> 7; matrix products, arithmetic and copies ran while one was open for 3% -> 3% of each run, Pallas kernels for 6% -> 6%
where the time goes in v20:
time: 33.5 us; the launch traced here: 33.3 us
  starting transfers between devices  17.6 us (53%)
  waiting for transfers between devices  9.61 us (29%)
  Pallas kernels  2.8 us (8%)
  between operations  2.09 us (6%)
  local copies, waits for them, and re-layouts  1.24 us (4%)
    ppermute x9, starting transfers between devices, exchange(): return lax.ppermute(x, axis, [(i, i ^ k) for i in range(n)])  11 us
    ppermute x9, waiting for transfers between devices, exchange(): return lax.ppermute(x, axis, [(i, i ^ k) for i in range(n)])  7.95 us
    ppermute x5, starting transfers between devices, chip_exchange(): lax.ppermute(x, 'img', [(i, i ^ 2 * distances[i % 2]) for i in range(n_im...  6.6 us
    ppermute x5, waiting for transfers between devices, chip_exchange(): lax.ppermute(x, 'img', [(i, i ^ 2 * distances[i % 2]) for i in range(n_im...  1.66 us
    unnamed x12, local copies, waits for them, and re-layouts  1.21 us
    pallas_call x1, Pallas kernels, per_device(): pl.pallas_call(functools.partial(image_kernel, n_img, n_txt, rows, cols),...  1.16 us
    pallas_call x1, Pallas kernels, per_device(): pl.pallas_call(functools.partial(text_kernel, n_img, n_txt, rows, cols),...  0.9 us
    pallas_call x1, Pallas kernels, per_device(): pl.pallas_call(functools.partial(sum_kernel, n_txt, chips), out_shape=[ja...  0.74 us
  transfers between devices with their start and end apart: 14, of which 7 were waited for; matrix products, arithmetic and copies ran while one was open for 3% of the time, Pallas kernels for 6%

profile of v20, /device:TPU:0, one launch (start us, length us, event | category | flops | bytes accessed | tf_op | source)
XLA Modules:
  0.0 33.3 jit_solution(2708280732680439219)
XLA Ops:
  0.6 0.0 copy-start.1
  0.6 0.0 copy-start.2
  0.7 5.1 %collective-permute-start = (f32[32,768]{1,0:T(8,128)}, f32[32,768]{1,0:T(8,128)S(1)}, u32[]{:S(2)}, u32[]{:S(2)}) collective-permute-start(f32[32,768]{1,0:T(8,128)} %param.5), channel_id=1, source_target_pairs={{0,3},{1,2},{2,1},{3,0},{4,7},{5,6},{6,5},{7,4},{8,11},{9,10},{10,... | collective-permute-start | bytes 294920 | tf_op jit(solution)/shard_map/ppermute | solution.py:16
  5.8 0.0 collective-permute-start.1
  5.8 0.0 collective-permute-start.2
  5.8 2.4 %collective-permute-start.5 = (f32[32,768]{1,0:T(8,128)}, f32[32,768]{1,0:T(8,128)S(1)}, u32[]{:S(2)}, u32[]{:S(2)}) collective-permute-start(f32[32,768]{1,0:T(8,128)} %param.6), channel_id=1, source_target_pairs={{0,24},{4,28},{8,16},{12,20},{16,8},{20,12},{24,0},{28,4},{1,25},{... | collective-permute-start | bytes 294920 | tf_op jit(solution)/shard_map/ppermute | solution.py:24
  8.2 0.9 %constant_dynamic-update-slice_fusion.5 = f32[136,768]{1,0:T(8,128)S(1)} fusion(f32[32,768]{1,0:T(8,128)} %param.5), kind=kLoop, calls=%fused_computation.6 | loop fusion | bytes 196608
  9.1 0.0 copy-done.2
  9.1 0.0 copy-done.1
  9.2 0.0 copy-start
  9.2 0.0 collective-permute-done.2
  9.2 0.6 %collective-permute-start.4 = (f32[64,768]{1,0:T(8,128)S(1)}, f32[64,768]{1,0:T(8,128)S(1)}, u32[]{:S(2)}, u32[]{:S(2)}) collective-permute-start(f32[64,768]{1,0:T(8,128)S(1)} %constant_dynamic-update-slice_fusion.both.refs_4_), channel_id=1, source_target_pairs={{0,8},{4,20},{8,0},{12,28},{16,24},{20,4},{24,16},{28,12},{1,9},{5... | collective-permute-start | bytes 589832 | tf_op jit(solution)/shard_map/ppermute | solution.py:24
  9.8 0.3 copy-done
  10.1 0.8 %collective-permute-start.3 = (f32[32,768]{1,0:T(8,128)S(1)}, f32[32,768]{1,0:T(8,128)S(1)}, u32[]{:S(2)}, u32[]{:S(2)}) collective-permute-start(f32[32,768]{1,0:T(8,128)S(1)} %copy-done), channel_id=1, source_target_pairs={{0,1},{1,0},{2,3},{3,2},{4,5},{5,4},{6,7},{7,6},{8,9},{9,8},{10,11... | collective-permute-start | bytes 294920 | tf_op jit(solution)/shard_map/ppermute | solution.py:16
  10.8 0.0 collective-permute-done
  10.9 3.5 %collective-permute-done.1 = f32[32,768]{1,0:T(8,128)S(1)} collective-permute-done((f32[32,768]{1,0:T(8,128)}, f32[32,768]{1,0:T(8,128)S(1)}, u32[]{:S(2)}, u32[]{:S(2)}) %collective-permute-start.1) | collective-permute-done | bytes 98336 | tf_op jit(solution)/shard_map/ppermute | solution.py:16
  14.4 1.9 %collective-permute-done.3 = f32[32,768]{1,0:T(8,128)S(1)} collective-permute-done((f32[32,768]{1,0:T(8,128)S(1)}, f32[32,768]{1,0:T(8,128)S(1)}, u32[]{:S(2)}, u32[]{:S(2)}) %collective-permute-start.3) | collective-permute-done | bytes 98336 | tf_op jit(solution)/shard_map/ppermute | solution.py:16
  16.3 0.1 collective-permute-start.10
  16.3 0.0 collective-permute-done.4
  16.4 0.0 collective-permute-done.5
  16.4 0.6 %collective-permute-start.6 = (f32[96,768]{1,0:T(8,128)S(1)}, f32[96,768]{1,0:T(8,128)S(1)}, u32[]{:S(2)}, u32[]{:S(2)}) collective-permute-start(f32[96,768]{1,0:T(8,128)S(1)} %constant_dynamic-update-slice_fusion.6.sent.refs_5_), channel_id=1, source_target_pairs={{0,4},{4,0},{8,12},{12,8},{16,20},{20,16},{24,28},{28,24},{1,5},{5... | collective-permute-start | bytes 884744 | tf_op jit(solution)/shard_map/ppermute | solution.py:16
  18.2 0.3 collective-permute-done.6.got.refs_6_
  18.5 1.2 %image_terms.1 = (f32[32,768]{1,0:T(8,128)S(1)}, f32[8,128]{1,0:T(8,128)S(1)}, f32[128,128]{1,0:T(8,128)S(1)}, f32[25,8,128]{2,1,0:T(8,128)S(1)}, f32[25,8,128]{2,1,0:T(8,128)S(1)}, /*index=5*/f32[25,8,128]{2,1,0:T(8,128)S(1)}) custom-call(f32[1]{0:T(128)S(6)} %copy.14.log_scale.refs_0_, f32[1]{0:T(128)S(6)} %copy.15.bias.refs_1_, ...), custom_call_target="tpu_custom_call" | custom-call | tf_op jit(solution)/shard_map/image_terms/pallas_call | solution.py:185
  19.7 0.1 collective-permute-start.7
  19.8 3.1 %collective-permute-start.8 = (f32[25,8,128]{2,1,0:T(8,128)S(1)}, f32[25,8,128]{2,1,0:T(8,128)S(1)}, u32[]{:S(2)}, u32[]{:S(2)}) collective-permute-start(f32[25,8,128]{2,1,0:T(8,128)S(1)} %get-tuple-element.21), channel_id=1, source_target_pairs={{0,2},{1,3},{2,0},{3,1},{4,6},{5,7},{6,4},{7,5},{8,10},{9,11},{10,... | collective-permute-start | bytes 307208 | tf_op jit(solution)/shard_map/ppermute | solution.py:16
  22.8 1.3 %collective-permute-start.9 = (f32[25,8,128]{2,1,0:T(8,128)S(1)}, f32[25,8,128]{2,1,0:T(8,128)S(1)}, u32[]{:S(2)}, u32[]{:S(2)}) collective-permute-start(f32[25,8,128]{2,1,0:T(8,128)S(1)} %get-tuple-element.22), channel_id=1, source_target_pairs={{0,3},{1,2},{2,1},{3,0},{4,7},{5,6},{6,5},{7,4},{8,11},{9,10},{10,... | collective-permute-start | bytes 307208 | tf_op jit(solution)/shard_map/ppermute | solution.py:16
  24.1 0.0 collective-permute-done.10.refs_3_
  24.1 0.9 %text_terms.1 = (f32[32,768]{1,0:T(8,128)S(1)}, f32[32,768]{1,0:T(8,128)S(1)}, f32[32,768]{1,0:T(8,128)S(1)}, f32[32,768]{1,0:T(8,128)S(1)}) custom-call(f32[1]{0:T(128)S(6)} %copy.14.log_scale.refs_0_, f32[1]{0:T(128)S(6)} %copy.15.bias.refs_1_, f32[136,768]{1,0:T(8,128)S(1)} %pad_dynamic-update-slice_fusion.bundle.refs_2_, ...), custom_call_target="tpu_custom_call" | custom-call | tf_op jit(solution)/shard_map/text_terms/pallas_call | solution.py:196
  25.0 1.8 %collective-permute-start.11 = (f32[32,768]{1,0:T(8,128)S(1)}, f32[32,768]{1,0:T(8,128)S(1)}, u32[]{:S(2)}, u32[]{:S(2)}) collective-permute-start(f32[32,768]{1,0:T(8,128)S(1)} %get-tuple-element.24), channel_id=1, source_target_pairs={{0,24},{4,28},{8,16},{12,20},{16,8},{20,12},{24,0},{28,4},{1,25},{... | collective-permute-start | bytes 294920 | tf_op jit(solution)/shard_map/ppermute | solution.py:24
  26.8 1.0 %collective-permute-start.12 = (f32[32,768]{1,0:T(8,128)S(1)}, f32[32,768]{1,0:T(8,128)S(1)}, u32[]{:S(2)}, u32[]{:S(2)}) collective-permute-start(f32[32,768]{1,0:T(8,128)S(1)} %get-tuple-element.26), channel_id=1, source_target_pairs={{0,8},{4,20},{8,0},{12,28},{16,24},{20,4},{24,16},{28,12},{1,9},{5... | collective-permute-start | bytes 294920 | tf_op jit(solution)/shard_map/ppermute | solution.py:24
  27.8 0.0 collective-permute-done.7.refs_0_
  27.8 0.8 %collective-permute-start.13 = (f32[32,768]{1,0:T(8,128)S(1)}, f32[32,768]{1,0:T(8,128)S(1)}, u32[]{:S(2)}, u32[]{:S(2)}) collective-permute-start(f32[32,768]{1,0:T(8,128)S(1)} %get-tuple-element.27), channel_id=1, source_target_pairs={{0,16},{4,12},{8,24},{12,4},{16,0},{20,28},{24,8},{28,20},{1,17},{... | collective-permute-start | bytes 294920 | tf_op jit(solution)/shard_map/ppermute | solution.py:24
  28.6 2.3 %collective-permute-done.8.refs_1_ = f32[25,8,128]{2,1,0:T(8,128)S(1)} collective-permute-done((f32[25,8,128]{2,1,0:T(8,128)S(1)}, f32[25,8,128]{2,1,0:T(8,128)S(1)}, u32[]{:S(2)}, u32[]{:S(2)}) %collective-permute-start.8) | collective-permute-done | bytes 102432 | tf_op jit(solution)/shard_map/ppermute | solution.py:16
  30.9 0.0 collective-permute-done.9.refs_2_
  30.9 0.7 %collective-permute-done.11.refs_3_ = f32[32,768]{1,0:T(8,128)S(1)} collective-permute-done((f32[32,768]{1,0:T(8,128)S(1)}, f32[32,768]{1,0:T(8,128)S(1)}, u32[]{:S(2)}, u32[]{:S(2)}) %collective-permute-start.11) | collective-permute-done | bytes 98336 | tf_op jit(solution)/shard_map/ppermute | solution.py:24
  31.7 0.4 %collective-permute-done.12.refs_5_ = f32[32,768]{1,0:T(8,128)S(1)} collective-permute-done((f32[32,768]{1,0:T(8,128)S(1)}, f32[32,768]{1,0:T(8,128)S(1)}, u32[]{:S(2)}, u32[]{:S(2)}) %collective-permute-start.12) | collective-permute-done | bytes 98336 | tf_op jit(solution)/shard_map/ppermute | solution.py:24
  32.1 0.5 %collective-permute-done.13.refs_6_ = f32[32,768]{1,0:T(8,128)S(1)} collective-permute-done((f32[32,768]{1,0:T(8,128)S(1)}, f32[32,768]{1,0:T(8,128)S(1)}, u32[]{:S(2)}, u32[]{:S(2)}) %collective-permute-start.13) | collective-permute-done | bytes 98336 | tf_op jit(solution)/shard_map/ppermute | solution.py:24
  32.6 0.7 %sums.1 = (f32[1,128]{1,0:T(1,128)}, f32[32,768]{1,0:T(8,128)}, f32[32,768]{1,0:T(8,128)}) custom-call(f32[32,768]{1,0:T(8,128)S(1)} %get-tuple-element.18.own_ref, f32[8,128]{1,0:T(8,128)S(1)} %get-tuple-element.19.loss_ref, f32[25,8,128]{2,1,0:T(8,128)S(1)} %collective-permute-done.7.refs_0_, f32[25,8,128]{2,1,0:T(8,128)S(1)} %collective-permute-done.8.refs_1_, ...), custom_call_target="tpu_custom_call" | custom-call | tf_op jit(solution)/shard_map/sums/pallas_call | solution.py:207
  (9 shorter events, 0.1 us)
Async XLA Ops:
  0.6 8.5 %copy-start.1 = (f32[32,768]{1,0:T(8,128)S(1)}, f32[32,768]{1,0:T(8,128)}, u32[]{:S(2)}) copy-start(f32[32,768]{1,0:T(8,128)} %param.6) | copy-start | bytes 294916
  0.6 8.5 %copy-start.2 = (s32[128]{0:T(128)S(1)}, s32[128]{0:T(128)}, u32[]{:S(2)}) copy-start(s32[128]{0:T(128)} %param.7) | copy-start | bytes 1540
  0.7 10.2 %collective-permute-start = (f32[32,768]{1,0:T(8,128)}, f32[32,768]{1,0:T(8,128)S(1)}, u32[]{:S(2)}, u32[]{:S(2)}) collective-permute-start(f32[32,768]{1,0:T(8,128)} %param.5), channel_id=1, source_target_pairs={{0,3},{1,2},{2,1},{3,0},{4,7},{5,6},{6,5},{7,4},{8,11},{9,10},{10,... | collective-permute-start | bytes 294920 | tf_op jit(solution)/shard_map/ppermute | solution.py:16
  5.8 8.6 %collective-permute-start.1 = (f32[32,768]{1,0:T(8,128)}, f32[32,768]{1,0:T(8,128)S(1)}, u32[]{:S(2)}, u32[]{:S(2)}) collective-permute-start(f32[32,768]{1,0:T(8,128)} %param.5), channel_id=1, source_target_pairs={{0,2},{1,3},{2,0},{3,1},{4,6},{5,7},{6,4},{7,5},{8,10},{9,11},{10,... | collective-permute-start | bytes 294920 | tf_op jit(solution)/shard_map/ppermute | solution.py:16
  5.8 3.4 %collective-permute-start.2 = (f32[32,768]{1,0:T(8,128)}, f32[32,768]{1,0:T(8,128)S(1)}, u32[]{:S(2)}, u32[]{:S(2)}) collective-permute-start(f32[32,768]{1,0:T(8,128)} %param.6), channel_id=1, source_target_pairs={{0,4},{4,0},{8,12},{12,8},{16,20},{20,16},{24,28},{28,24},{1,5},{5... | collective-permute-start | bytes 294920 | tf_op jit(solution)/shard_map/ppermute | solution.py:16
  5.8 10.6 %collective-permute-start.5 = (f32[32,768]{1,0:T(8,128)}, f32[32,768]{1,0:T(8,128)S(1)}, u32[]{:S(2)}, u32[]{:S(2)}) collective-permute-start(f32[32,768]{1,0:T(8,128)} %param.6), channel_id=1, source_target_pairs={{0,24},{4,28},{8,16},{12,20},{16,8},{20,12},{24,0},{28,4},{1,25},{... | collective-permute-start | bytes 294920 | tf_op jit(solution)/shard_map/ppermute | solution.py:24
  9.2 0.9 %copy-start = (f32[32,768]{1,0:T(8,128)S(1)}, f32[32,768]{1,0:T(8,128)}, u32[]{:S(2)}) copy-start(f32[32,768]{1,0:T(8,128)} %param.5) | copy-start | bytes 294916
  9.2 7.1 %collective-permute-start.4 = (f32[64,768]{1,0:T(8,128)S(1)}, f32[64,768]{1,0:T(8,128)S(1)}, u32[]{:S(2)}, u32[]{:S(2)}) collective-permute-start(f32[64,768]{1,0:T(8,128)S(1)} %constant_dynamic-update-slice_fusion.both.refs_4_), channel_id=1, source_target_pairs={{0,8},{4,20},{8,0},{12,28},{16,24},{20,4},{24,16},{28,12},{1,9},{5... | collective-permute-start | bytes 589832 | tf_op jit(solution)/shard_map/ppermute | solution.py:24
  10.1 6.2 %collective-permute-start.3 = (f32[32,768]{1,0:T(8,128)S(1)}, f32[32,768]{1,0:T(8,128)S(1)}, u32[]{:S(2)}, u32[]{:S(2)}) collective-permute-start(f32[32,768]{1,0:T(8,128)S(1)} %copy-done), channel_id=1, source_target_pairs={{0,1},{1,0},{2,3},{3,2},{4,5},{5,4},{6,7},{7,6},{8,9},{9,8},{10,11... | collective-permute-start | bytes 294920 | tf_op jit(solution)/shard_map/ppermute | solution.py:16
  16.3 7.9 %collective-permute-start.10 = (f32[136,768]{1,0:T(8,128)S(1)}, f32[136,768]{1,0:T(8,128)S(1)}, u32[]{:S(2)}, u32[]{:S(2)}) collective-permute-start(f32[136,768]{1,0:T(8,128)S(1)} %pad_dynamic-update-slice_fusion.bundle.refs_2_), channel_id=1, source_target_pairs={{0,4},{4,0},{8,12},{12,8},{16,20},{20,16},{24,28},{28,24},{1,5},{5... | collective-permute-start | bytes 1253384 | tf_op jit(solution)/shard_map/ppermute | solution.py:16
  16.4 2.1 %collective-permute-start.6 = (f32[96,768]{1,0:T(8,128)S(1)}, f32[96,768]{1,0:T(8,128)S(1)}, u32[]{:S(2)}, u32[]{:S(2)}) collective-permute-start(f32[96,768]{1,0:T(8,128)S(1)} %constant_dynamic-update-slice_fusion.6.sent.refs_5_), channel_id=1, source_target_pairs={{0,4},{4,0},{8,12},{12,8},{16,20},{20,16},{24,28},{28,24},{1,5},{5... | collective-permute-start | bytes 884744 | tf_op jit(solution)/shard_map/ppermute | solution.py:16
  19.7 8.1 %collective-permute-start.7 = (f32[25,8,128]{2,1,0:T(8,128)S(1)}, f32[25,8,128]{2,1,0:T(8,128)S(1)}, u32[]{:S(2)}, u32[]{:S(2)}) collective-permute-start(f32[25,8,128]{2,1,0:T(8,128)S(1)} %get-tuple-element.20), channel_id=1, source_target_pairs={{0,1},{1,0},{2,3},{3,2},{4,5},{5,4},{6,7},{7,6},{8,9},{9,8},{10,11... | collective-permute-start | bytes 307208 | tf_op jit(solution)/shard_map/ppermute | solution.py:16
  19.8 11.2 %collective-permute-start.8 = (f32[25,8,128]{2,1,0:T(8,128)S(1)}, f32[25,8,128]{2,1,0:T(8,128)S(1)}, u32[]{:S(2)}, u32[]{:S(2)}) collective-permute-start(f32[25,8,128]{2,1,0:T(8,128)S(1)} %get-tuple-element.21), channel_id=1, source_target_pairs={{0,2},{1,3},{2,0},{3,1},{4,6},{5,7},{6,4},{7,5},{8,10},{9,11},{10,... | collective-permute-start | bytes 307208 | tf_op jit(solution)/shard_map/ppermute | solution.py:16
  22.8 8.1 %collective-permute-start.9 = (f32[25,8,128]{2,1,0:T(8,128)S(1)}, f32[25,8,128]{2,1,0:T(8,128)S(1)}, u32[]{:S(2)}, u32[]{:S(2)}) collective-permute-start(f32[25,8,128]{2,1,0:T(8,128)S(1)} %get-tuple-element.22), channel_id=1, source_target_pairs={{0,3},{1,2},{2,1},{3,0},{4,7},{5,6},{6,5},{7,4},{8,11},{9,10},{10,... | collective-permute-start | bytes 307208 | tf_op jit(solution)/shard_map/ppermute | solution.py:16
  25.0 6.6 %collective-permute-start.11 = (f32[32,768]{1,0:T(8,128)S(1)}, f32[32,768]{1,0:T(8,128)S(1)}, u32[]{:S(2)}, u32[]{:S(2)}) collective-permute-start(f32[32,768]{1,0:T(8,128)S(1)} %get-tuple-element.24), channel_id=1, source_target_pairs={{0,24},{4,28},{8,16},{12,20},{16,8},{20,12},{24,0},{28,4},{1,25},{... | collective-permute-start | bytes 294920 | tf_op jit(solution)/shard_map/ppermute | solution.py:24
  26.8 5.3 %collective-permute-start.12 = (f32[32,768]{1,0:T(8,128)S(1)}, f32[32,768]{1,0:T(8,128)S(1)}, u32[]{:S(2)}, u32[]{:S(2)}) collective-permute-start(f32[32,768]{1,0:T(8,128)S(1)} %get-tuple-element.26), channel_id=1, source_target_pairs={{0,8},{4,20},{8,0},{12,28},{16,24},{20,4},{24,16},{28,12},{1,9},{5... | collective-permute-start | bytes 294920 | tf_op jit(solution)/shard_map/ppermute | solution.py:24
  27.8 4.8 %collective-permute-start.13 = (f32[32,768]{1,0:T(8,128)S(1)}, f32[32,768]{1,0:T(8,128)S(1)}, u32[]{:S(2)}, u32[]{:S(2)}) collective-permute-start(f32[32,768]{1,0:T(8,128)S(1)} %get-tuple-element.27), channel_id=1, source_target_pairs={{0,16},{4,12},{8,24},{12,4},{16,0},{20,28},{24,8},{28,20},{1,17},{... | collective-permute-start | bytes 294920 | tf_op jit(solution)/shard_map/ppermute | solution.py:24

commit v21 on v15

--- a/solution.py
+++ b/solution.py
@@ -190,7 +190,7 @@
         out_specs=[whole] * (2 + n_txt),
         name="image_terms",
     )(log_scale, bias, *in_vmem(bundle, both, sent, got))
-    messages = [exchange(messages[p - 1], "txt", n_txt, IMAGE_ORDER[p]) for p in (3, 2, 1)]
+    messages = [exchange(messages[p - 1], "txt", n_txt, IMAGE_ORDER[p]) for p in (3, 1, 2)]
 
     pair = exchange(bundle, "img", n_img, 1)
     blocks = pl.pallas_call(

time: 32.5 us -> 32.5 us (level)
  starting transfers between devices: 16.5 us -> 17.4 us
  waiting for transfers between devices: 9.69 us -> 8.85 us
    ppermute x9, waiting for transfers between devices: 9.68 us -> 7.21 us  [exchange(): return lax.ppermute(x, axis, [(i, i ^ k) for i in range(n)])]
    ppermute x5, waiting for transfers between devices: 0.01 us -> 1.64 us  [chip_exchange(): lax.ppermute(x, 'img', [(i, i ^ 2 * distances[i % 2]) for i in range(n_im...]
    ppermute x9, starting transfers between devices: 9.86 us -> 10.8 us  [exchange(): return lax.ppermute(x, axis, [(i, i ^ k) for i in range(n)])]
  transfers between devices with their start and end apart: 14 -> 14, of which waited for: 5 -> 7; matrix products, arithmetic and copies ran while one was open for 3% -> 3% of each run, Pallas kernels for 6% -> 6%
where the time goes in v21:
time: 32.5 us; the launch traced here: 32.3 us
  starting transfers between devices  17.4 us (54%)
  waiting for transfers between devices  8.85 us (27%)
  Pallas kernels  2.79 us (9%)
  between operations  2.09 us (6%)
  local copies, waits for them, and re-layouts  1.24 us (4%)
    ppermute x9, starting transfers between devices, exchange(): return lax.ppermute(x, axis, [(i, i ^ k) for i in range(n)])  10.8 us
    ppermute x9, waiting for transfers between devices, exchange(): return lax.ppermute(x, axis, [(i, i ^ k) for i in range(n)])  7.21 us
    ppermute x5, starting transfers between devices, chip_exchange(): lax.ppermute(x, 'img', [(i, i ^ 2 * distances[i % 2]) for i in range(n_im...  6.6 us
    ppermute x5, waiting for transfers between devices, chip_exchange(): lax.ppermute(x, 'img', [(i, i ^ 2 * distances[i % 2]) for i in range(n_im...  1.64 us
    unnamed x12, local copies, waits for them, and re-layouts  1.21 us
    pallas_call x1, Pallas kernels, per_device(): pl.pallas_call(functools.partial(image_kernel, n_img, n_txt, rows, cols),...  1.17 us
    pallas_call x1, Pallas kernels, per_device(): pl.pallas_call(functools.partial(text_kernel, n_img, n_txt, rows, cols),...  0.89 us
    pallas_call x1, Pallas kernels, per_device(): pl.pallas_call(functools.partial(sum_kernel, n_txt, chips), out_shape=[ja...  0.74 us
  transfers between devices with their start and end apart: 14, of which 7 were waited for; matrix products, arithmetic and copies ran while one was open for 3% of the time, Pallas kernels for 6%

profile of v21, /device:TPU:0, one launch (start us, length us, event | category | flops | bytes accessed | tf_op | source)
XLA Modules:
  0.0 32.3 jit_solution(17451656718781647651)
XLA Ops:
  0.6 0.0 copy-start.1
  0.6 0.0 copy-start.2
  0.7 4.1 %collective-permute-start = (f32[32,768]{1,0:T(8,128)}, f32[32,768]{1,0:T(8,128)S(1)}, u32[]{:S(2)}, u32[]{:S(2)}) collective-permute-start(f32[32,768]{1,0:T(8,128)} %param.5), channel_id=1, source_target_pairs={{0,2},{1,3},{2,0},{3,1},{4,6},{5,7},{6,4},{7,5},{8,10},{9,11},{10,... | collective-permute-start | bytes 294920 | tf_op jit(solution)/shard_map/ppermute | solution.py:16
  4.8 1.3 %collective-permute-start.1 = (f32[32,768]{1,0:T(8,128)}, f32[32,768]{1,0:T(8,128)S(1)}, u32[]{:S(2)}, u32[]{:S(2)}) collective-permute-start(f32[32,768]{1,0:T(8,128)} %param.5), channel_id=1, source_target_pairs={{0,3},{1,2},{2,1},{3,0},{4,7},{5,6},{6,5},{7,4},{8,11},{9,10},{10,... | collective-permute-start | bytes 294920 | tf_op jit(solution)/shard_map/ppermute | solution.py:16
  6.1 0.0 collective-permute-start.2
  6.1 2.4 %collective-permute-start.5 = (f32[32,768]{1,0:T(8,128)}, f32[32,768]{1,0:T(8,128)S(1)}, u32[]{:S(2)}, u32[]{:S(2)}) collective-permute-start(f32[32,768]{1,0:T(8,128)} %param.6), channel_id=1, source_target_pairs={{0,24},{4,28},{8,16},{12,20},{16,8},{20,12},{24,0},{28,4},{1,25},{... | collective-permute-start | bytes 294920 | tf_op jit(solution)/shard_map/ppermute | solution.py:24
  8.6 0.9 %constant_dynamic-update-slice_fusion.5 = f32[136,768]{1,0:T(8,128)S(1)} fusion(f32[32,768]{1,0:T(8,128)} %param.5), kind=kLoop, calls=%fused_computation.6 | loop fusion | bytes 196608
  9.5 0.0 copy-done.2
  9.5 0.0 copy-done.1
  9.5 0.0 copy-start
  9.5 0.0 collective-permute-done.2
  9.5 0.6 %collective-permute-start.4 = (f32[64,768]{1,0:T(8,128)S(1)}, f32[64,768]{1,0:T(8,128)S(1)}, u32[]{:S(2)}, u32[]{:S(2)}) collective-permute-start(f32[64,768]{1,0:T(8,128)S(1)} %constant_dynamic-update-slice_fusion.both.refs_4_), channel_id=1, source_target_pairs={{0,8},{4,20},{8,0},{12,28},{16,24},{20,4},{24,16},{28,12},{1,9},{5... | collective-permute-start | bytes 589832 | tf_op jit(solution)/shard_map/ppermute | solution.py:24
  10.1 0.3 copy-done
  10.4 0.2 collective-permute-start.3
  10.6 2.2 %collective-permute-done = f32[32,768]{1,0:T(8,128)S(1)} collective-permute-done((f32[32,768]{1,0:T(8,128)}, f32[32,768]{1,0:T(8,128)S(1)}, u32[]{:S(2)}, u32[]{:S(2)}) %collective-permute-start) | collective-permute-done | bytes 98336 | tf_op jit(solution)/shard_map/ppermute | solution.py:16
  12.8 0.0 collective-permute-done.1
  12.8 2.5 %collective-permute-done.3 = f32[32,768]{1,0:T(8,128)S(1)} collective-permute-done((f32[32,768]{1,0:T(8,128)S(1)}, f32[32,768]{1,0:T(8,128)S(1)}, u32[]{:S(2)}, u32[]{:S(2)}) %collective-permute-start.3) | collective-permute-done | bytes 98336 | tf_op jit(solution)/shard_map/ppermute | solution.py:16
  15.3 0.1 collective-permute-start.10
  15.4 0.0 collective-permute-done.4
  15.5 0.0 collective-permute-done.5
  15.5 0.6 %collective-permute-start.6 = (f32[96,768]{1,0:T(8,128)S(1)}, f32[96,768]{1,0:T(8,128)S(1)}, u32[]{:S(2)}, u32[]{:S(2)}) collective-permute-start(f32[96,768]{1,0:T(8,128)S(1)} %constant_dynamic-update-slice_fusion.6.sent.refs_5_), channel_id=1, source_target_pairs={{0,4},{4,0},{8,12},{12,8},{16,20},{20,16},{24,28},{28,24},{1,5},{5... | collective-permute-start | bytes 884744 | tf_op jit(solution)/shard_map/ppermute | solution.py:16
  17.3 0.3 collective-permute-done.6.got.refs_6_
  17.6 1.2 %image_terms.1 = (f32[32,768]{1,0:T(8,128)S(1)}, f32[8,128]{1,0:T(8,128)S(1)}, f32[128,128]{1,0:T(8,128)S(1)}, f32[25,8,128]{2,1,0:T(8,128)S(1)}, f32[25,8,128]{2,1,0:T(8,128)S(1)}, /*index=5*/f32[25,8,128]{2,1,0:T(8,128)S(1)}) custom-call(f32[1]{0:T(128)S(6)} %copy.14.log_scale.refs_0_, f32[1]{0:T(128)S(6)} %copy.15.bias.refs_1_, ...), custom_call_target="tpu_custom_call" | custom-call | tf_op jit(solution)/shard_map/image_terms/pallas_call | solution.py:185
  18.8 0.3 %collective-permute-start.7 = (f32[25,8,128]{2,1,0:T(8,128)S(1)}, f32[25,8,128]{2,1,0:T(8,128)S(1)}, u32[]{:S(2)}, u32[]{:S(2)}) collective-permute-start(f32[25,8,128]{2,1,0:T(8,128)S(1)} %get-tuple-element.20), channel_id=1, source_target_pairs={{0,1},{1,0},{2,3},{3,2},{4,5},{5,4},{6,7},{7,6},{8,9},{9,8},{10,11... | collective-permute-start | bytes 307208 | tf_op jit(solution)/shard_map/ppermute | solution.py:16
  19.1 2.8 %collective-permute-start.8 = (f32[25,8,128]{2,1,0:T(8,128)S(1)}, f32[25,8,128]{2,1,0:T(8,128)S(1)}, u32[]{:S(2)}, u32[]{:S(2)}) collective-permute-start(f32[25,8,128]{2,1,0:T(8,128)S(1)} %get-tuple-element.21), channel_id=1, source_target_pairs={{0,2},{1,3},{2,0},{3,1},{4,6},{5,7},{6,4},{7,5},{8,10},{9,11},{10,... | collective-permute-start | bytes 307208 | tf_op jit(solution)/shard_map/ppermute | solution.py:16
  21.9 1.3 %collective-permute-start.9 = (f32[25,8,128]{2,1,0:T(8,128)S(1)}, f32[25,8,128]{2,1,0:T(8,128)S(1)}, u32[]{:S(2)}, u32[]{:S(2)}) collective-permute-start(f32[25,8,128]{2,1,0:T(8,128)S(1)} %get-tuple-element.22), channel_id=1, source_target_pairs={{0,3},{1,2},{2,1},{3,0},{4,7},{5,6},{6,5},{7,4},{8,11},{9,10},{10,... | collective-permute-start | bytes 307208 | tf_op jit(solution)/shard_map/ppermute | solution.py:16
  23.2 0.0 collective-permute-done.10.refs_3_
  23.2 0.9 %text_terms.1 = (f32[32,768]{1,0:T(8,128)S(1)}, f32[32,768]{1,0:T(8,128)S(1)}, f32[32,768]{1,0:T(8,128)S(1)}, f32[32,768]{1,0:T(8,128)S(1)}) custom-call(f32[1]{0:T(128)S(6)} %copy.14.log_scale.refs_0_, f32[1]{0:T(128)S(6)} %copy.15.bias.refs_1_, f32[136,768]{1,0:T(8,128)S(1)} %pad_dynamic-update-slice_fusion.bundle.refs_2_, ...), custom_call_target="tpu_custom_call" | custom-call | tf_op jit(solution)/shard_map/text_terms/pallas_call | solution.py:196
  24.1 1.7 %collective-permute-start.11 = (f32[32,768]{1,0:T(8,128)S(1)}, f32[32,768]{1,0:T(8,128)S(1)}, u32[]{:S(2)}, u32[]{:S(2)}) collective-permute-start(f32[32,768]{1,0:T(8,128)S(1)} %get-tuple-element.24), channel_id=1, source_target_pairs={{0,24},{4,28},{8,16},{12,20},{16,8},{20,12},{24,0},{28,4},{1,25},{... | collective-permute-start | bytes 294920 | tf_op jit(solution)/shard_map/ppermute | solution.py:24
  25.8 1.0 %collective-permute-start.12 = (f32[32,768]{1,0:T(8,128)S(1)}, f32[32,768]{1,0:T(8,128)S(1)}, u32[]{:S(2)}, u32[]{:S(2)}) collective-permute-start(f32[32,768]{1,0:T(8,128)S(1)} %get-tuple-element.26), channel_id=1, source_target_pairs={{0,8},{4,20},{8,0},{12,28},{16,24},{20,4},{24,16},{28,12},{1,9},{5... | collective-permute-start | bytes 294920 | tf_op jit(solution)/shard_map/ppermute | solution.py:24
  26.8 0.0 collective-permute-done.7.refs_0_
  26.8 0.9 %collective-permute-start.13 = (f32[32,768]{1,0:T(8,128)S(1)}, f32[32,768]{1,0:T(8,128)S(1)}, u32[]{:S(2)}, u32[]{:S(2)}) collective-permute-start(f32[32,768]{1,0:T(8,128)S(1)} %get-tuple-element.27), channel_id=1, source_target_pairs={{0,16},{4,12},{8,24},{12,4},{16,0},{20,28},{24,8},{28,20},{1,17},{... | collective-permute-start | bytes 294920 | tf_op jit(solution)/shard_map/ppermute | solution.py:24
  27.7 2.3 %collective-permute-done.8.refs_1_ = f32[25,8,128]{2,1,0:T(8,128)S(1)} collective-permute-done((f32[25,8,128]{2,1,0:T(8,128)S(1)}, f32[25,8,128]{2,1,0:T(8,128)S(1)}, u32[]{:S(2)}, u32[]{:S(2)}) %collective-permute-start.8) | collective-permute-done | bytes 102432 | tf_op jit(solution)/shard_map/ppermute | solution.py:16
  30.0 0.0 collective-permute-done.9.refs_2_
  30.0 0.8 %collective-permute-done.11.refs_3_ = f32[32,768]{1,0:T(8,128)S(1)} collective-permute-done((f32[32,768]{1,0:T(8,128)S(1)}, f32[32,768]{1,0:T(8,128)S(1)}, u32[]{:S(2)}, u32[]{:S(2)}) %collective-permute-start.11) | collective-permute-done | bytes 98336 | tf_op jit(solution)/shard_map/ppermute | solution.py:24
  30.8 0.3 collective-permute-done.12.refs_5_
  31.1 0.5 %collective-permute-done.13.refs_6_ = f32[32,768]{1,0:T(8,128)S(1)} collective-permute-done((f32[32,768]{1,0:T(8,128)S(1)}, f32[32,768]{1,0:T(8,128)S(1)}, u32[]{:S(2)}, u32[]{:S(2)}) %collective-permute-start.13) | collective-permute-done | bytes 98336 | tf_op jit(solution)/shard_map/ppermute | solution.py:24
  31.6 0.7 %sums.1 = (f32[1,128]{1,0:T(1,128)}, f32[32,768]{1,0:T(8,128)}, f32[32,768]{1,0:T(8,128)}) custom-call(f32[32,768]{1,0:T(8,128)S(1)} %get-tuple-element.18.own_ref, f32[8,128]{1,0:T(8,128)S(1)} %get-tuple-element.19.loss_ref, f32[25,8,128]{2,1,0:T(8,128)S(1)} %collective-permute-done.7.refs_0_, f32[25,8,128]{2,1,0:T(8,128)S(1)} %collective-permute-done.8.refs_1_, ...), custom_call_target="tpu_custom_call" | custom-call | tf_op jit(solution)/shard_map/sums/pallas_call | solution.py:207
  (9 shorter events, 0.1 us)
Async XLA Ops:
  0.6 8.8 %copy-start.1 = (f32[32,768]{1,0:T(8,128)S(1)}, f32[32,768]{1,0:T(8,128)}, u32[]{:S(2)}) copy-start(f32[32,768]{1,0:T(8,128)} %param.6) | copy-start | bytes 294916
  0.6 8.8 %copy-start.2 = (s32[128]{0:T(128)S(1)}, s32[128]{0:T(128)}, u32[]{:S(2)}) copy-start(s32[128]{0:T(128)} %param.7) | copy-start | bytes 1540
  0.7 12.2 %collective-permute-start = (f32[32,768]{1,0:T(8,128)}, f32[32,768]{1,0:T(8,128)S(1)}, u32[]{:S(2)}, u32[]{:S(2)}) collective-permute-start(f32[32,768]{1,0:T(8,128)} %param.5), channel_id=1, source_target_pairs={{0,2},{1,3},{2,0},{3,1},{4,6},{5,7},{6,4},{7,5},{8,10},{9,11},{10,... | collective-permute-start | bytes 294920 | tf_op jit(solution)/shard_map/ppermute | solution.py:16
  4.8 8.1 %collective-permute-start.1 = (f32[32,768]{1,0:T(8,128)}, f32[32,768]{1,0:T(8,128)S(1)}, u32[]{:S(2)}, u32[]{:S(2)}) collective-permute-start(f32[32,768]{1,0:T(8,128)} %param.5), channel_id=1, source_target_pairs={{0,3},{1,2},{2,1},{3,0},{4,7},{5,6},{6,5},{7,4},{8,11},{9,10},{10,... | collective-permute-start | bytes 294920 | tf_op jit(solution)/shard_map/ppermute | solution.py:16
  6.1 3.4 %collective-permute-start.2 = (f32[32,768]{1,0:T(8,128)}, f32[32,768]{1,0:T(8,128)S(1)}, u32[]{:S(2)}, u32[]{:S(2)}) collective-permute-start(f32[32,768]{1,0:T(8,128)} %param.6), channel_id=1, source_target_pairs={{0,4},{4,0},{8,12},{12,8},{16,20},{20,16},{24,28},{28,24},{1,5},{5... | collective-permute-start | bytes 294920 | tf_op jit(solution)/shard_map/ppermute | solution.py:16
  6.1 9.4 %collective-permute-start.5 = (f32[32,768]{1,0:T(8,128)}, f32[32,768]{1,0:T(8,128)S(1)}, u32[]{:S(2)}, u32[]{:S(2)}) collective-permute-start(f32[32,768]{1,0:T(8,128)} %param.6), channel_id=1, source_target_pairs={{0,24},{4,28},{8,16},{12,20},{16,8},{20,12},{24,0},{28,4},{1,25},{... | collective-permute-start | bytes 294920 | tf_op jit(solution)/shard_map/ppermute | solution.py:24
  9.5 0.9 %copy-start = (f32[32,768]{1,0:T(8,128)S(1)}, f32[32,768]{1,0:T(8,128)}, u32[]{:S(2)}) copy-start(f32[32,768]{1,0:T(8,128)} %param.5) | copy-start | bytes 294916
  9.5 5.9 %collective-permute-start.4 = (f32[64,768]{1,0:T(8,128)S(1)}, f32[64,768]{1,0:T(8,128)S(1)}, u32[]{:S(2)}, u32[]{:S(2)}) collective-permute-start(f32[64,768]{1,0:T(8,128)S(1)} %constant_dynamic-update-slice_fusion.both.refs_4_), channel_id=1, source_target_pairs={{0,8},{4,20},{8,0},{12,28},{16,24},{20,4},{24,16},{28,12},{1,9},{5... | collective-permute-start | bytes 589832 | tf_op jit(solution)/shard_map/ppermute | solution.py:24
  10.4 4.9 %collective-permute-start.3 = (f32[32,768]{1,0:T(8,128)S(1)}, f32[32,768]{1,0:T(8,128)S(1)}, u32[]{:S(2)}, u32[]{:S(2)}) collective-permute-start(f32[32,768]{1,0:T(8,128)S(1)} %copy-done), channel_id=1, source_target_pairs={{0,1},{1,0},{2,3},{3,2},{4,5},{5,4},{6,7},{7,6},{8,9},{9,8},{10,11... | collective-permute-start | bytes 294920 | tf_op jit(solution)/shard_map/ppermute | solution.py:16
  15.3 7.9 %collective-permute-start.10 = (f32[136,768]{1,0:T(8,128)S(1)}, f32[136,768]{1,0:T(8,128)S(1)}, u32[]{:S(2)}, u32[]{:S(2)}) collective-permute-start(f32[136,768]{1,0:T(8,128)S(1)} %pad_dynamic-update-slice_fusion.bundle.refs_2_), channel_id=1, source_target_pairs={{0,4},{4,0},{8,12},{12,8},{16,20},{20,16},{24,28},{28,24},{1,5},{5... | collective-permute-start | bytes 1253384 | tf_op jit(solution)/shard_map/ppermute | solution.py:16
  15.5 2.1 %collective-permute-start.6 = (f32[96,768]{1,0:T(8,128)S(1)}, f32[96,768]{1,0:T(8,128)S(1)}, u32[]{:S(2)}, u32[]{:S(2)}) collective-permute-start(f32[96,768]{1,0:T(8,128)S(1)} %constant_dynamic-update-slice_fusion.6.sent.refs_5_), channel_id=1, source_target_pairs={{0,4},{4,0},{8,12},{12,8},{16,20},{20,16},{24,28},{28,24},{1,5},{5... | collective-permute-start | bytes 884744 | tf_op jit(solution)/shard_map/ppermute | solution.py:16
  18.8 8.0 %collective-permute-start.7 = (f32[25,8,128]{2,1,0:T(8,128)S(1)}, f32[25,8,128]{2,1,0:T(8,128)S(1)}, u32[]{:S(2)}, u32[]{:S(2)}) collective-permute-start(f32[25,8,128]{2,1,0:T(8,128)S(1)} %get-tuple-element.20), channel_id=1, source_target_pairs={{0,1},{1,0},{2,3},{3,2},{4,5},{5,4},{6,7},{7,6},{8,9},{9,8},{10,11... | collective-permute-start | bytes 307208 | tf_op jit(solution)/shard_map/ppermute | solution.py:16
  19.1 10.9 %collective-permute-start.8 = (f32[25,8,128]{2,1,0:T(8,128)S(1)}, f32[25,8,128]{2,1,0:T(8,128)S(1)}, u32[]{:S(2)}, u32[]{:S(2)}) collective-permute-start(f32[25,8,128]{2,1,0:T(8,128)S(1)} %get-tuple-element.21), channel_id=1, source_target_pairs={{0,2},{1,3},{2,0},{3,1},{4,6},{5,7},{6,4},{7,5},{8,10},{9,11},{10,... | collective-permute-start | bytes 307208 | tf_op jit(solution)/shard_map/ppermute | solution.py:16
  21.9 8.1 %collective-permute-start.9 = (f32[25,8,128]{2,1,0:T(8,128)S(1)}, f32[25,8,128]{2,1,0:T(8,128)S(1)}, u32[]{:S(2)}, u32[]{:S(2)}) collective-permute-start(f32[25,8,128]{2,1,0:T(8,128)S(1)} %get-tuple-element.22), channel_id=1, source_target_pairs={{0,3},{1,2},{2,1},{3,0},{4,7},{5,6},{6,5},{7,4},{8,11},{9,10},{10,... | collective-permute-start | bytes 307208 | tf_op jit(solution)/shard_map/ppermute | solution.py:16
  24.1 6.7 %collective-permute-start.11 = (f32[32,768]{1,0:T(8,128)S(1)}, f32[32,768]{1,0:T(8,128)S(1)}, u32[]{:S(2)}, u32[]{:S(2)}) collective-permute-start(f32[32,768]{1,0:T(8,128)S(1)} %get-tuple-element.24), channel_id=1, source_target_pairs={{0,24},{4,28},{8,16},{12,20},{16,8},{20,12},{24,0},{28,4},{1,25},{... | collective-permute-start | bytes 294920 | tf_op jit(solution)/shard_map/ppermute | solution.py:24
  25.8 5.3 %collective-permute-start.12 = (f32[32,768]{1,0:T(8,128)S(1)}, f32[32,768]{1,0:T(8,128)S(1)}, u32[]{:S(2)}, u32[]{:S(2)}) collective-permute-start(f32[32,768]{1,0:T(8,128)S(1)} %get-tuple-element.26), channel_id=1, source_target_pairs={{0,8},{4,20},{8,0},{12,28},{16,24},{20,4},{24,16},{28,12},{1,9},{5... | collective-permute-start | bytes 294920 | tf_op jit(solution)/shard_map/ppermute | solution.py:24
  26.8 4.8 %collective-permute-start.13 = (f32[32,768]{1,0:T(8,128)S(1)}, f32[32,768]{1,0:T(8,128)S(1)}, u32[]{:S(2)}, u32[]{:S(2)}) collective-permute-start(f32[32,768]{1,0:T(8,128)S(1)} %get-tuple-element.27), channel_id=1, source_target_pairs={{0,16},{4,12},{8,24},{12,4},{16,0},{20,28},{24,8},{28,20},{1,17},{... | collective-permute-start | bytes 294920 | tf_op jit(solution)/shard_map/ppermute | solution.py:24

commit v22 on v15

--- a/solution.py
+++ b/solution.py
@@ -192,7 +192,7 @@
     )(log_scale, bias, *in_vmem(bundle, both, sent, got))
     messages = [exchange(messages[p - 1], "txt", n_txt, IMAGE_ORDER[p]) for p in (3, 2, 1)]
 
-    pair = exchange(bundle, "img", n_img, 1)
+    pair = exchange(after(bundle, got), "img", n_img, 1)
     blocks = pl.pallas_call(
         functools.partial(text_kernel, n_img, n_txt, rows, cols),
         out_shape=[vmem((cols, width))] * chips,

time: 32.5 us -> 34.1 us (1.049)
  waiting for transfers between devices: 9.69 us -> 11 us
  other arithmetic: 0.01 us -> 0.66 us
  starting transfers between devices: 16.5 us -> 16.1 us
    ppermute x5, waiting for transfers between devices: 0.01 us -> 3.07 us  [chip_exchange(): lax.ppermute(x, 'img', [(i, i ^ 2 * distances[i % 2]) for i in range(n_im...]
    ppermute x9, waiting for transfers between devices: 9.68 us -> 7.97 us  [exchange(): return lax.ppermute(x, axis, [(i, i ^ k) for i in range(n)])]
    broadcast_in_dim x1, other arithmetic: 0.01 us -> 0.66 us  [per_device(): pairs.astype(jnp.float32)[None]]
    unnamed x12 -> x8, local copies, waits for them, and re-layouts: 1.21 us -> 1.21 us
  transfers between devices with their start and end apart: 14 -> 14, of which waited for: 5 -> 5; matrix products, arithmetic and copies ran while one was open for 3% -> 5% of each run, Pallas kernels for 6% -> 6%
where the time goes in v22:
time: 34.1 us; the launch traced here: 33.9 us
  starting transfers between devices  16.1 us (47%)
  waiting for transfers between devices  11 us (32%)
  Pallas kernels  2.8 us (8%)
  between operations  2.05 us (6%)
  local copies, waits for them, and re-layouts  1.23 us (4%)
  other arithmetic  0.66 us (2%)
    ppermute x9, starting transfers between devices, exchange(): return lax.ppermute(x, axis, [(i, i ^ k) for i in range(n)])  9.52 us
    ppermute x9, waiting for transfers between devices, exchange(): return lax.ppermute(x, axis, [(i, i ^ k) for i in range(n)])  7.97 us
    ppermute x5, starting transfers between devices, chip_exchange(): lax.ppermute(x, 'img', [(i, i ^ 2 * distances[i % 2]) for i in range(n_im...  6.6 us
    ppermute x5, waiting for transfers between devices, chip_exchange(): lax.ppermute(x, 'img', [(i, i ^ 2 * distances[i % 2]) for i in range(n_im...  3.07 us
    unnamed x8, local copies, waits for them, and re-layouts  1.21 us
    pallas_call x1, Pallas kernels, per_device(): pl.pallas_call(functools.partial(image_kernel, n_img, n_txt, rows, cols),...  1.17 us
    pallas_call x1, Pallas kernels, per_device(): pl.pallas_call(functools.partial(text_kernel, n_img, n_txt, rows, cols),...  0.9 us
    pallas_call x1, Pallas kernels, per_device(): pl.pallas_call(functools.partial(sum_kernel, n_txt, chips), out_shape=[ja...  0.74 us
  transfers between devices with their start and end apart: 14, of which 5 were waited for; matrix products, arithmetic and copies ran while one was open for 5% of the time, Pallas kernels for 6%

profile of v22, /device:TPU:0, one launch (start us, length us, event | category | flops | bytes accessed | tf_op | source)
XLA Modules:
  0.0 33.9 jit_solution(16337105608051587817)
XLA Ops:
  0.6 4.1 %collective-permute-start = (f32[32,768]{1,0:T(8,128)}, f32[32,768]{1,0:T(8,128)S(1)}, u32[]{:S(2)}, u32[]{:S(2)}) collective-permute-start(f32[32,768]{1,0:T(8,128)} %param.5), channel_id=1, source_target_pairs={{0,2},{1,3},{2,0},{3,1},{4,6},{5,7},{6,4},{7,5},{8,10},{9,11},{10,... | collective-permute-start | bytes 294920 | tf_op jit(solution)/shard_map/ppermute | solution.py:16
  4.7 1.3 %collective-permute-start.1 = (f32[32,768]{1,0:T(8,128)}, f32[32,768]{1,0:T(8,128)S(1)}, u32[]{:S(2)}, u32[]{:S(2)}) collective-permute-start(f32[32,768]{1,0:T(8,128)} %param.5), channel_id=1, source_target_pairs={{0,3},{1,2},{2,1},{3,0},{4,7},{5,6},{6,5},{7,4},{8,11},{9,10},{10,... | collective-permute-start | bytes 294920 | tf_op jit(solution)/shard_map/ppermute | solution.py:16
  6.1 0.0 collective-permute-start.2
  6.1 2.4 %collective-permute-start.5 = (f32[32,768]{1,0:T(8,128)}, f32[32,768]{1,0:T(8,128)S(1)}, u32[]{:S(2)}, u32[]{:S(2)}) collective-permute-start(f32[32,768]{1,0:T(8,128)} %param.6), channel_id=1, source_target_pairs={{0,24},{4,28},{8,16},{12,20},{16,8},{20,12},{24,0},{28,4},{1,25},{... | collective-permute-start | bytes 294920 | tf_op jit(solution)/shard_map/ppermute | solution.py:24
  8.5 0.7 %convert_bitcast_fusion = f32[1,128]{1,0:T(1,128)S(1)} fusion(s32[128]{0:T(128)} %param.7), kind=kLoop, calls=%fused_computation.9 | loop fusion | flops 128 | bytes 1024 | tf_op jit(solution)/shard_map/broadcast_in_dim | solution.py:182
  9.2 0.9 %constant_dynamic-update-slice_fusion.1 = f32[64,768]{1,0:T(8,128)S(1)} fusion(f32[32,768]{1,0:T(8,128)} %param.6), kind=kLoop, calls=%fused_computation.2 | loop fusion | bytes 196608
  10.1 0.0 copy-start
  10.1 0.0 collective-permute-done.2
  10.1 0.6 %collective-permute-start.4 = (f32[64,768]{1,0:T(8,128)S(1)}, f32[64,768]{1,0:T(8,128)S(1)}, u32[]{:S(2)}, u32[]{:S(2)}) collective-permute-start(f32[64,768]{1,0:T(8,128)S(1)} %constant_dynamic-update-slice_fusion.both.refs_4_), channel_id=1, source_target_pairs={{0,8},{4,20},{8,0},{12,28},{16,24},{20,4},{24,16},{28,12},{1,9},{5... | collective-permute-start | bytes 589832 | tf_op jit(solution)/shard_map/ppermute | solution.py:24
  10.7 0.3 copy-done
  11.0 0.3 collective-permute-start.3
  11.3 1.5 %collective-permute-done = f32[32,768]{1,0:T(8,128)S(1)} collective-permute-done((f32[32,768]{1,0:T(8,128)}, f32[32,768]{1,0:T(8,128)S(1)}, u32[]{:S(2)}, u32[]{:S(2)}) %collective-permute-start) | collective-permute-done | bytes 98336 | tf_op jit(solution)/shard_map/ppermute | solution.py:16
  12.8 3.1 %collective-permute-done.4 = f32[64,768]{1,0:T(8,128)S(1)} collective-permute-done((f32[64,768]{1,0:T(8,128)S(1)}, f32[64,768]{1,0:T(8,128)S(1)}, u32[]{:S(2)}, u32[]{:S(2)}) %collective-permute-start.4) | collective-permute-done | bytes 196640 | tf_op jit(solution)/shard_map/ppermute | solution.py:24
  15.9 0.0 collective-permute-done.5
  15.9 0.1 collective-permute-start.6
  16.0 0.0 collective-permute-done.1
  16.0 0.0 collective-permute-done.3
  16.0 1.5 %collective-permute-done.6.got.refs_6_ = f32[96,768]{1,0:T(8,128)S(1)} collective-permute-done((f32[96,768]{1,0:T(8,128)S(1)}, f32[96,768]{1,0:T(8,128)S(1)}, u32[]{:S(2)}, u32[]{:S(2)}) %collective-permute-start.6) | collective-permute-done | bytes 294944 | tf_op jit(solution)/shard_map/ppermute | solution.py:16
  17.6 0.1 collective-permute-start.10
  19.0 1.2 %image_terms.1 = (f32[32,768]{1,0:T(8,128)S(1)}, f32[8,128]{1,0:T(8,128)S(1)}, f32[128,128]{1,0:T(8,128)S(1)}, f32[25,8,128]{2,1,0:T(8,128)S(1)}, f32[25,8,128]{2,1,0:T(8,128)S(1)}, /*index=5*/f32[25,8,128]{2,1,0:T(8,128)S(1)}) custom-call(f32[1]{0:T(128)S(6)} %copy.14.log_scale.refs_0_, f32[1]{0:T(128)S(6)} %copy.15.bias.refs_1_, ...), custom_call_target="tpu_custom_call" | custom-call | tf_op jit(solution)/shard_map/image_terms/pallas_call | solution.py:185
  20.2 0.3 collective-permute-start.7
  20.5 2.9 %collective-permute-start.8 = (f32[25,8,128]{2,1,0:T(8,128)S(1)}, f32[25,8,128]{2,1,0:T(8,128)S(1)}, u32[]{:S(2)}, u32[]{:S(2)}) collective-permute-start(f32[25,8,128]{2,1,0:T(8,128)S(1)} %get-tuple-element.22), channel_id=1, source_target_pairs={{0,3},{1,2},{2,1},{3,0},{4,7},{5,6},{6,5},{7,4},{8,11},{9,10},{10,... | collective-permute-start | bytes 307208 | tf_op jit(solution)/shard_map/ppermute | solution.py:16
  23.4 0.3 collective-permute-start.9
  23.7 0.0 collective-permute-done.10.refs_3_
  23.7 0.9 %text_terms.1 = (f32[32,768]{1,0:T(8,128)S(1)}, f32[32,768]{1,0:T(8,128)S(1)}, f32[32,768]{1,0:T(8,128)S(1)}, f32[32,768]{1,0:T(8,128)S(1)}) custom-call(f32[1]{0:T(128)S(6)} %copy.14.log_scale.refs_0_, f32[1]{0:T(128)S(6)} %copy.15.bias.refs_1_, f32[136,768]{1,0:T(8,128)S(1)} %pad_dynamic-update-slice_fusion.bundle.refs_2_, ...), custom_call_target="tpu_custom_call" | custom-call | tf_op jit(solution)/shard_map/text_terms/pallas_call | solution.py:196
  24.6 1.1 %collective-permute-start.11 = (f32[32,768]{1,0:T(8,128)S(1)}, f32[32,768]{1,0:T(8,128)S(1)}, u32[]{:S(2)}, u32[]{:S(2)}) collective-permute-start(f32[32,768]{1,0:T(8,128)S(1)} %get-tuple-element.26), channel_id=1, source_target_pairs={{0,24},{4,28},{8,16},{12,20},{16,8},{20,12},{24,0},{28,4},{1,25},{... | collective-permute-start | bytes 294920 | tf_op jit(solution)/shard_map/ppermute | solution.py:24
  25.8 0.9 %collective-permute-start.12 = (f32[32,768]{1,0:T(8,128)S(1)}, f32[32,768]{1,0:T(8,128)S(1)}, u32[]{:S(2)}, u32[]{:S(2)}) collective-permute-start(f32[32,768]{1,0:T(8,128)S(1)} %get-tuple-element.28), channel_id=1, source_target_pairs={{0,8},{4,20},{8,0},{12,28},{16,24},{20,4},{24,16},{28,12},{1,9},{5... | collective-permute-start | bytes 294920 | tf_op jit(solution)/shard_map/ppermute | solution.py:24
  26.7 0.0 collective-permute-done.7.refs_0_
  26.7 1.5 %collective-permute-start.13 = (f32[32,768]{1,0:T(8,128)S(1)}, f32[32,768]{1,0:T(8,128)S(1)}, u32[]{:S(2)}, u32[]{:S(2)}) collective-permute-start(f32[32,768]{1,0:T(8,128)S(1)} %get-tuple-element.29), channel_id=1, source_target_pairs={{0,16},{4,12},{8,24},{12,4},{16,0},{20,28},{24,8},{28,20},{1,17},{... | collective-permute-start | bytes 294920 | tf_op jit(solution)/shard_map/ppermute | solution.py:24
  28.2 1.2 %collective-permute-done.8.refs_1_ = f32[25,8,128]{2,1,0:T(8,128)S(1)} collective-permute-done((f32[25,8,128]{2,1,0:T(8,128)S(1)}, f32[25,8,128]{2,1,0:T(8,128)S(1)}, u32[]{:S(2)}, u32[]{:S(2)}) %collective-permute-start.8) | collective-permute-done | bytes 102432 | tf_op jit(solution)/shard_map/ppermute | solution.py:16
  29.4 3.8 %collective-permute-done.9.refs_2_ = f32[25,8,128]{2,1,0:T(8,128)S(1)} collective-permute-done((f32[25,8,128]{2,1,0:T(8,128)S(1)}, f32[25,8,128]{2,1,0:T(8,128)S(1)}, u32[]{:S(2)}, u32[]{:S(2)}) %collective-permute-start.9) | collective-permute-done | bytes 102432 | tf_op jit(solution)/shard_map/ppermute | solution.py:16
  33.2 0.0 collective-permute-done.11.refs_3_
  33.2 0.0 collective-permute-done.12.refs_5_
  33.2 0.0 collective-permute-done.13.refs_6_
  33.2 0.7 %sums.1 = (f32[1,128]{1,0:T(1,128)}, f32[32,768]{1,0:T(8,128)}, f32[32,768]{1,0:T(8,128)}) custom-call(f32[32,768]{1,0:T(8,128)S(1)} %get-tuple-element.19.own_ref, f32[8,128]{1,0:T(8,128)S(1)} %get-tuple-element.20.loss_ref, f32[25,8,128]{2,1,0:T(8,128)S(1)} %collective-permute-done.7.refs_0_, f32[25,8,128]{2,1,0:T(8,128)S(1)} %collective-permute-done.8.refs_1_, ...), custom_call_target="tpu_custom_call" | custom-call | tf_op jit(solution)/shard_map/sums/pallas_call | solution.py:207
  (8 shorter events, 0.1 us)
Async XLA Ops:
  0.6 12.2 %collective-permute-start = (f32[32,768]{1,0:T(8,128)}, f32[32,768]{1,0:T(8,128)S(1)}, u32[]{:S(2)}, u32[]{:S(2)}) collective-permute-start(f32[32,768]{1,0:T(8,128)} %param.5), channel_id=1, source_target_pairs={{0,2},{1,3},{2,0},{3,1},{4,6},{5,7},{6,4},{7,5},{8,10},{9,11},{10,... | collective-permute-start | bytes 294920 | tf_op jit(solution)/shard_map/ppermute | solution.py:16
  4.7 11.3 %collective-permute-start.1 = (f32[32,768]{1,0:T(8,128)}, f32[32,768]{1,0:T(8,128)S(1)}, u32[]{:S(2)}, u32[]{:S(2)}) collective-permute-start(f32[32,768]{1,0:T(8,128)} %param.5), channel_id=1, source_target_pairs={{0,3},{1,2},{2,1},{3,0},{4,7},{5,6},{6,5},{7,4},{8,11},{9,10},{10,... | collective-permute-start | bytes 294920 | tf_op jit(solution)/shard_map/ppermute | solution.py:16
  6.1 4.0 %collective-permute-start.2 = (f32[32,768]{1,0:T(8,128)}, f32[32,768]{1,0:T(8,128)S(1)}, u32[]{:S(2)}, u32[]{:S(2)}) collective-permute-start(f32[32,768]{1,0:T(8,128)} %param.6), channel_id=1, source_target_pairs={{0,4},{4,0},{8,12},{12,8},{16,20},{20,16},{24,28},{28,24},{1,5},{5... | collective-permute-start | bytes 294920 | tf_op jit(solution)/shard_map/ppermute | solution.py:16
  6.1 9.8 %collective-permute-start.5 = (f32[32,768]{1,0:T(8,128)}, f32[32,768]{1,0:T(8,128)S(1)}, u32[]{:S(2)}, u32[]{:S(2)}) collective-permute-start(f32[32,768]{1,0:T(8,128)} %param.6), channel_id=1, source_target_pairs={{0,24},{4,28},{8,16},{12,20},{16,8},{20,12},{24,0},{28,4},{1,25},{... | collective-permute-start | bytes 294920 | tf_op jit(solution)/shard_map/ppermute | solution.py:24
  10.1 0.9 %copy-start = (f32[32,768]{1,0:T(8,128)S(1)}, f32[32,768]{1,0:T(8,128)}, u32[]{:S(2)}) copy-start(f32[32,768]{1,0:T(8,128)} %param.5) | copy-start | bytes 294916
  10.1 5.7 %collective-permute-start.4 = (f32[64,768]{1,0:T(8,128)S(1)}, f32[64,768]{1,0:T(8,128)S(1)}, u32[]{:S(2)}, u32[]{:S(2)}) collective-permute-start(f32[64,768]{1,0:T(8,128)S(1)} %constant_dynamic-update-slice_fusion.both.refs_4_), channel_id=1, source_target_pairs={{0,8},{4,20},{8,0},{12,28},{16,24},{20,4},{24,16},{28,12},{1,9},{5... | collective-permute-start | bytes 589832 | tf_op jit(solution)/shard_map/ppermute | solution.py:24
  11.0 5.0 %collective-permute-start.3 = (f32[32,768]{1,0:T(8,128)S(1)}, f32[32,768]{1,0:T(8,128)S(1)}, u32[]{:S(2)}, u32[]{:S(2)}) collective-permute-start(f32[32,768]{1,0:T(8,128)S(1)} %copy-done), channel_id=1, source_target_pairs={{0,1},{1,0},{2,3},{3,2},{4,5},{5,4},{6,7},{7,6},{8,9},{9,8},{10,11... | collective-permute-start | bytes 294920 | tf_op jit(solution)/shard_map/ppermute | solution.py:16
  15.9 1.6 %collective-permute-start.6 = (f32[96,768]{1,0:T(8,128)S(1)}, f32[96,768]{1,0:T(8,128)S(1)}, u32[]{:S(2)}, u32[]{:S(2)}) collective-permute-start(f32[96,768]{1,0:T(8,128)S(1)} %constant_dynamic-update-slice_fusion.6.sent.refs_5_), channel_id=1, source_target_pairs={{0,4},{4,0},{8,12},{12,8},{16,20},{20,16},{24,28},{28,24},{1,5},{5... | collective-permute-start | bytes 884744 | tf_op jit(solution)/shard_map/ppermute | solution.py:16
  17.6 6.2 %collective-permute-start.10 = (f32[136,768]{1,0:T(8,128)S(1)}, f32[136,768]{1,0:T(8,128)S(1)}, u32[]{:S(2)}, u32[]{:S(2)}) collective-permute-start(f32[136,768]{1,0:T(8,128)S(1)} %pad_dynamic-update-slice_fusion.bundle.refs_2_), channel_id=1, source_target_pairs={{0,4},{4,0},{8,12},{12,8},{16,20},{20,16},{24,28},{28,24},{1,5},{5... | collective-permute-start | bytes 1253384 | tf_op jit(solution)/shard_map/ppermute | solution.py:16
  20.2 6.5 %collective-permute-start.7 = (f32[25,8,128]{2,1,0:T(8,128)S(1)}, f32[25,8,128]{2,1,0:T(8,128)S(1)}, u32[]{:S(2)}, u32[]{:S(2)}) collective-permute-start(f32[25,8,128]{2,1,0:T(8,128)S(1)} %get-tuple-element.21), channel_id=1, source_target_pairs={{0,1},{1,0},{2,3},{3,2},{4,5},{5,4},{6,7},{7,6},{8,9},{9,8},{10,11... | collective-permute-start | bytes 307208 | tf_op jit(solution)/shard_map/ppermute | solution.py:16
  20.5 8.9 %collective-permute-start.8 = (f32[25,8,128]{2,1,0:T(8,128)S(1)}, f32[25,8,128]{2,1,0:T(8,128)S(1)}, u32[]{:S(2)}, u32[]{:S(2)}) collective-permute-start(f32[25,8,128]{2,1,0:T(8,128)S(1)} %get-tuple-element.22), channel_id=1, source_target_pairs={{0,3},{1,2},{2,1},{3,0},{4,7},{5,6},{6,5},{7,4},{8,11},{9,10},{10,... | collective-permute-start | bytes 307208 | tf_op jit(solution)/shard_map/ppermute | solution.py:16
  23.4 9.8 %collective-permute-start.9 = (f32[25,8,128]{2,1,0:T(8,128)S(1)}, f32[25,8,128]{2,1,0:T(8,128)S(1)}, u32[]{:S(2)}, u32[]{:S(2)}) collective-permute-start(f32[25,8,128]{2,1,0:T(8,128)S(1)} %get-tuple-element.23), channel_id=1, source_target_pairs={{0,2},{1,3},{2,0},{3,1},{4,6},{5,7},{6,4},{7,5},{8,10},{9,11},{10,... | collective-permute-start | bytes 307208 | tf_op jit(solution)/shard_map/ppermute | solution.py:16
  24.6 8.5 %collective-permute-start.11 = (f32[32,768]{1,0:T(8,128)S(1)}, f32[32,768]{1,0:T(8,128)S(1)}, u32[]{:S(2)}, u32[]{:S(2)}) collective-permute-start(f32[32,768]{1,0:T(8,128)S(1)} %get-tuple-element.26), channel_id=1, source_target_pairs={{0,24},{4,28},{8,16},{12,20},{16,8},{20,12},{24,0},{28,4},{1,25},{... | collective-permute-start | bytes 294920 | tf_op jit(solution)/shard_map/ppermute | solution.py:24
  25.8 7.4 %collective-permute-start.12 = (f32[32,768]{1,0:T(8,128)S(1)}, f32[32,768]{1,0:T(8,128)S(1)}, u32[]{:S(2)}, u32[]{:S(2)}) collective-permute-start(f32[32,768]{1,0:T(8,128)S(1)} %get-tuple-element.28), channel_id=1, source_target_pairs={{0,8},{4,20},{8,0},{12,28},{16,24},{20,4},{24,16},{28,12},{1,9},{5... | collective-permute-start | bytes 294920 | tf_op jit(solution)/shard_map/ppermute | solution.py:24
  26.7 6.5 %collective-permute-start.13 = (f32[32,768]{1,0:T(8,128)S(1)}, f32[32,768]{1,0:T(8,128)S(1)}, u32[]{:S(2)}, u32[]{:S(2)}) collective-permute-start(f32[32,768]{1,0:T(8,128)S(1)} %get-tuple-element.29), channel_id=1, source_target_pairs={{0,16},{4,12},{8,24},{12,4},{16,0},{20,28},{24,8},{28,20},{1,17},{... | collective-permute-start | bytes 294920 | tf_op jit(solution)/shard_map/ppermute | solution.py:24

commit v23 on v15

--- a/solution.py
+++ b/solution.py
@@ -136,7 +136,9 @@
     texts = halves(jnp.concatenate(own_core_texts(cols, both, sent, got)))
     ids = text_ids((texts[0].shape[0], count), n_img, cols, False)
     _, d = derivative(texts, others, ids, matched, log_scale, bias)
-    term = dot(halves(d_ref[...]), halves(bundle[:count]), (1, 0)) + dot(halves(d), others, (1, 0))
+    weights = jnp.concatenate([d_ref[...], d], axis=1)
+    images = [jnp.concatenate(parts) for parts in zip(halves(bundle[:count]), others)]
+    term = dot(halves(weights), images, (1, 0))
     for k, ref in enumerate(block_refs):
         ref[...] = term[k * cols:(k + 1) * cols]
 

time: 32.5 us -> 32.5 us (level)
  no operation moved by 1% of the time
where the time goes in v23:
time: 32.5 us; the launch traced here: 32.3 us
  starting transfers between devices  16.5 us (51%)
  waiting for transfers between devices  9.71 us (30%)
  Pallas kernels  2.78 us (9%)
  between operations  2.1 us (6%)
  local copies, waits for them, and re-layouts  1.24 us (4%)
    ppermute x9, starting transfers between devices, exchange(): return lax.ppermute(x, axis, [(i, i ^ k) for i in range(n)])  9.86 us
    ppermute x9, waiting for transfers between devices, exchange(): return lax.ppermute(x, axis, [(i, i ^ k) for i in range(n)])  9.7 us
    ppermute x5, starting transfers between devices, chip_exchange(): lax.ppermute(x, 'img', [(i, i ^ 2 * distances[i % 2]) for i in range(n_im...  6.6 us
    unnamed x12, local copies, waits for them, and re-layouts  1.21 us
    pallas_call x1, Pallas kernels, per_device(): pl.pallas_call(functools.partial(image_kernel, n_img, n_txt, rows, cols),...  1.17 us
    pallas_call x1, Pallas kernels, per_device(): pl.pallas_call(functools.partial(text_kernel, n_img, n_txt, rows, cols),...  0.87 us
    pallas_call x1, Pallas kernels, per_device(): pl.pallas_call(functools.partial(sum_kernel, n_txt, chips), out_shape=[ja...  0.74 us
  transfers between devices with their start and end apart: 14, of which 5 were waited for; matrix products, arithmetic and copies ran while one was open for 3% of the time, Pallas kernels for 6%

profile of v23, /device:TPU:0, one launch (start us, length us, event | category | flops | bytes accessed | tf_op | source)
XLA Modules:
  0.0 32.3 jit_solution(11345911239986919793)
XLA Ops:
  0.6 0.0 copy-start.1
  0.6 0.0 copy-start.2
  0.7 4.1 %collective-permute-start = (f32[32,768]{1,0:T(8,128)}, f32[32,768]{1,0:T(8,128)S(1)}, u32[]{:S(2)}, u32[]{:S(2)}) collective-permute-start(f32[32,768]{1,0:T(8,128)} %param.5), channel_id=1, source_target_pairs={{0,2},{1,3},{2,0},{3,1},{4,6},{5,7},{6,4},{7,5},{8,10},{9,11},{10,... | collective-permute-start | bytes 294920 | tf_op jit(solution)/shard_map/ppermute | solution.py:16
  4.8 1.3 %collective-permute-start.1 = (f32[32,768]{1,0:T(8,128)}, f32[32,768]{1,0:T(8,128)S(1)}, u32[]{:S(2)}, u32[]{:S(2)}) collective-permute-start(f32[32,768]{1,0:T(8,128)} %param.5), channel_id=1, source_target_pairs={{0,3},{1,2},{2,1},{3,0},{4,7},{5,6},{6,5},{7,4},{8,11},{9,10},{10,... | collective-permute-start | bytes 294920 | tf_op jit(solution)/shard_map/ppermute | solution.py:16
  6.1 0.0 collective-permute-start.2
  6.1 2.4 %collective-permute-start.5 = (f32[32,768]{1,0:T(8,128)}, f32[32,768]{1,0:T(8,128)S(1)}, u32[]{:S(2)}, u32[]{:S(2)}) collective-permute-start(f32[32,768]{1,0:T(8,128)} %param.6), channel_id=1, source_target_pairs={{0,24},{4,28},{8,16},{12,20},{16,8},{20,12},{24,0},{28,4},{1,25},{... | collective-permute-start | bytes 294920 | tf_op jit(solution)/shard_map/ppermute | solution.py:24
  8.6 0.9 %constant_dynamic-update-slice_fusion.5 = f32[136,768]{1,0:T(8,128)S(1)} fusion(f32[32,768]{1,0:T(8,128)} %param.5), kind=kLoop, calls=%fused_computation.6 | loop fusion | bytes 196608
  9.5 0.0 copy-done.2
  9.5 0.0 copy-done.1
  9.5 0.0 copy-start
  9.5 0.0 collective-permute-done.2
  9.5 0.6 %collective-permute-start.4 = (f32[64,768]{1,0:T(8,128)S(1)}, f32[64,768]{1,0:T(8,128)S(1)}, u32[]{:S(2)}, u32[]{:S(2)}) collective-permute-start(f32[64,768]{1,0:T(8,128)S(1)} %constant_dynamic-update-slice_fusion.both.refs_4_), channel_id=1, source_target_pairs={{0,8},{4,20},{8,0},{12,28},{16,24},{20,4},{24,16},{28,12},{1,9},{5... | collective-permute-start | bytes 589832 | tf_op jit(solution)/shard_map/ppermute | solution.py:24
  10.1 0.3 copy-done
  10.4 0.2 collective-permute-start.3
  10.6 2.2 %collective-permute-done = f32[32,768]{1,0:T(8,128)S(1)} collective-permute-done((f32[32,768]{1,0:T(8,128)}, f32[32,768]{1,0:T(8,128)S(1)}, u32[]{:S(2)}, u32[]{:S(2)}) %collective-permute-start) | collective-permute-done | bytes 98336 | tf_op jit(solution)/shard_map/ppermute | solution.py:16
  12.8 0.0 collective-permute-done.1
  12.8 2.5 %collective-permute-done.3 = f32[32,768]{1,0:T(8,128)S(1)} collective-permute-done((f32[32,768]{1,0:T(8,128)S(1)}, f32[32,768]{1,0:T(8,128)S(1)}, u32[]{:S(2)}, u32[]{:S(2)}) %collective-permute-start.3) | collective-permute-done | bytes 98336 | tf_op jit(solution)/shard_map/ppermute | solution.py:16
  15.3 0.1 collective-permute-start.10
  15.4 0.0 collective-permute-done.4
  15.5 0.0 collective-permute-done.5
  15.5 0.6 %collective-permute-start.6 = (f32[96,768]{1,0:T(8,128)S(1)}, f32[96,768]{1,0:T(8,128)S(1)}, u32[]{:S(2)}, u32[]{:S(2)}) collective-permute-start(f32[96,768]{1,0:T(8,128)S(1)} %constant_dynamic-update-slice_fusion.6.sent.refs_5_), channel_id=1, source_target_pairs={{0,4},{4,0},{8,12},{12,8},{16,20},{20,16},{24,28},{28,24},{1,5},{5... | collective-permute-start | bytes 884744 | tf_op jit(solution)/shard_map/ppermute | solution.py:16
  17.3 0.3 collective-permute-done.6.got.refs_6_
  17.6 1.2 %image_terms.1 = (f32[32,768]{1,0:T(8,128)S(1)}, f32[8,128]{1,0:T(8,128)S(1)}, f32[128,128]{1,0:T(8,128)S(1)}, f32[25,8,128]{2,1,0:T(8,128)S(1)}, f32[25,8,128]{2,1,0:T(8,128)S(1)}, /*index=5*/f32[25,8,128]{2,1,0:T(8,128)S(1)}) custom-call(f32[1]{0:T(128)S(6)} %copy.14.log_scale.refs_0_, f32[1]{0:T(128)S(6)} %copy.15.bias.refs_1_, ...), custom_call_target="tpu_custom_call" | custom-call | tf_op jit(solution)/shard_map/image_terms/pallas_call | solution.py:187
  18.8 0.3 %collective-permute-start.7 = (f32[25,8,128]{2,1,0:T(8,128)S(1)}, f32[25,8,128]{2,1,0:T(8,128)S(1)}, u32[]{:S(2)}, u32[]{:S(2)}) collective-permute-start(f32[25,8,128]{2,1,0:T(8,128)S(1)} %get-tuple-element.20), channel_id=1, source_target_pairs={{0,1},{1,0},{2,3},{3,2},{4,5},{5,4},{6,7},{7,6},{8,9},{9,8},{10,11... | collective-permute-start | bytes 307208 | tf_op jit(solution)/shard_map/ppermute | solution.py:16
  19.1 2.9 %collective-permute-start.8 = (f32[25,8,128]{2,1,0:T(8,128)S(1)}, f32[25,8,128]{2,1,0:T(8,128)S(1)}, u32[]{:S(2)}, u32[]{:S(2)}) collective-permute-start(f32[25,8,128]{2,1,0:T(8,128)S(1)} %get-tuple-element.21), channel_id=1, source_target_pairs={{0,3},{1,2},{2,1},{3,0},{4,7},{5,6},{6,5},{7,4},{8,11},{9,10},{10,... | collective-permute-start | bytes 307208 | tf_op jit(solution)/shard_map/ppermute | solution.py:16
  22.0 0.3 %collective-permute-start.9 = (f32[25,8,128]{2,1,0:T(8,128)S(1)}, f32[25,8,128]{2,1,0:T(8,128)S(1)}, u32[]{:S(2)}, u32[]{:S(2)}) collective-permute-start(f32[25,8,128]{2,1,0:T(8,128)S(1)} %get-tuple-element.22), channel_id=1, source_target_pairs={{0,2},{1,3},{2,0},{3,1},{4,6},{5,7},{6,4},{7,5},{8,10},{9,11},{10,... | collective-permute-start | bytes 307208 | tf_op jit(solution)/shard_map/ppermute | solution.py:16
  22.3 0.0 collective-permute-done.10.refs_3_
  22.3 0.9 %text_terms.1 = (f32[32,768]{1,0:T(8,128)S(1)}, f32[32,768]{1,0:T(8,128)S(1)}, f32[32,768]{1,0:T(8,128)S(1)}, f32[32,768]{1,0:T(8,128)S(1)}) custom-call(f32[1]{0:T(128)S(6)} %copy.14.log_scale.refs_0_, f32[1]{0:T(128)S(6)} %copy.15.bias.refs_1_, f32[136,768]{1,0:T(8,128)S(1)} %pad_dynamic-update-slice_fusion.bundle.refs_2_, ...), custom_call_target="tpu_custom_call" | custom-call | tf_op jit(solution)/shard_map/text_terms/pallas_call | solution.py:198
  23.2 1.9 %collective-permute-start.11 = (f32[32,768]{1,0:T(8,128)S(1)}, f32[32,768]{1,0:T(8,128)S(1)}, u32[]{:S(2)}, u32[]{:S(2)}) collective-permute-start(f32[32,768]{1,0:T(8,128)S(1)} %get-tuple-element.24), channel_id=1, source_target_pairs={{0,24},{4,28},{8,16},{12,20},{16,8},{20,12},{24,0},{28,4},{1,25},{... | collective-permute-start | bytes 294920 | tf_op jit(solution)/shard_map/ppermute | solution.py:24
  25.1 0.8 %collective-permute-start.12 = (f32[32,768]{1,0:T(8,128)S(1)}, f32[32,768]{1,0:T(8,128)S(1)}, u32[]{:S(2)}, u32[]{:S(2)}) collective-permute-start(f32[32,768]{1,0:T(8,128)S(1)} %get-tuple-element.26), channel_id=1, source_target_pairs={{0,8},{4,20},{8,0},{12,28},{16,24},{20,4},{24,16},{28,12},{1,9},{5... | collective-permute-start | bytes 294920 | tf_op jit(solution)/shard_map/ppermute | solution.py:24
  25.9 0.0 collective-permute-done.7.refs_0_
  25.9 0.9 %collective-permute-start.13 = (f32[32,768]{1,0:T(8,128)S(1)}, f32[32,768]{1,0:T(8,128)S(1)}, u32[]{:S(2)}, u32[]{:S(2)}) collective-permute-start(f32[32,768]{1,0:T(8,128)S(1)} %get-tuple-element.27), channel_id=1, source_target_pairs={{0,16},{4,12},{8,24},{12,4},{16,0},{20,28},{24,8},{28,20},{1,17},{... | collective-permute-start | bytes 294920 | tf_op jit(solution)/shard_map/ppermute | solution.py:24
  26.8 1.2 %collective-permute-done.8.refs_1_ = f32[25,8,128]{2,1,0:T(8,128)S(1)} collective-permute-done((f32[25,8,128]{2,1,0:T(8,128)S(1)}, f32[25,8,128]{2,1,0:T(8,128)S(1)}, u32[]{:S(2)}, u32[]{:S(2)}) %collective-permute-start.8) | collective-permute-done | bytes 102432 | tf_op jit(solution)/shard_map/ppermute | solution.py:16
  28.0 3.6 %collective-permute-done.9.refs_2_ = f32[25,8,128]{2,1,0:T(8,128)S(1)} collective-permute-done((f32[25,8,128]{2,1,0:T(8,128)S(1)}, f32[25,8,128]{2,1,0:T(8,128)S(1)}, u32[]{:S(2)}, u32[]{:S(2)}) %collective-permute-start.9) | collective-permute-done | bytes 102432 | tf_op jit(solution)/shard_map/ppermute | solution.py:16
  31.5 0.0 collective-permute-done.11.refs_3_
  31.5 0.0 collective-permute-done.12.refs_5_
  31.5 0.0 collective-permute-done.13.refs_6_
  31.5 0.7 %sums.1 = (f32[1,128]{1,0:T(1,128)}, f32[32,768]{1,0:T(8,128)}, f32[32,768]{1,0:T(8,128)}) custom-call(f32[32,768]{1,0:T(8,128)S(1)} %get-tuple-element.18.own_ref, f32[8,128]{1,0:T(8,128)S(1)} %get-tuple-element.19.loss_ref, f32[25,8,128]{2,1,0:T(8,128)S(1)} %collective-permute-done.7.refs_0_, f32[25,8,128]{2,1,0:T(8,128)S(1)} %collective-permute-done.8.refs_1_, ...), custom_call_target="tpu_custom_call" | custom-call | tf_op jit(solution)/shard_map/sums/pallas_call | solution.py:209
  (9 shorter events, 0.1 us)
Async XLA Ops:
  0.6 8.8 %copy-start.1 = (f32[32,768]{1,0:T(8,128)S(1)}, f32[32,768]{1,0:T(8,128)}, u32[]{:S(2)}) copy-start(f32[32,768]{1,0:T(8,128)} %param.6) | copy-start | bytes 294916
  0.6 8.8 %copy-start.2 = (s32[128]{0:T(128)S(1)}, s32[128]{0:T(128)}, u32[]{:S(2)}) copy-start(s32[128]{0:T(128)} %param.7) | copy-start | bytes 1540
  0.7 12.2 %collective-permute-start = (f32[32,768]{1,0:T(8,128)}, f32[32,768]{1,0:T(8,128)S(1)}, u32[]{:S(2)}, u32[]{:S(2)}) collective-permute-start(f32[32,768]{1,0:T(8,128)} %param.5), channel_id=1, source_target_pairs={{0,2},{1,3},{2,0},{3,1},{4,6},{5,7},{6,4},{7,5},{8,10},{9,11},{10,... | collective-permute-start | bytes 294920 | tf_op jit(solution)/shard_map/ppermute | solution.py:16
  4.8 8.1 %collective-permute-start.1 = (f32[32,768]{1,0:T(8,128)}, f32[32,768]{1,0:T(8,128)S(1)}, u32[]{:S(2)}, u32[]{:S(2)}) collective-permute-start(f32[32,768]{1,0:T(8,128)} %param.5), channel_id=1, source_target_pairs={{0,3},{1,2},{2,1},{3,0},{4,7},{5,6},{6,5},{7,4},{8,11},{9,10},{10,... | collective-permute-start | bytes 294920 | tf_op jit(solution)/shard_map/ppermute | solution.py:16
  6.1 3.4 %collective-permute-start.2 = (f32[32,768]{1,0:T(8,128)}, f32[32,768]{1,0:T(8,128)S(1)}, u32[]{:S(2)}, u32[]{:S(2)}) collective-permute-start(f32[32,768]{1,0:T(8,128)} %param.6), channel_id=1, source_target_pairs={{0,4},{4,0},{8,12},{12,8},{16,20},{20,16},{24,28},{28,24},{1,5},{5... | collective-permute-start | bytes 294920 | tf_op jit(solution)/shard_map/ppermute | solution.py:16
  6.1 9.4 %collective-permute-start.5 = (f32[32,768]{1,0:T(8,128)}, f32[32,768]{1,0:T(8,128)S(1)}, u32[]{:S(2)}, u32[]{:S(2)}) collective-permute-start(f32[32,768]{1,0:T(8,128)} %param.6), channel_id=1, source_target_pairs={{0,24},{4,28},{8,16},{12,20},{16,8},{20,12},{24,0},{28,4},{1,25},{... | collective-permute-start | bytes 294920 | tf_op jit(solution)/shard_map/ppermute | solution.py:24
  9.5 0.9 %copy-start = (f32[32,768]{1,0:T(8,128)S(1)}, f32[32,768]{1,0:T(8,128)}, u32[]{:S(2)}) copy-start(f32[32,768]{1,0:T(8,128)} %param.5) | copy-start | bytes 294916
  9.5 5.9 %collective-permute-start.4 = (f32[64,768]{1,0:T(8,128)S(1)}, f32[64,768]{1,0:T(8,128)S(1)}, u32[]{:S(2)}, u32[]{:S(2)}) collective-permute-start(f32[64,768]{1,0:T(8,128)S(1)} %constant_dynamic-update-slice_fusion.both.refs_4_), channel_id=1, source_target_pairs={{0,8},{4,20},{8,0},{12,28},{16,24},{20,4},{24,16},{28,12},{1,9},{5... | collective-permute-start | bytes 589832 | tf_op jit(solution)/shard_map/ppermute | solution.py:24
  10.4 4.9 %collective-permute-start.3 = (f32[32,768]{1,0:T(8,128)S(1)}, f32[32,768]{1,0:T(8,128)S(1)}, u32[]{:S(2)}, u32[]{:S(2)}) collective-permute-start(f32[32,768]{1,0:T(8,128)S(1)} %copy-done), channel_id=1, source_target_pairs={{0,1},{1,0},{2,3},{3,2},{4,5},{5,4},{6,7},{7,6},{8,9},{9,8},{10,11... | collective-permute-start | bytes 294920 | tf_op jit(solution)/shard_map/ppermute | solution.py:16
  15.3 7.0 %collective-permute-start.10 = (f32[136,768]{1,0:T(8,128)S(1)}, f32[136,768]{1,0:T(8,128)S(1)}, u32[]{:S(2)}, u32[]{:S(2)}) collective-permute-start(f32[136,768]{1,0:T(8,128)S(1)} %pad_dynamic-update-slice_fusion.bundle.refs_2_), channel_id=1, source_target_pairs={{0,4},{4,0},{8,12},{12,8},{16,20},{20,16},{24,28},{28,24},{1,5},{5... | collective-permute-start | bytes 1253384 | tf_op jit(solution)/shard_map/ppermute | solution.py:16
  15.5 2.1 %collective-permute-start.6 = (f32[96,768]{1,0:T(8,128)S(1)}, f32[96,768]{1,0:T(8,128)S(1)}, u32[]{:S(2)}, u32[]{:S(2)}) collective-permute-start(f32[96,768]{1,0:T(8,128)S(1)} %constant_dynamic-update-slice_fusion.6.sent.refs_5_), channel_id=1, source_target_pairs={{0,4},{4,0},{8,12},{12,8},{16,20},{20,16},{24,28},{28,24},{1,5},{5... | collective-permute-start | bytes 884744 | tf_op jit(solution)/shard_map/ppermute | solution.py:16
  18.8 7.1 %collective-permute-start.7 = (f32[25,8,128]{2,1,0:T(8,128)S(1)}, f32[25,8,128]{2,1,0:T(8,128)S(1)}, u32[]{:S(2)}, u32[]{:S(2)}) collective-permute-start(f32[25,8,128]{2,1,0:T(8,128)S(1)} %get-tuple-element.20), channel_id=1, source_target_pairs={{0,1},{1,0},{2,3},{3,2},{4,5},{5,4},{6,7},{7,6},{8,9},{9,8},{10,11... | collective-permute-start | bytes 307208 | tf_op jit(solution)/shard_map/ppermute | solution.py:16
  19.1 8.9 %collective-permute-start.8 = (f32[25,8,128]{2,1,0:T(8,128)S(1)}, f32[25,8,128]{2,1,0:T(8,128)S(1)}, u32[]{:S(2)}, u32[]{:S(2)}) collective-permute-start(f32[25,8,128]{2,1,0:T(8,128)S(1)} %get-tuple-element.21), channel_id=1, source_target_pairs={{0,3},{1,2},{2,1},{3,0},{4,7},{5,6},{6,5},{7,4},{8,11},{9,10},{10,... | collective-permute-start | bytes 307208 | tf_op jit(solution)/shard_map/ppermute | solution.py:16
  22.0 9.6 %collective-permute-start.9 = (f32[25,8,128]{2,1,0:T(8,128)S(1)}, f32[25,8,128]{2,1,0:T(8,128)S(1)}, u32[]{:S(2)}, u32[]{:S(2)}) collective-permute-start(f32[25,8,128]{2,1,0:T(8,128)S(1)} %get-tuple-element.22), channel_id=1, source_target_pairs={{0,2},{1,3},{2,0},{3,1},{4,6},{5,7},{6,4},{7,5},{8,10},{9,11},{10,... | collective-permute-start | bytes 307208 | tf_op jit(solution)/shard_map/ppermute | solution.py:16
  23.2 8.3 %collective-permute-start.11 = (f32[32,768]{1,0:T(8,128)S(1)}, f32[32,768]{1,0:T(8,128)S(1)}, u32[]{:S(2)}, u32[]{:S(2)}) collective-permute-start(f32[32,768]{1,0:T(8,128)S(1)} %get-tuple-element.24), channel_id=1, source_target_pairs={{0,24},{4,28},{8,16},{12,20},{16,8},{20,12},{24,0},{28,4},{1,25},{... | collective-permute-start | bytes 294920 | tf_op jit(solution)/shard_map/ppermute | solution.py:24
  25.1 6.4 %collective-permute-start.12 = (f32[32,768]{1,0:T(8,128)S(1)}, f32[32,768]{1,0:T(8,128)S(1)}, u32[]{:S(2)}, u32[]{:S(2)}) collective-permute-start(f32[32,768]{1,0:T(8,128)S(1)} %get-tuple-element.26), channel_id=1, source_target_pairs={{0,8},{4,20},{8,0},{12,28},{16,24},{20,4},{24,16},{28,12},{1,9},{5... | collective-permute-start | bytes 294920 | tf_op jit(solution)/shard_map/ppermute | solution.py:24
  25.9 5.7 %collective-permute-start.13 = (f32[32,768]{1,0:T(8,128)S(1)}, f32[32,768]{1,0:T(8,128)S(1)}, u32[]{:S(2)}, u32[]{:S(2)}) collective-permute-start(f32[32,768]{1,0:T(8,128)S(1)} %get-tuple-element.27), channel_id=1, source_target_pairs={{0,16},{4,12},{8,24},{12,4},{16,0},{20,28},{24,8},{28,20},{1,17},{... | collective-permute-start | bytes 294920 | tf_op jit(solution)/shard_map/ppermute | solution.py:24
